TPU v7x, 32 devices: a whole 2x2x4 slice. The times are simulated.
32 devices in a mesh: groups: 2 (over x), tok: 16 (over z, y, core).
Axes of the slice: x: 2, y: 2, z: 4, core: 2. Of those that a mesh axis runs over, the one named last changes fastest.
Arguments:
- query_tokens: bfloat16 [3, 4096, 1024], P(None, ('groups', 'tok')), parts along dimension 1, may hold values from -6 to 6
- key_tokens: bfloat16 [3, 4096, 1024], P(None, ('groups', 'tok')), parts along dimension 1, may hold values from -6 to 6
- value_tokens: bfloat16 [3, 4096, 1024], P(None, ('groups', 'tok')), parts along dimension 1, may hold values from -6 to 6
- learn_rates: float32 [3, 4096, 2], P(None, ('groups', 'tok')), parts along dimension 1, may hold values from 0.0009765625 to 0.00390625
- fast_first: bfloat16 [2, 512, 512], P(None, 'tok'), may hold values from -0.25 to 0.25
- fast_third: bfloat16 [2, 512, 512], P(None, 'tok'), may hold values from -0.25 to 0.25
- fast_second: bfloat16 [2, 512, 512], P(None, 'tok'), may hold values from -0.25 to 0.25
- momentum_decay: float32 [2], replicated, may hold values from 0.3 to 0.95
Outputs:
- readout: bfloat16 [3, 4096, 1024], P(None, ('groups', 'tok')), parts along dimension 1
There are 2 independent parts, one for each index of `groups`. A program takes and returns all parts, laid end to end along the dimension named above; an argument that names none is the same for every part. Nothing has to cross between parts.
All inputs are finite; a program needn't handle non-finite values.
Results may differ from a plain program's by a relative error of at most 0.0089.
Values may be sent and summed in bfloat16 or wider, within the bound.
No kernel may reach another device: no remote copies, remote signals or barrier semaphores. Data moves between devices by JAX's collectives and lax.ppermute only.
A program may use at most 64 MiB of HBM per device.

v0:
```python
import jax
import jax.numpy as jnp
from jax import lax
from jax.sharding import PartitionSpec as P


def forward_parts(weights, inputs):
    first, third, second = weights
    length = inputs.shape[0]
    head_count = first.shape[0]
    shaped = inputs.reshape(length, head_count, -1)
    pre_gate = jnp.einsum("thd,hfd->htf", shaped, first, preferred_element_type=jnp.float32)
    pre_up = jnp.einsum("thd,hfd->htf", shaped, third, preferred_element_type=jnp.float32)
    hidden = (jax.nn.silu(pre_gate) * pre_up).astype(jnp.bfloat16)
    return (shaped, pre_gate, pre_up, hidden)


def apply_block(weights, inputs):
    shaped, pre_gate, pre_up, hidden = forward_parts(weights, inputs)
    result = jnp.einsum("htf,hdf->thd", hidden, weights[2], preferred_element_type=jnp.float32)
    return result.reshape(inputs.shape[0], -1).astype(jnp.bfloat16)


def partial_steps(weights, keys, values, rates):
    shaped, pre_gate, pre_up, hidden = forward_parts(weights, keys)
    length = keys.shape[0]
    head_count = weights[0].shape[0]
    scaled = (
        rates[:, :, None] * values.reshape(length, head_count, -1).astype(jnp.float32)
    ).astype(jnp.bfloat16)
    step_second = jnp.einsum("thd,htf->hdf", scaled, hidden, preferred_element_type=jnp.float32)
    back = jnp.einsum("thd,hdf->htf", scaled, weights[2], preferred_element_type=jnp.float32)
    sig_gate = jax.nn.sigmoid(pre_gate)
    d_gate = (back * pre_up * sig_gate * (1.0 + pre_gate * (1.0 - sig_gate))).astype(jnp.bfloat16)
    d_up = (back * pre_gate * sig_gate).astype(jnp.bfloat16)
    step_first = jnp.einsum("htf,thd->hfd", d_gate, shaped, preferred_element_type=jnp.float32)
    step_third = jnp.einsum("htf,thd->hfd", d_up, shaped, preferred_element_type=jnp.float32)
    return (step_first, step_third, step_second)


def summed_steps(terms):
    return (
        lax.psum_scatter(terms[0], "tok", scatter_dimension=1, tiled=True),
        lax.psum_scatter(terms[1], "tok", scatter_dimension=1, tiled=True),
        lax.psum_scatter(terms[2], "tok", scatter_dimension=1, tiled=True),
    )


def renorm(old, moved):
    old_norm = jnp.sqrt(jnp.sum(old * old, axis=-1, keepdims=True) + 1e-06)
    moved_norm = jnp.sqrt(jnp.sum(moved * moved, axis=-1, keepdims=True) + 1e-06)
    return moved * old_norm / moved_norm


def full_steps(owned):
    return (
        lax.all_gather(owned[0], "tok", axis=1, tiled=True),
        lax.all_gather(owned[1], "tok", axis=1, tiled=True),
        lax.all_gather(owned[2], "tok", axis=1, tiled=True),
    )


def shards(
    query_tokens,
    key_tokens,
    value_tokens,
    learn_rates,
    fast_first,
    fast_third,
    fast_second,
    momentum_decay,
):
    full_zero = (
        lax.all_gather(fast_first, "tok", axis=1, tiled=True),
        lax.all_gather(fast_third, "tok", axis=1, tiled=True),
        lax.all_gather(fast_second, "tok", axis=1, tiled=True),
    )
    out_zero = apply_block(full_zero, query_tokens[0])
    terms_zero = partial_steps(full_zero, key_tokens[0], value_tokens[0], learn_rates[0])
    terms_one = partial_steps(full_zero, key_tokens[1], value_tokens[1], learn_rates[1])
    step_zero = summed_steps(terms_zero)
    decay = momentum_decay[:, None, None]
    weights_zero = tuple((w.astype(jnp.float32) for w in full_zero))
    whole_zero = full_steps(step_zero)
    weights_one = tuple((renorm(w, w + m) for w, m in zip(weights_zero, whole_zero)))
    full_one = tuple((w.astype(jnp.bfloat16) for w in weights_one))
    out_one = apply_block(full_one, query_tokens[1])
    step_one = summed_steps(terms_one)
    whole_one = full_steps(step_one)
    moment = tuple((decay * m + s for m, s in zip(whole_zero, whole_one)))
    weights_two = tuple((renorm(w, w + m) for w, m in zip(weights_one, moment)))
    full_two = tuple((w.astype(jnp.bfloat16) for w in weights_two))
    out_two = apply_block(full_two, query_tokens[2])
    return jnp.stack([out_zero, out_one, out_two])


def solution(mesh):
    placed = (
        P(None, ("groups", "tok"), None),
        P(None, ("groups", "tok"), None),
        P(None, ("groups", "tok"), None),
        P(None, ("groups", "tok"), None),
        P(None, "tok", None),
        P(None, "tok", None),
        P(None, "tok", None),
        P(),
    )
    return jax.shard_map(
        shards,
        mesh=mesh,
        in_specs=placed,
        out_specs=P(None, ("groups", "tok"), None),
        check_vma=False,
    )
```

profile of v0, /device:TPU:0, one launch (start us, length us, event | category | flops | bytes accessed | tf_op | source)
XLA Modules:
  0.0 798.7 jit_solution(18446105568856472642)
XLA Ops:
  10.6 39.6 %all-gather.10.cloned.1.call-done = bf16[2,512,512]{2,1,0:T(8,128)(2,1)} async-done(((bf16[2,32,512]{2,1,0:T(8,128)(2,1)}), bf16[2,512,512]{2,1,0:T(8,128)(2,1)}) %all-gather.10.cloned.1.call-update) | async-done | bytes 1048592 | tf_op jit(solution)/shard_map/all_gather | solution.py:74
  51.9 37.4 %all-gather.12.cloned.1.call-done = bf16[2,512,512]{2,1,0:T(8,128)(2,1)} async-done(((bf16[2,32,512]{2,1,0:T(8,128)(2,1)}), bf16[2,512,512]{2,1,0:T(8,128)(2,1)}) %all-gather.12.cloned.1.call-update) | async-done | bytes 1048592 | tf_op jit(solution)/shard_map/all_gather | solution.py:75
  91.0 1.9 fusion.33
  93.0 35.4 %all-gather.14.cloned.1.call-done = bf16[2,512,512]{2,1,0:T(8,128)(2,1)} async-done(((bf16[2,32,512]{2,1,0:T(8,128)(2,1)}), bf16[2,512,512]{2,1,0:T(8,128)(2,1)}) %all-gather.14.cloned.1.call-update) | async-done | bytes 1048592 | tf_op jit(solution)/shard_map/all_gather | solution.py:76
  130.0 1.9 fusion.34
  132.0 1.8 fusion.35
  137.1 1.9 fusion.36
  141.4 1.9 fusion.37
  143.3 3.1 fusion.38
  146.5 46.1 %reduce-scatter.7.cloned.1.call-done = f32[2,32,512]{2,1,0:T(8,128)} async-done(((f32[2,512,512]{2,1,0:T(8,128)}), f32[2,32,512]{2,1,0:T(8,128)}) %reduce-scatter.7.cloned.1.call-update) | async-done | bytes 131088 | tf_op jit(solution)/shard_map/reduce_scatter | solution.py:45
  192.6 64.6 %reduce-scatter.9.cloned.1.call-done = f32[2,32,512]{2,1,0:T(8,128)} async-done(((f32[2,512,512]{2,1,0:T(8,128)}), f32[2,32,512]{2,1,0:T(8,128)}) %reduce-scatter.9.cloned.1.call-update) | async-done | bytes 131088 | tf_op jit(solution)/shard_map/reduce_scatter | solution.py:43
  257.3 64.1 %reduce-scatter.11.cloned.1.call-done = f32[2,32,512]{2,1,0:T(8,128)} async-done(((f32[2,512,512]{2,1,0:T(8,128)}), f32[2,32,512]{2,1,0:T(8,128)}) %reduce-scatter.11.cloned.1.call-update) | async-done | bytes 131088 | tf_op jit(solution)/shard_map/reduce_scatter | solution.py:44
  321.5 64.7 %reduce-scatter.13.cloned.1.call-done = f32[2,32,512]{2,1,0:T(8,128)} async-done(((f32[2,512,512]{2,1,0:T(8,128)}), f32[2,32,512]{2,1,0:T(8,128)}) %reduce-scatter.13.cloned.1.call-update) | async-done | bytes 131088 | tf_op jit(solution)/shard_map/reduce_scatter | solution.py:45
  386.3 64.3 %reduce-scatter.15.cloned.1.call-done = f32[2,32,512]{2,1,0:T(8,128)} async-done(((f32[2,512,512]{2,1,0:T(8,128)}), f32[2,32,512]{2,1,0:T(8,128)}) %reduce-scatter.15.cloned.1.call-update) | async-done | bytes 131088 | tf_op jit(solution)/shard_map/reduce_scatter | solution.py:43
  450.8 64.5 %reduce-scatter.17.cloned.1.call-done = f32[2,32,512]{2,1,0:T(8,128)} async-done(((f32[2,512,512]{2,1,0:T(8,128)}), f32[2,32,512]{2,1,0:T(8,128)}) %reduce-scatter.17.cloned.1.call-update) | async-done | bytes 131088 | tf_op jit(solution)/shard_map/reduce_scatter | solution.py:44
  515.3 2.0 fusion.63
  518.5 1.8 copy.70
  520.2 1.8 copy.72
  523.3 2.6 fusion.8
  527.0 30.7 %all-gather.16.cloned.1.call-done = f32[2,512,512]{2,1,0:T(8,128)} async-done(((f32[2,32,512]{2,1,0:T(8,128)}), f32[2,512,512]{2,1,0:T(8,128)}) %all-gather.16.cloned.1.call-update) | async-done | bytes 2097168 | tf_op jit(solution)/shard_map/all_gather | solution.py:59
  557.8 2.1 fusion
  559.9 40.3 %all-gather.18.cloned.1.call-done = f32[2,512,512]{2,1,0:T(8,128)} async-done(((f32[2,32,512]{2,1,0:T(8,128)}), f32[2,512,512]{2,1,0:T(8,128)}) %all-gather.18.cloned.1.call-update) | async-done | bytes 2097168 | tf_op jit(solution)/shard_map/all_gather | solution.py:57
  600.2 2.1 fusion.1
  602.3 40.2 %all-gather.20.cloned.1.call-done = f32[2,512,512]{2,1,0:T(8,128)} async-done(((f32[2,32,512]{2,1,0:T(8,128)}), f32[2,512,512]{2,1,0:T(8,128)}) %all-gather.20.cloned.1.call-update) | async-done | bytes 2097168 | tf_op jit(solution)/shard_map/all_gather | solution.py:58
  642.5 2.1 fusion.2
  644.6 40.3 %all-gather.22.cloned.1.call-done = f32[2,512,512]{2,1,0:T(8,128)} async-done(((f32[2,32,512]{2,1,0:T(8,128)}), f32[2,512,512]{2,1,0:T(8,128)}) %all-gather.22.cloned.1.call-update) | async-done | bytes 2097168 | tf_op jit(solution)/shard_map/all_gather | solution.py:59
  684.9 42.3 %all-gather.24.cloned.1.call-done = f32[2,512,512]{2,1,0:T(8,128)} async-done(((f32[2,32,512]{2,1,0:T(8,128)}), f32[2,512,512]{2,1,0:T(8,128)}) %all-gather.24.cloned.1.call-update) | async-done | bytes 2097168 | tf_op jit(solution)/shard_map/all_gather | solution.py:57
  727.2 42.3 %all-gather.26.cloned.1.call-done = f32[2,512,512]{2,1,0:T(8,128)} async-done(((f32[2,32,512]{2,1,0:T(8,128)}), f32[2,512,512]{2,1,0:T(8,128)}) %all-gather.26.cloned.1.call-update) | async-done | bytes 2097168 | tf_op jit(solution)/shard_map/all_gather | solution.py:58
  769.5 7.4 multiply_reduce_fusion
  778.5 4.1 convolution_convert_fusion
  782.6 3.1 convolution_bitcast_fusion.3
  785.8 4.2 convolution_convert_fusion.1
  (86 shorter events, 22.6 us)
Async XLA Ops:
  6.5 3.5 copy-start.9
  6.5 43.7 %all-gather.10.cloned.1.call-start = ((), (), s32[]{:S(2)}) async-start(), calls=%async_computation.6 | async-start | bytes 1114112 | tf_op jit(solution)/shard_map/all_gather | solution.py:74
  7.3 82.1 %all-gather.12.cloned.1.call-start = ((), (), s32[]{:S(2)}) async-start(), calls=%async_computation.7 | async-start | bytes 1114112 | tf_op jit(solution)/shard_map/all_gather | solution.py:75
  8.0 120.4 %all-gather.14.cloned.1.call-start = ((), (), s32[]{:S(2)}) async-start(), calls=%async_computation.8 | async-start | bytes 1114112 | tf_op jit(solution)/shard_map/all_gather | solution.py:76
  8.7 1.9 copy-start.12
  8.8 183.8 %reduce-scatter.7.cloned.1.call-start = ((), (), s32[]{:S(2)}) async-start(), calls=%async_computation.9 | async-start | bytes 2228224 | tf_op jit(solution)/shard_map/reduce_scatter | solution.py:45
  93.0 164.3 %reduce-scatter.9.cloned.1.call-start = ((), (), s32[]{:S(2)}) async-start(), calls=%async_computation.11 | async-start | bytes 2228224 | tf_op jit(solution)/shard_map/reduce_scatter | solution.py:43
  131.9 189.5 %reduce-scatter.11.cloned.1.call-start = ((), (), s32[]{:S(2)}) async-start(), calls=%async_computation.13 | async-start | bytes 2228224 | tf_op jit(solution)/shard_map/reduce_scatter | solution.py:44
  133.8 1.5 copy-start
  133.8 2.0 copy-start.1
  133.8 252.4 %reduce-scatter.13.cloned.1.call-start = ((), (), s32[]{:S(2)}) async-start(), calls=%async_computation.15 | async-start | bytes 2228224 | tf_op jit(solution)/shard_map/reduce_scatter | solution.py:45
  135.3 1.8 copy-start.8
  135.8 0.8 copy-start.3
  136.3 0.8 copy-start.5
  137.1 2.0 copy-start.2
  139.0 311.5 %reduce-scatter.15.cloned.1.call-start = ((), (), s32[]{:S(2)}) async-start(), calls=%async_computation.17 | async-start | bytes 2228224 | tf_op jit(solution)/shard_map/reduce_scatter | solution.py:43
  139.1 2.3 copy-start.4
  139.1 2.3 copy-start.6
  140.6 0.8 copy-start.7
  143.3 372.0 %reduce-scatter.17.cloned.1.call-start = ((), (), s32[]{:S(2)}) async-start(), calls=%async_computation.19 | async-start | bytes 2228224 | tf_op jit(solution)/shard_map/reduce_scatter | solution.py:44
  146.4 411.3 %all-gather.16.cloned.1.call-start = ((), (), s32[]{:S(2)}) async-start(), calls=%async_computation.10 | async-start | bytes 2228224 | tf_op jit(solution)/shard_map/all_gather | solution.py:59
  192.6 407.6 %all-gather.18.cloned.1.call-start = ((), (), s32[]{:S(2)}) async-start(), calls=%async_computation.12 | async-start | bytes 2228224 | tf_op jit(solution)/shard_map/all_gather | solution.py:57
  257.2 385.2 %all-gather.20.cloned.1.call-start = ((), (), s32[]{:S(2)}) async-start(), calls=%async_computation.14 | async-start | bytes 2228224 | tf_op jit(solution)/shard_map/all_gather | solution.py:58
  321.4 363.5 %all-gather.22.cloned.1.call-start = ((), (), s32[]{:S(2)}) async-start(), calls=%async_computation.16 | async-start | bytes 2228224 | tf_op jit(solution)/shard_map/all_gather | solution.py:59
  386.2 341.0 %all-gather.24.cloned.1.call-start = ((), (), s32[]{:S(2)}) async-start(), calls=%async_computation.18 | async-start | bytes 2228224 | tf_op jit(solution)/shard_map/all_gather | solution.py:57
  450.5 318.9 %all-gather.26.cloned.1.call-start = ((), (), s32[]{:S(2)}) async-start(), calls=%async_computation.20 | async-start | bytes 2228224 | tf_op jit(solution)/shard_map/all_gather | solution.py:58
  602.3 167.2 %copy-start.13 = (f32[2]{0:T(128)S(1)}, f32[2]{0:T(128)}, u32[]{:S(2)}) copy-start(f32[2]{0:T(128)} %param.15) | copy-start | bytes 28
  769.5 7.6 copy-start.10
  785.8 4.2 copy-start.11
Sparse Core Ops, SparseCore 0:
  9.5 40.6 all-gather.9
  52.4 36.8 all-gather.11
  91.5 36.8 all-gather.13
  132.0 60.4 reduce-scatter.6
  196.6 60.5 reduce-scatter.8
  260.8 60.5 reduce-scatter.10
  325.6 60.5 reduce-scatter.12
  389.9 60.5 reduce-scatter.14
  454.7 60.5 reduce-scatter.16
  517.3 40.4 all-gather.15
  560.0 40.1 all-gather.17
  602.2 40.1 all-gather.19
  644.7 40.1 all-gather.21
  686.9 40.1 all-gather.23
  729.2 40.1 all-gather.25
where the time goes:
time: 799 us
  waiting for transfers between devices  719 us (90%)
  matrix products  36.7 us (5%)
  other arithmetic  14.9 us (2%)
  local copies, waits for them, and re-layouts  13.7 us (2%)
  between operations  13.6 us (2%)
    reduce_scatter x2, waiting for transfers between devices, summed_steps(): lax.psum_scatter(terms[0], 'tok', scatter_dimension=1, tiled=True)  129 us
    reduce_scatter x2, waiting for transfers between devices, summed_steps(): lax.psum_scatter(terms[1], 'tok', scatter_dimension=1, tiled=True)  129 us
    reduce_scatter x2, waiting for transfers between devices, summed_steps(): lax.psum_scatter(terms[2], 'tok', scatter_dimension=1, tiled=True)  111 us
    all_gather x2, waiting for transfers between devices, full_steps(): lax.all_gather(owned[0], 'tok', axis=1, tiled=True)  82.6 us
    all_gather x2, waiting for transfers between devices, full_steps(): lax.all_gather(owned[1], 'tok', axis=1, tiled=True)  82.4 us
    all_gather x2, waiting for transfers between devices, full_steps(): lax.all_gather(owned[2], 'tok', axis=1, tiled=True)  71.1 us
    all_gather x1, waiting for transfers between devices, shards(): lax.all_gather(fast_first, 'tok', axis=1, tiled=True)  39.6 us
    all_gather x1, waiting for transfers between devices, shards(): lax.all_gather(fast_third, 'tok', axis=1, tiled=True)  37.4 us
  transfers between devices with their start and end apart: 15, of which 15 were waited for; matrix products, arithmetic and copies ran while one was open for 5% of the time, Pallas kernels for 0%

commit v1 on v0

--- a/solution.py
+++ b/solution.py
@@ -38,26 +38,10 @@
     return (step_first, step_third, step_second)
 
 
-def summed_steps(terms):
-    return (
-        lax.psum_scatter(terms[0], "tok", scatter_dimension=1, tiled=True),
-        lax.psum_scatter(terms[1], "tok", scatter_dimension=1, tiled=True),
-        lax.psum_scatter(terms[2], "tok", scatter_dimension=1, tiled=True),
-    )
-
-
 def renorm(old, moved):
     old_norm = jnp.sqrt(jnp.sum(old * old, axis=-1, keepdims=True) + 1e-06)
     moved_norm = jnp.sqrt(jnp.sum(moved * moved, axis=-1, keepdims=True) + 1e-06)
     return moved * old_norm / moved_norm
-
-
-def full_steps(owned):
-    return (
-        lax.all_gather(owned[0], "tok", axis=1, tiled=True),
-        lax.all_gather(owned[1], "tok", axis=1, tiled=True),
-        lax.all_gather(owned[2], "tok", axis=1, tiled=True),
-    )
 
 
 def shards(
@@ -70,27 +54,26 @@
     fast_second,
     momentum_decay,
 ):
-    full_zero = (
-        lax.all_gather(fast_first, "tok", axis=1, tiled=True),
-        lax.all_gather(fast_third, "tok", axis=1, tiled=True),
-        lax.all_gather(fast_second, "tok", axis=1, tiled=True),
-    )
+    own = jnp.stack([fast_first, fast_third, fast_second])
+    full_zero = lax.all_gather(own, "tok", axis=2, tiled=True)
+    terms = [
+        jnp.stack(partial_steps(full_zero, key_tokens[b], value_tokens[b], learn_rates[b]))
+        for b in range(2)
+    ]
+    low = jnp.stack(terms).astype(jnp.bfloat16)
+    summed = lax.psum_scatter(low, "tok", scatter_dimension=3, tiled=True)
     out_zero = apply_block(full_zero, query_tokens[0])
-    terms_zero = partial_steps(full_zero, key_tokens[0], value_tokens[0], learn_rates[0])
-    terms_one = partial_steps(full_zero, key_tokens[1], value_tokens[1], learn_rates[1])
-    step_zero = summed_steps(terms_zero)
-    decay = momentum_decay[:, None, None]
-    weights_zero = tuple((w.astype(jnp.float32) for w in full_zero))
-    whole_zero = full_steps(step_zero)
-    weights_one = tuple((renorm(w, w + m) for w, m in zip(weights_zero, whole_zero)))
-    full_one = tuple((w.astype(jnp.bfloat16) for w in weights_one))
-    out_one = apply_block(full_one, query_tokens[1])
-    step_one = summed_steps(terms_one)
-    whole_one = full_steps(step_one)
-    moment = tuple((decay * m + s for m, s in zip(whole_zero, whole_one)))
-    weights_two = tuple((renorm(w, w + m) for w, m in zip(weights_one, moment)))
-    full_two = tuple((w.astype(jnp.bfloat16) for w in weights_two))
-    out_two = apply_block(full_two, query_tokens[2])
+    step_zero = summed[0].astype(jnp.float32)
+    step_one = summed[1].astype(jnp.float32)
+    decay = momentum_decay[None, :, None, None]
+    weights_zero = own.astype(jnp.float32)
+    weights_one = renorm(weights_zero, weights_zero + step_zero)
+    moment = decay * step_zero + step_one
+    weights_two = renorm(weights_one, weights_one + moment)
+    both = jnp.stack([weights_one, weights_two]).astype(jnp.bfloat16)
+    full = lax.all_gather(both, "tok", axis=3, tiled=True)
+    out_one = apply_block(full[0], query_tokens[1])
+    out_two = apply_block(full[1], query_tokens[2])
     return jnp.stack([out_zero, out_one, out_two])
 
 

time: 799 us -> 236 us (0.30)
  waiting for transfers between devices: 719 us -> 179 us
  matrix products: 36.7 us -> 21 us
    reduce_scatter x6 -> x1, waiting for transfers between devices: 368 us -> 84.1 us  [shards(): summed = lax.psum_scatter(low, 'tok', scatter_dimension=3, tiled=True)]
    all_gather x9 -> x2, waiting for transfers between devices: 349 us -> 95.3 us  [the longest x1 49 us: shards(): full = lax.all_gather(both, 'tok', axis=3, tiled=True)]
  transfers between devices with their start and end apart: 15 -> 3, of which waited for: 15 -> 3; matrix products, arithmetic and copies ran while one was open for 5% -> 6% of each run, Pallas kernels for 0% -> 0%
where the time goes in v1:
time: 236 us
  waiting for transfers between devices  179 us (76%)
  matrix products  21 us (9%)
  between operations  13.4 us (6%)
  other arithmetic  12.2 us (5%)
  local copies, waits for them, and re-layouts  9.58 us (4%)
    reduce_scatter x1, waiting for transfers between devices, shards(): summed = lax.psum_scatter(low, 'tok', scatter_dimension=3, tiled=True)  84.1 us
    all_gather x1, waiting for transfers between devices, shards(): full = lax.all_gather(both, 'tok', axis=3, tiled=True)  49 us
    all_gather x1, waiting for transfers between devices, shards(): full_zero = lax.all_gather(own, 'tok', axis=2, tiled=True)  46.3 us
    dot_general x5, matrix products, forward_parts(): jnp.einsum('thd,hfd->htf', shaped, first, preferred_element_type=jnp.floa...  7.74 us
    dot_general x3, matrix products, apply_block(): jnp.einsum('htf,hdf->thd', hidden, weights[2], preferred_element_type=jnp...  7.33 us
    unnamed x23, local copies, waits for them, and re-layouts  4.8 us
  transfers between devices with their start and end apart: 3, of which 3 were waited for; matrix products, arithmetic and copies ran while one was open for 6% of the time, Pallas kernels for 0%

profile of v1, /device:TPU:0, one launch (start us, length us, event | category | flops | bytes accessed | tf_op | source)
XLA Modules:
  0.0 235.7 jit_solution(14436471936075358880)
XLA Ops:
  6.5 1.6 pad_maximum_fusion.3
  8.2 1.1 fusion.62
  9.7 1.1 slice_convert_fusion.1
  11.2 46.3 %all-gather.3.cloned.1.call-done = bf16[3,2,512,512]{3,2,1,0:T(8,128)(2,1)} async-done(((bf16[3,2,32,512]{3,2,1,0:T(8,128)(2,1)}), bf16[3,2,512,512]{3,2,1,0:T(8,128)(2,1)}) %all-gather.3.cloned.1.call-update) | async-done | bytes 3145744 | tf_op jit(solution)/shard_map/all_gather | solution.py:58
  57.5 1.8 convolution_bitcast_fusion.6
  59.3 1.7 convolution_bitcast_fusion.7
  61.0 0.5 fusion.2
  61.5 0.5 fusion.13
  62.0 0.5 fusion
  63.8 0.5 fusion.5
  64.3 0.5 fusion.12
  64.9 0.5 fusion.3
  65.8 0.7 maximum_bitcast_fusion
  66.5 3.2 %pad_maximum_fusion = bf16[2,3,2,512,512]{4,3,2,1,0:T(8,128)(2,1)} fusion(bf16[1,3,2,512,512]{4,3,2,1,0:T(8,128)(2,1)S(1)} %get-tuple-element.21, bf16[1,3,2,512,512]{4,3,2,1,0:T(8,128)(2,1)S(1)} %get-tuple-element.20), kind=kLoop, calls=%fused_computation | loop fusion | flops 3145728 | bytes 12582912 | tf_op jit(solution)/shard_map/stack | solution.py:63
  69.8 84.1 %reduce-scatter.2.cloned.1.call-done = bf16[2,3,2,32,512]{4,3,2,1,0:T(8,128)(2,1)} async-done(((bf16[2,3,2,512,512]{4,3,2,1,0:T(8,128)(2,1)}), bf16[2,3,2,32,512]{4,3,2,1,0:T(8,128)(2,1)}) %reduce-scatter.2.cloned.1.call-update) | async-done | bytes 393232 | tf_op jit(solution)/shard_map/reduce_scatter | solution.py:64
  153.9 1.1 fusion.31
  155.0 1.3 multiply_reduce_fusion
  156.4 1.3 fusion.51
  157.7 0.8 pad_maximum_fusion.2
  158.5 1.9 fusion.61
  160.4 1.8 copy.79
  162.2 1.8 copy.82
  164.0 0.8 copy.83
  164.9 2.2 convolution_bitcast_fusion.9
  167.1 2.6 %convolution_convert_fusion.8 = bf16[2,512,128]{2,1,0:T(8,128)(2,1)} fusion(bf16[128,2,512]{0,2,1:T(8,128)(2,1)} %bitcast.185, bf16[3,2,512,512]{3,2,1,0:T(8,128)(2,1)S(1)} %copy-done.1, f32[2,128,512]{1,2,0:T(8,128)} %convolution_bitcast_fusion.9), kind=kOutput, calls=%fused_computation.33 | convolution fusion | flops 269352960 | bytes 3145728 | tf_op jit(solution)/shard_map/htf,hdf->thd/dot_general | solution.py:20
  169.7 1.1 copy.54
  170.8 49.0 %all-gather.5.cloned.1.call-done = bf16[2,3,2,512,512]{4,3,2,1,0:T(8,128)(2,1)} async-done(((bf16[2,3,2,32,512]{4,3,2,1,0:T(8,128)(2,1)}), bf16[2,3,2,512,512]{4,3,2,1,0:T(8,128)(2,1)}) %all-gather.5.cloned.1.call-update) | async-done | bytes 6291472 | tf_op jit(solution)/shard_map/all_gather | solution.py:74
  219.8 1.6 convolution_bitcast_fusion.3
  221.5 2.4 %convolution_convert_fusion.7 = bf16[2,512,128]{2,1,0:T(8,128)(2,1)S(1)} fusion(bf16[128,2,512]{0,2,1:T(8,128)(2,1)S(1)} %bitcast.183, bf16[2,3,2,512,512]{4,3,2,1,0:T(8,128)(2,1)} %all-gather.5.cloned.1.call-done, f32[2,128,512]{1,2,0:T(8,128)S(1)} %convolution_bitcast_fusion.3), kind=kOutput, calls=%fused_computation.32 | convolution fusion | flops 269352960 | bytes 3145728 | tf_op jit(solution)/shard_map/htf,hdf->thd/dot_general | solution.py:20
  224.0 1.7 convolution_bitcast_fusion.1
  225.7 2.3 convolution_convert_fusion.6
  228.2 1.0 pad_maximum_fusion.1
  (39 shorter events, 3.0 us)
Async XLA Ops:
  6.5 51.0 %all-gather.3.cloned.1.call-start = ((), (), s32[]{:S(2)}) async-start(), calls=%async_computation.1 | async-start | bytes 3342336 | tf_op jit(solution)/shard_map/all_gather | solution.py:58
  6.5 4.7 %copy-start.8 = (f32[3,128,2]{1,2,0:T(2,128)S(1)}, f32[3,128,2]{1,2,0:T(2,128)}, u32[]{:S(2)}) copy-start(f32[3,128,2]{1,2,0:T(2,128)} %param.11) | copy-start | bytes 9220
  8.2 145.7 %reduce-scatter.2.cloned.1.call-start = ((), (), s32[]{:S(2)}) async-start(), calls=%async_computation.2 | async-start | bytes 6684672 | tf_op jit(solution)/shard_map/reduce_scatter | solution.py:64
  57.5 4.0 %copy-start = (bf16[3,2,512,512]{3,2,1,0:T(8,128)(2,1)S(1)}, bf16[3,2,512,512]{3,2,1,0:T(8,128)(2,1)}, u32[]{:S(2)}) copy-start(bf16[3,2,512,512]{3,2,1,0:T(8,128)(2,1)} %all-gather.3.cloned.1.call-done) | copy-start | bytes 9437188
  69.7 84.2 %copy-start.2 = (bf16[2,32,512]{2,1,0:T(8,128)(2,1)S(1)}, bf16[2,32,512]{2,1,0:T(8,128)(2,1)}, u32[]{:S(2)}) copy-start(bf16[2,32,512]{2,1,0:T(8,128)(2,1)} %param.14) | copy-start | bytes 196612
  69.7 84.2 %copy-start.3 = (bf16[2,32,512]{2,1,0:T(8,128)(2,1)S(1)}, bf16[2,32,512]{2,1,0:T(8,128)(2,1)}, u32[]{:S(2)}) copy-start(bf16[2,32,512]{2,1,0:T(8,128)(2,1)} %param.13) | copy-start | bytes 196612
  69.7 84.2 %copy-start.4 = (bf16[2,32,512]{2,1,0:T(8,128)(2,1)S(1)}, bf16[2,32,512]{2,1,0:T(8,128)(2,1)}, u32[]{:S(2)}) copy-start(bf16[2,32,512]{2,1,0:T(8,128)(2,1)} %param.12) | copy-start | bytes 196612
  69.7 85.3 %copy-start.7 = (f32[2]{0:T(128)S(1)}, f32[2]{0:T(128)}, u32[]{:S(2)}) copy-start(f32[2]{0:T(128)} %param.15) | copy-start | bytes 28
  69.7 95.1 %copy-start.1 = (bf16[3,2,512,512]{3,2,1,0:T(8,128)(2,1)S(1)}, bf16[3,2,512,512]{3,2,1,0:T(8,128)(2,1)}, u32[]{:S(2)}) copy-start(bf16[3,2,512,512]{3,2,1,0:T(8,128)(2,1)} %all-gather.3.cloned.1.call-done) | copy-start | bytes 9437188
  69.7 150.1 %all-gather.5.cloned.1.call-start = ((), (), s32[]{:S(2)}) async-start(), calls=%async_computation.3 | async-start | bytes 6684672 | tf_op jit(solution)/shard_map/all_gather | solution.py:74
  167.1 52.8 %copy-start.6 = (bf16[1,128,1024]{1,2,0:T(8,128)(2,1)S(1)}, bf16[1,128,1024]{1,2,0:T(8,128)(2,1)}, u32[]{:S(2)}) copy-start(bf16[1,128,1024]{1,2,0:T(8,128)(2,1)} %copy.82) | copy-start | bytes 786436
  221.5 2.5 %copy-start.5 = (bf16[1,128,1024]{1,2,0:T(8,128)(2,1)S(1)}, bf16[1,128,1024]{1,2,0:T(8,128)(2,1)}, u32[]{:S(2)}) copy-start(bf16[1,128,1024]{1,2,0:T(8,128)(2,1)} %copy.83) | copy-start | bytes 786436
Sparse Core Ops, SparseCore 0:
  9.5 47.9 all-gather.2
  69.9 83.9 reduce-scatter.1
  158.6 61.1 all-gather.4

commit v2 on v1

v2 whole, which is shorter than its diff:
```python
import jax
import jax.numpy as jnp
from jax import lax
from jax.sharding import PartitionSpec as P

LOW = jnp.bfloat16
WIDE = jnp.float32


def dot(a, b, dims):
    return lax.dot_general(a, b, ((dims[:1], dims[1:]), ((), ())), preferred_element_type=WIDE)


def forward_parts(weights, inputs):
    pre_gate = dot(inputs, weights[0], (1, 1))
    pre_up = dot(inputs, weights[1], (1, 1))
    hidden = (jax.nn.silu(pre_gate) * pre_up).astype(LOW)
    return pre_gate, pre_up, hidden


def partial_readout(weights, inputs):
    hidden = forward_parts(weights, inputs)[2]
    return dot(hidden, weights[2], (1, 1))


def partial_steps(weights, keys, scaled):
    pre_gate, pre_up, hidden = forward_parts(weights, keys)
    step_second = dot(scaled, hidden, (0, 0))
    back = dot(scaled, weights[2], (1, 0))
    sig_gate = jax.nn.sigmoid(pre_gate)
    d_gate = (back * pre_up * sig_gate * (1.0 + pre_gate * (1.0 - sig_gate))).astype(LOW)
    d_up = (back * pre_gate * sig_gate).astype(LOW)
    step_first = dot(d_gate, keys, (0, 0))
    step_third = dot(d_up, keys, (0, 0))
    return step_first, step_third, step_second


def renorm(old, moved):
    def norm(parts):
        return jnp.sqrt(sum(jnp.sum(p * p, axis=-1, keepdims=True) for p in parts) + 1e-06)

    factor = norm(old), norm(moved)
    return [m * factor[0] / factor[1] for m in moved]


def shards(
    query_tokens,
    key_tokens,
    value_tokens,
    learn_rates,
    fast_first,
    fast_third,
    fast_second,
    momentum_decay,
):
    count = lax.axis_size("tok")
    planes = count // 4
    index = lax.axis_index("tok")
    z, y, c = index // 4, (index // 2) % 2, index % 2
    width = fast_first.shape[2]
    half = width // 2
    rows = 2 * fast_first.shape[1]

    def send(array, dz, dy, dc):
        pairs = []
        for t in range(count):
            tz, ty, tc = t // 4, (t // 2) % 2, t % 2
            pairs.append((t, ((tz + dz) % planes) * 4 + (ty ^ dy) * 2 + (tc ^ dc)))
        return lax.ppermute(array, "tok", pairs)

    def swapped(flag, a, b, axis):
        return jnp.where(flag == 0, jnp.concatenate([a, b], axis), jnp.concatenate([b, a], axis))

    def head(array, which):
        return lax.dynamic_slice_in_dim(array, which * width, width, array.ndim - 1)

    quad = [(0, 0), (0, 1), (1, 0), (1, 1)]

    def in_quad(array):
        pieces = [head(array, c)]
        pieces += [send(head(array, c ^ dc), 0, dy, dc) for dy, dc in quad[1:]]
        return jnp.concatenate(pieces, axis=array.ndim - 2)

    def from_quad(partial):
        tokens = partial.shape[0] // 4
        pieces = [partial[i * tokens : (i + 1) * tokens] for i in range(4)]
        got = [send(pieces[i].astype(LOW), 0, *quad[i]).astype(WIDE) for i in range(1, 4)]
        mine = (pieces[0] + got[1]).astype(LOW)
        other = (got[0] + got[2]).astype(LOW)
        return swapped(c, mine, other, 1)

    def rolled(array):
        double = jnp.concatenate([array, array], axis=0)
        return lax.dynamic_slice_in_dim(double, planes - z, planes, 0)

    def gathered(same, other):
        sames = jnp.stack([same] + [send(same, planes - s, 0, 0) for s in range(1, planes)])
        others = jnp.stack([send(other, (planes - s) % planes, 1, 0) for s in range(planes)])
        sames, others = rolled(sames), rolled(others)
        first = sames[:, :, :width].reshape(half, width)
        third = sames[:, :, width : 2 * width].reshape(half, width)
        second = swapped(y, sames[:, None, :, 2 * width :], others[:, None], 1)
        return first, third, second.reshape(width, half)

    def reduced(steps):
        first = steps[0].reshape(planes, rows, width)
        third = steps[1].reshape(planes, rows, width)
        second = steps[2].reshape(planes, 2, rows, half)

        def same_for(s):
            at = (z + s) % planes
            return jnp.concatenate([first[at], third[at], second[at, y]], axis=1)

        same = same_for(0)
        for s in range(1, planes):
            same = same + send(same_for(s).astype(LOW), s, 0, 0).astype(WIDE)
        other = 0.0
        for s in range(planes):
            piece = second[(z + s) % planes, 1 - y].astype(LOW)
            other = other + send(piece, s, 1, 0).astype(WIDE)
        return same[:, :width], same[:, width : 2 * width], same[:, 2 * width :], other

    def updated(old, step):
        moved = [o + s for o, s in zip(old, step)]
        return renorm(old[:1], moved[:1]) + renorm(old[1:2], moved[1:2]) + renorm(old[2:], moved[2:])

    def spread(weights):
        low = [w.astype(LOW) for w in weights]
        return gathered(jnp.concatenate(low[:3], axis=1), low[3])

    own = jnp.stack([fast_first, fast_third, fast_second])
    mine = lax.dynamic_index_in_dim(own, c, 1, False)
    given = send(lax.dynamic_index_in_dim(own, c ^ 1, 1, False), 0, 0, 1)
    chip = swapped(c, mine, given, 1)
    columns = chip[2].reshape(rows, planes, 2, rows)
    second_same = lax.dynamic_index_in_dim(columns, y, 2, False).reshape(rows, half)
    second_other = lax.dynamic_index_in_dim(columns, 1 - y, 2, False).reshape(rows, half)
    zero = [chip[0], chip[1], second_same, second_other]
    full_zero = spread(zero)

    tokens = key_tokens.shape[1]
    scaled = learn_rates[:2, :, :, None] * value_tokens[:2].reshape(2, tokens, 2, width).astype(WIDE)
    scaled = scaled.astype(LOW).reshape(2, tokens, 2 * width)
    terms = []
    for b in range(2):
        pair = in_quad(jnp.stack([key_tokens[b], scaled[b]]))
        terms.append(partial_steps(full_zero, pair[0], pair[1]))
    queries = in_quad(query_tokens)
    out_zero = from_quad(partial_readout(full_zero, queries[0]))

    step_zero = reduced(terms[0])
    weights_zero = [w.astype(WIDE) for w in zero]
    weights_one = updated(weights_zero, step_zero)
    full_one = spread(weights_one)
    out_one = from_quad(partial_readout(full_one, queries[1]))
    step_one = reduced(terms[1])
    decay = lax.dynamic_index_in_dim(momentum_decay, c, 0, False)
    moment = [decay * m + s for m, s in zip(step_zero, step_one)]
    weights_two = updated(weights_one, moment)
    full_two = spread(weights_two)
    out_two = from_quad(partial_readout(full_two, queries[2]))
    return jnp.stack([out_zero, out_one, out_two])


def solution(mesh):
    placed = (
        P(None, ("groups", "tok"), None),
        P(None, ("groups", "tok"), None),
        P(None, ("groups", "tok"), None),
        P(None, ("groups", "tok"), None),
        P(None, "tok", None),
        P(None, "tok", None),
        P(None, "tok", None),
        P(),
    )
    return jax.shard_map(
        shards,
        mesh=mesh,
        in_specs=placed,
        out_specs=P(None, ("groups", "tok"), None),
        check_vma=False,
    )
```

time: 236 us -> 238 us (level)
  waiting for transfers between devices: 179 us -> 85.4 us
  starting transfers between devices: 0.09 us -> 68.5 us
  local copies, waits for them, and re-layouts: 9.58 us -> 38 us
  between operations: 13.4 us -> 1.25 us
  other arithmetic: 12.2 us -> 20.4 us
  matrix products: 21 us -> 23.7 us
    all_gather x2 -> x0, waiting for transfers between devices: 95.3 us -> none  [the longest x1 49 us: shards(): full = lax.all_gather(both, 'tok', axis=3, tiled=True)]
    ppermute x0 -> x54, waiting for transfers between devices: none -> 85.4 us  [send(): return lax.ppermute(array, 'tok', pairs)]
    reduce_scatter x1 -> x0, waiting for transfers between devices: 84.1 us -> none  [shards(): summed = lax.psum_scatter(low, 'tok', scatter_dimension=3, tiled=True)]
    ppermute x0 -> x54, starting transfers between devices: none -> 68.5 us  [send(): return lax.ppermute(array, 'tok', pairs)]
    dot_general x0 -> x8, local copies, waits for them, and re-layouts: none -> 12.2 us  [dot(): lax.dot_general(a, b, ((dims[:1], dims[1:]), ((), ())), preferred_element...]
    concatenate x0 -> x18, other arithmetic: none -> 10.8 us  [the longest x6 4.09 us: swapped(): jnp.concatenate([a, b], axis)]
    squeeze x0 -> x8, local copies, waits for them, and re-layouts: none -> 5.33 us  [the longest x6 5.29 us: same_for(): return jnp.concatenate([first[at], third[at], second[at, y]], axis=1)]
    another operation x4 -> x2, other arithmetic: 5.96 us -> 0.79 us  [shards(): pair = in_quad(jnp.stack([key_tokens[b], scaled[b]]))]
  transfers between devices with their start and end apart: 3 -> 54, of which waited for: 3 -> 21; matrix products, arithmetic and copies ran while one was open for 6% -> 30% of each run, Pallas kernels for 0% -> 0%
where the time goes in v2:
time: 238 us; the launch traced here: 237 us
  waiting for transfers between devices  85.4 us (36%)
  starting transfers between devices  68.5 us (29%)
  local copies, waits for them, and re-layouts  38 us (16%)
  matrix products  23.7 us (10%)
  other arithmetic  20.4 us (9%)
    ppermute x54, waiting for transfers between devices, send(): return lax.ppermute(array, 'tok', pairs)  85.4 us
    ppermute x54, starting transfers between devices, send(): return lax.ppermute(array, 'tok', pairs)  68.5 us
    dot_general x18, matrix products, dot(): lax.dot_general(a, b, ((dims[:1], dims[1:]), ((), ())), preferred_element...  23.7 us
    dot_general x8, local copies, waits for them, and re-layouts, dot(): lax.dot_general(a, b, ((dims[:1], dims[1:]), ((), ())), preferred_element...  12.2 us
    unnamed x102, local copies, waits for them, and re-layouts  5.79 us
    squeeze x6, local copies, waits for them, and re-layouts, same_for(): return jnp.concatenate([first[at], third[at], second[at, y]], axis=1)  5.29 us
  transfers between devices with their start and end apart: 54, of which 21 were waited for; matrix products, arithmetic and copies ran while one was open for 30% of the time, Pallas kernels for 0%

profile of v2, /device:TPU:0, one launch (start us, length us, event | category | flops | bytes accessed | tf_op | source)
XLA Modules:
  0.0 237.2 jit_solution(14069281731819547220)
XLA Ops:
  2.6 2.6 %collective-permute-start.2 = (bf16[3,128,512]{2,1,0:T(8,128)(2,1)}, bf16[3,128,512]{2,1,0:T(8,128)(2,1)}, u32[]{:S(2)}, u32[]{:S(2)}) collective-permute-start(bf16[3,128,512]{2,1,0:T(8,128)(2,1)} %get-tuple-element.42), channel_id=1, source_target_pairs={{0,3},{1,2},{2,1},{3,0},{4,7},{5,6},{6,5},{7,4},{8,11},{9,10},{10,... | collective-permute-start | bytes 1179656 | tf_op jit(solution)/shard_map/ppermute | solution.py:69
  14.3 7.2 %collective-permute-done.7 = bf16[64,256]{1,0:T(8,128)(2,1)S(1)} collective-permute-done((bf16[64,256]{1,0:T(8,128)(2,1)S(1)}, bf16[64,256]{1,0:T(8,128)(2,1)S(1)}, u32[]{:S(2)}, u32[]{:S(2)}) %collective-permute-start.7) | collective-permute-done | bytes 32800 | tf_op jit(solution)/shard_map/ppermute | solution.py:69
  21.5 4.7 %collective-permute-start.8 = (bf16[64,256]{1,0:T(8,128)(2,1)S(1)}, bf16[64,256]{1,0:T(8,128)(2,1)S(1)}, u32[]{:S(2)}, u32[]{:S(2)}) collective-permute-start(bf16[64,256]{1,0:T(8,128)(2,1)S(1)} %reshape.338), channel_id=1, source_target_pairs={{0,14},{1,15},{2,12},{3,13},{4,2},{5,3},{6,0},{7,1},{8,6},{9,7},{1... | collective-permute-start | bytes 98312 | tf_op jit(solution)/shard_map/ppermute | solution.py:69
  27.7 2.2 collective-permute-start.9
  29.9 3.5 %collective-permute-done.9 = bf16[64,256]{1,0:T(8,128)(2,1)S(1)} collective-permute-done((bf16[64,256]{1,0:T(8,128)(2,1)S(1)}, bf16[64,256]{1,0:T(8,128)(2,1)S(1)}, u32[]{:S(2)}, u32[]{:S(2)}) %collective-permute-start.9) | collective-permute-done | bytes 32800 | tf_op jit(solution)/shard_map/ppermute | solution.py:69
  35.2 5.6 %collective-permute-done.10 = bf16[64,256]{1,0:T(8,128)(2,1)S(1)} collective-permute-done((bf16[64,256]{1,0:T(8,128)(2,1)S(1)}, bf16[64,256]{1,0:T(8,128)(2,1)S(1)}, u32[]{:S(2)}, u32[]{:S(2)}) %collective-permute-start.10) | collective-permute-done | bytes 32800 | tf_op jit(solution)/shard_map/ppermute | solution.py:69
  42.4 4.6 %collective-permute-done.4 = bf16[64,1280]{1,0:T(8,128)(2,1)S(1)} collective-permute-done((bf16[64,1280]{1,0:T(8,128)(2,1)S(1)}, bf16[64,1280]{1,0:T(8,128)(2,1)S(1)}, u32[]{:S(2)}, u32[]{:S(2)}) %collective-permute-start.4) | collective-permute-done | bytes 163872 | tf_op jit(solution)/shard_map/ppermute | solution.py:69
  47.7 8.6 %collective-permute-done.5 = bf16[64,1280]{1,0:T(8,128)(2,1)S(1)} collective-permute-done((bf16[64,1280]{1,0:T(8,128)(2,1)S(1)}, bf16[64,1280]{1,0:T(8,128)(2,1)S(1)}, u32[]{:S(2)}, u32[]{:S(2)}) %collective-permute-start.5) | collective-permute-done | bytes 163872 | tf_op jit(solution)/shard_map/ppermute | solution.py:69
  56.9 6.4 %collective-permute-done.6 = bf16[64,1280]{1,0:T(8,128)(2,1)S(1)} collective-permute-done((bf16[64,1280]{1,0:T(8,128)(2,1)S(1)}, bf16[64,1280]{1,0:T(8,128)(2,1)S(1)}, u32[]{:S(2)}, u32[]{:S(2)}) %collective-permute-start.6) | collective-permute-done | bytes 163872 | tf_op jit(solution)/shard_map/ppermute | solution.py:69
  77.0 7.5 %collective-permute-done.35 = bf16[2,128,512]{2,1,0:T(8,128)(2,1)S(1)} collective-permute-done((bf16[2,128,512]{2,1,0:T(8,128)(2,1)S(1)}, bf16[2,128,512]{2,1,0:T(8,128)(2,1)S(1)}, u32[]{:S(2)}, u32[]{:S(2)}) %collective-permute-start.35) | collective-permute-done | bytes 262176 | tf_op jit(solution)/shard_map/ppermute | solution.py:69
  92.7 2.5 %fusion.28 = (bf16[256,512]{1,0:T(8,128)(2,1)}, bf16[256,512]{1,0:T(8,128)(2,1)}) fusion(f32[512,256]{0,1:T(8,128)} %fusion.32, f32[512,256]{0,1:T(8,128)} %fusion.34, bf16[512,256]{1,0:T(8,128)(2,1)} %bitcast.378, bf16[2,512,512]{2,1,0:T(8,128)(2,1)S(1)} %pad_maximum_fusion.1), kind=kOutput, calls=%fused_computation.51 | convolution fusion | flops 135921664 | bytes 2359296 | tf_op jit(solution)/shard_map/dot_general | solution.py:11
  99.3 2.6 %fusion.9 = (bf16[256,512]{1,0:T(8,128)(2,1)}, bf16[256,512]{1,0:T(8,128)(2,1)}) fusion(f32[512,256]{0,1:T(8,128)} %fusion.13, f32[512,256]{0,1:T(8,128)} %fusion.15, bf16[512,256]{1,0:T(8,128)(2,1)} %bitcast.379, bf16[2,512,512]{2,1,0:T(8,128)(2,1)S(1)} %pad_maximum_fusion.2), kind=kOutput, calls=%fused_computation.28 | convolution fusion | flops 135921664 | bytes 2359296 | tf_op jit(solution)/shard_map/dot_general | solution.py:11
  120.5 3.8 %collective-permute-start.23 = (bf16[64,256]{1,0:T(8,128)(2,1)S(1)}, bf16[64,256]{1,0:T(8,128)(2,1)S(1)}, u32[]{:S(2)}, u32[]{:S(2)}) collective-permute-start(bf16[64,256]{1,0:T(8,128)(2,1)S(1)} %copy-done.30), channel_id=1, source_target_pairs={{0,14},{1,15},{2,12},{3,13},{4,2},{5,3},{6,0},{7,1},{8,6},{9,7},{1... | collective-permute-start | bytes 98312 | tf_op jit(solution)/shard_map/ppermute | solution.py:69
  128.1 2.9 %collective-permute-start.18 = (bf16[64,1280]{1,0:T(8,128)(2,1)}, bf16[64,1280]{1,0:T(8,128)(2,1)}, u32[]{:S(2)}, u32[]{:S(2)}) collective-permute-start(bf16[64,1280]{1,0:T(8,128)(2,1)} %pad_maximum_fusion.7), channel_id=1, source_target_pairs={{0,8},{1,9},{2,10},{3,11},{4,12},{5,13},{6,14},{7,15},{8,0},{9,1},... | collective-permute-start | bytes 491528 | tf_op jit(solution)/shard_map/ppermute | solution.py:69
  135.8 2.9 %fusion.131 = (bf16[512,512]{0,1:T(8,128)(2,1)}, f32[512,512]{0,1:T(8,128)}) fusion(bf16[512,256]{1,0:T(8,128)(2,1)} %bitcast.380, f32[512,256]{1,0:T(8,128)S(1)} %fusion.39, bf16[256,512]{1,0:T(8,128)(2,1)S(1)} %bitcast.367, bf16[3,512,512]{2,1,0:T(8,128)(2,1)S(1)} %pad_maximum_fusion), kind=kOutput, calls=%fused_computation.330 | convolution fusion | flops 269484032 | bytes 3145728 | tf_op jit(solution)/shard_map/dot_general | solution.py:11
  139.8 2.9 %collective-permute-start.39 = (bf16[64,1280]{1,0:T(8,128)(2,1)S(1)}, bf16[64,1280]{1,0:T(8,128)(2,1)S(1)}, u32[]{:S(2)}, u32[]{:S(2)}) collective-permute-start(bf16[64,1280]{1,0:T(8,128)(2,1)S(1)} %copy-done.21), channel_id=1, source_target_pairs={{0,12},{1,13},{2,14},{3,15},{4,0},{5,1},{6,2},{7,3},{8,4},{9,5},{1... | collective-permute-start | bytes 491528 | tf_op jit(solution)/shard_map/ppermute | solution.py:69
  142.8 4.7 %collective-permute-done.18 = bf16[64,1280]{1,0:T(8,128)(2,1)} collective-permute-done((bf16[64,1280]{1,0:T(8,128)(2,1)}, bf16[64,1280]{1,0:T(8,128)(2,1)}, u32[]{:S(2)}, u32[]{:S(2)}) %collective-permute-start.18) | collective-permute-done | bytes 163872 | tf_op jit(solution)/shard_map/ppermute | solution.py:69
  147.6 6.1 %collective-permute-start.41 = (bf16[64,256]{1,0:T(8,128)(2,1)}, bf16[64,256]{1,0:T(8,128)(2,1)S(1)}, u32[]{:S(2)}, u32[]{:S(2)}) collective-permute-start(bf16[64,256]{1,0:T(8,128)(2,1)} %get-tuple-element.67), channel_id=1, source_target_pairs={{0,6},{1,7},{2,4},{3,5},{4,10},{5,11},{6,8},{7,9},{8,14},{9,15},{1... | collective-permute-start | bytes 98312 | tf_op jit(solution)/shard_map/ppermute | solution.py:69
  155.6 2.9 %collective-permute-start.42 = (bf16[64,256]{1,0:T(8,128)(2,1)S(1)}, bf16[64,256]{1,0:T(8,128)(2,1)S(1)}, u32[]{:S(2)}, u32[]{:S(2)}) collective-permute-start(bf16[64,256]{1,0:T(8,128)(2,1)S(1)} %copy-done.29), channel_id=1, source_target_pairs={{0,10},{1,11},{2,8},{3,9},{4,14},{5,15},{6,12},{7,13},{8,2},{9,3},... | collective-permute-start | bytes 98312 | tf_op jit(solution)/shard_map/ppermute | solution.py:69
  158.4 3.4 %collective-permute-start.43 = (bf16[64,256]{1,0:T(8,128)(2,1)S(1)}, bf16[64,256]{1,0:T(8,128)(2,1)S(1)}, u32[]{:S(2)}, u32[]{:S(2)}) collective-permute-start(bf16[64,256]{1,0:T(8,128)(2,1)S(1)} %copy-done.28), channel_id=1, source_target_pairs={{0,14},{1,15},{2,12},{3,13},{4,2},{5,3},{6,0},{7,1},{8,6},{9,7},{1... | collective-permute-start | bytes 98312 | tf_op jit(solution)/shard_map/ppermute | solution.py:69
  169.5 2.8 %collective-permute-done.27 = bf16[64,256]{1,0:T(8,128)(2,1)S(1)} collective-permute-done((bf16[64,256]{1,0:T(8,128)(2,1)S(1)}, bf16[64,256]{1,0:T(8,128)(2,1)S(1)}, u32[]{:S(2)}, u32[]{:S(2)}) %collective-permute-start.27) | collective-permute-done | bytes 32800 | tf_op jit(solution)/shard_map/ppermute | solution.py:69
  173.3 4.8 %collective-permute-done.29 = bf16[64,256]{1,0:T(8,128)(2,1)S(1)} collective-permute-done((bf16[64,256]{1,0:T(8,128)(2,1)S(1)}, bf16[64,256]{1,0:T(8,128)(2,1)S(1)}, u32[]{:S(2)}, u32[]{:S(2)}) %collective-permute-start.29) | collective-permute-done | bytes 32800 | tf_op jit(solution)/shard_map/ppermute | solution.py:69
  182.0 2.5 %collective-permute-done.48 = bf16[64,256]{1,0:T(8,128)(2,1)S(1)} collective-permute-done((bf16[64,256]{1,0:T(8,128)(2,1)S(1)}, bf16[64,256]{1,0:T(8,128)(2,1)S(1)}, u32[]{:S(2)}, u32[]{:S(2)}) %collective-permute-start.48) | collective-permute-done | bytes 32800 | tf_op jit(solution)/shard_map/ppermute | solution.py:69
  184.6 3.5 %collective-permute-done.49 = bf16[64,256]{1,0:T(8,128)(2,1)S(1)} collective-permute-done((bf16[64,256]{1,0:T(8,128)(2,1)S(1)}, bf16[64,256]{1,0:T(8,128)(2,1)S(1)}, u32[]{:S(2)}, u32[]{:S(2)}) %collective-permute-start.49) | collective-permute-done | bytes 32800 | tf_op jit(solution)/shard_map/ppermute | solution.py:69
  188.6 2.5 %collective-permute-done.50 = bf16[64,256]{1,0:T(8,128)(2,1)S(1)} collective-permute-done((bf16[64,256]{1,0:T(8,128)(2,1)S(1)}, bf16[64,256]{1,0:T(8,128)(2,1)S(1)}, u32[]{:S(2)}, u32[]{:S(2)}) %collective-permute-start.50) | collective-permute-done | bytes 32800 | tf_op jit(solution)/shard_map/ppermute | solution.py:69
  194.2 3.9 %collective-permute-start.44 = (bf16[64,1280]{1,0:T(8,128)(2,1)S(1)}, bf16[64,1280]{1,0:T(8,128)(2,1)S(1)}, u32[]{:S(2)}, u32[]{:S(2)}) collective-permute-start(bf16[64,1280]{1,0:T(8,128)(2,1)S(1)} %pad_maximum_fusion.13), channel_id=1, source_target_pairs={{0,12},{1,13},{2,14},{3,15},{4,0},{5,1},{6,2},{7,3},{8,4},{9,5},{1... | collective-permute-start | bytes 491528 | tf_op jit(solution)/shard_map/ppermute | solution.py:69
  198.2 4.7 %collective-permute-start.46 = (bf16[64,1280]{1,0:T(8,128)(2,1)S(1)}, bf16[64,1280]{1,0:T(8,128)(2,1)S(1)}, u32[]{:S(2)}, u32[]{:S(2)}) collective-permute-start(bf16[64,1280]{1,0:T(8,128)(2,1)S(1)} %pad_maximum_fusion.13), channel_id=1, source_target_pairs={{0,4},{1,5},{2,6},{3,7},{4,8},{5,9},{6,10},{7,11},{8,12},{9,13},{1... | collective-permute-start | bytes 491528 | tf_op jit(solution)/shard_map/ppermute | solution.py:69
  202.9 7.6 %collective-permute-done.25 = bf16[64,1280]{1,0:T(8,128)(2,1)S(1)} collective-permute-done((bf16[64,1280]{1,0:T(8,128)(2,1)S(1)}, bf16[64,1280]{1,0:T(8,128)(2,1)S(1)}, u32[]{:S(2)}, u32[]{:S(2)}) %collective-permute-start.25) | collective-permute-done | bytes 163872 | tf_op jit(solution)/shard_map/ppermute | solution.py:69
  210.6 5.0 %collective-permute-done.45 = bf16[64,1280]{1,0:T(8,128)(2,1)S(1)} collective-permute-done((bf16[64,1280]{1,0:T(8,128)(2,1)S(1)}, bf16[64,1280]{1,0:T(8,128)(2,1)S(1)}, u32[]{:S(2)}, u32[]{:S(2)}) %collective-permute-start.45) | collective-permute-done | bytes 163872 | tf_op jit(solution)/shard_map/ppermute | solution.py:69
  218.4 2.8 %fusion.130 = (bf16[512,512]{0,1:T(8,128)(2,1)S(1)}, f32[512,512]{0,1:T(8,128)}) fusion(bf16[512,256]{1,0:T(8,128)(2,1)} %bitcast.382, f32[512,256]{1,0:T(8,128)S(1)} %fusion.42, bf16[256,512]{1,0:T(8,128)(2,1)} %bitcast.375, bf16[3,512,512]{2,1,0:T(8,128)(2,1)S(1)} %pad_maximum_fusion), kind=kOutput, calls=%fused_computation.329 | convolution fusion | flops 269484032 | bytes 3145728 | tf_op jit(solution)/shard_map/dot_general | solution.py:11
  224.5 2.7 %fusion.129 = (bf16[512,512]{0,1:T(8,128)(2,1)S(1)}, f32[512,512]{0,1:T(8,128)}) fusion(bf16[512,256]{1,0:T(8,128)(2,1)S(1)} %bitcast.381, f32[512,256]{1,0:T(8,128)S(1)} %fusion.45, bf16[256,512]{1,0:T(8,128)(2,1)} %bitcast.372, bf16[3,512,512]{2,1,0:T(8,128)(2,1)S(1)} %pad_maximum_fusion), kind=kOutput, calls=%fused_computation.328 | convolution fusion | flops 269484032 | bytes 3145728 | tf_op jit(solution)/shard_map/dot_general | solution.py:11
  230.5 3.2 %collective-permute-done.51 = bf16[128,512]{0,1:T(8,128)(2,1)S(1)} collective-permute-done((bf16[128,512]{0,1:T(8,128)(2,1)S(1)}, bf16[128,512]{0,1:T(8,128)(2,1)S(1)}, u32[]{:S(2)}, u32[]{:S(2)}) %collective-permute-start.51) | collective-permute-done | bytes 131104 | tf_op jit(solution)/shard_map/ppermute | solution.py:69
  (313 shorter events, 102.4 us)
Async XLA Ops:
  2.2 128.9 %collective-permute-start = (bf16[3,128,512]{2,1,0:T(8,128)(2,1)}, bf16[3,128,512]{2,1,0:T(8,128)(2,1)}, u32[]{:S(2)}, u32[]{:S(2)}) collective-permute-start(bf16[3,128,512]{2,1,0:T(8,128)(2,1)} %get-tuple-element.42), channel_id=1, source_target_pairs={{0,1},{1,0},{2,3},{3,2},{4,5},{5,4},{6,7},{7,6},{8,9},{9,8},{10,11... | collective-permute-start | bytes 1179656 | tf_op jit(solution)/shard_map/ppermute | solution.py:69
  2.6 130.6 %collective-permute-start.2 = (bf16[3,128,512]{2,1,0:T(8,128)(2,1)}, bf16[3,128,512]{2,1,0:T(8,128)(2,1)}, u32[]{:S(2)}, u32[]{:S(2)}) collective-permute-start(bf16[3,128,512]{2,1,0:T(8,128)(2,1)} %get-tuple-element.42), channel_id=1, source_target_pairs={{0,3},{1,2},{2,1},{3,0},{4,7},{5,6},{6,5},{7,4},{8,11},{9,10},{10,... | collective-permute-start | bytes 1179656 | tf_op jit(solution)/shard_map/ppermute | solution.py:69
  7.7 61.7 %collective-permute-start.14 = (bf16[2,128,512]{2,1,0:T(8,128)(2,1)S(1)}, bf16[2,128,512]{2,1,0:T(8,128)(2,1)S(1)}, u32[]{:S(2)}, u32[]{:S(2)}) collective-permute-start(bf16[2,128,512]{2,1,0:T(8,128)(2,1)S(1)} %get-tuple-element.89), channel_id=1, source_target_pairs={{0,1},{1,0},{2,3},{3,2},{4,5},{5,4},{6,7},{7,6},{8,9},{9,8},{10,11... | collective-permute-start | bytes 786440 | tf_op jit(solution)/shard_map/ppermute | solution.py:69
  7.8 62.3 %collective-permute-start.16 = (bf16[2,128,512]{2,1,0:T(8,128)(2,1)S(1)}, bf16[2,128,512]{2,1,0:T(8,128)(2,1)S(1)}, u32[]{:S(2)}, u32[]{:S(2)}) collective-permute-start(bf16[2,128,512]{2,1,0:T(8,128)(2,1)S(1)} %get-tuple-element.89), channel_id=1, source_target_pairs={{0,3},{1,2},{2,1},{3,0},{4,7},{5,6},{6,5},{7,4},{8,11},{9,10},{10,... | collective-permute-start | bytes 786440 | tf_op jit(solution)/shard_map/ppermute | solution.py:69
  12.5 8.9 %collective-permute-start.7 = (bf16[64,256]{1,0:T(8,128)(2,1)S(1)}, bf16[64,256]{1,0:T(8,128)(2,1)S(1)}, u32[]{:S(2)}, u32[]{:S(2)}) collective-permute-start(bf16[64,256]{1,0:T(8,128)(2,1)S(1)} %reshape.338), channel_id=1, source_target_pairs={{0,2},{1,3},{2,0},{3,1},{4,6},{5,7},{6,4},{7,5},{8,10},{9,11},{10,... | collective-permute-start | bytes 98312 | tf_op jit(solution)/shard_map/ppermute | solution.py:69
  47.0 9.3 %collective-permute-start.5 = (bf16[64,1280]{1,0:T(8,128)(2,1)S(1)}, bf16[64,1280]{1,0:T(8,128)(2,1)S(1)}, u32[]{:S(2)}, u32[]{:S(2)}) collective-permute-start(bf16[64,1280]{1,0:T(8,128)(2,1)S(1)} %pad_maximum_fusion.5), channel_id=1, source_target_pairs={{0,8},{1,9},{2,10},{3,11},{4,12},{5,13},{6,14},{7,15},{8,0},{9,1},... | collective-permute-start | bytes 491528 | tf_op jit(solution)/shard_map/ppermute | solution.py:69
  69.7 14.8 %collective-permute-start.36 = (bf16[2,128,512]{2,1,0:T(8,128)(2,1)}, bf16[2,128,512]{2,1,0:T(8,128)(2,1)S(1)}, u32[]{:S(2)}, u32[]{:S(2)}) collective-permute-start(bf16[2,128,512]{2,1,0:T(8,128)(2,1)} %get-tuple-element.72), channel_id=1, source_target_pairs={{0,3},{1,2},{2,1},{3,0},{4,7},{5,6},{6,5},{7,4},{8,11},{9,10},{10,... | collective-permute-start | bytes 786440 | tf_op jit(solution)/shard_map/ppermute | solution.py:69
  70.8 13.7 %collective-permute-start.35 = (bf16[2,128,512]{2,1,0:T(8,128)(2,1)S(1)}, bf16[2,128,512]{2,1,0:T(8,128)(2,1)S(1)}, u32[]{:S(2)}, u32[]{:S(2)}) collective-permute-start(bf16[2,128,512]{2,1,0:T(8,128)(2,1)S(1)} %get-tuple-element.71), channel_id=1, source_target_pairs={{0,2},{1,3},{2,0},{3,1},{4,6},{5,7},{6,4},{7,5},{8,10},{9,11},{10,... | collective-permute-start | bytes 786440 | tf_op jit(solution)/shard_map/ppermute | solution.py:69
  76.5 55.7 %collective-permute-start.1 = (bf16[3,128,512]{2,1,0:T(8,128)(2,1)}, bf16[3,128,512]{2,1,0:T(8,128)(2,1)}, u32[]{:S(2)}, u32[]{:S(2)}) collective-permute-start(bf16[3,128,512]{2,1,0:T(8,128)(2,1)} %get-tuple-element.41), channel_id=1, source_target_pairs={{0,2},{1,3},{2,0},{3,1},{4,6},{5,7},{6,4},{7,5},{8,10},{9,11},{10,... | collective-permute-start | bytes 1179656 | tf_op jit(solution)/shard_map/ppermute | solution.py:69
  112.3 8.2 %collective-permute-start.21 = (bf16[64,256]{1,0:T(8,128)(2,1)}, bf16[64,256]{1,0:T(8,128)(2,1)S(1)}, u32[]{:S(2)}, u32[]{:S(2)}) collective-permute-start(bf16[64,256]{1,0:T(8,128)(2,1)} %get-tuple-element.78), channel_id=1, source_target_pairs={{0,6},{1,7},{2,4},{3,5},{4,10},{5,11},{6,8},{7,9},{8,14},{9,15},{1... | collective-permute-start | bytes 98312 | tf_op jit(solution)/shard_map/ppermute | solution.py:69
  125.8 14.0 %collective-permute-start.17 = (bf16[64,1280]{1,0:T(8,128)(2,1)}, bf16[64,1280]{1,0:T(8,128)(2,1)}, u32[]{:S(2)}, u32[]{:S(2)}) collective-permute-start(bf16[64,1280]{1,0:T(8,128)(2,1)} %pad_maximum_fusion.6), channel_id=1, source_target_pairs={{0,4},{1,5},{2,6},{3,7},{4,8},{5,9},{6,10},{7,11},{8,12},{9,13},{1... | collective-permute-start | bytes 491528 | tf_op jit(solution)/shard_map/ppermute | solution.py:69
  128.1 19.4 %collective-permute-start.18 = (bf16[64,1280]{1,0:T(8,128)(2,1)}, bf16[64,1280]{1,0:T(8,128)(2,1)}, u32[]{:S(2)}, u32[]{:S(2)}) collective-permute-start(bf16[64,1280]{1,0:T(8,128)(2,1)} %pad_maximum_fusion.7), channel_id=1, source_target_pairs={{0,8},{1,9},{2,10},{3,11},{4,12},{5,13},{6,14},{7,15},{8,0},{9,1},... | collective-permute-start | bytes 491528 | tf_op jit(solution)/shard_map/ppermute | solution.py:69
  131.1 16.4 %collective-permute-start.19 = (bf16[64,1280]{1,0:T(8,128)(2,1)}, bf16[64,1280]{1,0:T(8,128)(2,1)}, u32[]{:S(2)}, u32[]{:S(2)}) collective-permute-start(bf16[64,1280]{1,0:T(8,128)(2,1)} %pad_maximum_fusion.8), channel_id=1, source_target_pairs={{0,12},{1,13},{2,14},{3,15},{4,0},{5,1},{6,2},{7,3},{8,4},{9,5},{1... | collective-permute-start | bytes 491528 | tf_op jit(solution)/shard_map/ppermute | solution.py:69
  132.3 23.2 %collective-permute-start.37 = (bf16[64,1280]{1,0:T(8,128)(2,1)}, bf16[64,1280]{1,0:T(8,128)(2,1)}, u32[]{:S(2)}, u32[]{:S(2)}) collective-permute-start(bf16[64,1280]{1,0:T(8,128)(2,1)} %pad_maximum_fusion.10), channel_id=1, source_target_pairs={{0,4},{1,5},{2,6},{3,7},{4,8},{5,9},{6,10},{7,11},{8,12},{9,13},{1... | collective-permute-start | bytes 491528 | tf_op jit(solution)/shard_map/ppermute | solution.py:69
  133.2 25.2 %collective-permute-start.38 = (bf16[64,1280]{1,0:T(8,128)(2,1)}, bf16[64,1280]{1,0:T(8,128)(2,1)}, u32[]{:S(2)}, u32[]{:S(2)}) collective-permute-start(bf16[64,1280]{1,0:T(8,128)(2,1)} %pad_maximum_fusion.11), channel_id=1, source_target_pairs={{0,8},{1,9},{2,10},{3,11},{4,12},{5,13},{6,14},{7,15},{8,0},{9,1},... | collective-permute-start | bytes 491528 | tf_op jit(solution)/shard_map/ppermute | solution.py:69
  139.8 22.0 %collective-permute-start.39 = (bf16[64,1280]{1,0:T(8,128)(2,1)S(1)}, bf16[64,1280]{1,0:T(8,128)(2,1)S(1)}, u32[]{:S(2)}, u32[]{:S(2)}) collective-permute-start(bf16[64,1280]{1,0:T(8,128)(2,1)S(1)} %copy-done.21), channel_id=1, source_target_pairs={{0,12},{1,13},{2,14},{3,15},{4,0},{5,1},{6,2},{7,3},{8,4},{9,5},{1... | collective-permute-start | bytes 491528 | tf_op jit(solution)/shard_map/ppermute | solution.py:69
  147.5 17.5 %collective-permute-start.40 = (bf16[64,256]{1,0:T(8,128)(2,1)}, bf16[64,256]{1,0:T(8,128)(2,1)S(1)}, u32[]{:S(2)}, u32[]{:S(2)}) collective-permute-start(bf16[64,256]{1,0:T(8,128)(2,1)} %get-tuple-element.68), channel_id=1, source_target_pairs={{0,2},{1,3},{2,0},{3,1},{4,6},{5,7},{6,4},{7,5},{8,10},{9,11},{10,... | collective-permute-start | bytes 98312 | tf_op jit(solution)/shard_map/ppermute | solution.py:69
  147.6 17.5 %collective-permute-start.41 = (bf16[64,256]{1,0:T(8,128)(2,1)}, bf16[64,256]{1,0:T(8,128)(2,1)S(1)}, u32[]{:S(2)}, u32[]{:S(2)}) collective-permute-start(bf16[64,256]{1,0:T(8,128)(2,1)} %get-tuple-element.67), channel_id=1, source_target_pairs={{0,6},{1,7},{2,4},{3,5},{4,10},{5,11},{6,8},{7,9},{8,14},{9,15},{1... | collective-permute-start | bytes 98312 | tf_op jit(solution)/shard_map/ppermute | solution.py:69
  155.6 11.0 %collective-permute-start.42 = (bf16[64,256]{1,0:T(8,128)(2,1)S(1)}, bf16[64,256]{1,0:T(8,128)(2,1)S(1)}, u32[]{:S(2)}, u32[]{:S(2)}) collective-permute-start(bf16[64,256]{1,0:T(8,128)(2,1)S(1)} %copy-done.29), channel_id=1, source_target_pairs={{0,10},{1,11},{2,8},{3,9},{4,14},{5,15},{6,12},{7,13},{8,2},{9,3},... | collective-permute-start | bytes 98312 | tf_op jit(solution)/shard_map/ppermute | solution.py:69
  158.4 8.8 %collective-permute-start.43 = (bf16[64,256]{1,0:T(8,128)(2,1)S(1)}, bf16[64,256]{1,0:T(8,128)(2,1)S(1)}, u32[]{:S(2)}, u32[]{:S(2)}) collective-permute-start(bf16[64,256]{1,0:T(8,128)(2,1)S(1)} %copy-done.28), channel_id=1, source_target_pairs={{0,14},{1,15},{2,12},{3,13},{4,2},{5,3},{6,0},{7,1},{8,6},{9,7},{1... | collective-permute-start | bytes 98312 | tf_op jit(solution)/shard_map/ppermute | solution.py:69
  161.8 31.3 %collective-permute-start.11 = (bf16[128,512]{0,1:T(8,128)(2,1)S(1)}, bf16[128,512]{0,1:T(8,128)(2,1)S(1)}, u32[]{:S(2)}, u32[]{:S(2)}) collective-permute-start(bf16[128,512]{0,1:T(8,128)(2,1)S(1)} %get-tuple-element.47), channel_id=1, source_target_pairs={{0,2},{1,3},{2,0},{3,1},{4,6},{5,7},{6,4},{7,5},{8,10},{9,11},{10,... | collective-permute-start | bytes 393224 | tf_op jit(solution)/shard_map/ppermute | solution.py:69
  165.0 29.2 %collective-permute-start.12 = (bf16[128,512]{0,1:T(8,128)(2,1)S(1)}, bf16[128,512]{0,1:T(8,128)(2,1)S(1)}, u32[]{:S(2)}, u32[]{:S(2)}) collective-permute-start(bf16[128,512]{0,1:T(8,128)(2,1)S(1)} %get-tuple-element.49), channel_id=1, source_target_pairs={{0,1},{1,0},{2,3},{3,2},{4,5},{5,4},{6,7},{7,6},{8,9},{9,8},{10,11... | collective-permute-start | bytes 393224 | tf_op jit(solution)/shard_map/ppermute | solution.py:69
  165.1 32.9 %collective-permute-start.13 = (bf16[128,512]{0,1:T(8,128)(2,1)S(1)}, bf16[128,512]{0,1:T(8,128)(2,1)S(1)}, u32[]{:S(2)}, u32[]{:S(2)}) collective-permute-start(bf16[128,512]{0,1:T(8,128)(2,1)S(1)} %get-tuple-element.48), channel_id=1, source_target_pairs={{0,3},{1,2},{2,1},{3,0},{4,7},{5,6},{6,5},{7,4},{8,11},{9,10},{10,... | collective-permute-start | bytes 393224 | tf_op jit(solution)/shard_map/ppermute | solution.py:69
  188.2 10.0 %collective-permute-start.24 = (bf16[64,1280]{1,0:T(8,128)(2,1)S(1)}, bf16[64,1280]{1,0:T(8,128)(2,1)S(1)}, u32[]{:S(2)}, u32[]{:S(2)}) collective-permute-start(bf16[64,1280]{1,0:T(8,128)(2,1)S(1)} %pad_maximum_fusion.9), channel_id=1, source_target_pairs={{0,12},{1,13},{2,14},{3,15},{4,0},{5,1},{6,2},{7,3},{8,4},{9,5},{1... | collective-permute-start | bytes 491528 | tf_op jit(solution)/shard_map/ppermute | solution.py:69
  191.1 19.3 %collective-permute-start.25 = (bf16[64,1280]{1,0:T(8,128)(2,1)S(1)}, bf16[64,1280]{1,0:T(8,128)(2,1)S(1)}, u32[]{:S(2)}, u32[]{:S(2)}) collective-permute-start(bf16[64,1280]{1,0:T(8,128)(2,1)S(1)} %pad_maximum_fusion.9), channel_id=1, source_target_pairs={{0,8},{1,9},{2,10},{3,11},{4,12},{5,13},{6,14},{7,15},{8,0},{9,1},... | collective-permute-start | bytes 491528 | tf_op jit(solution)/shard_map/ppermute | solution.py:69
  193.1 17.4 %collective-permute-start.26 = (bf16[64,1280]{1,0:T(8,128)(2,1)S(1)}, bf16[64,1280]{1,0:T(8,128)(2,1)S(1)}, u32[]{:S(2)}, u32[]{:S(2)}) collective-permute-start(bf16[64,1280]{1,0:T(8,128)(2,1)S(1)} %pad_maximum_fusion.9), channel_id=1, source_target_pairs={{0,4},{1,5},{2,6},{3,7},{4,8},{5,9},{6,10},{7,11},{8,12},{9,13},{1... | collective-permute-start | bytes 491528 | tf_op jit(solution)/shard_map/ppermute | solution.py:69
  194.2 16.5 %collective-permute-start.44 = (bf16[64,1280]{1,0:T(8,128)(2,1)S(1)}, bf16[64,1280]{1,0:T(8,128)(2,1)S(1)}, u32[]{:S(2)}, u32[]{:S(2)}) collective-permute-start(bf16[64,1280]{1,0:T(8,128)(2,1)S(1)} %pad_maximum_fusion.13), channel_id=1, source_target_pairs={{0,12},{1,13},{2,14},{3,15},{4,0},{5,1},{6,2},{7,3},{8,4},{9,5},{1... | collective-permute-start | bytes 491528 | tf_op jit(solution)/shard_map/ppermute | solution.py:69
  198.0 17.6 %collective-permute-start.45 = (bf16[64,1280]{1,0:T(8,128)(2,1)S(1)}, bf16[64,1280]{1,0:T(8,128)(2,1)S(1)}, u32[]{:S(2)}, u32[]{:S(2)}) collective-permute-start(bf16[64,1280]{1,0:T(8,128)(2,1)S(1)} %pad_maximum_fusion.13), channel_id=1, source_target_pairs={{0,8},{1,9},{2,10},{3,11},{4,12},{5,13},{6,14},{7,15},{8,0},{9,1},... | collective-permute-start | bytes 491528 | tf_op jit(solution)/shard_map/ppermute | solution.py:69
  198.2 18.3 %collective-permute-start.46 = (bf16[64,1280]{1,0:T(8,128)(2,1)S(1)}, bf16[64,1280]{1,0:T(8,128)(2,1)S(1)}, u32[]{:S(2)}, u32[]{:S(2)}) collective-permute-start(bf16[64,1280]{1,0:T(8,128)(2,1)S(1)} %pad_maximum_fusion.13), channel_id=1, source_target_pairs={{0,4},{1,5},{2,6},{3,7},{4,8},{5,9},{6,10},{7,11},{8,12},{9,13},{1... | collective-permute-start | bytes 491528 | tf_op jit(solution)/shard_map/ppermute | solution.py:69
  222.5 12.2 %collective-permute-start.32 = (bf16[128,512]{0,1:T(8,128)(2,1)}, bf16[128,512]{0,1:T(8,128)(2,1)}, u32[]{:S(2)}, u32[]{:S(2)}) collective-permute-start(bf16[128,512]{0,1:T(8,128)(2,1)} %get-tuple-element.52), channel_id=1, source_target_pairs={{0,1},{1,0},{2,3},{3,2},{4,5},{5,4},{6,7},{7,6},{8,9},{9,8},{10,11... | collective-permute-start | bytes 393224 | tf_op jit(solution)/shard_map/ppermute | solution.py:69
  222.5 12.2 %collective-permute-start.33 = (bf16[128,512]{0,1:T(8,128)(2,1)}, bf16[128,512]{0,1:T(8,128)(2,1)}, u32[]{:S(2)}, u32[]{:S(2)}) collective-permute-start(bf16[128,512]{0,1:T(8,128)(2,1)} %get-tuple-element.51), channel_id=1, source_target_pairs={{0,3},{1,2},{2,1},{3,0},{4,7},{5,6},{6,5},{7,4},{8,11},{9,10},{10,... | collective-permute-start | bytes 393224 | tf_op jit(solution)/shard_map/ppermute | solution.py:69
  227.9 7.9 %collective-permute-start.52 = (bf16[128,512]{0,1:T(8,128)(2,1)S(1)}, bf16[128,512]{0,1:T(8,128)(2,1)S(1)}, u32[]{:S(2)}, u32[]{:S(2)}) collective-permute-start(bf16[128,512]{0,1:T(8,128)(2,1)S(1)} %get-tuple-element.55), channel_id=1, source_target_pairs={{0,1},{1,0},{2,3},{3,2},{4,5},{5,4},{6,7},{7,6},{8,9},{9,8},{10,11... | collective-permute-start | bytes 393224 | tf_op jit(solution)/shard_map/ppermute | solution.py:69
  (56 other events, 227.3 us)

commit v3 on v1

v3 whole, which is shorter than its diff:
```python
import jax
import jax.numpy as jnp
from jax import lax
from jax.sharding import Mesh, PartitionSpec as P

LOW = jnp.bfloat16
WIDE = jnp.float32


def dot(a, b, dims):
    return lax.dot_general(a, b, ((dims[:1], dims[1:]), ((), ())), preferred_element_type=WIDE)


def forward_parts(weights, inputs):
    pre_gate = dot(inputs, weights[0], (1, 1))
    pre_up = dot(inputs, weights[1], (1, 1))
    hidden = (jax.nn.silu(pre_gate) * pre_up).astype(LOW)
    return pre_gate, pre_up, hidden


def partial_readout(weights, inputs):
    hidden = forward_parts(weights, inputs)[2]
    return dot(hidden, weights[2], (1, 1))


def partial_steps(weights, keys, scaled):
    pre_gate, pre_up, hidden = forward_parts(weights, keys)
    step_second = dot(scaled, hidden, (0, 0))
    back = dot(scaled, weights[2], (1, 0))
    sig_gate = jax.nn.sigmoid(pre_gate)
    d_gate = (back * pre_up * sig_gate * (1.0 + pre_gate * (1.0 - sig_gate))).astype(LOW)
    d_up = (back * pre_gate * sig_gate).astype(LOW)
    step_first = dot(d_gate, keys, (0, 0))
    step_third = dot(d_up, keys, (0, 0))
    return step_first, step_third, step_second


def renorm(old, moved):
    old_norm = jnp.sqrt(jnp.sum(old * old, axis=-1, keepdims=True) + 1e-06)
    moved_norm = jnp.sqrt(jnp.sum(moved * moved, axis=-1, keepdims=True) + 1e-06)
    return moved * old_norm / moved_norm


def shards(
    query_tokens,
    key_tokens,
    value_tokens,
    learn_rates,
    fast_first,
    fast_third,
    fast_second,
    momentum_decay,
):
    planes = lax.axis_size("plane")
    index = lax.axis_index("quad")
    y, c = index // 2, index % 2
    width = fast_first.shape[2]
    half = width // 2
    own_rows = fast_first.shape[1]
    rows = 2 * own_rows
    tokens = key_tokens.shape[1]

    def quad_swap(array):
        return lax.all_to_all(array, "quad", 0, 0, tiled=True)

    def plane_swap(array):
        return lax.all_to_all(array, "plane", 0, 0, tiled=True)

    def across(array):
        return lax.ppermute(array, "quad", [(0, 2), (1, 3), (2, 0), (3, 1)])

    def by_head(array):
        split = array.reshape(-1, tokens, 2, width).transpose(2, 0, 1, 3)
        return jnp.concatenate([split, split], axis=0)

    def joined(array):
        return array.transpose(1, 0, 2, 3).reshape(array.shape[1], 4 * tokens, width)

    def from_quad(partial):
        got = quad_swap(partial.astype(LOW).reshape(4, tokens, width)).astype(WIDE)
        return jnp.concatenate([got[0] + got[2], got[1] + got[3]], axis=1).astype(LOW)

    def pick(flag, pair):
        return jnp.where(flag == 0, pair[0], pair[1])

    def spread(payload):
        got = plane_swap(jnp.broadcast_to(payload[None], (planes,) + payload.shape))
        first = got[:, :, :width].reshape(half, width)
        third = got[:, :, width : 2 * width].reshape(half, width)
        second = got[:, :, 2 * width :].reshape(planes, rows, 2, half).transpose(0, 2, 1, 3)
        return first, third, second.reshape(width, half)

    def halves(second):
        got = across(pick(1 - y, (second[:, 0], second[:, 1])))
        kept = pick(y, (second[:, 0], second[:, 1]))
        return jnp.where(
            y == 0, jnp.concatenate([kept, got], 1), jnp.concatenate([got, kept], 1)
        )

    def reduced(steps):
        second = steps[2].reshape(planes, 2, rows, half).transpose(0, 2, 1, 3)
        sent = jnp.concatenate(
            [
                steps[0].reshape(planes, rows, width),
                steps[1].reshape(planes, rows, width),
                second.reshape(planes, rows, width),
            ],
            axis=2,
        ).astype(LOW)
        total = jnp.sum(plane_swap(sent).astype(WIDE), axis=0)
        return total[:, :width], total[:, width : 2 * width], halves(total[:, 2 * width :].reshape(rows, 2, half))

    def as_three(parts):
        return jnp.stack([p.reshape(rows, width) for p in parts])

    own = jnp.stack([fast_first, fast_third, fast_second])
    moved = jnp.concatenate([own.transpose(1, 0, 2, 3)] * 2, axis=0)
    chip = quad_swap(moved)
    chip = chip.reshape(2, 2, 3, own_rows, width).transpose(0, 2, 1, 3, 4).reshape(2, 3, rows, width)
    mine = pick(y, (chip[0], chip[1]))
    second_all = chip[:, 2].reshape(2, rows, planes, 2, rows)
    second_y = pick(y, (second_all[:, :, :, 0], second_all[:, :, :, 1])).reshape(2, rows, half)
    full_zero = spread(jnp.concatenate([mine[0], mine[1], second_y[0], second_y[1]], axis=1))
    second_own = mine[2].reshape(rows, planes, 2, rows).transpose(0, 2, 1, 3)
    weights_zero = as_three([mine[0], mine[1], second_own]).astype(WIDE)

    scaled = learn_rates[:2, :, :, None] * value_tokens[:2].reshape(2, tokens, 2, width).astype(WIDE)
    scaled = scaled.astype(LOW).reshape(2, tokens, 2 * width)
    terms = []
    for b in range(2):
        pair = joined(quad_swap(by_head(jnp.stack([key_tokens[b], scaled[b]]))))
        terms.append(partial_steps(full_zero, pair[0], pair[1]))
    queries = joined(quad_swap(by_head(query_tokens)))
    out_zero = from_quad(partial_readout(full_zero, queries[0]))

    def payload_of(weights):
        low = weights.astype(LOW)
        return jnp.concatenate([low[0], low[1], halves(low[2].reshape(rows, 2, half))], axis=1)

    step_zero = as_three(reduced(terms[0]))
    weights_one = renorm(weights_zero, weights_zero + step_zero)
    full_one = spread(payload_of(weights_one))
    out_one = from_quad(partial_readout(full_one, queries[1]))
    step_one = as_three(reduced(terms[1]))
    decay = pick(c, momentum_decay)
    weights_two = renorm(weights_one, weights_one + (decay * step_zero + step_one))
    full_two = spread(payload_of(weights_two))
    out_two = from_quad(partial_readout(full_two, queries[2]))
    return jnp.stack([out_zero, out_one, out_two])


def solution(mesh):
    groups, count = mesh.shape["groups"], mesh.shape["tok"]
    split = Mesh(mesh.devices.reshape(groups, count // 4, 4), ("groups", "plane", "quad"))
    everywhere = P(None, ("groups", "plane", "quad"), None)
    rows = P(None, ("plane", "quad"), None)
    return jax.shard_map(
        shards,
        mesh=split,
        in_specs=(everywhere,) * 4 + (rows,) * 3 + (P(),),
        out_specs=everywhere,
        check_vma=False,
    )
```

time: 236 us -> 255 us (1.081)
  starting transfers between devices: 0.09 us -> 49.2 us
  waiting for transfers between devices: 179 us -> 139 us
  local copies, waits for them, and re-layouts: 9.58 us -> 34.1 us
  between operations: 13.4 us -> 2.1 us
  other arithmetic: 12.2 us -> 8.38 us
    all_to_all x0 -> x12, waiting for transfers between devices: none -> 125 us  [the longest x5 64.5 us: plane_swap(): return lax.all_to_all(array, 'plane', 0, 0, tiled=True)]
    all_gather x2 -> x0, waiting for transfers between devices: 95.3 us -> none  [the longest x1 49 us: shards(): full = lax.all_gather(both, 'tok', axis=3, tiled=True)]
    reduce_scatter x1 -> x0, waiting for transfers between devices: 84.1 us -> none  [shards(): summed = lax.psum_scatter(low, 'tok', scatter_dimension=3, tiled=True)]
    all_to_all x0 -> x12, starting transfers between devices: none -> 45.7 us  [the longest x7 25.6 us: quad_swap(): return lax.all_to_all(array, 'quad', 0, 0, tiled=True)]
    ppermute x0 -> x4, waiting for transfers between devices: none -> 13.3 us  [across(): return lax.ppermute(array, 'quad', [(0, 2), (1, 3), (2, 0), (3, 1)])]
    another operation x5 -> x3, other arithmetic: 7.58 us -> 0.22 us  [the longest x2 3.93 us: shards(): low = jnp.stack(terms).astype(jnp.bfloat16)]
    dot_general x0 -> x4, local copies, waits for them, and re-layouts: none -> 6.32 us  [dot(): lax.dot_general(a, b, ((dims[:1], dims[1:]), ((), ())), preferred_element...]
    slice x2 -> x19, local copies, waits for them, and re-layouts: 3.02 us -> 7.98 us  [the longest x1 1.96 us: spread(): got[:, :, 2 * width:].reshape(planes, rows, 2, half).transpose(0, 2, 1, 3)]
  transfers between devices with their start and end apart: 3 -> 16, of which waited for: 3 -> 14; matrix products, arithmetic and copies ran while one was open for 6% -> 16% of each run, Pallas kernels for 0% -> 0%
where the time goes in v3:
time: 255 us; the launch traced here: 254 us
  waiting for transfers between devices  139 us (55%)
  starting transfers between devices  49.2 us (19%)
  local copies, waits for them, and re-layouts  34.1 us (13%)
  matrix products  21 us (8%)
  other arithmetic  8.38 us (3%)
    all_to_all x5, waiting for transfers between devices, plane_swap(): return lax.all_to_all(array, 'plane', 0, 0, tiled=True)  64.5 us
    all_to_all x7, waiting for transfers between devices, quad_swap(): return lax.all_to_all(array, 'quad', 0, 0, tiled=True)  60.9 us
    all_to_all x7, starting transfers between devices, quad_swap(): return lax.all_to_all(array, 'quad', 0, 0, tiled=True)  25.6 us
    dot_general x18, matrix products, dot(): lax.dot_general(a, b, ((dims[:1], dims[1:]), ((), ())), preferred_element...  21 us
    all_to_all x5, starting transfers between devices, plane_swap(): return lax.all_to_all(array, 'plane', 0, 0, tiled=True)  20.2 us
    ppermute x4, waiting for transfers between devices, across(): return lax.ppermute(array, 'quad', [(0, 2), (1, 3), (2, 0), (3, 1)])  13.3 us
    dot_general x4, local copies, waits for them, and re-layouts, dot(): lax.dot_general(a, b, ((dims[:1], dims[1:]), ((), ())), preferred_element...  6.32 us
  transfers between devices with their start and end apart: 16, of which 14 were waited for; matrix products, arithmetic and copies ran while one was open for 16% of the time, Pallas kernels for 0%

profile of v3, /device:TPU:0, one launch (start us, length us, event | category | flops | bytes accessed | tf_op | source)
XLA Modules:
  0.0 253.5 jit_solution(5860020049064291036)
XLA Ops:
  1.8 4.4 %all-to-all-start.1 = ((bf16[4,3,32,512]{3,2,1,0:T(8,128)(2,1)}), bf16[4,3,32,512]{3,2,1,0:T(8,128)(2,1)S(1)}, u32[]{:S(2)}, u32[]{:S(2)}) async-start(bf16[4,3,32,512]{3,2,1,0:T(8,128)(2,1)} %pad_maximum_fusion.5), calls=%async_computation.1 | async-start | bytes 786432 | tf_op jit(solution)/shard_map/all_to_all | solution.py:64
  9.2 4.4 %all-to-all-done.1 = bf16[4,3,32,512]{3,2,1,0:T(8,128)(2,1)S(1)} async-done(((bf16[4,3,32,512]{3,2,1,0:T(8,128)(2,1)}), bf16[4,3,32,512]{3,2,1,0:T(8,128)(2,1)S(1)}, u32[]{:S(2)}, u32[]{:S(2)}) %all-to-all-start.1) | async-done | bytes 393248 | tf_op jit(solution)/shard_map/all_to_all | solution.py:64
  13.6 3.5 %all-to-all-start.4 = ((bf16[4,2,128,512]{3,2,1,0:T(8,128)(2,1)}), bf16[4,2,128,512]{3,2,1,0:T(8,128)(2,1)S(1)}, u32[]{:S(2)}, u32[]{:S(2)}) async-start(bf16[4,2,128,512]{3,2,1,0:T(8,128)(2,1)} %copy.122), calls=%async_computation.4 | async-start | bytes 2097152 | tf_op jit(solution)/shard_map/all_to_all | solution.py:64
  18.5 13.0 %all-to-all-done.4 = bf16[4,2,128,512]{3,2,1,0:T(8,128)(2,1)S(1)} async-done(((bf16[4,2,128,512]{3,2,1,0:T(8,128)(2,1)}), bf16[4,2,128,512]{3,2,1,0:T(8,128)(2,1)S(1)}, u32[]{:S(2)}, u32[]{:S(2)}) %all-to-all-start.4) | async-done | bytes 1048608 | tf_op jit(solution)/shard_map/all_to_all | solution.py:64
  31.5 3.5 %all-to-all-start.8 = ((bf16[4,2,128,512]{3,2,1,0:T(8,128)(2,1)}), bf16[4,2,128,512]{3,2,1,0:T(8,128)(2,1)S(1)}, u32[]{:S(2)}, u32[]{:S(2)}) async-start(bf16[4,2,128,512]{3,2,1,0:T(8,128)(2,1)} %copy.136), calls=%async_computation.8 | async-start | bytes 2097152 | tf_op jit(solution)/shard_map/all_to_all | solution.py:64
  38.0 11.5 %all-to-all-done.8 = bf16[4,2,128,512]{3,2,1,0:T(8,128)(2,1)S(1)} async-done(((bf16[4,2,128,512]{3,2,1,0:T(8,128)(2,1)}), bf16[4,2,128,512]{3,2,1,0:T(8,128)(2,1)S(1)}, u32[]{:S(2)}, u32[]{:S(2)}) %all-to-all-start.8) | async-done | bytes 1048608 | tf_op jit(solution)/shard_map/all_to_all | solution.py:64
  50.4 3.6 %all-to-all-start = ((bf16[4,3,128,512]{2,3,1,0:T(8,128)(2,1)}), bf16[4,3,128,512]{2,3,1,0:T(8,128)(2,1)S(1)}, u32[]{:S(2)}, u32[]{:S(2)}) async-start(bf16[4,3,128,512]{2,3,1,0:T(8,128)(2,1)} %copy.114), calls=%async_computation | async-start | bytes 3145728 | tf_op jit(solution)/shard_map/all_to_all | solution.py:64
  55.8 18.3 %all-to-all-done = bf16[4,3,128,512]{2,3,1,0:T(8,128)(2,1)S(1)} async-done(((bf16[4,3,128,512]{2,3,1,0:T(8,128)(2,1)}), bf16[4,3,128,512]{2,3,1,0:T(8,128)(2,1)S(1)}, u32[]{:S(2)}, u32[]{:S(2)}) %all-to-all-start) | async-done | bytes 1572896 | tf_op jit(solution)/shard_map/all_to_all | solution.py:64
  75.1 5.5 %all-to-all-start.2 = ((bf16[4,64,1536]{2,1,0:T(8,128)(2,1)}), bf16[4,64,1536]{2,1,0:T(8,128)(2,1)}, u32[]{:S(2)}, u32[]{:S(2)}) async-start(bf16[4,64,1536]{2,1,0:T(8,128)(2,1)} %broadcast_in_dim.6), calls=%async_computation.2 | async-start | bytes 1572864 | tf_op jit(solution)/shard_map/all_to_all | solution.py:67
  89.4 11.2 %all-to-all-done.2 = bf16[4,64,1536]{2,1,0:T(8,128)(2,1)} async-done(((bf16[4,64,1536]{2,1,0:T(8,128)(2,1)}), bf16[4,64,1536]{2,1,0:T(8,128)(2,1)}, u32[]{:S(2)}, u32[]{:S(2)}) %all-to-all-start.2) | async-done | bytes 786464 | tf_op jit(solution)/shard_map/all_to_all | solution.py:67
  108.0 2.5 fusion.20
  115.1 3.5 %all-to-all-start.5 = ((bf16[4,64,1536]{2,1,0:T(8,128)(2,1)}), bf16[4,64,1536]{2,1,0:T(8,128)(2,1)S(1)}, u32[]{:S(2)}, u32[]{:S(2)}) async-start(bf16[4,64,1536]{2,1,0:T(8,128)(2,1)} %pad_maximum_fusion.3), calls=%async_computation.5 | async-start | bytes 1572864 | tf_op jit(solution)/shard_map/all_to_all | solution.py:67
  119.8 2.0 copy.140
  121.8 2.7 %fusion.11 = (bf16[256,512]{1,0:T(8,128)(2,1)}, bf16[256,512]{1,0:T(8,128)(2,1)}, f32[512,256]{0,1:T(8,128)}) fusion(f32[256,512]{1,0:T(8,128)} %fusion.79, f32[512,256]{0,1:T(8,128)} %fusion.80, bf16[512,512]{1,0:T(8,128)(2,1)S(1)} %bitcast.225, bf16[256,512]{1,0:T(8,128)(2,1)} %bitcast.259), kind=kOutput, calls=%fused_computation.37 | convolution fusion | flops 135921664 | bytes 2883584 | tf_op jit(solution)/shard_map/dot_general | solution.py:11
  124.5 2.0 copy.139
  129.9 8.2 %all-to-all-done.5 = bf16[4,64,1536]{2,1,0:T(8,128)(2,1)S(1)} async-done(((bf16[4,64,1536]{2,1,0:T(8,128)(2,1)}), bf16[4,64,1536]{2,1,0:T(8,128)(2,1)S(1)}, u32[]{:S(2)}, u32[]{:S(2)}) %all-to-all-start.5) | async-done | bytes 786464 | tf_op jit(solution)/shard_map/all_to_all | solution.py:67
  138.2 4.2 %all-to-all-start.9 = ((bf16[4,64,1536]{2,1,0:T(8,128)(2,1)}), bf16[4,64,1536]{2,1,0:T(8,128)(2,1)}, u32[]{:S(2)}, u32[]{:S(2)}) async-start(bf16[4,64,1536]{2,1,0:T(8,128)(2,1)} %pad_maximum_fusion.4), calls=%async_computation.9 | async-start | bytes 1572864 | tf_op jit(solution)/shard_map/all_to_all | solution.py:67
  146.5 15.6 %all-to-all-done.9 = bf16[4,64,1536]{2,1,0:T(8,128)(2,1)} async-done(((bf16[4,64,1536]{2,1,0:T(8,128)(2,1)}), bf16[4,64,1536]{2,1,0:T(8,128)(2,1)}, u32[]{:S(2)}, u32[]{:S(2)}) %all-to-all-start.9) | async-done | bytes 786464 | tf_op jit(solution)/shard_map/all_to_all | solution.py:67
  162.0 3.7 %all-to-all-start.3 = ((bf16[4,128,512]{2,1,0:T(8,128)(2,1)}), bf16[4,128,512]{2,1,0:T(8,128)(2,1)S(1)}, u32[]{:S(2)}, u32[]{:S(2)}) async-start(bf16[4,128,512]{2,1,0:T(8,128)(2,1)} %bitcast.17), calls=%async_computation.3 | async-start | bytes 1048576 | tf_op jit(solution)/shard_map/all_to_all | solution.py:64
  169.5 6.2 %collective-permute-done.2 = f32[64,256]{1,0:T(8,128)S(1)} collective-permute-done((f32[64,256]{1,0:T(8,128)S(1)}, f32[64,256]{1,0:T(8,128)S(1)}, u32[]{:S(2)}, u32[]{:S(2)}) %collective-permute-start.2) | collective-permute-done | bytes 65568 | tf_op jit(solution)/shard_map/ppermute | solution.py:70
  176.7 3.6 %collective-permute-done.3 = bf16[64,256]{1,0:T(8,128)(2,1)S(1)} collective-permute-done((bf16[64,256]{1,0:T(8,128)(2,1)S(1)}, bf16[64,256]{1,0:T(8,128)(2,1)S(1)}, u32[]{:S(2)}, u32[]{:S(2)}) %collective-permute-start.3) | collective-permute-done | bytes 32800 | tf_op jit(solution)/shard_map/ppermute | solution.py:70
  181.2 3.5 %all-to-all-start.10 = ((bf16[4,64,1536]{2,1,0:T(8,128)(2,1)}), bf16[4,64,1536]{2,1,0:T(8,128)(2,1)S(1)}, u32[]{:S(2)}, u32[]{:S(2)}) async-start(bf16[4,64,1536]{2,1,0:T(8,128)(2,1)} %broadcast_in_dim.8), calls=%async_computation.10 | async-start | bytes 1572864 | tf_op jit(solution)/shard_map/all_to_all | solution.py:67
  185.3 3.6 %collective-permute-done.1 = bf16[64,256]{1,0:T(8,128)(2,1)S(1)} collective-permute-done((bf16[64,256]{1,0:T(8,128)(2,1)S(1)}, bf16[64,256]{1,0:T(8,128)(2,1)S(1)}, u32[]{:S(2)}, u32[]{:S(2)}) %collective-permute-start.1) | collective-permute-done | bytes 32800 | tf_op jit(solution)/shard_map/ppermute | solution.py:70
  188.9 14.8 %all-to-all-done.10 = bf16[4,64,1536]{2,1,0:T(8,128)(2,1)S(1)} async-done(((bf16[4,64,1536]{2,1,0:T(8,128)(2,1)}), bf16[4,64,1536]{2,1,0:T(8,128)(2,1)S(1)}, u32[]{:S(2)}, u32[]{:S(2)}) %all-to-all-start.10) | async-done | bytes 786464 | tf_op jit(solution)/shard_map/all_to_all | solution.py:67
  204.7 3.5 %all-to-all-start.6 = ((bf16[4,64,1536]{2,1,0:T(8,128)(2,1)}), bf16[4,64,1536]{2,1,0:T(8,128)(2,1)S(1)}, u32[]{:S(2)}, u32[]{:S(2)}) async-start(bf16[4,64,1536]{2,1,0:T(8,128)(2,1)} %broadcast_in_dim.7), calls=%async_computation.6 | async-start | bytes 1572864 | tf_op jit(solution)/shard_map/all_to_all | solution.py:67
  210.6 2.5 convolution_convert_fusion
  213.1 14.7 %all-to-all-done.6 = bf16[4,64,1536]{2,1,0:T(8,128)(2,1)S(1)} async-done(((bf16[4,64,1536]{2,1,0:T(8,128)(2,1)}), bf16[4,64,1536]{2,1,0:T(8,128)(2,1)S(1)}, u32[]{:S(2)}, u32[]{:S(2)}) %all-to-all-start.6) | async-done | bytes 786464 | tf_op jit(solution)/shard_map/all_to_all | solution.py:67
  227.7 3.5 %all-to-all-start.11 = ((bf16[4,128,512]{2,1,0:T(8,128)(2,1)}), bf16[4,128,512]{2,1,0:T(8,128)(2,1)S(1)}, u32[]{:S(2)}, u32[]{:S(2)}) async-start(bf16[4,128,512]{2,1,0:T(8,128)(2,1)} %bitcast.272), calls=%async_computation.11 | async-start | bytes 1048576 | tf_op jit(solution)/shard_map/all_to_all | solution.py:64
  232.4 2.5 convolution_convert_fusion.1
  234.9 5.1 %all-to-all-done.11 = bf16[4,128,512]{2,1,0:T(8,128)(2,1)S(1)} async-done(((bf16[4,128,512]{2,1,0:T(8,128)(2,1)}), bf16[4,128,512]{2,1,0:T(8,128)(2,1)S(1)}, u32[]{:S(2)}, u32[]{:S(2)}) %all-to-all-start.11) | async-done | bytes 524320 | tf_op jit(solution)/shard_map/all_to_all | solution.py:64
  240.0 3.5 %all-to-all-start.7 = ((bf16[4,128,512]{2,1,0:T(8,128)(2,1)}), bf16[4,128,512]{2,1,0:T(8,128)(2,1)S(1)}, u32[]{:S(2)}, u32[]{:S(2)}) async-start(bf16[4,128,512]{2,1,0:T(8,128)(2,1)} %bitcast.50), calls=%async_computation.7 | async-start | bytes 1048576 | tf_op jit(solution)/shard_map/all_to_all | solution.py:64
  243.8 8.5 %all-to-all-done.7 = bf16[4,128,512]{2,1,0:T(8,128)(2,1)S(1)} async-done(((bf16[4,128,512]{2,1,0:T(8,128)(2,1)}), bf16[4,128,512]{2,1,0:T(8,128)(2,1)S(1)}, u32[]{:S(2)}, u32[]{:S(2)}) %all-to-all-start.7) | async-done | bytes 524320 | tf_op jit(solution)/shard_map/all_to_all | solution.py:64
  (155 shorter events, 52.8 us)
Async XLA Ops:
  0.0 6.1 %slice-start = ((bf16[3,128,1024]{2,1,0:T(8,128)(2,1)}), bf16[2,128,1024]{2,1,0:T(8,128)(2,1)S(1)}, s32[]{:S(2)}) async-start(bf16[3,128,1024]{2,1,0:T(8,128)(2,1)} %param.10), calls=%async_computation.12 | async-start | bytes 1048576 | tf_op jit(solution)/shard_map/slice | solution.py:127
  1.8 4.7 %slice-start.1 = ((f32[3,128,2]{1,2,0:T(2,128)}), f32[2,128,2]{1,2,0:T(2,128)S(1)}, s32[]{:S(2)}) async-start(f32[3,128,2]{1,2,0:T(2,128)} %param.11), calls=%async_computation.13 | async-start | bytes 4096 | tf_op jit(solution)/shard_map/slice | solution.py:127
  1.8 11.8 %all-to-all-start.1 = ((bf16[4,3,32,512]{3,2,1,0:T(8,128)(2,1)}), bf16[4,3,32,512]{3,2,1,0:T(8,128)(2,1)S(1)}, u32[]{:S(2)}, u32[]{:S(2)}) async-start(bf16[4,3,32,512]{3,2,1,0:T(8,128)(2,1)} %pad_maximum_fusion.5), calls=%async_computation.1 | async-start | bytes 786432 | tf_op jit(solution)/shard_map/all_to_all | solution.py:64
  13.6 18.0 %all-to-all-start.4 = ((bf16[4,2,128,512]{3,2,1,0:T(8,128)(2,1)}), bf16[4,2,128,512]{3,2,1,0:T(8,128)(2,1)S(1)}, u32[]{:S(2)}, u32[]{:S(2)}) async-start(bf16[4,2,128,512]{3,2,1,0:T(8,128)(2,1)} %copy.122), calls=%async_computation.4 | async-start | bytes 2097152 | tf_op jit(solution)/shard_map/all_to_all | solution.py:64
  31.5 5.1 %copy-start.3 = (bf16[4,2,128,512]{3,2,1,0:T(8,128)(2,1)}, bf16[4,2,128,512]{3,2,1,0:T(8,128)(2,1)S(1)}, u32[]{:S(2)}) copy-start(bf16[4,2,128,512]{3,2,1,0:T(8,128)(2,1)S(1)} %all-to-all-done.4) | copy-start | bytes 3145732
  31.5 18.0 %all-to-all-start.8 = ((bf16[4,2,128,512]{3,2,1,0:T(8,128)(2,1)}), bf16[4,2,128,512]{3,2,1,0:T(8,128)(2,1)S(1)}, u32[]{:S(2)}, u32[]{:S(2)}) async-start(bf16[4,2,128,512]{3,2,1,0:T(8,128)(2,1)} %copy.136), calls=%async_computation.8 | async-start | bytes 2097152 | tf_op jit(solution)/shard_map/all_to_all | solution.py:64
  50.4 23.6 %all-to-all-start = ((bf16[4,3,128,512]{2,3,1,0:T(8,128)(2,1)}), bf16[4,3,128,512]{2,3,1,0:T(8,128)(2,1)S(1)}, u32[]{:S(2)}, u32[]{:S(2)}) async-start(bf16[4,3,128,512]{2,3,1,0:T(8,128)(2,1)} %copy.114), calls=%async_computation | async-start | bytes 3145728 | tf_op jit(solution)/shard_map/all_to_all | solution.py:64
  55.8 24.8 %copy-start.17 = (f32[2]{0:T(128)S(1)}, f32[2]{0:T(128)}, u32[]{:S(2)}) copy-start(f32[2]{0:T(128)} %param.15) | copy-start | bytes 28
  74.1 8.6 %copy-start = (bf16[4,3,128,512]{2,3,1,0:T(8,128)(2,1)}, bf16[4,3,128,512]{2,3,1,0:T(8,128)(2,1)S(1)}, u32[]{:S(2)}) copy-start(bf16[4,3,128,512]{2,3,1,0:T(8,128)(2,1)S(1)} %all-to-all-done) | copy-start | bytes 4718596
  75.1 25.5 %all-to-all-start.2 = ((bf16[4,64,1536]{2,1,0:T(8,128)(2,1)}), bf16[4,64,1536]{2,1,0:T(8,128)(2,1)}, u32[]{:S(2)}, u32[]{:S(2)}) async-start(bf16[4,64,1536]{2,1,0:T(8,128)(2,1)} %broadcast_in_dim.6), calls=%async_computation.2 | async-start | bytes 1572864 | tf_op jit(solution)/shard_map/all_to_all | solution.py:67
  83.4 2.4 copy-start.5
  103.3 2.2 copy-start.2
  103.3 3.4 %copy-start.6 = (bf16[4,64,512]{2,1,0:T(8,128)(2,1)S(1)}, bf16[4,64,512]{2,1,0:T(8,128)(2,1)}, u32[]{:S(2)}) copy-start(bf16[4,64,512]{2,1,0:T(8,128)(2,1)} %get-tuple-element.39) | copy-start | bytes 786436
  111.8 1.7 copy-start.15
  111.8 2.0 copy-start.13
  114.2 4.5 %copy-start.7 = (bf16[4,64,512]{2,1,0:T(8,128)(2,1)S(1)}, bf16[4,64,512]{2,1,0:T(8,128)(2,1)}, u32[]{:S(2)}) copy-start(bf16[4,64,512]{2,1,0:T(8,128)(2,1)} %get-tuple-element.39) | copy-start | bytes 786436
  115.1 23.1 %all-to-all-start.5 = ((bf16[4,64,1536]{2,1,0:T(8,128)(2,1)}), bf16[4,64,1536]{2,1,0:T(8,128)(2,1)S(1)}, u32[]{:S(2)}, u32[]{:S(2)}) async-start(bf16[4,64,1536]{2,1,0:T(8,128)(2,1)} %pad_maximum_fusion.3), calls=%async_computation.5 | async-start | bytes 1572864 | tf_op jit(solution)/shard_map/all_to_all | solution.py:67
  126.5 1.9 copy-start.16
  126.5 2.2 copy-start.14
  138.2 23.9 %all-to-all-start.9 = ((bf16[4,64,1536]{2,1,0:T(8,128)(2,1)}), bf16[4,64,1536]{2,1,0:T(8,128)(2,1)}, u32[]{:S(2)}, u32[]{:S(2)}) async-start(bf16[4,64,1536]{2,1,0:T(8,128)(2,1)} %pad_maximum_fusion.4), calls=%async_computation.9 | async-start | bytes 1572864 | tf_op jit(solution)/shard_map/all_to_all | solution.py:67
  145.7 23.4 %collective-permute-start = (f32[64,256]{1,0:T(8,128)S(1)}, f32[64,256]{1,0:T(8,128)S(1)}, u32[]{:S(2)}, u32[]{:S(2)}) collective-permute-start(f32[64,256]{1,0:T(8,128)S(1)} %bitcast.284), channel_id=1, source_target_pairs={{0,2},{1,3},{2,0},{3,1},{4,6},{5,7},{6,4},{7,5},{8,10},{9,11},{10,... | collective-permute-start | bytes 196616 | tf_op jit(solution)/shard_map/ppermute | solution.py:70
  162.0 18.3 %all-to-all-start.3 = ((bf16[4,128,512]{2,1,0:T(8,128)(2,1)}), bf16[4,128,512]{2,1,0:T(8,128)(2,1)S(1)}, u32[]{:S(2)}, u32[]{:S(2)}) async-start(bf16[4,128,512]{2,1,0:T(8,128)(2,1)} %bitcast.17), calls=%async_computation.3 | async-start | bytes 1048576 | tf_op jit(solution)/shard_map/all_to_all | solution.py:64
  165.7 3.5 %copy-start.11 = (bf16[1,64,512]{2,1,0:T(8,128)(2,1)S(1)}, bf16[1,64,512]{2,1,0:T(8,128)(2,1)}, u32[]{:S(2)}) copy-start(bf16[1,64,512]{2,1,0:T(8,128)(2,1)} %stack_reshape.3) | copy-start | bytes 196612
  167.3 8.5 %collective-permute-start.2 = (f32[64,256]{1,0:T(8,128)S(1)}, f32[64,256]{1,0:T(8,128)S(1)}, u32[]{:S(2)}, u32[]{:S(2)}) collective-permute-start(f32[64,256]{1,0:T(8,128)S(1)} %get-tuple-element.66), channel_id=1, source_target_pairs={{0,2},{1,3},{2,0},{3,1},{4,6},{5,7},{6,4},{7,5},{8,10},{9,11},{10,... | collective-permute-start | bytes 196616 | tf_op jit(solution)/shard_map/ppermute | solution.py:70
  176.3 4.0 %collective-permute-start.3 = (bf16[64,256]{1,0:T(8,128)(2,1)S(1)}, bf16[64,256]{1,0:T(8,128)(2,1)S(1)}, u32[]{:S(2)}, u32[]{:S(2)}) collective-permute-start(bf16[64,256]{1,0:T(8,128)(2,1)S(1)} %get-tuple-element.64), channel_id=1, source_target_pairs={{0,2},{1,3},{2,0},{3,1},{4,6},{5,7},{6,4},{7,5},{8,10},{9,11},{10,... | collective-permute-start | bytes 98312 | tf_op jit(solution)/shard_map/ppermute | solution.py:70
  181.2 22.5 %all-to-all-start.10 = ((bf16[4,64,1536]{2,1,0:T(8,128)(2,1)}), bf16[4,64,1536]{2,1,0:T(8,128)(2,1)S(1)}, u32[]{:S(2)}, u32[]{:S(2)}) async-start(bf16[4,64,1536]{2,1,0:T(8,128)(2,1)} %broadcast_in_dim.8), calls=%async_computation.10 | async-start | bytes 1572864 | tf_op jit(solution)/shard_map/all_to_all | solution.py:67
  184.9 4.0 %collective-permute-start.1 = (bf16[64,256]{1,0:T(8,128)(2,1)S(1)}, bf16[64,256]{1,0:T(8,128)(2,1)S(1)}, u32[]{:S(2)}, u32[]{:S(2)}) collective-permute-start(bf16[64,256]{1,0:T(8,128)(2,1)S(1)} %get-tuple-element.62), channel_id=1, source_target_pairs={{0,2},{1,3},{2,0},{3,1},{4,6},{5,7},{6,4},{7,5},{8,10},{9,11},{10,... | collective-permute-start | bytes 98312 | tf_op jit(solution)/shard_map/ppermute | solution.py:70
  204.7 23.1 %all-to-all-start.6 = ((bf16[4,64,1536]{2,1,0:T(8,128)(2,1)}), bf16[4,64,1536]{2,1,0:T(8,128)(2,1)S(1)}, u32[]{:S(2)}, u32[]{:S(2)}) async-start(bf16[4,64,1536]{2,1,0:T(8,128)(2,1)} %broadcast_in_dim.7), calls=%async_computation.6 | async-start | bytes 1572864 | tf_op jit(solution)/shard_map/all_to_all | solution.py:67
  208.3 1.9 copy-start.9
  213.1 18.9 %copy-start.8 = (bf16[1,4,128,512]{3,2,1,0:T(8,128)(2,1)S(1)}, bf16[1,4,128,512]{3,2,1,0:T(8,128)(2,1)}, u32[]{:S(2)}) copy-start(bf16[1,4,128,512]{3,2,1,0:T(8,128)(2,1)} %get-tuple-element.15) | copy-start | bytes 1572868
  227.7 12.3 %all-to-all-start.11 = ((bf16[4,128,512]{2,1,0:T(8,128)(2,1)}), bf16[4,128,512]{2,1,0:T(8,128)(2,1)S(1)}, u32[]{:S(2)}, u32[]{:S(2)}) async-start(bf16[4,128,512]{2,1,0:T(8,128)(2,1)} %bitcast.272), calls=%async_computation.11 | async-start | bytes 1048576 | tf_op jit(solution)/shard_map/all_to_all | solution.py:64
  240.0 12.3 %all-to-all-start.7 = ((bf16[4,128,512]{2,1,0:T(8,128)(2,1)}), bf16[4,128,512]{2,1,0:T(8,128)(2,1)S(1)}, u32[]{:S(2)}, u32[]{:S(2)}) async-start(bf16[4,128,512]{2,1,0:T(8,128)(2,1)} %bitcast.50), calls=%async_computation.7 | async-start | bytes 1048576 | tf_op jit(solution)/shard_map/all_to_all | solution.py:64
  (4 other events, 4.0 us)

commit v4 on v3

v4 whole, which is shorter than its diff:
```python
import functools

import jax
import jax.numpy as jnp
from jax import lax
from jax.experimental import pallas as pl
from jax.experimental.pallas import tpu as pltpu
from jax.sharding import Mesh, PartitionSpec as P

LOW = jnp.bfloat16
WIDE = jnp.float32


def call(kernel, outs, flops, *operands):
    shapes = [jax.ShapeDtypeStruct(s, d) for s, d in outs]
    moved = sum(a.size * a.dtype.itemsize for a in operands)
    moved += sum(s.size * s.dtype.itemsize for s in shapes)
    return pl.pallas_call(
        kernel,
        out_shape=shapes,
        in_specs=[pl.BlockSpec(memory_space=pltpu.VMEM)] * len(operands),
        out_specs=[pl.BlockSpec(memory_space=pltpu.VMEM)] * len(shapes),
        compiler_params=pltpu.CompilerParams(vmem_limit_bytes=40 * 2**20),
        cost_estimate=pl.CostEstimate(flops=flops, bytes_accessed=moved, transcendentals=0),
    )(*operands)


def dot(a, b, dims):
    return lax.dot_general(a, b, ((dims[:1], dims[1:]), ((), ())), preferred_element_type=WIDE)


def loaded(full):
    planes, rows, columns = full.shape
    width = columns // 3
    half = width // 2
    first = full[:, :, :width].reshape(half, width)
    third = full[:, :, width : 2 * width].reshape(half, width)
    pieces = []
    for z in range(planes):
        for y in range(2):
            start = 2 * width + y * half
            pieces.append(full[z, :, start : start + half])
    return first, third, jnp.concatenate(pieces, axis=0)


def steps_kernel(block, full, own, near, far, cross, sent):
    planes, rows, columns = full.shape
    width = columns // 3
    half = width // 2
    first, third, second = loaded(full)
    parts = (own, near, far, cross)
    keys = jnp.concatenate([p[2 * block] for p in parts], axis=0)
    scaled = jnp.concatenate([p[2 * block + 1] for p in parts], axis=0)
    pre_gate = dot(keys, first, (1, 1))
    pre_up = dot(keys, third, (1, 1))
    back = dot(scaled, second, (1, 0))
    sig_gate = jax.nn.sigmoid(pre_gate)
    silu = pre_gate * sig_gate
    hidden = (silu * pre_up).astype(LOW)
    d_gate = (back * pre_up * sig_gate * (1.0 + pre_gate * (1.0 - sig_gate))).astype(LOW)
    d_up = (back * silu).astype(LOW)
    step_first = dot(d_gate, keys, (0, 0)).astype(LOW)
    step_third = dot(d_up, keys, (0, 0)).astype(LOW)
    step_second = dot(scaled, hidden, (0, 0)).astype(LOW)
    sent[:, :, :width] = step_first.reshape(planes, rows, width)
    sent[:, :, width : 2 * width] = step_third.reshape(planes, rows, width)
    for z in range(planes):
        for y in range(2):
            start = 2 * width + y * half
            at = (2 * z + y) * rows
            sent[z, :, start : start + half] = step_second[at : at + rows]


def readout_kernel(block, full, own, near, far, cross, kept, to_near, to_far, to_cross):
    tokens = kept.shape[0]
    first, third, second = loaded(full)
    inputs = jnp.concatenate([p[block] for p in (own, near, far, cross)], axis=0)
    pre_gate = dot(inputs, first, (1, 1))
    pre_up = dot(inputs, third, (1, 1))
    hidden = (pre_gate * jax.nn.sigmoid(pre_gate) * pre_up).astype(LOW)
    result = dot(hidden, second, (1, 1))
    kept[...] = result[:tokens]
    for i, out in enumerate((to_near, to_far, to_cross)):
        out[...] = result[(i + 1) * tokens : (i + 2) * tokens].astype(LOW)


def square_sums(array, width):
    half = width // 2
    columns = []
    for y in range(2):
        piece = array[:, 2 * width + y * half : 2 * width + (y + 1) * half]
        columns.append(jnp.sum(piece * piece, axis=1, keepdims=True))
    return columns


def moved_kernel(got, old, momentum, decay, new_momentum, moved, sums):
    planes, rows, columns = got.shape
    width = columns // 3
    total = got[0].astype(WIDE)
    for z in range(1, planes):
        total = total + got[z].astype(WIDE)
    before = old[...].astype(WIDE)
    if momentum is not None:
        total = decay[0:1, 0:1] * momentum[...] + total
    after = before + total
    if new_momentum is not None:
        new_momentum[...] = total
    moved[...] = after
    parts = square_sums(after, width) + square_sums(before, width)
    sums[...] = jnp.concatenate(parts + [jnp.zeros((rows, 124), WIDE)], axis=1)


def first_moved_kernel(got, old, new_momentum, moved, sums):
    moved_kernel(got, old, None, None, new_momentum, moved, sums)


def second_moved_kernel(got, old, momentum, decay, moved, sums):
    moved_kernel(got, old, momentum, decay, None, moved, sums)


def scaled_kernel(moved, old, own_sums, far_sums, new, payload):
    planes, rows, columns = payload.shape
    width = columns // 3
    half = width // 2
    after = moved[...]
    before = old[...].astype(WIDE)
    sums = own_sums[...] + far_sums[...]

    def factor(old_sum, moved_sum):
        return jnp.sqrt(old_sum + 1e-06), jnp.sqrt(moved_sum + 1e-06)

    pieces = []
    for m in range(2):
        a = after[:, m * width : (m + 1) * width]
        b = before[:, m * width : (m + 1) * width]
        up, down = factor(
            jnp.sum(b * b, axis=1, keepdims=True), jnp.sum(a * a, axis=1, keepdims=True)
        )
        pieces.append(a * (up / down))
    for y in range(2):
        a = after[:, 2 * width + y * half : 2 * width + (y + 1) * half]
        up, down = factor(sums[:, y + 2 : y + 3], sums[:, y : y + 1])
        pieces.append(a * (up / down))
    result = jnp.concatenate(pieces, axis=1)
    if new is not None:
        new[...] = result
    low = result.astype(LOW)
    for z in range(planes):
        payload[z] = low


def last_scaled_kernel(moved, old, own_sums, far_sums, payload):
    scaled_kernel(moved, old, own_sums, far_sums, None, payload)


def shards(
    query_tokens,
    key_tokens,
    value_tokens,
    learn_rates,
    fast_first,
    fast_third,
    fast_second,
    momentum_decay,
):
    planes = lax.axis_size("plane")
    index = lax.axis_index("quad")
    y, c = index // 2, index % 2
    width = fast_first.shape[2]
    half = width // 2
    own_rows = fast_first.shape[1]
    rows = 2 * own_rows
    tokens = key_tokens.shape[1]

    def send(array, offset):
        return lax.ppermute(array, "quad", [(q, q ^ offset) for q in range(4)])

    def plane_swap(array):
        return lax.all_to_all(array, "plane", 0, 0, tiled=True)

    def heads(array):
        low, high = array[..., :width], array[..., width:]
        return jnp.where(c == 0, low, high), jnp.where(c == 0, high, low)

    def ordered(flag, a, b, axis):
        return jnp.where(flag == 0, jnp.concatenate([a, b], axis), jnp.concatenate([b, a], axis))

    def to_quad(array):
        mine, other = heads(array)
        return mine, send(other, 1), send(mine, 2), send(other, 3)

    columns = fast_second.reshape(2, own_rows, planes, 2, rows)
    split = [columns[:, :, :, i].reshape(2, own_rows, half) for i in range(2)]
    second_same = jnp.where(y == 0, split[0], split[1])
    second_far = jnp.where(y == 0, split[1], split[0])
    same = jnp.concatenate([fast_first, fast_third, second_same], axis=2)
    same_mine, same_other = jnp.where(c == 0, same[0], same[1]), jnp.where(c == 0, same[1], same[0])
    far_mine = jnp.where(c == 0, second_far[0], second_far[1])
    far_other = jnp.where(c == 0, second_far[1], second_far[0])
    same_rows = ordered(c, same_mine, send(same_other, 1), 0)
    far_rows = ordered(c, send(far_mine, 2), send(far_other, 3), 0)
    second_rows = ordered(y, same_rows[:, 2 * width :], far_rows, 1)
    zero = jnp.concatenate([same_rows[:, : 2 * width], second_rows], axis=1)
    full_zero = plane_swap(jnp.broadcast_to(zero[None], (planes,) + zero.shape))

    scaled = learn_rates[:2, :, :, None] * value_tokens[:2].reshape(2, tokens, 2, width).astype(WIDE)
    scaled = scaled.astype(LOW).reshape(2, tokens, 2 * width)
    pairs = jnp.stack([key_tokens[0], scaled[0], key_tokens[1], scaled[1]])
    pairs, zero = lax.optimization_barrier((pairs, zero))
    pairs = to_quad(pairs)
    query_tokens, pairs = lax.optimization_barrier((query_tokens, pairs))
    queries = to_quad(query_tokens)

    layout = (planes, rows, 3 * width)
    flat = layout[1:]
    unit = 2 * 4 * tokens * width * half

    def steps(block):
        kernel = functools.partial(steps_kernel, block)
        return call(kernel, [(layout, LOW)], 6 * unit, full_zero, *pairs)[0]

    def readout(block, full):
        kernel = functools.partial(readout_kernel, block)
        piece = (tokens, width)
        outs = [(piece, WIDE), (piece, LOW), (piece, LOW), (piece, LOW)]
        kept, near, far, cross = call(kernel, outs, 3 * unit, full, *queries)
        near, far, cross = send(near, 1), send(far, 2), send(cross, 3)
        mine = (kept + far.astype(WIDE)).astype(LOW)
        other = (near.astype(WIDE) + cross.astype(WIDE)).astype(LOW)
        return ordered(c, mine, other, 1)

    got_zero = plane_swap(steps(0))
    got_one = plane_swap(steps(1))
    out_zero = readout(0, full_zero)

    sums_shape = (rows, 128)
    step_zero, moved, sums = call(
        first_moved_kernel, [(flat, WIDE), (flat, WIDE), (sums_shape, WIDE)], 0, got_zero, zero
    )
    weights_one, payload = call(
        scaled_kernel, [(flat, WIDE), (layout, LOW)], 0, moved, zero, sums, send(sums, 2)
    )
    full_one = plane_swap(payload)
    out_one = readout(1, full_one)

    decay = jnp.broadcast_to(jnp.where(c == 0, momentum_decay[0], momentum_decay[1]), (8, 128))
    moved, sums = call(
        second_moved_kernel,
        [(flat, WIDE), (sums_shape, WIDE)],
        0,
        got_one,
        weights_one,
        step_zero,
        decay,
    )
    payload = call(
        last_scaled_kernel, [(layout, LOW)], 0, moved, weights_one, sums, send(sums, 2)
    )[0]
    full_two = plane_swap(payload)
    out_two = readout(2, full_two)
    return jnp.stack([out_zero, out_one, out_two])


def solution(mesh):
    groups, count = mesh.shape["groups"], mesh.shape["tok"]
    split = Mesh(mesh.devices.reshape(groups, count // 4, 4), ("groups", "plane", "quad"))
    everywhere = P(None, ("groups", "plane", "quad"), None)
    rows = P(None, ("plane", "quad"), None)
    return jax.shard_map(
        shards,
        mesh=split,
        in_specs=(everywhere,) * 4 + (rows,) * 3 + (P(),),
        out_specs=everywhere,
        check_vma=False,
    )
```

time: 255 us -> 150 us (0.59)
  waiting for transfers between devices: 139 us -> 86.2 us
  local copies, waits for them, and re-layouts: 34.1 us -> 9.74 us
  matrix products: 21 us -> 0 us
  starting transfers between devices: 49.2 us -> 38.5 us
  Pallas kernels: 0 us -> 9.83 us
  other arithmetic: 8.38 us -> 3.18 us
    all_to_all x7 -> x0, waiting for transfers between devices: 60.9 us -> none  [quad_swap(): return lax.all_to_all(array, 'quad', 0, 0, tiled=True)]
    all_to_all x7 -> x0, starting transfers between devices: 25.6 us -> none  [quad_swap(): return lax.all_to_all(array, 'quad', 0, 0, tiled=True)]
    ppermute x4 -> x20, waiting for transfers between devices: 13.3 us -> 37.1 us  [send(): return lax.ppermute(array, 'quad', [(q, q ^ offset) for q in range(4)])]
    dot_general x18 -> x0, matrix products: 21 us -> none  [dot(): lax.dot_general(a, b, ((dims[:1], dims[1:]), ((), ())), preferred_element...]
    all_to_all x5, waiting for transfers between devices: 64.5 us -> 49 us  [plane_swap(): return lax.all_to_all(array, 'plane', 0, 0, tiled=True)]
    ppermute x4 -> x20, starting transfers between devices: 3.46 us -> 17.2 us  [send(): return lax.ppermute(array, 'quad', [(q, q ^ offset) for q in range(4)])]
    pallas_call x0 -> x9, Pallas kernels: none -> 9.83 us  [call(): pl.pallas_call(kernel, out_shape=shapes, in_specs=[pl.BlockSpec(memory_sp...]
    slice x17 -> x8, local copies, waits for them, and re-layouts: 7.97 us -> 1.52 us  [the longest x4 0.74 us: shards(): pairs = jnp.stack([key_tokens[0], scaled[0], key_tokens[1], scaled[1]])]
  transfers between devices with their start and end apart: 16 -> 25, of which waited for: 14 -> 11; matrix products, arithmetic and copies ran while one was open for 16% -> 3% of each run, Pallas kernels for 0% -> 5%
where the time goes in v4:
time: 150 us; the launch traced here: 149 us
  waiting for transfers between devices  86.2 us (57%)
  starting transfers between devices  38.5 us (26%)
  Pallas kernels  9.83 us (7%)
  local copies, waits for them, and re-layouts  9.74 us (6%)
  other arithmetic  3.18 us (2%)
  between operations  1.68 us (1%)
    all_to_all x5, waiting for transfers between devices, plane_swap(): return lax.all_to_all(array, 'plane', 0, 0, tiled=True)  49 us
    ppermute x20, waiting for transfers between devices, send(): return lax.ppermute(array, 'quad', [(q, q ^ offset) for q in range(4)])  37.1 us
    all_to_all x5, starting transfers between devices, plane_swap(): return lax.all_to_all(array, 'plane', 0, 0, tiled=True)  21.3 us
    ppermute x20, starting transfers between devices, send(): return lax.ppermute(array, 'quad', [(q, q ^ offset) for q in range(4)])  17.2 us
    pallas_call x9, Pallas kernels, call(): pl.pallas_call(kernel, out_shape=shapes, in_specs=[pl.BlockSpec(memory_sp...  9.83 us
    unnamed x26, local copies, waits for them, and re-layouts  4.46 us
  transfers between devices with their start and end apart: 25, of which 11 were waited for; matrix products, arithmetic and copies ran while one was open for 3% of the time, Pallas kernels for 5%

profile of v4, /device:TPU:0, one launch (start us, length us, event | category | flops | bytes accessed | tf_op | source)
XLA Modules:
  0.0 149.1 jit_solution(6817280589882909363)
XLA Ops:
  0.0 1.0 reshape.196
  1.4 2.5 %collective-permute-start.2 = (bf16[32,256]{1,0:T(8,128)(2,1)S(1)}, bf16[32,256]{1,0:T(8,128)(2,1)S(1)}, u32[]{:S(2)}, u32[]{:S(2)}) collective-permute-start(bf16[32,256]{1,0:T(8,128)(2,1)S(1)} %select_n.174), channel_id=1, source_target_pairs={{0,3},{1,2},{2,1},{3,0},{4,7},{5,6},{6,5},{7,4},{8,11},{9,10},{10,... | collective-permute-start | bytes 49160 | tf_op jit(solution)/shard_map/ppermute | solution.py:176
  9.0 4.9 %all-to-all-start = ((bf16[4,64,1536]{2,1,0:T(8,128)(2,1)}), bf16[4,64,1536]{2,1,0:T(8,128)(2,1)S(1)}, u32[]{:S(2)}, u32[]{:S(2)}) async-start(bf16[4,64,1536]{2,1,0:T(8,128)(2,1)} %broadcast_in_dim.4), calls=%async_computation | async-start | bytes 1572864 | tf_op jit(solution)/shard_map/all_to_all | solution.py:179
  15.7 1.3 collective-permute-start.5
  17.9 11.9 %collective-permute-done.5.cross = bf16[4,128,512]{2,1,0:T(8,128)(2,1)S(1)} collective-permute-done((bf16[4,128,512]{2,1,0:T(8,128)(2,1)S(1)}, bf16[4,128,512]{2,1,0:T(8,128)(2,1)S(1)}, u32[]{:S(2)}, u32[]{:S(2)}) %collective-permute-start.5) | collective-permute-done | bytes 524320 | tf_op jit(solution)/shard_map/ppermute | solution.py:176
  29.7 11.5 %collective-permute-done.4.far = bf16[4,128,512]{2,1,0:T(8,128)(2,1)S(1)} collective-permute-done((bf16[4,128,512]{2,1,0:T(8,128)(2,1)S(1)}, bf16[4,128,512]{2,1,0:T(8,128)(2,1)S(1)}, u32[]{:S(2)}, u32[]{:S(2)}) %collective-permute-start.4) | collective-permute-done | bytes 524320 | tf_op jit(solution)/shard_map/ppermute | solution.py:176
  41.2 2.1 %shard_map.83 = bf16[4,64,1536]{2,1,0:T(8,128)(2,1)} custom-call(bf16[4,64,1536]{2,1,0:T(8,128)(2,1)S(1)} %all-to-all-done.full, bf16[4,128,512]{2,1,0:T(8,128)(2,1)S(1)} %get-tuple-element.37.own, bf16[4,128,512]{2,1,0:T(8,128)(2,1)S(1)} %collective-permute-done.3.near, bf16[4,128,512]{2,1,0:T(8,128)(2,1)S(1)} %collective-permute-done.4.far, ...), custom_call_target="tpu_custom_call" | custom-call | flops 805306368 | bytes 3670016 | tf_op jit(solution)/shard_map/pallas_call | solution.py:18
  43.3 5.1 %all-to-all-start.1 = ((bf16[4,64,1536]{2,1,0:T(8,128)(2,1)}), bf16[4,64,1536]{2,1,0:T(8,128)(2,1)S(1)}, u32[]{:S(2)}, u32[]{:S(2)}) async-start(bf16[4,64,1536]{2,1,0:T(8,128)(2,1)} %shard_map.83), calls=%async_computation.1 | async-start | bytes 1572864 | tf_op jit(solution)/shard_map/all_to_all | solution.py:179
  48.4 1.0 copy-done.1
  49.5 1.0 copy-done.3
  50.5 2.1 %shard_map.87 = bf16[4,64,1536]{2,1,0:T(8,128)(2,1)} custom-call(bf16[4,64,1536]{2,1,0:T(8,128)(2,1)S(1)} %all-to-all-done.full, bf16[4,128,512]{2,1,0:T(8,128)(2,1)S(1)} %get-tuple-element.37.own, bf16[4,128,512]{2,1,0:T(8,128)(2,1)S(1)} %copy-done.1, bf16[4,128,512]{2,1,0:T(8,128)(2,1)S(1)} %copy-done.3, bf16[4,128,512]{2,1,0:T(8,128)(2,1)S(1)} %collective-permute-done.5.cross), custom_call_target="tpu_custom_call" | custom-call | flops 805306368 | bytes 3670016 | tf_op jit(solution)/shard_map/pallas_call | solution.py:18
  52.6 16.2 %all-to-all-done.1.got = bf16[4,64,1536]{2,1,0:T(8,128)(2,1)S(1)} async-done(((bf16[4,64,1536]{2,1,0:T(8,128)(2,1)}), bf16[4,64,1536]{2,1,0:T(8,128)(2,1)S(1)}, u32[]{:S(2)}, u32[]{:S(2)}) %all-to-all-start.1) | async-done | bytes 786464 | tf_op jit(solution)/shard_map/all_to_all | solution.py:179
  68.8 3.5 %all-to-all-start.3 = ((bf16[4,64,1536]{2,1,0:T(8,128)(2,1)}), bf16[4,64,1536]{2,1,0:T(8,128)(2,1)S(1)}, u32[]{:S(2)}, u32[]{:S(2)}) async-start(bf16[4,64,1536]{2,1,0:T(8,128)(2,1)} %shard_map.87), calls=%async_computation.3 | async-start | bytes 1572864 | tf_op jit(solution)/shard_map/all_to_all | solution.py:179
  73.3 1.4 collective-permute-start.12
  74.7 2.5 %collective-permute-done.12.far_sums = f32[64,128]{1,0:T(8,128)S(1)} collective-permute-done((f32[64,128]{1,0:T(8,128)S(1)}, f32[64,128]{1,0:T(8,128)S(1)}, u32[]{:S(2)}, u32[]{:S(2)}) %collective-permute-start.12) | collective-permute-done | bytes 32800 | tf_op jit(solution)/shard_map/ppermute | solution.py:176
  77.2 1.1 shard_map.85
  78.4 13.6 %all-to-all-done.3.got = bf16[4,64,1536]{2,1,0:T(8,128)(2,1)S(1)} async-done(((bf16[4,64,1536]{2,1,0:T(8,128)(2,1)}), bf16[4,64,1536]{2,1,0:T(8,128)(2,1)S(1)}, u32[]{:S(2)}, u32[]{:S(2)}) %all-to-all-start.3) | async-done | bytes 786464 | tf_op jit(solution)/shard_map/all_to_all | solution.py:179
  91.9 3.6 %all-to-all-start.2 = ((bf16[4,64,1536]{2,1,0:T(8,128)(2,1)}), bf16[4,64,1536]{2,1,0:T(8,128)(2,1)S(1)}, u32[]{:S(2)}, u32[]{:S(2)}) async-start(bf16[4,64,1536]{2,1,0:T(8,128)(2,1)} %get-tuple-element.44), calls=%async_computation.2 | async-start | bytes 1572864 | tf_op jit(solution)/shard_map/all_to_all | solution.py:179
  97.6 1.5 collective-permute-start.16
  100.8 1.2 collective-permute-start.7
  102.0 1.1 shard_map.89
  103.1 12.0 %all-to-all-done.2.full = bf16[4,64,1536]{2,1,0:T(8,128)(2,1)S(1)} async-done(((bf16[4,64,1536]{2,1,0:T(8,128)(2,1)}), bf16[4,64,1536]{2,1,0:T(8,128)(2,1)S(1)}, u32[]{:S(2)}, u32[]{:S(2)}) %all-to-all-start.2) | async-done | bytes 786464 | tf_op jit(solution)/shard_map/all_to_all | solution.py:179
  115.1 4.2 %all-to-all-start.4 = ((bf16[4,64,1536]{2,1,0:T(8,128)(2,1)}), bf16[4,64,1536]{2,1,0:T(8,128)(2,1)}, u32[]{:S(2)}, u32[]{:S(2)}) async-start(bf16[4,64,1536]{2,1,0:T(8,128)(2,1)} %shard_map.89), calls=%async_computation.4 | async-start | bytes 1572864 | tf_op jit(solution)/shard_map/all_to_all | solution.py:179
  120.1 1.5 %collective-permute-start.11 = (bf16[128,512]{1,0:T(8,128)(2,1)S(1)}, bf16[128,512]{1,0:T(8,128)(2,1)S(1)}, u32[]{:S(2)}, u32[]{:S(2)}) collective-permute-start(bf16[128,512]{1,0:T(8,128)(2,1)S(1)} %get-tuple-element.36), channel_id=1, source_target_pairs={{0,3},{1,2},{2,1},{3,0},{4,7},{5,6},{6,5},{7,4},{8,11},{9,10},{10,... | collective-permute-start | bytes 393224 | tf_op jit(solution)/shard_map/ppermute | solution.py:176
  122.2 3.2 %collective-permute-done.11 = bf16[128,512]{1,0:T(8,128)(2,1)S(1)} collective-permute-done((bf16[128,512]{1,0:T(8,128)(2,1)S(1)}, bf16[128,512]{1,0:T(8,128)(2,1)S(1)}, u32[]{:S(2)}, u32[]{:S(2)}) %collective-permute-start.11) | collective-permute-done | bytes 131104 | tf_op jit(solution)/shard_map/ppermute | solution.py:176
  125.4 3.3 %collective-permute-done.9 = bf16[128,512]{1,0:T(8,128)(2,1)S(1)} collective-permute-done((bf16[128,512]{1,0:T(8,128)(2,1)S(1)}, bf16[128,512]{1,0:T(8,128)(2,1)S(1)}, u32[]{:S(2)}, u32[]{:S(2)}) %collective-permute-start.9) | collective-permute-done | bytes 131104 | tf_op jit(solution)/shard_map/ppermute | solution.py:176
  129.4 1.5 collective-permute-start.13
  131.8 7.2 %all-to-all-done.4.full = bf16[4,64,1536]{2,1,0:T(8,128)(2,1)} async-done(((bf16[4,64,1536]{2,1,0:T(8,128)(2,1)}), bf16[4,64,1536]{2,1,0:T(8,128)(2,1)}, u32[]{:S(2)}, u32[]{:S(2)}) %all-to-all-start.4) | async-done | bytes 786464 | tf_op jit(solution)/shard_map/all_to_all | solution.py:179
  139.0 1.7 %shard_map.90 = (f32[128,512]{1,0:T(8,128)S(1)}, bf16[128,512]{1,0:T(8,128)(2,1)S(1)}, bf16[128,512]{1,0:T(8,128)(2,1)S(1)}, bf16[128,512]{1,0:T(8,128)(2,1)S(1)}) custom-call(bf16[4,64,1536]{2,1,0:T(8,128)(2,1)} %all-to-all-done.4.full, bf16[3,128,512]{2,1,0:T(8,128)(2,1)S(1)} %get-tuple-element.60.own, ...), custom_call_target="tpu_custom_call" | custom-call | flops 402653184 | bytes 3014656 | tf_op jit(solution)/shard_map/pallas_call | solution.py:18
  140.7 1.5 collective-permute-start.17
  143.1 3.2 %collective-permute-done.17 = bf16[128,512]{1,0:T(8,128)(2,1)S(1)} collective-permute-done((bf16[128,512]{1,0:T(8,128)(2,1)S(1)}, bf16[128,512]{1,0:T(8,128)(2,1)S(1)}, u32[]{:S(2)}, u32[]{:S(2)}) %collective-permute-start.17) | collective-permute-done | bytes 131104 | tf_op jit(solution)/shard_map/ppermute | solution.py:176
  146.4 1.6 %collective-permute-done.19 = bf16[128,512]{1,0:T(8,128)(2,1)S(1)} collective-permute-done((bf16[128,512]{1,0:T(8,128)(2,1)S(1)}, bf16[128,512]{1,0:T(8,128)(2,1)S(1)}, u32[]{:S(2)}, u32[]{:S(2)}) %collective-permute-start.19) | collective-permute-done | bytes 131104 | tf_op jit(solution)/shard_map/ppermute | solution.py:176
  (94 shorter events, 16.5 us)
Async XLA Ops:
  1.0 3.8 %copy-start.9 = (bf16[2,32,512]{2,1,0:T(8,128)(2,1)S(1)}, bf16[2,32,512]{2,1,0:T(8,128)(2,1)}, u32[]{:S(2)}) copy-start(bf16[2,32,512]{2,1,0:T(8,128)(2,1)} %param.12) | copy-start | bytes 196612
  1.2 5.3 %copy-start.7 = (bf16[3,128,1024]{2,1,0:T(8,128)(2,1)S(1)}, bf16[3,128,1024]{2,1,0:T(8,128)(2,1)}, u32[]{:S(2)}) copy-start(bf16[3,128,1024]{2,1,0:T(8,128)(2,1)} %param.10) | copy-start | bytes 2359300
  1.4 6.5 %collective-permute-start.2 = (bf16[32,256]{1,0:T(8,128)(2,1)S(1)}, bf16[32,256]{1,0:T(8,128)(2,1)S(1)}, u32[]{:S(2)}, u32[]{:S(2)}) collective-permute-start(bf16[32,256]{1,0:T(8,128)(2,1)S(1)} %select_n.174), channel_id=1, source_target_pairs={{0,3},{1,2},{2,1},{3,0},{4,7},{5,6},{6,5},{7,4},{8,11},{9,10},{10,... | collective-permute-start | bytes 49160 | tf_op jit(solution)/shard_map/ppermute | solution.py:176
  4.0 4.0 %collective-permute-start.1 = (bf16[32,256]{1,0:T(8,128)(2,1)S(1)}, bf16[32,256]{1,0:T(8,128)(2,1)S(1)}, u32[]{:S(2)}, u32[]{:S(2)}) collective-permute-start(bf16[32,256]{1,0:T(8,128)(2,1)S(1)} %select_n.172), channel_id=1, source_target_pairs={{0,2},{1,3},{2,0},{3,1},{4,6},{5,7},{6,4},{7,5},{8,10},{9,11},{10,... | collective-permute-start | bytes 49160 | tf_op jit(solution)/shard_map/ppermute | solution.py:176
  5.6 2.4 %collective-permute-start = (bf16[32,1280]{1,0:T(8,128)(2,1)S(1)}, bf16[32,1280]{1,0:T(8,128)(2,1)S(1)}, u32[]{:S(2)}, u32[]{:S(2)}) collective-permute-start(bf16[32,1280]{1,0:T(8,128)(2,1)S(1)} %get-tuple-element.68), channel_id=1, source_target_pairs={{0,1},{1,0},{2,3},{3,2},{4,5},{5,4},{6,7},{7,6},{8,9},{9,8},{10,11... | collective-permute-start | bytes 245768 | tf_op jit(solution)/shard_map/ppermute | solution.py:176
  9.0 32.2 %all-to-all-start = ((bf16[4,64,1536]{2,1,0:T(8,128)(2,1)}), bf16[4,64,1536]{2,1,0:T(8,128)(2,1)S(1)}, u32[]{:S(2)}, u32[]{:S(2)}) async-start(bf16[4,64,1536]{2,1,0:T(8,128)(2,1)} %broadcast_in_dim.4), calls=%async_computation | async-start | bytes 1572864 | tf_op jit(solution)/shard_map/all_to_all | solution.py:179
  15.7 14.1 %collective-permute-start.5 = (bf16[4,128,512]{2,1,0:T(8,128)(2,1)S(1)}, bf16[4,128,512]{2,1,0:T(8,128)(2,1)S(1)}, u32[]{:S(2)}, u32[]{:S(2)}) collective-permute-start(bf16[4,128,512]{2,1,0:T(8,128)(2,1)S(1)} %get-tuple-element.57), channel_id=1, source_target_pairs={{0,3},{1,2},{2,1},{3,0},{4,7},{5,6},{6,5},{7,4},{8,11},{9,10},{10,... | collective-permute-start | bytes 1572872 | tf_op jit(solution)/shard_map/ppermute | solution.py:176
  17.0 12.8 %collective-permute-start.3 = (bf16[4,128,512]{2,1,0:T(8,128)(2,1)S(1)}, bf16[4,128,512]{2,1,0:T(8,128)(2,1)S(1)}, u32[]{:S(2)}, u32[]{:S(2)}) collective-permute-start(bf16[4,128,512]{2,1,0:T(8,128)(2,1)S(1)} %get-tuple-element.57), channel_id=1, source_target_pairs={{0,1},{1,0},{2,3},{3,2},{4,5},{5,4},{6,7},{7,6},{8,9},{9,8},{10,11... | collective-permute-start | bytes 1572872 | tf_op jit(solution)/shard_map/ppermute | solution.py:176
  17.3 23.9 %collective-permute-start.4 = (bf16[4,128,512]{2,1,0:T(8,128)(2,1)S(1)}, bf16[4,128,512]{2,1,0:T(8,128)(2,1)S(1)}, u32[]{:S(2)}, u32[]{:S(2)}) collective-permute-start(bf16[4,128,512]{2,1,0:T(8,128)(2,1)S(1)} %get-tuple-element.37.own), channel_id=1, source_target_pairs={{0,2},{1,3},{2,0},{3,1},{4,6},{5,7},{6,4},{7,5},{8,10},{9,11},{10,... | collective-permute-start | bytes 1572872 | tf_op jit(solution)/shard_map/ppermute | solution.py:176
  29.7 13.6 %copy-start = (bf16[4,128,512]{2,1,0:T(8,128)(2,1)}, bf16[4,128,512]{2,1,0:T(8,128)(2,1)S(1)}, u32[]{:S(2)}) copy-start(bf16[4,128,512]{2,1,0:T(8,128)(2,1)S(1)} %collective-permute-done.3.near) | copy-start | bytes 1572868
  41.2 2.1 %copy-start.2 = (bf16[4,128,512]{2,1,0:T(8,128)(2,1)}, bf16[4,128,512]{2,1,0:T(8,128)(2,1)S(1)}, u32[]{:S(2)}) copy-start(bf16[4,128,512]{2,1,0:T(8,128)(2,1)S(1)} %collective-permute-done.4.far) | copy-start | bytes 1572868
  43.3 25.5 %all-to-all-start.1 = ((bf16[4,64,1536]{2,1,0:T(8,128)(2,1)}), bf16[4,64,1536]{2,1,0:T(8,128)(2,1)S(1)}, u32[]{:S(2)}, u32[]{:S(2)}) async-start(bf16[4,64,1536]{2,1,0:T(8,128)(2,1)} %shard_map.83), calls=%async_computation.1 | async-start | bytes 1572864 | tf_op jit(solution)/shard_map/all_to_all | solution.py:179
  68.8 23.1 %all-to-all-start.3 = ((bf16[4,64,1536]{2,1,0:T(8,128)(2,1)}), bf16[4,64,1536]{2,1,0:T(8,128)(2,1)S(1)}, u32[]{:S(2)}, u32[]{:S(2)}) async-start(bf16[4,64,1536]{2,1,0:T(8,128)(2,1)} %shard_map.87), calls=%async_computation.3 | async-start | bytes 1572864 | tf_op jit(solution)/shard_map/all_to_all | solution.py:179
  73.3 3.9 %collective-permute-start.12 = (f32[64,128]{1,0:T(8,128)S(1)}, f32[64,128]{1,0:T(8,128)S(1)}, u32[]{:S(2)}, u32[]{:S(2)}) collective-permute-start(f32[64,128]{1,0:T(8,128)S(1)} %get-tuple-element.43.own_sums), channel_id=1, source_target_pairs={{0,2},{1,3},{2,0},{3,1},{4,6},{5,7},{6,4},{7,5},{8,10},{9,11},{10,... | collective-permute-start | bytes 98312 | tf_op jit(solution)/shard_map/ppermute | solution.py:176
  91.9 3.6 %copy-start.11 = (f32[2]{0:T(128)S(1)}, f32[2]{0:T(128)}, u32[]{:S(2)}) copy-start(f32[2]{0:T(128)} %param.15) | copy-start | bytes 28
  91.9 5.4 %copy-start.5 = (f32[64,1536]{1,0:T(8,128)S(1)}, f32[64,1536]{1,0:T(8,128)}, u32[]{:S(2)}) copy-start(f32[64,1536]{1,0:T(8,128)} %copy-done.4) | copy-start | bytes 1179652
  91.9 23.2 %all-to-all-start.2 = ((bf16[4,64,1536]{2,1,0:T(8,128)(2,1)}), bf16[4,64,1536]{2,1,0:T(8,128)(2,1)S(1)}, u32[]{:S(2)}, u32[]{:S(2)}) async-start(bf16[4,64,1536]{2,1,0:T(8,128)(2,1)} %get-tuple-element.44), calls=%async_computation.2 | async-start | bytes 1572864 | tf_op jit(solution)/shard_map/all_to_all | solution.py:179
  97.4 1.7 %copy-start.6 = (bf16[3,128,1024]{2,1,0:T(8,128)(2,1)S(1)}, bf16[3,128,1024]{2,1,0:T(8,128)(2,1)}, u32[]{:S(2)}) copy-start(bf16[3,128,1024]{2,1,0:T(8,128)(2,1)} %param.8) | copy-start | bytes 2359300
  97.6 4.4 %collective-permute-start.16 = (f32[64,128]{1,0:T(8,128)S(1)}, f32[64,128]{1,0:T(8,128)S(1)}, u32[]{:S(2)}, u32[]{:S(2)}) collective-permute-start(f32[64,128]{1,0:T(8,128)S(1)} %get-tuple-element.52.own_sums), channel_id=1, source_target_pairs={{0,2},{1,3},{2,0},{3,1},{4,6},{5,7},{6,4},{7,5},{8,10},{9,11},{10,... | collective-permute-start | bytes 98312 | tf_op jit(solution)/shard_map/ppermute | solution.py:176
  99.9 19.4 %collective-permute-start.8 = (bf16[3,128,512]{2,1,0:T(8,128)(2,1)}, bf16[3,128,512]{2,1,0:T(8,128)(2,1)S(1)}, u32[]{:S(2)}, u32[]{:S(2)}) collective-permute-start(bf16[3,128,512]{2,1,0:T(8,128)(2,1)} %get-tuple-element.59), channel_id=1, source_target_pairs={{0,3},{1,2},{2,1},{3,0},{4,7},{5,6},{6,5},{7,4},{8,11},{9,10},{10,... | collective-permute-start | bytes 1179656 | tf_op jit(solution)/shard_map/ppermute | solution.py:176
  99.9 19.4 %collective-permute-start.6 = (bf16[3,128,512]{2,1,0:T(8,128)(2,1)}, bf16[3,128,512]{2,1,0:T(8,128)(2,1)S(1)}, u32[]{:S(2)}, u32[]{:S(2)}) collective-permute-start(bf16[3,128,512]{2,1,0:T(8,128)(2,1)} %get-tuple-element.59), channel_id=1, source_target_pairs={{0,1},{1,0},{2,3},{3,2},{4,5},{5,4},{6,7},{7,6},{8,9},{9,8},{10,11... | collective-permute-start | bytes 1179656 | tf_op jit(solution)/shard_map/ppermute | solution.py:176
  100.8 18.5 %collective-permute-start.7 = (bf16[3,128,512]{2,1,0:T(8,128)(2,1)S(1)}, bf16[3,128,512]{2,1,0:T(8,128)(2,1)S(1)}, u32[]{:S(2)}, u32[]{:S(2)}) collective-permute-start(bf16[3,128,512]{2,1,0:T(8,128)(2,1)S(1)} %get-tuple-element.60.own), channel_id=1, source_target_pairs={{0,2},{1,3},{2,0},{3,1},{4,6},{5,7},{6,4},{7,5},{8,10},{9,11},{10,... | collective-permute-start | bytes 1179656 | tf_op jit(solution)/shard_map/ppermute | solution.py:176
  115.1 23.9 %all-to-all-start.4 = ((bf16[4,64,1536]{2,1,0:T(8,128)(2,1)}), bf16[4,64,1536]{2,1,0:T(8,128)(2,1)}, u32[]{:S(2)}, u32[]{:S(2)}) async-start(bf16[4,64,1536]{2,1,0:T(8,128)(2,1)} %shard_map.89), calls=%async_computation.4 | async-start | bytes 1572864 | tf_op jit(solution)/shard_map/all_to_all | solution.py:179
  120.0 2.2 %collective-permute-start.10 = (bf16[128,512]{1,0:T(8,128)(2,1)S(1)}, bf16[128,512]{1,0:T(8,128)(2,1)S(1)}, u32[]{:S(2)}, u32[]{:S(2)}) collective-permute-start(bf16[128,512]{1,0:T(8,128)(2,1)S(1)} %get-tuple-element.35), channel_id=1, source_target_pairs={{0,1},{1,0},{2,3},{3,2},{4,5},{5,4},{6,7},{7,6},{8,9},{9,8},{10,11... | collective-permute-start | bytes 393224 | tf_op jit(solution)/shard_map/ppermute | solution.py:176
  120.1 5.3 %collective-permute-start.11 = (bf16[128,512]{1,0:T(8,128)(2,1)S(1)}, bf16[128,512]{1,0:T(8,128)(2,1)S(1)}, u32[]{:S(2)}, u32[]{:S(2)}) collective-permute-start(bf16[128,512]{1,0:T(8,128)(2,1)S(1)} %get-tuple-element.36), channel_id=1, source_target_pairs={{0,3},{1,2},{2,1},{3,0},{4,7},{5,6},{6,5},{7,4},{8,11},{9,10},{10,... | collective-permute-start | bytes 393224 | tf_op jit(solution)/shard_map/ppermute | solution.py:176
  121.6 7.2 %collective-permute-start.9 = (bf16[128,512]{1,0:T(8,128)(2,1)S(1)}, bf16[128,512]{1,0:T(8,128)(2,1)S(1)}, u32[]{:S(2)}, u32[]{:S(2)}) collective-permute-start(bf16[128,512]{1,0:T(8,128)(2,1)S(1)} %get-tuple-element.34), channel_id=1, source_target_pairs={{0,2},{1,3},{2,0},{3,1},{4,6},{5,7},{6,4},{7,5},{8,10},{9,11},{10,... | collective-permute-start | bytes 393224 | tf_op jit(solution)/shard_map/ppermute | solution.py:176
  129.4 12.8 %collective-permute-start.13 = (bf16[128,512]{1,0:T(8,128)(2,1)S(1)}, bf16[128,512]{1,0:T(8,128)(2,1)S(1)}, u32[]{:S(2)}, u32[]{:S(2)}) collective-permute-start(bf16[128,512]{1,0:T(8,128)(2,1)S(1)} %get-tuple-element.46), channel_id=1, source_target_pairs={{0,2},{1,3},{2,0},{3,1},{4,6},{5,7},{6,4},{7,5},{8,10},{9,11},{10,... | collective-permute-start | bytes 393224 | tf_op jit(solution)/shard_map/ppermute | solution.py:176
  130.9 12.0 %collective-permute-start.14 = (bf16[128,512]{1,0:T(8,128)(2,1)S(1)}, bf16[128,512]{1,0:T(8,128)(2,1)S(1)}, u32[]{:S(2)}, u32[]{:S(2)}) collective-permute-start(bf16[128,512]{1,0:T(8,128)(2,1)S(1)} %get-tuple-element.47), channel_id=1, source_target_pairs={{0,1},{1,0},{2,3},{3,2},{4,5},{5,4},{6,7},{7,6},{8,9},{9,8},{10,11... | collective-permute-start | bytes 393224 | tf_op jit(solution)/shard_map/ppermute | solution.py:176
  131.0 12.0 %collective-permute-start.15 = (bf16[128,512]{1,0:T(8,128)(2,1)S(1)}, bf16[128,512]{1,0:T(8,128)(2,1)S(1)}, u32[]{:S(2)}, u32[]{:S(2)}) collective-permute-start(bf16[128,512]{1,0:T(8,128)(2,1)S(1)} %get-tuple-element.48), channel_id=1, source_target_pairs={{0,3},{1,2},{2,1},{3,0},{4,7},{5,6},{6,5},{7,4},{8,11},{9,10},{10,... | collective-permute-start | bytes 393224 | tf_op jit(solution)/shard_map/ppermute | solution.py:176
  140.7 5.6 %collective-permute-start.17 = (bf16[128,512]{1,0:T(8,128)(2,1)S(1)}, bf16[128,512]{1,0:T(8,128)(2,1)S(1)}, u32[]{:S(2)}, u32[]{:S(2)}) collective-permute-start(bf16[128,512]{1,0:T(8,128)(2,1)S(1)} %get-tuple-element.54), channel_id=1, source_target_pairs={{0,2},{1,3},{2,0},{3,1},{4,6},{5,7},{6,4},{7,5},{8,10},{9,11},{10,... | collective-permute-start | bytes 393224 | tf_op jit(solution)/shard_map/ppermute | solution.py:176
  142.2 4.2 %collective-permute-start.18 = (bf16[128,512]{1,0:T(8,128)(2,1)S(1)}, bf16[128,512]{1,0:T(8,128)(2,1)S(1)}, u32[]{:S(2)}, u32[]{:S(2)}) collective-permute-start(bf16[128,512]{1,0:T(8,128)(2,1)S(1)} %get-tuple-element.55), channel_id=1, source_target_pairs={{0,1},{1,0},{2,3},{3,2},{4,5},{5,4},{6,7},{7,6},{8,9},{9,8},{10,11... | collective-permute-start | bytes 393224 | tf_op jit(solution)/shard_map/ppermute | solution.py:176
  142.2 5.8 %collective-permute-start.19 = (bf16[128,512]{1,0:T(8,128)(2,1)S(1)}, bf16[128,512]{1,0:T(8,128)(2,1)S(1)}, u32[]{:S(2)}, u32[]{:S(2)}) collective-permute-start(bf16[128,512]{1,0:T(8,128)(2,1)S(1)} %get-tuple-element.56), channel_id=1, source_target_pairs={{0,3},{1,2},{2,1},{3,0},{4,7},{5,6},{6,5},{7,4},{8,11},{9,10},{10,... | collective-permute-start | bytes 393224 | tf_op jit(solution)/shard_map/ppermute | solution.py:176
  (6 other events, 5.5 us)

commit v5 on v4

v5 whole, which is shorter than its diff:
```python
import functools

import jax
import jax.numpy as jnp
from jax import lax
from jax.experimental import pallas as pl
from jax.experimental.pallas import tpu as pltpu
from jax.sharding import Mesh, PartitionSpec as P

LOW = jnp.bfloat16
WIDE = jnp.float32


def call(kernel, outs, flops, *operands, scratch=()):
    shapes = [jax.ShapeDtypeStruct(s, d) for s, d in outs]
    moved = sum(a.size * a.dtype.itemsize for a in operands)
    moved += sum(s.size * s.dtype.itemsize for s in shapes)
    return pl.pallas_call(
        kernel,
        out_shape=shapes,
        in_specs=[
            pl.BlockSpec(memory_space=pltpu.SMEM if a.ndim == 1 else pltpu.VMEM) for a in operands
        ],
        out_specs=[pl.BlockSpec(memory_space=pltpu.VMEM)] * len(shapes),
        scratch_shapes=[pltpu.VMEM(s, d) for s, d in scratch],
        compiler_params=pltpu.CompilerParams(vmem_limit_bytes=40 * 2**20),
        cost_estimate=pl.CostEstimate(flops=flops, bytes_accessed=moved, transcendentals=0),
    )(*operands)


def dot(a, b, dims):
    return lax.dot_general(a, b, ((dims[:1], dims[1:]), ((), ())), preferred_element_type=WIDE)


def place(pieces, where, first, third, second):
    rows, columns = pieces[0].shape
    width = columns // 3
    half = width // 2
    for distance, piece in enumerate(pieces):
        z = where[0] ^ distance
        at = pl.multiple_of(z * rows, rows)
        first[pl.ds(at, rows), :] = piece[:, :width]
        third[pl.ds(at, rows), :] = piece[:, width : 2 * width]
        for y in range(2):
            start = 2 * width + y * half
            at = pl.multiple_of((2 * z + y) * rows, rows)
            second[pl.ds(at, rows), :] = piece[:, start : start + half]


def steps_kernel(planes, where, *refs):
    pieces, parts, refs = refs[:planes], refs[planes : planes + 4], refs[planes + 4 :]
    sent, (first, third, second, new_first, new_third, new_second) = refs[:planes], refs[planes:]
    rows, columns = pieces[0].shape
    width = columns // 3
    half = width // 2
    place(pieces, where, first, third, second)
    keys = jnp.concatenate([p[0] for p in parts], axis=0)
    scaled = jnp.concatenate([p[1] for p in parts], axis=0)
    pre_gate = dot(keys, first[...], (1, 1))
    pre_up = dot(keys, third[...], (1, 1))
    back = dot(scaled, second[...], (1, 0))
    sig_gate = jax.nn.sigmoid(pre_gate)
    silu = pre_gate * sig_gate
    hidden = (silu * pre_up).astype(LOW)
    d_gate = (back * pre_up * sig_gate * (1.0 + pre_gate * (1.0 - sig_gate))).astype(LOW)
    d_up = (back * silu).astype(LOW)
    new_first[...] = dot(d_gate, keys, (0, 0))
    new_third[...] = dot(d_up, keys, (0, 0))
    new_second[...] = dot(scaled, hidden, (0, 0))
    for distance, out in enumerate(sent):
        z = where[0] ^ distance
        at = pl.ds(pl.multiple_of(z * rows, rows), rows)
        out[:, :width] = new_first[at, :].astype(out.dtype)
        out[:, width : 2 * width] = new_third[at, :].astype(out.dtype)
        for y in range(2):
            start = 2 * width + y * half
            at = pl.ds(pl.multiple_of((2 * z + y) * rows, rows), rows)
            out[:, start : start + half] = new_second[at, :].astype(out.dtype)


def readout_kernel(planes, block, where, *refs):
    pieces, parts, refs = refs[:planes], refs[planes : planes + 4], refs[planes + 4 :]
    kept, to_near, to_far, to_cross, first, third, second = refs
    tokens = kept.shape[0]
    place(pieces, where, first, third, second)
    inputs = jnp.concatenate([p[block] for p in parts], axis=0)
    pre_gate = dot(inputs, first[...], (1, 1))
    pre_up = dot(inputs, third[...], (1, 1))
    hidden = (pre_gate * jax.nn.sigmoid(pre_gate) * pre_up).astype(LOW)
    result = dot(hidden, second[...], (1, 1))
    kept[...] = result[:tokens]
    for i, out in enumerate((to_near, to_far, to_cross)):
        out[...] = result[(i + 1) * tokens : (i + 2) * tokens].astype(LOW)


def square_sums(array, width):
    half = width // 2
    columns = []
    for y in range(2):
        piece = array[:, 2 * width + y * half : 2 * width + (y + 1) * half]
        columns.append(jnp.sum(piece * piece, axis=1, keepdims=True))
    return columns


def moved_kernel(got, old, momentum, decay, new_momentum, moved, sums):
    rows, columns = old.shape
    width = columns // 3
    total = got[0][...].astype(WIDE)
    for part in got[1:]:
        total = total + part[...].astype(WIDE)
    before = old[...].astype(WIDE)
    if momentum is not None:
        total = decay[0:1, 0:1] * momentum[...] + total
    after = before + total
    if new_momentum is not None:
        new_momentum[...] = total
    moved[...] = after
    parts = square_sums(after, width) + square_sums(before, width)
    sums[...] = jnp.concatenate(parts + [jnp.zeros((rows, 124), WIDE)], axis=1)


def first_moved_kernel(old, *refs):
    moved_kernel(refs[:-3], old, None, None, *refs[-3:])


def second_moved_kernel(old, momentum, decay, *refs):
    moved_kernel(refs[:-2], old, momentum, decay, None, *refs[-2:])


def scaled_kernel(moved, old, own_sums, far_sums, new, payload):
    rows, columns = payload.shape
    width = columns // 3
    half = width // 2
    after = moved[...]
    before = old[...].astype(WIDE)
    sums = own_sums[...] + far_sums[...]

    def factor(old_sum, moved_sum):
        return jnp.sqrt(old_sum + 1e-06) / jnp.sqrt(moved_sum + 1e-06)

    pieces = []
    for m in range(2):
        a = after[:, m * width : (m + 1) * width]
        b = before[:, m * width : (m + 1) * width]
        old_sum = jnp.sum(b * b, axis=1, keepdims=True)
        pieces.append(a * factor(old_sum, jnp.sum(a * a, axis=1, keepdims=True)))
    for y in range(2):
        a = after[:, 2 * width + y * half : 2 * width + (y + 1) * half]
        pieces.append(a * factor(sums[:, y + 2 : y + 3], sums[:, y : y + 1]))
    result = jnp.concatenate(pieces, axis=1)
    if new is not None:
        new[...] = result
    payload[...] = result.astype(LOW)


def last_scaled_kernel(moved, old, own_sums, far_sums, payload):
    scaled_kernel(moved, old, own_sums, far_sums, None, payload)


def shards(
    query_tokens,
    key_tokens,
    value_tokens,
    learn_rates,
    fast_first,
    fast_third,
    fast_second,
    momentum_decay,
):
    planes = lax.axis_size("plane")
    index = lax.axis_index("quad")
    y, c = index // 2, index % 2
    width = fast_first.shape[2]
    half = width // 2
    own_rows = fast_first.shape[1]
    rows = 2 * own_rows
    tokens = key_tokens.shape[1]

    def send(array, offset):
        return lax.ppermute(array, "quad", [(q, q ^ offset) for q in range(4)])

    def to_plane(array, bit):
        return lax.ppermute(array, "plane", [(z, z ^ bit) for z in range(planes)])

    def spread(own):
        pieces = {0: own}
        bit = planes // 2
        while bit:
            for distance in list(pieces):
                pieces[distance | bit] = to_plane(pieces[distance], bit)
            bit //= 2
        return [pieces[d] for d in range(planes)]

    def gathered_sum(parts):
        parts = [[p] for p in parts]
        terms = list(parts[0])
        bit = 1
        while bit < planes:
            for distance in range(planes - bit, 0, -2 * bit):
                total = parts[distance][0]
                if len(parts[distance]) > 1:
                    total = sum(p.astype(WIDE) for p in parts[distance]).astype(LOW)
                came = to_plane(total, bit)
                parts[distance ^ bit].append(came)
                if distance == bit:
                    terms.append(came)
            bit *= 2
        return terms

    def heads(array):
        low, high = array[..., :width], array[..., width:]
        return jnp.where(c == 0, low, high), jnp.where(c == 0, high, low)

    def ordered(flag, a, b, axis):
        return jnp.where(flag == 0, jnp.concatenate([a, b], axis), jnp.concatenate([b, a], axis))

    def to_quad(array):
        mine, other = heads(array)
        return mine, send(other, 1), send(mine, 2), send(other, 3)

    columns = fast_second.reshape(2, own_rows, planes, 2, rows)
    split = [columns[:, :, :, i].reshape(2, own_rows, half) for i in range(2)]
    second_same = jnp.where(y == 0, split[0], split[1])
    second_far = jnp.where(y == 0, split[1], split[0])
    same = jnp.concatenate([fast_first, fast_third, second_same], axis=2)
    same_mine, same_other = jnp.where(c == 0, same[0], same[1]), jnp.where(c == 0, same[1], same[0])
    far_mine = jnp.where(c == 0, second_far[0], second_far[1])
    far_other = jnp.where(c == 0, second_far[1], second_far[0])
    same_rows = ordered(c, same_mine, send(same_other, 1), 0)
    far_rows = ordered(c, send(far_mine, 2), send(far_other, 3), 0)
    second_rows = ordered(y, same_rows[:, 2 * width :], far_rows, 1)
    zero = jnp.concatenate([same_rows[:, : 2 * width], second_rows], axis=1)
    full_zero = spread(zero)

    scaled = learn_rates[:2, :, :, None] * value_tokens[:2].reshape(2, tokens, 2, width).astype(WIDE)
    scaled = scaled.astype(LOW).reshape(2, tokens, 2 * width)
    pairs = [jnp.stack([key_tokens[b], scaled[b]]) for b in range(2)]
    first_pair, zero = lax.optimization_barrier((pairs[0], zero))
    pairs[0] = to_quad(first_pair)
    second_pair, pairs[0] = lax.optimization_barrier((pairs[1], pairs[0]))
    pairs[1] = to_quad(second_pair)
    query_tokens, pairs[1] = lax.optimization_barrier((query_tokens, pairs[1]))
    queries = to_quad(query_tokens)

    flat = (rows, 3 * width)
    unit = 2 * 4 * tokens * width * half
    where = lax.axis_index("plane").astype(jnp.int32).reshape(1)
    held = [((half, width), LOW), ((half, width), LOW), ((width, half), LOW)]

    def steps(block):
        kernel = functools.partial(steps_kernel, planes)
        outs = [(flat, WIDE if d % 2 == 0 else LOW) for d in range(planes)]
        made = [(s, WIDE) for s, _ in held]
        return call(
            kernel, outs, 6 * unit, where, *full_zero, *pairs[block], scratch=held + made
        )

    def readout(block, full):
        kernel = functools.partial(readout_kernel, planes, block)
        piece = (tokens, width)
        outs = [(piece, WIDE), (piece, LOW), (piece, LOW), (piece, LOW)]
        kept, near, far, cross = call(
            kernel, outs, 3 * unit, where, *full, *queries, scratch=held
        )
        near, far, cross = send(near, 1), send(far, 2), send(cross, 3)
        mine = (kept + far.astype(WIDE)).astype(LOW)
        other = (near.astype(WIDE) + cross.astype(WIDE)).astype(LOW)
        return ordered(c, mine, other, 1)

    got_zero = gathered_sum(steps(0))
    got_one = gathered_sum(steps(1))
    out_zero = readout(0, full_zero)

    sums_shape = (rows, 128)
    step_zero, moved, sums = call(
        first_moved_kernel, [(flat, WIDE), (flat, WIDE), (sums_shape, WIDE)], 0, zero, *got_zero
    )
    weights_one, payload = call(
        scaled_kernel, [(flat, WIDE), (flat, LOW)], 0, moved, zero, sums, send(sums, 2)
    )
    full_one = spread(payload)

    got_one, queries = lax.optimization_barrier((got_one, queries))
    decay = jnp.broadcast_to(jnp.where(c == 0, momentum_decay[0], momentum_decay[1]), (8, 128))
    moved, sums = call(
        second_moved_kernel,
        [(flat, WIDE), (sums_shape, WIDE)],
        0,
        weights_one,
        step_zero,
        decay,
        *got_one,
    )
    payload = call(last_scaled_kernel, [(flat, LOW)], 0, moved, weights_one, sums, send(sums, 2))[0]
    full_two = spread(payload)
    out_one = readout(1, full_one)
    out_two = readout(2, full_two)
    return jnp.stack([out_zero, out_one, out_two])


def solution(mesh):
    groups, count = mesh.shape["groups"], mesh.shape["tok"]
    split = Mesh(mesh.devices.reshape(groups, count // 4, 4), ("groups", "plane", "quad"))
    everywhere = P(None, ("groups", "plane", "quad"), None)
    rows = P(None, ("plane", "quad"), None)
    return jax.shard_map(
        shards,
        mesh=split,
        in_specs=(everywhere,) * 4 + (rows,) * 3 + (P(),),
        out_specs=everywhere,
        check_vma=False,
    )
```

time: 150 us -> 120 us (0.80)
  waiting for transfers between devices: 86.2 us -> 60.6 us
  starting transfers between devices: 38.5 us -> 36.6 us
    all_to_all x5 -> x0, waiting for transfers between devices: 49 us -> none  [plane_swap(): return lax.all_to_all(array, 'plane', 0, 0, tiled=True)]
    ppermute x0 -> x15, waiting for transfers between devices: none -> 48.5 us  [to_plane(): return lax.ppermute(array, 'plane', [(z, z ^ bit) for z in range(planes)])]
    ppermute x20 -> x23, waiting for transfers between devices: 37.1 us -> 12.1 us  [send(): return lax.ppermute(array, 'quad', [(q, q ^ offset) for q in range(4)])]
    all_to_all x5 -> x0, starting transfers between devices: 21.3 us -> none  [plane_swap(): return lax.all_to_all(array, 'plane', 0, 0, tiled=True)]
    ppermute x0 -> x15, starting transfers between devices: none -> 17.2 us  [to_plane(): return lax.ppermute(array, 'plane', [(z, z ^ bit) for z in range(planes)])]
    ppermute x20 -> x23, starting transfers between devices: 17.2 us -> 19.4 us  [send(): return lax.ppermute(array, 'quad', [(q, q ^ offset) for q in range(4)])]
    unnamed x26 -> x34, local copies, waits for them, and re-layouts: 4.46 us -> 3.76 us
  transfers between devices with their start and end apart: 25 -> 38, of which waited for: 11 -> 15; matrix products, arithmetic and copies ran while one was open for 3% -> 4% of each run, Pallas kernels for 5% -> 7%
where the time goes in v5:
time: 120 us
  waiting for transfers between devices  60.6 us (50%)
  starting transfers between devices  36.6 us (30%)
  Pallas kernels  8.63 us (7%)
  local copies, waits for them, and re-layouts  8.34 us (7%)
  other arithmetic  3.87 us (3%)
  between operations  1.8 us (2%)
    ppermute x15, waiting for transfers between devices, to_plane(): return lax.ppermute(array, 'plane', [(z, z ^ bit) for z in range(planes)])  48.5 us
    ppermute x23, starting transfers between devices, send(): return lax.ppermute(array, 'quad', [(q, q ^ offset) for q in range(4)])  19.4 us
    ppermute x15, starting transfers between devices, to_plane(): return lax.ppermute(array, 'plane', [(z, z ^ bit) for z in range(planes)])  17.2 us
    ppermute x23, waiting for transfers between devices, send(): return lax.ppermute(array, 'quad', [(q, q ^ offset) for q in range(4)])  12.1 us
    pallas_call x9, Pallas kernels, call(): pl.pallas_call(kernel, out_shape=shapes, in_specs=[pl.BlockSpec(memory_sp...  8.63 us
    unnamed x34, local copies, waits for them, and re-layouts  3.76 us
  transfers between devices with their start and end apart: 38, of which 15 were waited for; matrix products, arithmetic and copies ran while one was open for 4% of the time, Pallas kernels for 7%

profile of v5, /device:TPU:0, one launch (start us, length us, event | category | flops | bytes accessed | tf_op | source)
XLA Modules:
  0.0 119.8 jit_solution(4170646574864123203)
XLA Ops:
  1.4 2.5 %collective-permute-start.2 = (bf16[32,256]{1,0:T(8,128)(2,1)S(1)}, bf16[32,256]{1,0:T(8,128)(2,1)S(1)}, u32[]{:S(2)}, u32[]{:S(2)}) collective-permute-start(bf16[32,256]{1,0:T(8,128)(2,1)S(1)} %select_n.182), channel_id=1, source_target_pairs={{0,3},{1,2},{2,1},{3,0},{4,7},{5,6},{6,5},{7,4},{8,11},{9,10},{10,... | collective-permute-start | bytes 49160 | tf_op jit(solution)/shard_map/ppermute | solution.py:180
  9.9 1.5 %collective-permute-start.7 = (bf16[2,128,512]{2,1,0:T(8,128)(2,1)S(1)}, bf16[2,128,512]{2,1,0:T(8,128)(2,1)S(1)}, u32[]{:S(2)}, u32[]{:S(2)}) collective-permute-start(bf16[2,128,512]{2,1,0:T(8,128)(2,1)S(1)} %get-tuple-element.59.refs_4_), channel_id=1, source_target_pairs={{0,2},{1,3},{2,0},{3,1},{4,6},{5,7},{6,4},{7,5},{8,10},{9,11},{10,... | collective-permute-start | bytes 786440 | tf_op jit(solution)/shard_map/ppermute | solution.py:180
  11.4 2.8 %collective-permute-start.4 = (bf16[64,1536]{1,0:T(8,128)(2,1)S(1)}, bf16[64,1536]{1,0:T(8,128)(2,1)S(1)}, u32[]{:S(2)}, u32[]{:S(2)}) collective-permute-start(bf16[64,1536]{1,0:T(8,128)(2,1)S(1)} %pad_maximum_fusion.3.refs_0_.old), channel_id=1, source_target_pairs={{0,8},{4,12},{8,0},{12,4},{1,9},{5,13},{9,1},{13,5},{2,10},{6,14},... | collective-permute-start | bytes 589832 | tf_op jit(solution)/shard_map/ppermute | solution.py:183
  14.4 1.6 %collective-permute-start.3 = (bf16[64,1536]{1,0:T(8,128)(2,1)S(1)}, bf16[64,1536]{1,0:T(8,128)(2,1)S(1)}, u32[]{:S(2)}, u32[]{:S(2)}) collective-permute-start(bf16[64,1536]{1,0:T(8,128)(2,1)S(1)} %pad_maximum_fusion.3.refs_0_.old), channel_id=1, source_target_pairs={{0,4},{4,0},{8,12},{12,8},{1,5},{5,1},{9,13},{13,9},{2,6},{6,2},{1... | collective-permute-start | bytes 589832 | tf_op jit(solution)/shard_map/ppermute | solution.py:183
  16.1 8.0 %collective-permute-done.4.refs_2_ = bf16[64,1536]{1,0:T(8,128)(2,1)S(1)} collective-permute-done((bf16[64,1536]{1,0:T(8,128)(2,1)S(1)}, bf16[64,1536]{1,0:T(8,128)(2,1)S(1)}, u32[]{:S(2)}, u32[]{:S(2)}) %collective-permute-start.4) | collective-permute-done | bytes 196640 | tf_op jit(solution)/shard_map/ppermute | solution.py:183
  25.4 1.5 %collective-permute-start.10 = (bf16[2,128,512]{2,1,0:T(8,128)(2,1)S(1)}, bf16[2,128,512]{2,1,0:T(8,128)(2,1)S(1)}, u32[]{:S(2)}, u32[]{:S(2)}) collective-permute-start(bf16[2,128,512]{2,1,0:T(8,128)(2,1)S(1)} %get-tuple-element.70.refs_4_), channel_id=1, source_target_pairs={{0,2},{1,3},{2,0},{3,1},{4,6},{5,7},{6,4},{7,5},{8,10},{9,11},{10,... | collective-permute-start | bytes 786440 | tf_op jit(solution)/shard_map/ppermute | solution.py:180
  27.3 3.3 %collective-permute-done.5.refs_3_ = bf16[64,1536]{1,0:T(8,128)(2,1)S(1)} collective-permute-done((bf16[64,1536]{1,0:T(8,128)(2,1)S(1)}, bf16[64,1536]{1,0:T(8,128)(2,1)S(1)}, u32[]{:S(2)}, u32[]{:S(2)}) %collective-permute-start.5) | collective-permute-done | bytes 196640 | tf_op jit(solution)/shard_map/ppermute | solution.py:183
  30.6 1.3 %shard_map.83 = (f32[64,1536]{1,0:T(8,128)S(1)}, bf16[64,1536]{1,0:T(8,128)(2,1)S(1)}, f32[64,1536]{1,0:T(8,128)S(1)}, bf16[64,1536]{1,0:T(8,128)(2,1)S(1)}) custom-call(s32[1]{0:T(128)} %bitcast.where, bf16[64,1536]{1,0:T(8,128)(2,1)S(1)} %pad_maximum_fusion.3.refs_0_.old, bf16[64,1536]{1,0:T(8,128)(2,1)S(1)} %collective-permute-done.3.refs_1_, ...), custom_call_target="tpu_custom_call" | custom-call | flops 805306368 | bytes 3014660 | tf_op jit(solution)/shard_map/pallas_call | solution.py:18
  31.9 1.0 collective-permute-start.18
  32.9 1.1 collective-permute-start.19
  34.5 4.9 %collective-permute-done.11.refs_7_ = bf16[2,128,512]{2,1,0:T(8,128)(2,1)} collective-permute-done((bf16[2,128,512]{2,1,0:T(8,128)(2,1)}, bf16[2,128,512]{2,1,0:T(8,128)(2,1)}, u32[]{:S(2)}, u32[]{:S(2)}) %collective-permute-start.11) | collective-permute-done | bytes 262176 | tf_op jit(solution)/shard_map/ppermute | solution.py:180
  40.0 1.2 collective-permute-start.14
  42.2 2.9 %shard_map.86 = (f32[64,1536]{1,0:T(8,128)S(1)}, bf16[64,1536]{1,0:T(8,128)(2,1)}, f32[64,1536]{1,0:T(8,128)S(1)}, bf16[64,1536]{1,0:T(8,128)(2,1)S(1)}) custom-call(s32[1]{0:T(128)} %bitcast.where, bf16[64,1536]{1,0:T(8,128)(2,1)S(1)} %pad_maximum_fusion.3.refs_0_.old, bf16[64,1536]{1,0:T(8,128)(2,1)S(1)} %collective-permute-done.3.refs_1_, ...), custom_call_target="tpu_custom_call" | custom-call | flops 805306368 | bytes 3014660 | tf_op jit(solution)/shard_map/pallas_call | solution.py:18
  45.1 1.4 %collective-permute-start.26 = (bf16[64,1536]{1,0:T(8,128)(2,1)S(1)}, bf16[64,1536]{1,0:T(8,128)(2,1)S(1)}, u32[]{:S(2)}, u32[]{:S(2)}) collective-permute-start(bf16[64,1536]{1,0:T(8,128)(2,1)S(1)} %get-tuple-element.77), channel_id=1, source_target_pairs={{0,4},{4,0},{8,12},{12,8},{1,5},{5,1},{9,13},{13,9},{2,6},{6,2},{1... | collective-permute-start | bytes 589832 | tf_op jit(solution)/shard_map/ppermute | solution.py:183
  47.1 5.2 %collective-permute-done.26 = bf16[64,1536]{1,0:T(8,128)(2,1)S(1)} collective-permute-done((bf16[64,1536]{1,0:T(8,128)(2,1)S(1)}, bf16[64,1536]{1,0:T(8,128)(2,1)S(1)}, u32[]{:S(2)}, u32[]{:S(2)}) %collective-permute-start.26) | collective-permute-done | bytes 196640 | tf_op jit(solution)/shard_map/ppermute | solution.py:183
  52.3 3.4 %collective-permute-start.20 = (bf16[64,1536]{1,0:T(8,128)(2,1)S(1)}, bf16[64,1536]{1,0:T(8,128)(2,1)S(1)}, u32[]{:S(2)}, u32[]{:S(2)}) collective-permute-start(bf16[64,1536]{1,0:T(8,128)(2,1)S(1)} %add_convert_fusion.1), channel_id=1, source_target_pairs={{0,8},{4,12},{8,0},{12,4},{1,9},{5,13},{9,1},{13,5},{2,10},{6,14},... | collective-permute-start | bytes 589832 | tf_op jit(solution)/shard_map/ppermute | solution.py:183
  56.6 8.0 %collective-permute-done.20.refs_2_ = bf16[64,1536]{1,0:T(8,128)(2,1)S(1)} collective-permute-done((bf16[64,1536]{1,0:T(8,128)(2,1)S(1)}, bf16[64,1536]{1,0:T(8,128)(2,1)S(1)}, u32[]{:S(2)}, u32[]{:S(2)}) %collective-permute-start.20) | collective-permute-done | bytes 196640 | tf_op jit(solution)/shard_map/ppermute | solution.py:183
  65.7 1.3 %shard_map.82 = (f32[128,512]{1,0:T(8,128)S(1)}, bf16[128,512]{1,0:T(8,128)(2,1)S(1)}, bf16[128,512]{1,0:T(8,128)(2,1)}, bf16[128,512]{1,0:T(8,128)(2,1)S(1)}) custom-call(s32[1]{0:T(128)} %bitcast.where, bf16[64,1536]{1,0:T(8,128)(2,1)S(1)} %pad_maximum_fusion.3.refs_0_.old, bf16[64,1536]{1,0:T(8,128)(2,1)S(1)} %copy-done.1, ...), custom_call_target="tpu_custom_call" | custom-call | flops 402653184 | bytes 3014660 | tf_op jit(solution)/shard_map/pallas_call | solution.py:18
  68.3 1.3 %collective-permute-start.15 = (bf16[128,512]{1,0:T(8,128)(2,1)}, bf16[128,512]{1,0:T(8,128)(2,1)S(1)}, u32[]{:S(2)}, u32[]{:S(2)}) collective-permute-start(bf16[128,512]{1,0:T(8,128)(2,1)} %get-tuple-element.55), channel_id=1, source_target_pairs={{0,2},{1,3},{2,0},{3,1},{4,6},{5,7},{6,4},{7,5},{8,10},{9,11},{10,... | collective-permute-start | bytes 393224 | tf_op jit(solution)/shard_map/ppermute | solution.py:180
  71.8 3.8 %collective-permute-done.27.refs_2_ = bf16[64,1536]{1,0:T(8,128)(2,1)} collective-permute-done((bf16[64,1536]{1,0:T(8,128)(2,1)}, bf16[64,1536]{1,0:T(8,128)(2,1)}, u32[]{:S(2)}, u32[]{:S(2)}) %collective-permute-start.27) | collective-permute-done | bytes 196640 | tf_op jit(solution)/shard_map/ppermute | solution.py:183
  75.7 1.3 %shard_map.88 = (f32[64,1536]{1,0:T(8,128)S(1)}, f32[64,128]{1,0:T(8,128)S(1)}) custom-call(f32[64,1536]{1,0:T(8,128)S(1)} %get-tuple-element.86.old, f32[64,1536]{1,0:T(8,128)S(1)} %get-tuple-element.87.momentum, f32[8,128]{1,0:T(8,128)S(1)} %broadcast_in_dim.4.decay, f32[64,1536]{1,0:T(8,128)S(1)} %get-tuple-element.88.refs_0_, ...), custom_call_target="tpu_custom_call" | custom-call | bytes 2002944 | tf_op jit(solution)/shard_map/pallas_call | solution.py:18
  77.6 2.8 %collective-permute-start.23 = (bf16[64,1536]{1,0:T(8,128)(2,1)S(1)}, bf16[64,1536]{1,0:T(8,128)(2,1)S(1)}, u32[]{:S(2)}, u32[]{:S(2)}) collective-permute-start(bf16[64,1536]{1,0:T(8,128)(2,1)S(1)} %get-tuple-element.69.refs_0_), channel_id=1, source_target_pairs={{0,8},{4,12},{8,0},{12,4},{1,9},{5,13},{9,1},{13,5},{2,10},{6,14},... | collective-permute-start | bytes 589832 | tf_op jit(solution)/shard_map/ppermute | solution.py:183
  80.9 1.0 collective-permute-start.16
  82.4 11.1 %collective-permute-done.23.refs_2_ = bf16[64,1536]{1,0:T(8,128)(2,1)S(1)} collective-permute-done((bf16[64,1536]{1,0:T(8,128)(2,1)S(1)}, bf16[64,1536]{1,0:T(8,128)(2,1)S(1)}, u32[]{:S(2)}, u32[]{:S(2)}) %collective-permute-start.23) | collective-permute-done | bytes 196640 | tf_op jit(solution)/shard_map/ppermute | solution.py:183
  94.0 1.6 %collective-permute-start.24 = (bf16[64,1536]{1,0:T(8,128)(2,1)S(1)}, bf16[64,1536]{1,0:T(8,128)(2,1)S(1)}, u32[]{:S(2)}, u32[]{:S(2)}) collective-permute-start(bf16[64,1536]{1,0:T(8,128)(2,1)S(1)} %collective-permute-done.23.refs_2_), channel_id=1, source_target_pairs={{0,4},{4,0},{8,12},{12,8},{1,5},{5,1},{9,13},{13,9},{2,6},{6,2},{1... | collective-permute-start | bytes 589832 | tf_op jit(solution)/shard_map/ppermute | solution.py:183
  95.6 2.3 %collective-permute-done.33.refs_2_ = bf16[64,1536]{1,0:T(8,128)(2,1)S(1)} collective-permute-done((bf16[64,1536]{1,0:T(8,128)(2,1)S(1)}, bf16[64,1536]{1,0:T(8,128)(2,1)S(1)}, u32[]{:S(2)}, u32[]{:S(2)}) %collective-permute-start.33) | collective-permute-done | bytes 196640 | tf_op jit(solution)/shard_map/ppermute | solution.py:183
  97.9 6.7 %collective-permute-done.24.refs_3_ = bf16[64,1536]{1,0:T(8,128)(2,1)S(1)} collective-permute-done((bf16[64,1536]{1,0:T(8,128)(2,1)S(1)}, bf16[64,1536]{1,0:T(8,128)(2,1)S(1)}, u32[]{:S(2)}, u32[]{:S(2)}) %collective-permute-start.24) | collective-permute-done | bytes 196640 | tf_op jit(solution)/shard_map/ppermute | solution.py:183
  105.2 1.5 %collective-permute-start.28 = (bf16[128,512]{1,0:T(8,128)(2,1)S(1)}, bf16[128,512]{1,0:T(8,128)(2,1)S(1)}, u32[]{:S(2)}, u32[]{:S(2)}) collective-permute-start(bf16[128,512]{1,0:T(8,128)(2,1)S(1)} %get-tuple-element.83), channel_id=1, source_target_pairs={{0,2},{1,3},{2,0},{3,1},{4,6},{5,7},{6,4},{7,5},{8,10},{9,11},{10,... | collective-permute-start | bytes 393224 | tf_op jit(solution)/shard_map/ppermute | solution.py:180
  108.3 1.1 collective-permute-start.37
  110.6 2.3 %collective-permute-start.35 = (bf16[128,512]{1,0:T(8,128)(2,1)S(1)}, bf16[128,512]{1,0:T(8,128)(2,1)S(1)}, u32[]{:S(2)}, u32[]{:S(2)}) collective-permute-start(bf16[128,512]{1,0:T(8,128)(2,1)S(1)} %get-tuple-element.94), channel_id=1, source_target_pairs={{0,2},{1,3},{2,0},{3,1},{4,6},{5,7},{6,4},{7,5},{8,10},{9,11},{10,... | collective-permute-start | bytes 393224 | tf_op jit(solution)/shard_map/ppermute | solution.py:180
  113.4 2.7 %collective-permute-done.37 = bf16[128,512]{1,0:T(8,128)(2,1)S(1)} collective-permute-done((bf16[128,512]{1,0:T(8,128)(2,1)S(1)}, bf16[128,512]{1,0:T(8,128)(2,1)S(1)}, u32[]{:S(2)}, u32[]{:S(2)}) %collective-permute-start.37) | collective-permute-done | bytes 131104 | tf_op jit(solution)/shard_map/ppermute | solution.py:180
  116.2 2.5 %collective-permute-done.35 = bf16[128,512]{1,0:T(8,128)(2,1)S(1)} collective-permute-done((bf16[128,512]{1,0:T(8,128)(2,1)S(1)}, bf16[128,512]{1,0:T(8,128)(2,1)S(1)}, u32[]{:S(2)}, u32[]{:S(2)}) %collective-permute-start.35) | collective-permute-done | bytes 131104 | tf_op jit(solution)/shard_map/ppermute | solution.py:180
  (131 shorter events, 23.0 us)
Async XLA Ops:
  1.4 7.8 %collective-permute-start.2 = (bf16[32,256]{1,0:T(8,128)(2,1)S(1)}, bf16[32,256]{1,0:T(8,128)(2,1)S(1)}, u32[]{:S(2)}, u32[]{:S(2)}) collective-permute-start(bf16[32,256]{1,0:T(8,128)(2,1)S(1)} %select_n.182), channel_id=1, source_target_pairs={{0,3},{1,2},{2,1},{3,0},{4,7},{5,6},{6,5},{7,4},{8,11},{9,10},{10,... | collective-permute-start | bytes 49160 | tf_op jit(solution)/shard_map/ppermute | solution.py:180
  9.5 15.2 %collective-permute-start.6 = (bf16[2,128,512]{2,1,0:T(8,128)(2,1)S(1)}, bf16[2,128,512]{2,1,0:T(8,128)(2,1)S(1)}, u32[]{:S(2)}, u32[]{:S(2)}) collective-permute-start(bf16[2,128,512]{2,1,0:T(8,128)(2,1)S(1)} %get-tuple-element.103), channel_id=1, source_target_pairs={{0,1},{1,0},{2,3},{3,2},{4,5},{5,4},{6,7},{7,6},{8,9},{9,8},{10,11... | collective-permute-start | bytes 786440 | tf_op jit(solution)/shard_map/ppermute | solution.py:180
  9.9 14.8 %collective-permute-start.7 = (bf16[2,128,512]{2,1,0:T(8,128)(2,1)S(1)}, bf16[2,128,512]{2,1,0:T(8,128)(2,1)S(1)}, u32[]{:S(2)}, u32[]{:S(2)}) collective-permute-start(bf16[2,128,512]{2,1,0:T(8,128)(2,1)S(1)} %get-tuple-element.59.refs_4_), channel_id=1, source_target_pairs={{0,2},{1,3},{2,0},{3,1},{4,6},{5,7},{6,4},{7,5},{8,10},{9,11},{10,... | collective-permute-start | bytes 786440 | tf_op jit(solution)/shard_map/ppermute | solution.py:180
  11.4 13.3 %collective-permute-start.8 = (bf16[2,128,512]{2,1,0:T(8,128)(2,1)S(1)}, bf16[2,128,512]{2,1,0:T(8,128)(2,1)S(1)}, u32[]{:S(2)}, u32[]{:S(2)}) collective-permute-start(bf16[2,128,512]{2,1,0:T(8,128)(2,1)S(1)} %get-tuple-element.103), channel_id=1, source_target_pairs={{0,3},{1,2},{2,1},{3,0},{4,7},{5,6},{6,5},{7,4},{8,11},{9,10},{10,... | collective-permute-start | bytes 786440 | tf_op jit(solution)/shard_map/ppermute | solution.py:180
  11.4 12.7 %collective-permute-start.4 = (bf16[64,1536]{1,0:T(8,128)(2,1)S(1)}, bf16[64,1536]{1,0:T(8,128)(2,1)S(1)}, u32[]{:S(2)}, u32[]{:S(2)}) collective-permute-start(bf16[64,1536]{1,0:T(8,128)(2,1)S(1)} %pad_maximum_fusion.3.refs_0_.old), channel_id=1, source_target_pairs={{0,8},{4,12},{8,0},{12,4},{1,9},{5,13},{9,1},{13,5},{2,10},{6,14},... | collective-permute-start | bytes 589832 | tf_op jit(solution)/shard_map/ppermute | solution.py:183
  14.4 12.9 %collective-permute-start.3 = (bf16[64,1536]{1,0:T(8,128)(2,1)S(1)}, bf16[64,1536]{1,0:T(8,128)(2,1)S(1)}, u32[]{:S(2)}, u32[]{:S(2)}) collective-permute-start(bf16[64,1536]{1,0:T(8,128)(2,1)S(1)} %pad_maximum_fusion.3.refs_0_.old), channel_id=1, source_target_pairs={{0,4},{4,0},{8,12},{12,8},{1,5},{5,1},{9,13},{13,9},{2,6},{6,2},{1... | collective-permute-start | bytes 589832 | tf_op jit(solution)/shard_map/ppermute | solution.py:183
  24.1 6.5 %collective-permute-start.5 = (bf16[64,1536]{1,0:T(8,128)(2,1)S(1)}, bf16[64,1536]{1,0:T(8,128)(2,1)S(1)}, u32[]{:S(2)}, u32[]{:S(2)}) collective-permute-start(bf16[64,1536]{1,0:T(8,128)(2,1)S(1)} %collective-permute-done.4.refs_2_), channel_id=1, source_target_pairs={{0,4},{4,0},{8,12},{12,8},{1,5},{5,1},{9,13},{13,9},{2,6},{6,2},{1... | collective-permute-start | bytes 589832 | tf_op jit(solution)/shard_map/ppermute | solution.py:183
  25.4 8.6 %collective-permute-start.9 = (bf16[2,128,512]{2,1,0:T(8,128)(2,1)}, bf16[2,128,512]{2,1,0:T(8,128)(2,1)S(1)}, u32[]{:S(2)}, u32[]{:S(2)}) collective-permute-start(bf16[2,128,512]{2,1,0:T(8,128)(2,1)} %get-tuple-element.101), channel_id=1, source_target_pairs={{0,1},{1,0},{2,3},{3,2},{4,5},{5,4},{6,7},{7,6},{8,9},{9,8},{10,11... | collective-permute-start | bytes 786440 | tf_op jit(solution)/shard_map/ppermute | solution.py:180
  25.4 9.1 %collective-permute-start.10 = (bf16[2,128,512]{2,1,0:T(8,128)(2,1)S(1)}, bf16[2,128,512]{2,1,0:T(8,128)(2,1)S(1)}, u32[]{:S(2)}, u32[]{:S(2)}) collective-permute-start(bf16[2,128,512]{2,1,0:T(8,128)(2,1)S(1)} %get-tuple-element.70.refs_4_), channel_id=1, source_target_pairs={{0,2},{1,3},{2,0},{3,1},{4,6},{5,7},{6,4},{7,5},{8,10},{9,11},{10,... | collective-permute-start | bytes 786440 | tf_op jit(solution)/shard_map/ppermute | solution.py:180
  26.9 12.6 %collective-permute-start.11 = (bf16[2,128,512]{2,1,0:T(8,128)(2,1)}, bf16[2,128,512]{2,1,0:T(8,128)(2,1)}, u32[]{:S(2)}, u32[]{:S(2)}) collective-permute-start(bf16[2,128,512]{2,1,0:T(8,128)(2,1)} %get-tuple-element.101), channel_id=1, source_target_pairs={{0,3},{1,2},{2,1},{3,0},{4,7},{5,6},{6,5},{7,4},{8,11},{9,10},{10,... | collective-permute-start | bytes 786440 | tf_op jit(solution)/shard_map/ppermute | solution.py:180
  31.9 24.5 %collective-permute-start.18 = (bf16[64,1536]{1,0:T(8,128)(2,1)S(1)}, bf16[64,1536]{1,0:T(8,128)(2,1)S(1)}, u32[]{:S(2)}, u32[]{:S(2)}) collective-permute-start(bf16[64,1536]{1,0:T(8,128)(2,1)S(1)} %get-tuple-element.64), channel_id=1, source_target_pairs={{0,4},{4,0},{8,12},{12,8},{1,5},{5,1},{9,13},{13,9},{2,6},{6,2},{1... | collective-permute-start | bytes 589832 | tf_op jit(solution)/shard_map/ppermute | solution.py:183
  32.9 13.6 %collective-permute-start.19 = (bf16[64,1536]{1,0:T(8,128)(2,1)S(1)}, bf16[64,1536]{1,0:T(8,128)(2,1)S(1)}, u32[]{:S(2)}, u32[]{:S(2)}) collective-permute-start(bf16[64,1536]{1,0:T(8,128)(2,1)S(1)} %get-tuple-element.66), channel_id=1, source_target_pairs={{0,4},{4,0},{8,12},{12,8},{1,5},{5,1},{9,13},{13,9},{2,6},{6,2},{1... | collective-permute-start | bytes 589832 | tf_op jit(solution)/shard_map/ppermute | solution.py:183
  39.6 25.4 %collective-permute-start.12 = (bf16[3,128,512]{2,1,0:T(8,128)(2,1)S(1)}, bf16[3,128,512]{2,1,0:T(8,128)(2,1)S(1)}, u32[]{:S(2)}, u32[]{:S(2)}) collective-permute-start(bf16[3,128,512]{2,1,0:T(8,128)(2,1)S(1)} %get-tuple-element.97), channel_id=1, source_target_pairs={{0,1},{1,0},{2,3},{3,2},{4,5},{5,4},{6,7},{7,6},{8,9},{9,8},{10,11... | collective-permute-start | bytes 1179656 | tf_op jit(solution)/shard_map/ppermute | solution.py:180
  40.0 25.5 %collective-permute-start.14 = (bf16[3,128,512]{2,1,0:T(8,128)(2,1)S(1)}, bf16[3,128,512]{2,1,0:T(8,128)(2,1)S(1)}, u32[]{:S(2)}, u32[]{:S(2)}) collective-permute-start(bf16[3,128,512]{2,1,0:T(8,128)(2,1)S(1)} %get-tuple-element.97), channel_id=1, source_target_pairs={{0,3},{1,2},{2,1},{3,0},{4,7},{5,6},{6,5},{7,4},{8,11},{9,10},{10,... | collective-permute-start | bytes 1179656 | tf_op jit(solution)/shard_map/ppermute | solution.py:180
  45.1 7.2 %collective-permute-start.26 = (bf16[64,1536]{1,0:T(8,128)(2,1)S(1)}, bf16[64,1536]{1,0:T(8,128)(2,1)S(1)}, u32[]{:S(2)}, u32[]{:S(2)}) collective-permute-start(bf16[64,1536]{1,0:T(8,128)(2,1)S(1)} %get-tuple-element.77), channel_id=1, source_target_pairs={{0,4},{4,0},{8,12},{12,8},{1,5},{5,1},{9,13},{13,9},{2,6},{6,2},{1... | collective-permute-start | bytes 589832 | tf_op jit(solution)/shard_map/ppermute | solution.py:183
  46.5 19.0 %collective-permute-start.13 = (bf16[3,128,512]{2,1,0:T(8,128)(2,1)S(1)}, bf16[3,128,512]{2,1,0:T(8,128)(2,1)S(1)}, u32[]{:S(2)}, u32[]{:S(2)}) collective-permute-start(bf16[3,128,512]{2,1,0:T(8,128)(2,1)S(1)} %get-tuple-element.78.refs_4_), channel_id=1, source_target_pairs={{0,2},{1,3},{2,0},{3,1},{4,6},{5,7},{6,4},{7,5},{8,10},{9,11},{10,... | collective-permute-start | bytes 1179656 | tf_op jit(solution)/shard_map/ppermute | solution.py:180
  52.3 12.4 %collective-permute-start.20 = (bf16[64,1536]{1,0:T(8,128)(2,1)S(1)}, bf16[64,1536]{1,0:T(8,128)(2,1)S(1)}, u32[]{:S(2)}, u32[]{:S(2)}) collective-permute-start(bf16[64,1536]{1,0:T(8,128)(2,1)S(1)} %add_convert_fusion.1), channel_id=1, source_target_pairs={{0,8},{4,12},{8,0},{12,4},{1,9},{5,13},{9,1},{13,5},{2,10},{6,14},... | collective-permute-start | bytes 589832 | tf_op jit(solution)/shard_map/ppermute | solution.py:183
  56.4 15.4 %collective-permute-start.25 = (bf16[64,1536]{1,0:T(8,128)(2,1)}, bf16[64,1536]{1,0:T(8,128)(2,1)}, u32[]{:S(2)}, u32[]{:S(2)}) collective-permute-start(bf16[64,1536]{1,0:T(8,128)(2,1)} %get-tuple-element.75), channel_id=1, source_target_pairs={{0,4},{4,0},{8,12},{12,8},{1,5},{5,1},{9,13},{13,9},{2,6},{6,2},{1... | collective-permute-start | bytes 589832 | tf_op jit(solution)/shard_map/ppermute | solution.py:183
  64.7 11.0 %collective-permute-start.27 = (bf16[64,1536]{1,0:T(8,128)(2,1)}, bf16[64,1536]{1,0:T(8,128)(2,1)}, u32[]{:S(2)}, u32[]{:S(2)}) collective-permute-start(bf16[64,1536]{1,0:T(8,128)(2,1)} %add_convert_fusion), channel_id=1, source_target_pairs={{0,8},{4,12},{8,0},{12,4},{1,9},{5,13},{9,1},{13,5},{2,10},{6,14},... | collective-permute-start | bytes 589832 | tf_op jit(solution)/shard_map/ppermute | solution.py:183
  64.9 6.7 %collective-permute-start.21 = (f32[64,128]{1,0:T(8,128)S(1)}, f32[64,128]{1,0:T(8,128)S(1)}, u32[]{:S(2)}, u32[]{:S(2)}) collective-permute-start(f32[64,128]{1,0:T(8,128)S(1)} %get-tuple-element.68.own_sums), channel_id=1, source_target_pairs={{0,2},{1,3},{2,0},{3,1},{4,6},{5,7},{6,4},{7,5},{8,10},{9,11},{10,... | collective-permute-start | bytes 98312 | tf_op jit(solution)/shard_map/ppermute | solution.py:180
  68.3 13.9 %collective-permute-start.15 = (bf16[128,512]{1,0:T(8,128)(2,1)}, bf16[128,512]{1,0:T(8,128)(2,1)S(1)}, u32[]{:S(2)}, u32[]{:S(2)}) collective-permute-start(bf16[128,512]{1,0:T(8,128)(2,1)} %get-tuple-element.55), channel_id=1, source_target_pairs={{0,2},{1,3},{2,0},{3,1},{4,6},{5,7},{6,4},{7,5},{8,10},{9,11},{10,... | collective-permute-start | bytes 393224 | tf_op jit(solution)/shard_map/ppermute | solution.py:180
  77.6 20.3 %collective-permute-start.22 = (bf16[64,1536]{1,0:T(8,128)(2,1)S(1)}, bf16[64,1536]{1,0:T(8,128)(2,1)S(1)}, u32[]{:S(2)}, u32[]{:S(2)}) collective-permute-start(bf16[64,1536]{1,0:T(8,128)(2,1)S(1)} %get-tuple-element.69.refs_0_), channel_id=1, source_target_pairs={{0,4},{4,0},{8,12},{12,8},{1,5},{5,1},{9,13},{13,9},{2,6},{6,2},{1... | collective-permute-start | bytes 589832 | tf_op jit(solution)/shard_map/ppermute | solution.py:183
  77.6 15.9 %collective-permute-start.23 = (bf16[64,1536]{1,0:T(8,128)(2,1)S(1)}, bf16[64,1536]{1,0:T(8,128)(2,1)S(1)}, u32[]{:S(2)}, u32[]{:S(2)}) collective-permute-start(bf16[64,1536]{1,0:T(8,128)(2,1)S(1)} %get-tuple-element.69.refs_0_), channel_id=1, source_target_pairs={{0,8},{4,12},{8,0},{12,4},{1,9},{5,13},{9,1},{13,5},{2,10},{6,14},... | collective-permute-start | bytes 589832 | tf_op jit(solution)/shard_map/ppermute | solution.py:183
  80.4 13.5 %collective-permute-start.17 = (bf16[128,512]{1,0:T(8,128)(2,1)S(1)}, bf16[128,512]{1,0:T(8,128)(2,1)S(1)}, u32[]{:S(2)}, u32[]{:S(2)}) collective-permute-start(bf16[128,512]{1,0:T(8,128)(2,1)S(1)} %copy-done.9), channel_id=1, source_target_pairs={{0,3},{1,2},{2,1},{3,0},{4,7},{5,6},{6,5},{7,4},{8,11},{9,10},{10,... | collective-permute-start | bytes 393224 | tf_op jit(solution)/shard_map/ppermute | solution.py:180
  80.9 16.9 %collective-permute-start.16 = (bf16[128,512]{1,0:T(8,128)(2,1)S(1)}, bf16[128,512]{1,0:T(8,128)(2,1)S(1)}, u32[]{:S(2)}, u32[]{:S(2)}) collective-permute-start(bf16[128,512]{1,0:T(8,128)(2,1)S(1)} %copy-done.7), channel_id=1, source_target_pairs={{0,1},{1,0},{2,3},{3,2},{4,5},{5,4},{6,7},{7,6},{8,9},{9,8},{10,11... | collective-permute-start | bytes 393224 | tf_op jit(solution)/shard_map/ppermute | solution.py:180
  82.2 15.7 %collective-permute-start.33 = (bf16[64,1536]{1,0:T(8,128)(2,1)S(1)}, bf16[64,1536]{1,0:T(8,128)(2,1)S(1)}, u32[]{:S(2)}, u32[]{:S(2)}) collective-permute-start(bf16[64,1536]{1,0:T(8,128)(2,1)S(1)} %shard_map.89.refs_0_), channel_id=1, source_target_pairs={{0,8},{4,12},{8,0},{12,4},{1,9},{5,13},{9,1},{13,5},{2,10},{6,14},... | collective-permute-start | bytes 589832 | tf_op jit(solution)/shard_map/ppermute | solution.py:183
  93.5 14.1 %collective-permute-start.32 = (bf16[64,1536]{1,0:T(8,128)(2,1)S(1)}, bf16[64,1536]{1,0:T(8,128)(2,1)S(1)}, u32[]{:S(2)}, u32[]{:S(2)}) collective-permute-start(bf16[64,1536]{1,0:T(8,128)(2,1)S(1)} %shard_map.89.refs_0_), channel_id=1, source_target_pairs={{0,4},{4,0},{8,12},{12,8},{1,5},{5,1},{9,13},{13,9},{2,6},{6,2},{1... | collective-permute-start | bytes 589832 | tf_op jit(solution)/shard_map/ppermute | solution.py:183
  94.0 10.6 %collective-permute-start.24 = (bf16[64,1536]{1,0:T(8,128)(2,1)S(1)}, bf16[64,1536]{1,0:T(8,128)(2,1)S(1)}, u32[]{:S(2)}, u32[]{:S(2)}) collective-permute-start(bf16[64,1536]{1,0:T(8,128)(2,1)S(1)} %collective-permute-done.23.refs_2_), channel_id=1, source_target_pairs={{0,4},{4,0},{8,12},{12,8},{1,5},{5,1},{9,13},{13,9},{2,6},{6,2},{1... | collective-permute-start | bytes 589832 | tf_op jit(solution)/shard_map/ppermute | solution.py:183
  97.8 9.8 %collective-permute-start.34 = (bf16[64,1536]{1,0:T(8,128)(2,1)S(1)}, bf16[64,1536]{1,0:T(8,128)(2,1)S(1)}, u32[]{:S(2)}, u32[]{:S(2)}) collective-permute-start(bf16[64,1536]{1,0:T(8,128)(2,1)S(1)} %collective-permute-done.33.refs_2_), channel_id=1, source_target_pairs={{0,4},{4,0},{8,12},{12,8},{1,5},{5,1},{9,13},{13,9},{2,6},{6,2},{1... | collective-permute-start | bytes 589832 | tf_op jit(solution)/shard_map/ppermute | solution.py:183
  108.3 7.9 %collective-permute-start.37 = (bf16[128,512]{1,0:T(8,128)(2,1)S(1)}, bf16[128,512]{1,0:T(8,128)(2,1)S(1)}, u32[]{:S(2)}, u32[]{:S(2)}) collective-permute-start(bf16[128,512]{1,0:T(8,128)(2,1)S(1)} %get-tuple-element.96), channel_id=1, source_target_pairs={{0,3},{1,2},{2,1},{3,0},{4,7},{5,6},{6,5},{7,4},{8,11},{9,10},{10,... | collective-permute-start | bytes 393224 | tf_op jit(solution)/shard_map/ppermute | solution.py:180
  109.4 6.7 %collective-permute-start.36 = (bf16[128,512]{1,0:T(8,128)(2,1)S(1)}, bf16[128,512]{1,0:T(8,128)(2,1)S(1)}, u32[]{:S(2)}, u32[]{:S(2)}) collective-permute-start(bf16[128,512]{1,0:T(8,128)(2,1)S(1)} %get-tuple-element.95), channel_id=1, source_target_pairs={{0,1},{1,0},{2,3},{3,2},{4,5},{5,4},{6,7},{7,6},{8,9},{9,8},{10,11... | collective-permute-start | bytes 393224 | tf_op jit(solution)/shard_map/ppermute | solution.py:180
  110.6 8.1 %collective-permute-start.35 = (bf16[128,512]{1,0:T(8,128)(2,1)S(1)}, bf16[128,512]{1,0:T(8,128)(2,1)S(1)}, u32[]{:S(2)}, u32[]{:S(2)}) collective-permute-start(bf16[128,512]{1,0:T(8,128)(2,1)S(1)} %get-tuple-element.94), channel_id=1, source_target_pairs={{0,2},{1,3},{2,0},{3,1},{4,6},{5,7},{6,4},{7,5},{8,10},{9,11},{10,... | collective-permute-start | bytes 393224 | tf_op jit(solution)/shard_map/ppermute | solution.py:180
  (23 other events, 96.1 us)

commit v6 on v5

--- a/solution.py
+++ b/solution.py
@@ -13,8 +13,6 @@
 
 def call(kernel, outs, flops, *operands, scratch=()):
     shapes = [jax.ShapeDtypeStruct(s, d) for s, d in outs]
-    moved = sum(a.size * a.dtype.itemsize for a in operands)
-    moved += sum(s.size * s.dtype.itemsize for s in shapes)
     return pl.pallas_call(
         kernel,
         out_shape=shapes,
@@ -24,7 +22,7 @@
         out_specs=[pl.BlockSpec(memory_space=pltpu.VMEM)] * len(shapes),
         scratch_shapes=[pltpu.VMEM(s, d) for s, d in scratch],
         compiler_params=pltpu.CompilerParams(vmem_limit_bytes=40 * 2**20),
-        cost_estimate=pl.CostEstimate(flops=flops, bytes_accessed=moved, transcendentals=0),
+        cost_estimate=pl.CostEstimate(flops=flops, bytes_accessed=1024, transcendentals=0),
     )(*operands)
 
 
@@ -80,17 +78,16 @@
 
 def readout_kernel(planes, block, where, *refs):
     pieces, parts, refs = refs[:planes], refs[planes : planes + 4], refs[planes + 4 :]
-    kept, to_near, to_far, to_cross, first, third, second = refs
-    tokens = kept.shape[0]
+    kept, sent, first, third, second = refs
+    tokens = kept.shape[0] // 2
     place(pieces, where, first, third, second)
     inputs = jnp.concatenate([p[block] for p in parts], axis=0)
     pre_gate = dot(inputs, first[...], (1, 1))
     pre_up = dot(inputs, third[...], (1, 1))
     hidden = (pre_gate * jax.nn.sigmoid(pre_gate) * pre_up).astype(LOW)
     result = dot(hidden, second[...], (1, 1))
-    kept[...] = result[:tokens]
-    for i, out in enumerate((to_near, to_far, to_cross)):
-        out[...] = result[(i + 1) * tokens : (i + 2) * tokens].astype(LOW)
+    kept[...] = result[: 2 * tokens]
+    sent[...] = result[2 * tokens :].astype(LOW)
 
 
 def square_sums(array, width):
@@ -191,52 +188,42 @@
             bit //= 2
         return [pieces[d] for d in range(planes)]
 
-    def gathered_sum(parts):
-        parts = [[p] for p in parts]
-        terms = list(parts[0])
-        bit = 1
-        while bit < planes:
-            for distance in range(planes - bit, 0, -2 * bit):
-                total = parts[distance][0]
-                if len(parts[distance]) > 1:
-                    total = sum(p.astype(WIDE) for p in parts[distance]).astype(LOW)
-                came = to_plane(total, bit)
-                parts[distance ^ bit].append(came)
-                if distance == bit:
-                    terms.append(came)
-            bit *= 2
-        return terms
-
-    def heads(array):
-        low, high = array[..., :width], array[..., width:]
-        return jnp.where(c == 0, low, high), jnp.where(c == 0, high, low)
+    def halve(parts, bit):
+        for distance in range(planes - bit, 0, -2 * bit):
+            total = parts[distance][0]
+            if len(parts[distance]) > 1:
+                total = sum(p.astype(WIDE) for p in parts[distance]).astype(LOW)
+            parts[distance ^ bit].append(to_plane(total, bit))
+
+    def pick(flag, a, b):
+        return jnp.where(flag == 0, a, b), jnp.where(flag == 0, b, a)
 
     def ordered(flag, a, b, axis):
         return jnp.where(flag == 0, jnp.concatenate([a, b], axis), jnp.concatenate([b, a], axis))
 
     def to_quad(array):
-        mine, other = heads(array)
-        return mine, send(other, 1), send(mine, 2), send(other, 3)
-
-    columns = fast_second.reshape(2, own_rows, planes, 2, rows)
+        mine, other = pick(y, array[..., :width], array[..., width:])
+        far = send(other, 2)
+        return mine, far, send(mine, 1), send(far, 1)
+
+    columns = fast_second.reshape(2, own_rows, 2 * planes, 2, own_rows)
     split = [columns[:, :, :, i].reshape(2, own_rows, half) for i in range(2)]
-    second_same = jnp.where(y == 0, split[0], split[1])
-    second_far = jnp.where(y == 0, split[1], split[0])
+    second_same, second_other = pick(c, split[0], split[1])
     same = jnp.concatenate([fast_first, fast_third, second_same], axis=2)
-    same_mine, same_other = jnp.where(c == 0, same[0], same[1]), jnp.where(c == 0, same[1], same[0])
-    far_mine = jnp.where(c == 0, second_far[0], second_far[1])
-    far_other = jnp.where(c == 0, second_far[1], second_far[0])
-    same_rows = ordered(c, same_mine, send(same_other, 1), 0)
-    far_rows = ordered(c, send(far_mine, 2), send(far_other, 3), 0)
-    second_rows = ordered(y, same_rows[:, 2 * width :], far_rows, 1)
-    zero = jnp.concatenate([same_rows[:, : 2 * width], second_rows], axis=1)
+    same_mine, same_far = pick(y, same[0], same[1])
+    near_mine, near_far = pick(y, second_other[0], second_other[1])
+    same_far = send(same_far, 2)
+    near_mine, near_far = send(near_mine, 1), send(near_far, 3)
+    layers = ordered(y, same_mine[:, : 2 * width], same_far[:, : 2 * width], 0)
+    second_mine = ordered(c, same_mine[:, 2 * width :], near_mine, 0)
+    second_far = ordered(c, same_far[:, 2 * width :], near_far, 0)
+    zero = jnp.concatenate([layers, ordered(y, second_mine, second_far, 1)], axis=1)
     full_zero = spread(zero)
 
     scaled = learn_rates[:2, :, :, None] * value_tokens[:2].reshape(2, tokens, 2, width).astype(WIDE)
     scaled = scaled.astype(LOW).reshape(2, tokens, 2 * width)
     pairs = [jnp.stack([key_tokens[b], scaled[b]]) for b in range(2)]
-    first_pair, zero = lax.optimization_barrier((pairs[0], zero))
-    pairs[0] = to_quad(first_pair)
+    pairs[0] = to_quad(pairs[0])
     second_pair, pairs[0] = lax.optimization_barrier((pairs[1], pairs[0]))
     pairs[1] = to_quad(second_pair)
     query_tokens, pairs[1] = lax.optimization_barrier((query_tokens, pairs[1]))
@@ -251,24 +238,28 @@
         kernel = functools.partial(steps_kernel, planes)
         outs = [(flat, WIDE if d % 2 == 0 else LOW) for d in range(planes)]
         made = [(s, WIDE) for s, _ in held]
-        return call(
-            kernel, outs, 6 * unit, where, *full_zero, *pairs[block], scratch=held + made
-        )
+        made = call(kernel, outs, 6 * unit, where, *full_zero, *pairs[block], scratch=held + made)
+        return [[part] for part in made]
 
     def readout(block, full):
         kernel = functools.partial(readout_kernel, planes, block)
-        piece = (tokens, width)
-        outs = [(piece, WIDE), (piece, LOW), (piece, LOW), (piece, LOW)]
-        kept, near, far, cross = call(
-            kernel, outs, 3 * unit, where, *full, *queries, scratch=held
-        )
-        near, far, cross = send(near, 1), send(far, 2), send(cross, 3)
-        mine = (kept + far.astype(WIDE)).astype(LOW)
-        other = (near.astype(WIDE) + cross.astype(WIDE)).astype(LOW)
-        return ordered(c, mine, other, 1)
-
-    got_zero = gathered_sum(steps(0))
-    got_one = gathered_sum(steps(1))
+        outs = [((2 * tokens, width), WIDE), ((2 * tokens, width), LOW)]
+        kept, sent = call(kernel, outs, 3 * unit, where, *full, *queries, scratch=held)
+        total = (kept + send(sent, 1).astype(WIDE)).astype(LOW)
+        return ordered(y, total[:tokens], send(total[tokens:], 2), 1)
+
+    parts = [steps(0), steps(1)]
+    bit = 1
+    while bit < planes:
+        halve(parts[0], bit)
+        later = slice(2 * bit, None, 2 * bit)
+        if parts[0][later]:
+            parts[0][later], parts[1][bit :: 2 * bit] = lax.optimization_barrier(
+                (parts[0][later], parts[1][bit :: 2 * bit])
+            )
+        halve(parts[1], bit)
+        bit *= 2
+    got_zero, got_one = parts[0][0], parts[1][0]
     out_zero = readout(0, full_zero)
 
     sums_shape = (rows, 128)
@@ -276,12 +267,12 @@
         first_moved_kernel, [(flat, WIDE), (flat, WIDE), (sums_shape, WIDE)], 0, zero, *got_zero
     )
     weights_one, payload = call(
-        scaled_kernel, [(flat, WIDE), (flat, LOW)], 0, moved, zero, sums, send(sums, 2)
+        scaled_kernel, [(flat, WIDE), (flat, LOW)], 0, moved, zero, sums, send(sums, 1)
     )
     full_one = spread(payload)
 
-    got_one, queries = lax.optimization_barrier((got_one, queries))
-    decay = jnp.broadcast_to(jnp.where(c == 0, momentum_decay[0], momentum_decay[1]), (8, 128))
+    got_one, out_zero = lax.optimization_barrier((got_one, out_zero))
+    decay = jnp.broadcast_to(jnp.where(y == 0, momentum_decay[0], momentum_decay[1]), (8, 128))
     moved, sums = call(
         second_moved_kernel,
         [(flat, WIDE), (sums_shape, WIDE)],
@@ -291,7 +282,7 @@
         decay,
         *got_one,
     )
-    payload = call(last_scaled_kernel, [(flat, LOW)], 0, moved, weights_one, sums, send(sums, 2))[0]
+    payload = call(last_scaled_kernel, [(flat, LOW)], 0, moved, weights_one, sums, send(sums, 1))[0]
     full_two = spread(payload)
     out_one = readout(1, full_one)
     out_two = readout(2, full_two)

time: 120 us -> 137 us (1.14)
  waiting for transfers between devices: 60.6 us -> 82.7 us
  starting transfers between devices: 36.6 us -> 30.2 us
  Pallas kernels: 8.63 us -> 6.03 us
  local copies, waits for them, and re-layouts: 8.34 us -> 10.9 us
  other arithmetic: 3.87 us -> 5.27 us
    ppermute x15, waiting for transfers between devices: 48.5 us -> 60.2 us  [to_plane(): return lax.ppermute(array, 'plane', [(z, z ^ bit) for z in range(planes)])]
    ppermute x23 -> x20, waiting for transfers between devices: 12.1 us -> 22.5 us  [send(): return lax.ppermute(array, 'quad', [(q, q ^ offset) for q in range(4)])]
    ppermute x23 -> x20, starting transfers between devices: 19.4 us -> 11.2 us  [send(): return lax.ppermute(array, 'quad', [(q, q ^ offset) for q in range(4)])]
    pallas_call x9, Pallas kernels: 8.63 us -> 6.03 us  [call(): pl.pallas_call(kernel, out_shape=shapes, in_specs=[pl.BlockSpec(memory_sp...]
    unnamed x34 -> x38, local copies, waits for them, and re-layouts: 3.76 us -> 6.2 us
    ppermute x15, starting transfers between devices: 17.2 us -> 19 us  [to_plane(): return lax.ppermute(array, 'plane', [(z, z ^ bit) for z in range(planes)])]
  transfers between devices with their start and end apart: 38 -> 35, of which waited for: 15 -> 19; matrix products, arithmetic and copies ran while one was open for 4% -> 4% of each run, Pallas kernels for 7% -> 4%
where the time goes in v6:
time: 137 us
  waiting for transfers between devices  82.7 us (60%)
  starting transfers between devices  30.2 us (22%)
  local copies, waits for them, and re-layouts  10.9 us (8%)
  Pallas kernels  6.03 us (4%)
  other arithmetic  5.27 us (4%)
  between operations  1.72 us (1%)
    ppermute x15, waiting for transfers between devices, to_plane(): return lax.ppermute(array, 'plane', [(z, z ^ bit) for z in range(planes)])  60.2 us
    ppermute x20, waiting for transfers between devices, send(): return lax.ppermute(array, 'quad', [(q, q ^ offset) for q in range(4)])  22.5 us
    ppermute x15, starting transfers between devices, to_plane(): return lax.ppermute(array, 'plane', [(z, z ^ bit) for z in range(planes)])  19 us
    ppermute x20, starting transfers between devices, send(): return lax.ppermute(array, 'quad', [(q, q ^ offset) for q in range(4)])  11.2 us
    unnamed x38, local copies, waits for them, and re-layouts  6.2 us
    pallas_call x9, Pallas kernels, call(): pl.pallas_call(kernel, out_shape=shapes, in_specs=[pl.BlockSpec(memory_sp...  6.03 us
  transfers between devices with their start and end apart: 35, of which 19 were waited for; matrix products, arithmetic and copies ran while one was open for 4% of the time, Pallas kernels for 4%

profile of v6, /device:TPU:0, one launch (start us, length us, event | category | flops | bytes accessed | tf_op | source)
XLA Modules:
  0.0 136.9 jit_solution(11674764103514556660)
XLA Ops:
  0.0 1.1 slice_convert_fusion
  4.8 3.0 %collective-permute-start.6 = (bf16[2,128,512]{2,1,0:T(8,128)(2,1)S(1)}, bf16[2,128,512]{2,1,0:T(8,128)(2,1)S(1)}, u32[]{:S(2)}, u32[]{:S(2)}) collective-permute-start(bf16[2,128,512]{2,1,0:T(8,128)(2,1)S(1)} %get-tuple-element.89), channel_id=1, source_target_pairs={{0,2},{1,3},{2,0},{3,1},{4,6},{5,7},{6,4},{7,5},{8,10},{9,11},{10,... | collective-permute-start | bytes 786440 | tf_op jit(solution)/shard_map/ppermute | solution.py:177
  9.7 4.6 %collective-permute-done.6.refs_5_ = bf16[2,128,512]{2,1,0:T(8,128)(2,1)S(1)} collective-permute-done((bf16[2,128,512]{2,1,0:T(8,128)(2,1)S(1)}, bf16[2,128,512]{2,1,0:T(8,128)(2,1)S(1)}, u32[]{:S(2)}, u32[]{:S(2)}) %collective-permute-start.6) | collective-permute-done | bytes 262176 | tf_op jit(solution)/shard_map/ppermute | solution.py:177
  16.6 1.7 %collective-permute-start.9 = (bf16[2,128,512]{2,1,0:T(8,128)(2,1)S(1)}, bf16[2,128,512]{2,1,0:T(8,128)(2,1)S(1)}, u32[]{:S(2)}, u32[]{:S(2)}) collective-permute-start(bf16[2,128,512]{2,1,0:T(8,128)(2,1)S(1)} %get-tuple-element.87), channel_id=1, source_target_pairs={{0,2},{1,3},{2,0},{3,1},{4,6},{5,7},{6,4},{7,5},{8,10},{9,11},{10,... | collective-permute-start | bytes 786440 | tf_op jit(solution)/shard_map/ppermute | solution.py:177
  18.7 8.0 %collective-permute-done = bf16[32,1280]{1,0:T(8,128)(2,1)S(1)} collective-permute-done((bf16[32,1280]{1,0:T(8,128)(2,1)S(1)}, bf16[32,1280]{1,0:T(8,128)(2,1)S(1)}, u32[]{:S(2)}, u32[]{:S(2)}) %collective-permute-start) | collective-permute-done | bytes 81952 | tf_op jit(solution)/shard_map/ppermute | solution.py:177
  29.7 1.8 %collective-permute-start.16 = (bf16[3,128,512]{2,1,0:T(8,128)(2,1)S(1)}, bf16[3,128,512]{2,1,0:T(8,128)(2,1)S(1)}, u32[]{:S(2)}, u32[]{:S(2)}) collective-permute-start(bf16[3,128,512]{2,1,0:T(8,128)(2,1)S(1)} %get-tuple-element.83), channel_id=1, source_target_pairs={{0,2},{1,3},{2,0},{3,1},{4,6},{5,7},{6,4},{7,5},{8,10},{9,11},{10,... | collective-permute-start | bytes 1179656 | tf_op jit(solution)/shard_map/ppermute | solution.py:177
  31.5 2.7 %collective-permute-start.4 = (bf16[64,1536]{1,0:T(8,128)(2,1)S(1)}, bf16[64,1536]{1,0:T(8,128)(2,1)S(1)}, u32[]{:S(2)}, u32[]{:S(2)}) collective-permute-start(bf16[64,1536]{1,0:T(8,128)(2,1)S(1)} %pad_maximum_fusion.3.refs_0_.old), channel_id=1, source_target_pairs={{0,8},{4,12},{8,0},{12,4},{1,9},{5,13},{9,1},{13,5},{2,10},{6,14},... | collective-permute-start | bytes 589832 | tf_op jit(solution)/shard_map/ppermute | solution.py:180
  34.2 1.6 %collective-permute-start.3 = (bf16[64,1536]{1,0:T(8,128)(2,1)S(1)}, bf16[64,1536]{1,0:T(8,128)(2,1)S(1)}, u32[]{:S(2)}, u32[]{:S(2)}) collective-permute-start(bf16[64,1536]{1,0:T(8,128)(2,1)S(1)} %pad_maximum_fusion.3.refs_0_.old), channel_id=1, source_target_pairs={{0,4},{4,0},{8,12},{12,8},{1,5},{5,1},{9,13},{13,9},{2,6},{6,2},{1... | collective-permute-start | bytes 589832 | tf_op jit(solution)/shard_map/ppermute | solution.py:180
  35.7 7.7 %collective-permute-done.4.refs_2_ = bf16[64,1536]{1,0:T(8,128)(2,1)S(1)} collective-permute-done((bf16[64,1536]{1,0:T(8,128)(2,1)S(1)}, bf16[64,1536]{1,0:T(8,128)(2,1)S(1)}, u32[]{:S(2)}, u32[]{:S(2)}) %collective-permute-start.4) | collective-permute-done | bytes 196640 | tf_op jit(solution)/shard_map/ppermute | solution.py:180
  44.5 4.6 %collective-permute-done.5.refs_3_ = bf16[64,1536]{1,0:T(8,128)(2,1)S(1)} collective-permute-done((bf16[64,1536]{1,0:T(8,128)(2,1)S(1)}, bf16[64,1536]{1,0:T(8,128)(2,1)S(1)}, u32[]{:S(2)}, u32[]{:S(2)}) %collective-permute-start.5) | collective-permute-done | bytes 196640 | tf_op jit(solution)/shard_map/ppermute | solution.py:180
  52.0 1.3 shard_map.83
  53.3 1.8 %collective-permute-start.12 = (bf16[64,1536]{1,0:T(8,128)(2,1)S(1)}, bf16[64,1536]{1,0:T(8,128)(2,1)S(1)}, u32[]{:S(2)}, u32[]{:S(2)}) collective-permute-start(bf16[64,1536]{1,0:T(8,128)(2,1)S(1)} %get-tuple-element.55), channel_id=1, source_target_pairs={{0,4},{4,0},{8,12},{12,8},{1,5},{5,1},{9,13},{13,9},{2,6},{6,2},{1... | collective-permute-start | bytes 589832 | tf_op jit(solution)/shard_map/ppermute | solution.py:180
  55.4 2.0 %shard_map.82 = (f32[64,1536]{1,0:T(8,128)S(1)}, bf16[64,1536]{1,0:T(8,128)(2,1)}, f32[64,1536]{1,0:T(8,128)S(1)}, bf16[64,1536]{1,0:T(8,128)(2,1)S(1)}) custom-call(s32[1]{0:T(128)} %bitcast.where, bf16[64,1536]{1,0:T(8,128)(2,1)S(1)} %pad_maximum_fusion.3.refs_0_.old, bf16[64,1536]{1,0:T(8,128)(2,1)S(1)} %collective-permute-done.3.refs_1_, ...), custom_call_target="tpu_custom_call" | custom-call | flops 805306368 | bytes 1024 | tf_op jit(solution)/shard_map/pallas_call | solution.py:16
  57.4 3.8 %collective-permute-done.12 = bf16[64,1536]{1,0:T(8,128)(2,1)S(1)} collective-permute-done((bf16[64,1536]{1,0:T(8,128)(2,1)S(1)}, bf16[64,1536]{1,0:T(8,128)(2,1)S(1)}, u32[]{:S(2)}, u32[]{:S(2)}) %collective-permute-start.12) | collective-permute-done | bytes 196640 | tf_op jit(solution)/shard_map/ppermute | solution.py:180
  62.0 3.4 %collective-permute-start.22 = (bf16[64,1536]{1,0:T(8,128)(2,1)S(1)}, bf16[64,1536]{1,0:T(8,128)(2,1)S(1)}, u32[]{:S(2)}, u32[]{:S(2)}) collective-permute-start(bf16[64,1536]{1,0:T(8,128)(2,1)S(1)} %add_convert_fusion.3), channel_id=1, source_target_pairs={{0,8},{4,12},{8,0},{12,4},{1,9},{5,13},{9,1},{13,5},{2,10},{6,14},... | collective-permute-start | bytes 589832 | tf_op jit(solution)/shard_map/ppermute | solution.py:180
  65.4 9.8 %collective-permute-done.22.refs_2_ = bf16[64,1536]{1,0:T(8,128)(2,1)S(1)} collective-permute-done((bf16[64,1536]{1,0:T(8,128)(2,1)S(1)}, bf16[64,1536]{1,0:T(8,128)(2,1)S(1)}, u32[]{:S(2)}, u32[]{:S(2)}) %collective-permute-start.22) | collective-permute-done | bytes 196640 | tf_op jit(solution)/shard_map/ppermute | solution.py:180
  76.3 1.3 collective-permute-start.14
  77.8 2.2 %collective-permute-start.25 = (bf16[64,1536]{1,0:T(8,128)(2,1)S(1)}, bf16[64,1536]{1,0:T(8,128)(2,1)S(1)}, u32[]{:S(2)}, u32[]{:S(2)}) collective-permute-start(bf16[64,1536]{1,0:T(8,128)(2,1)S(1)} %get-tuple-element.71.refs_0_), channel_id=1, source_target_pairs={{0,8},{4,12},{8,0},{12,4},{1,9},{5,13},{9,1},{13,5},{2,10},{6,14},... | collective-permute-start | bytes 589832 | tf_op jit(solution)/shard_map/ppermute | solution.py:180
  81.3 10.1 %collective-permute-done.14 = bf16[64,1536]{1,0:T(8,128)(2,1)S(1)} collective-permute-done((bf16[64,1536]{1,0:T(8,128)(2,1)S(1)}, bf16[64,1536]{1,0:T(8,128)(2,1)S(1)}, u32[]{:S(2)}, u32[]{:S(2)}) %collective-permute-start.14) | collective-permute-done | bytes 196640 | tf_op jit(solution)/shard_map/ppermute | solution.py:180
  92.1 1.6 %collective-permute-start.15 = (bf16[64,1536]{1,0:T(8,128)(2,1)}, bf16[64,1536]{1,0:T(8,128)(2,1)S(1)}, u32[]{:S(2)}, u32[]{:S(2)}) collective-permute-start(bf16[64,1536]{1,0:T(8,128)(2,1)} %add_convert_fusion.4), channel_id=1, source_target_pairs={{0,8},{4,12},{8,0},{12,4},{1,9},{5,13},{9,1},{13,5},{2,10},{6,14},... | collective-permute-start | bytes 589832 | tf_op jit(solution)/shard_map/ppermute | solution.py:180
  95.6 2.5 %collective-permute-start.24 = (bf16[64,1536]{1,0:T(8,128)(2,1)S(1)}, bf16[64,1536]{1,0:T(8,128)(2,1)S(1)}, u32[]{:S(2)}, u32[]{:S(2)}) collective-permute-start(bf16[64,1536]{1,0:T(8,128)(2,1)S(1)} %get-tuple-element.71.refs_0_), channel_id=1, source_target_pairs={{0,4},{4,0},{8,12},{12,8},{1,5},{5,1},{9,13},{13,9},{2,6},{6,2},{1... | collective-permute-start | bytes 589832 | tf_op jit(solution)/shard_map/ppermute | solution.py:180
  98.3 1.2 maximum_select_fusion
  99.4 4.6 %collective-permute-done.15.refs_2_ = bf16[64,1536]{1,0:T(8,128)(2,1)S(1)} collective-permute-done((bf16[64,1536]{1,0:T(8,128)(2,1)}, bf16[64,1536]{1,0:T(8,128)(2,1)S(1)}, u32[]{:S(2)}, u32[]{:S(2)}) %collective-permute-start.15) | collective-permute-done | bytes 196640 | tf_op jit(solution)/shard_map/ppermute | solution.py:180
  104.4 1.2 collective-permute-done.29.far_sums
  105.8 1.4 collective-permute-done.24.refs_1_
  107.2 2.9 %collective-permute-done.26.refs_3_ = bf16[64,1536]{1,0:T(8,128)(2,1)S(1)} collective-permute-done((bf16[64,1536]{1,0:T(8,128)(2,1)S(1)}, bf16[64,1536]{1,0:T(8,128)(2,1)S(1)}, u32[]{:S(2)}, u32[]{:S(2)}) %collective-permute-start.26) | collective-permute-done | bytes 196640 | tf_op jit(solution)/shard_map/ppermute | solution.py:180
  110.9 7.0 %collective-permute-done.31.refs_2_ = bf16[64,1536]{1,0:T(8,128)(2,1)S(1)} collective-permute-done((bf16[64,1536]{1,0:T(8,128)(2,1)S(1)}, bf16[64,1536]{1,0:T(8,128)(2,1)S(1)}, u32[]{:S(2)}, u32[]{:S(2)}) %collective-permute-start.31) | collective-permute-done | bytes 196640 | tf_op jit(solution)/shard_map/ppermute | solution.py:180
  117.9 4.1 %collective-permute-done.30.refs_1_ = bf16[64,1536]{1,0:T(8,128)(2,1)S(1)} collective-permute-done((bf16[64,1536]{1,0:T(8,128)(2,1)S(1)}, bf16[64,1536]{1,0:T(8,128)(2,1)S(1)}, u32[]{:S(2)}, u32[]{:S(2)}) %collective-permute-start.30) | collective-permute-done | bytes 196640 | tf_op jit(solution)/shard_map/ppermute | solution.py:180
  122.0 4.2 %collective-permute-done.32.refs_3_ = bf16[64,1536]{1,0:T(8,128)(2,1)S(1)} collective-permute-done((bf16[64,1536]{1,0:T(8,128)(2,1)S(1)}, bf16[64,1536]{1,0:T(8,128)(2,1)S(1)}, u32[]{:S(2)}, u32[]{:S(2)}) %collective-permute-start.32) | collective-permute-done | bytes 196640 | tf_op jit(solution)/shard_map/ppermute | solution.py:180
  129.3 4.1 %collective-permute-done.28 = bf16[128,512]{1,0:T(8,128)(2,1)S(1)} collective-permute-done((bf16[128,512]{1,0:T(8,128)(2,1)S(1)}, bf16[128,512]{1,0:T(8,128)(2,1)S(1)}, u32[]{:S(2)}, u32[]{:S(2)}) %collective-permute-start.28) | collective-permute-done | bytes 131104 | tf_op jit(solution)/shard_map/ppermute | solution.py:177
  133.5 2.3 %collective-permute-done.34 = bf16[128,512]{1,0:T(8,128)(2,1)S(1)} collective-permute-done((bf16[128,512]{1,0:T(8,128)(2,1)S(1)}, bf16[128,512]{1,0:T(8,128)(2,1)S(1)}, u32[]{:S(2)}, u32[]{:S(2)}) %collective-permute-start.34) | collective-permute-done | bytes 131104 | tf_op jit(solution)/shard_map/ppermute | solution.py:177
  135.9 1.0 pad_maximum_fusion
  (131 shorter events, 24.6 us)
Async XLA Ops:
  4.8 9.5 %collective-permute-start.6 = (bf16[2,128,512]{2,1,0:T(8,128)(2,1)S(1)}, bf16[2,128,512]{2,1,0:T(8,128)(2,1)S(1)}, u32[]{:S(2)}, u32[]{:S(2)}) collective-permute-start(bf16[2,128,512]{2,1,0:T(8,128)(2,1)S(1)} %get-tuple-element.89), channel_id=1, source_target_pairs={{0,2},{1,3},{2,0},{3,1},{4,6},{5,7},{6,4},{7,5},{8,10},{9,11},{10,... | collective-permute-start | bytes 786440 | tf_op jit(solution)/shard_map/ppermute | solution.py:177
  8.6 18.6 %collective-permute-start.2 = (bf16[32,256]{1,0:T(8,128)(2,1)S(1)}, bf16[32,256]{1,0:T(8,128)(2,1)S(1)}, u32[]{:S(2)}, u32[]{:S(2)}) collective-permute-start(bf16[32,256]{1,0:T(8,128)(2,1)S(1)} %select_n.181), channel_id=1, source_target_pairs={{0,3},{1,2},{2,1},{3,0},{4,7},{5,6},{6,5},{7,4},{8,11},{9,10},{10,... | collective-permute-start | bytes 49160 | tf_op jit(solution)/shard_map/ppermute | solution.py:177
  8.9 9.8 %collective-permute-start.1 = (bf16[32,256]{1,0:T(8,128)(2,1)S(1)}, bf16[32,256]{1,0:T(8,128)(2,1)S(1)}, u32[]{:S(2)}, u32[]{:S(2)}) collective-permute-start(bf16[32,256]{1,0:T(8,128)(2,1)S(1)} %select_n.178), channel_id=1, source_target_pairs={{0,1},{1,0},{2,3},{3,2},{4,5},{5,4},{6,7},{7,6},{8,9},{9,8},{10,11... | collective-permute-start | bytes 49160 | tf_op jit(solution)/shard_map/ppermute | solution.py:177
  9.6 5.5 %collective-permute-start.7 = (bf16[2,128,512]{2,1,0:T(8,128)(2,1)S(1)}, bf16[2,128,512]{2,1,0:T(8,128)(2,1)S(1)}, u32[]{:S(2)}, u32[]{:S(2)}) collective-permute-start(bf16[2,128,512]{2,1,0:T(8,128)(2,1)S(1)} %get-tuple-element.50.refs_4_), channel_id=1, source_target_pairs={{0,1},{1,0},{2,3},{3,2},{4,5},{5,4},{6,7},{7,6},{8,9},{9,8},{10,11... | collective-permute-start | bytes 786440 | tf_op jit(solution)/shard_map/ppermute | solution.py:177
  16.6 10.1 %collective-permute-start.9 = (bf16[2,128,512]{2,1,0:T(8,128)(2,1)S(1)}, bf16[2,128,512]{2,1,0:T(8,128)(2,1)S(1)}, u32[]{:S(2)}, u32[]{:S(2)}) collective-permute-start(bf16[2,128,512]{2,1,0:T(8,128)(2,1)S(1)} %get-tuple-element.87), channel_id=1, source_target_pairs={{0,2},{1,3},{2,0},{3,1},{4,6},{5,7},{6,4},{7,5},{8,10},{9,11},{10,... | collective-permute-start | bytes 786440 | tf_op jit(solution)/shard_map/ppermute | solution.py:177
  18.3 8.3 %collective-permute-start = (bf16[32,1280]{1,0:T(8,128)(2,1)S(1)}, bf16[32,1280]{1,0:T(8,128)(2,1)S(1)}, u32[]{:S(2)}, u32[]{:S(2)}) collective-permute-start(bf16[32,1280]{1,0:T(8,128)(2,1)S(1)} %get-tuple-element.104), channel_id=1, source_target_pairs={{0,2},{1,3},{2,0},{3,1},{4,6},{5,7},{6,4},{7,5},{8,10},{9,11},{10,... | collective-permute-start | bytes 245768 | tf_op jit(solution)/shard_map/ppermute | solution.py:177
  26.7 2.2 %collective-permute-start.11 = (bf16[2,128,512]{2,1,0:T(8,128)(2,1)S(1)}, bf16[2,128,512]{2,1,0:T(8,128)(2,1)S(1)}, u32[]{:S(2)}, u32[]{:S(2)}) collective-permute-start(bf16[2,128,512]{2,1,0:T(8,128)(2,1)S(1)} %collective-permute-done.9.refs_5_), channel_id=1, source_target_pairs={{0,1},{1,0},{2,3},{3,2},{4,5},{5,4},{6,7},{7,6},{8,9},{9,8},{10,11... | collective-permute-start | bytes 786440 | tf_op jit(solution)/shard_map/ppermute | solution.py:177
  29.7 14.3 %collective-permute-start.16 = (bf16[3,128,512]{2,1,0:T(8,128)(2,1)S(1)}, bf16[3,128,512]{2,1,0:T(8,128)(2,1)S(1)}, u32[]{:S(2)}, u32[]{:S(2)}) collective-permute-start(bf16[3,128,512]{2,1,0:T(8,128)(2,1)S(1)} %get-tuple-element.83), channel_id=1, source_target_pairs={{0,2},{1,3},{2,0},{3,1},{4,6},{5,7},{6,4},{7,5},{8,10},{9,11},{10,... | collective-permute-start | bytes 1179656 | tf_op jit(solution)/shard_map/ppermute | solution.py:177
  31.5 11.9 %collective-permute-start.4 = (bf16[64,1536]{1,0:T(8,128)(2,1)S(1)}, bf16[64,1536]{1,0:T(8,128)(2,1)S(1)}, u32[]{:S(2)}, u32[]{:S(2)}) collective-permute-start(bf16[64,1536]{1,0:T(8,128)(2,1)S(1)} %pad_maximum_fusion.3.refs_0_.old), channel_id=1, source_target_pairs={{0,8},{4,12},{8,0},{12,4},{1,9},{5,13},{9,1},{13,5},{2,10},{6,14},... | collective-permute-start | bytes 589832 | tf_op jit(solution)/shard_map/ppermute | solution.py:180
  34.2 10.4 %collective-permute-start.3 = (bf16[64,1536]{1,0:T(8,128)(2,1)S(1)}, bf16[64,1536]{1,0:T(8,128)(2,1)S(1)}, u32[]{:S(2)}, u32[]{:S(2)}) collective-permute-start(bf16[64,1536]{1,0:T(8,128)(2,1)S(1)} %pad_maximum_fusion.3.refs_0_.old), channel_id=1, source_target_pairs={{0,4},{4,0},{8,12},{12,8},{1,5},{5,1},{9,13},{13,9},{2,6},{6,2},{1... | collective-permute-start | bytes 589832 | tf_op jit(solution)/shard_map/ppermute | solution.py:180
  43.5 5.7 %collective-permute-start.5 = (bf16[64,1536]{1,0:T(8,128)(2,1)S(1)}, bf16[64,1536]{1,0:T(8,128)(2,1)S(1)}, u32[]{:S(2)}, u32[]{:S(2)}) collective-permute-start(bf16[64,1536]{1,0:T(8,128)(2,1)S(1)} %collective-permute-done.4.refs_2_), channel_id=1, source_target_pairs={{0,4},{4,0},{8,12},{12,8},{1,5},{5,1},{9,13},{13,9},{2,6},{6,2},{1... | collective-permute-start | bytes 589832 | tf_op jit(solution)/shard_map/ppermute | solution.py:180
  44.0 17.2 %collective-permute-start.17 = (bf16[3,128,512]{2,1,0:T(8,128)(2,1)S(1)}, bf16[3,128,512]{2,1,0:T(8,128)(2,1)S(1)}, u32[]{:S(2)}, u32[]{:S(2)}) collective-permute-start(bf16[3,128,512]{2,1,0:T(8,128)(2,1)S(1)} %get-tuple-element.84.refs_4_), channel_id=1, source_target_pairs={{0,1},{1,0},{2,3},{3,2},{4,5},{5,4},{6,7},{7,6},{8,9},{9,8},{10,11... | collective-permute-start | bytes 1179656 | tf_op jit(solution)/shard_map/ppermute | solution.py:177
  44.0 17.2 %collective-permute-start.18 = (bf16[3,128,512]{2,1,0:T(8,128)(2,1)S(1)}, bf16[3,128,512]{2,1,0:T(8,128)(2,1)S(1)}, u32[]{:S(2)}, u32[]{:S(2)}) collective-permute-start(bf16[3,128,512]{2,1,0:T(8,128)(2,1)S(1)} %collective-permute-done.16.refs_5_), channel_id=1, source_target_pairs={{0,1},{1,0},{2,3},{3,2},{4,5},{5,4},{6,7},{7,6},{8,9},{9,8},{10,11... | collective-permute-start | bytes 1179656 | tf_op jit(solution)/shard_map/ppermute | solution.py:177
  53.3 7.9 %collective-permute-start.12 = (bf16[64,1536]{1,0:T(8,128)(2,1)S(1)}, bf16[64,1536]{1,0:T(8,128)(2,1)S(1)}, u32[]{:S(2)}, u32[]{:S(2)}) collective-permute-start(bf16[64,1536]{1,0:T(8,128)(2,1)S(1)} %get-tuple-element.55), channel_id=1, source_target_pairs={{0,4},{4,0},{8,12},{12,8},{1,5},{5,1},{9,13},{13,9},{2,6},{6,2},{1... | collective-permute-start | bytes 589832 | tf_op jit(solution)/shard_map/ppermute | solution.py:180
  55.1 10.3 %collective-permute-start.21 = (bf16[64,1536]{1,0:T(8,128)(2,1)S(1)}, bf16[64,1536]{1,0:T(8,128)(2,1)S(1)}, u32[]{:S(2)}, u32[]{:S(2)}) collective-permute-start(bf16[64,1536]{1,0:T(8,128)(2,1)S(1)} %get-tuple-element.66), channel_id=1, source_target_pairs={{0,4},{4,0},{8,12},{12,8},{1,5},{5,1},{9,13},{13,9},{2,6},{6,2},{1... | collective-permute-start | bytes 589832 | tf_op jit(solution)/shard_map/ppermute | solution.py:180
  61.9 18.1 %collective-permute-start.19 = (bf16[256,512]{1,0:T(8,128)(2,1)S(1)}, bf16[256,512]{1,0:T(8,128)(2,1)S(1)}, u32[]{:S(2)}, u32[]{:S(2)}) collective-permute-start(bf16[256,512]{1,0:T(8,128)(2,1)S(1)} %get-tuple-element.63), channel_id=1, source_target_pairs={{0,1},{1,0},{2,3},{3,2},{4,5},{5,4},{6,7},{7,6},{8,9},{9,8},{10,11... | collective-permute-start | bytes 786440 | tf_op jit(solution)/shard_map/ppermute | solution.py:177
  62.0 13.2 %collective-permute-start.22 = (bf16[64,1536]{1,0:T(8,128)(2,1)S(1)}, bf16[64,1536]{1,0:T(8,128)(2,1)S(1)}, u32[]{:S(2)}, u32[]{:S(2)}) collective-permute-start(bf16[64,1536]{1,0:T(8,128)(2,1)S(1)} %add_convert_fusion.3), channel_id=1, source_target_pairs={{0,8},{4,12},{8,0},{12,4},{1,9},{5,13},{9,1},{13,5},{2,10},{6,14},... | collective-permute-start | bytes 589832 | tf_op jit(solution)/shard_map/ppermute | solution.py:180
  75.4 2.2 %collective-permute-start.23 = (f32[64,128]{1,0:T(8,128)S(1)}, f32[64,128]{1,0:T(8,128)S(1)}, u32[]{:S(2)}, u32[]{:S(2)}) collective-permute-start(f32[64,128]{1,0:T(8,128)S(1)} %get-tuple-element.70.own_sums), channel_id=1, source_target_pairs={{0,1},{1,0},{2,3},{3,2},{4,5},{5,4},{6,7},{7,6},{8,9},{9,8},{10,11... | collective-permute-start | bytes 98312 | tf_op jit(solution)/shard_map/ppermute | solution.py:177
  75.5 24.0 %collective-permute-start.13 = (bf16[64,1536]{1,0:T(8,128)(2,1)}, bf16[64,1536]{1,0:T(8,128)(2,1)S(1)}, u32[]{:S(2)}, u32[]{:S(2)}) collective-permute-start(bf16[64,1536]{1,0:T(8,128)(2,1)} %get-tuple-element.58), channel_id=1, source_target_pairs={{0,4},{4,0},{8,12},{12,8},{1,5},{5,1},{9,13},{13,9},{2,6},{6,2},{1... | collective-permute-start | bytes 589832 | tf_op jit(solution)/shard_map/ppermute | solution.py:180
  76.3 15.1 %collective-permute-start.14 = (bf16[64,1536]{1,0:T(8,128)(2,1)S(1)}, bf16[64,1536]{1,0:T(8,128)(2,1)S(1)}, u32[]{:S(2)}, u32[]{:S(2)}) collective-permute-start(bf16[64,1536]{1,0:T(8,128)(2,1)S(1)} %get-tuple-element.60), channel_id=1, source_target_pairs={{0,4},{4,0},{8,12},{12,8},{1,5},{5,1},{9,13},{13,9},{2,6},{6,2},{1... | collective-permute-start | bytes 589832 | tf_op jit(solution)/shard_map/ppermute | solution.py:180
  77.8 20.4 %collective-permute-start.25 = (bf16[64,1536]{1,0:T(8,128)(2,1)S(1)}, bf16[64,1536]{1,0:T(8,128)(2,1)S(1)}, u32[]{:S(2)}, u32[]{:S(2)}) collective-permute-start(bf16[64,1536]{1,0:T(8,128)(2,1)S(1)} %get-tuple-element.71.refs_0_), channel_id=1, source_target_pairs={{0,8},{4,12},{8,0},{12,4},{1,9},{5,13},{9,1},{13,5},{2,10},{6,14},... | collective-permute-start | bytes 589832 | tf_op jit(solution)/shard_map/ppermute | solution.py:180
  80.8 17.5 %collective-permute-start.20 = (bf16[128,512]{1,0:T(8,128)(2,1)}, bf16[128,512]{1,0:T(8,128)(2,1)}, u32[]{:S(2)}, u32[]{:S(2)}) collective-permute-start(bf16[128,512]{1,0:T(8,128)(2,1)} %get-tuple-element.100), channel_id=1, source_target_pairs={{0,2},{1,3},{2,0},{3,1},{4,6},{5,7},{6,4},{7,5},{8,10},{9,11},{10,... | collective-permute-start | bytes 393224 | tf_op jit(solution)/shard_map/ppermute | solution.py:177
  92.1 11.9 %collective-permute-start.15 = (bf16[64,1536]{1,0:T(8,128)(2,1)}, bf16[64,1536]{1,0:T(8,128)(2,1)S(1)}, u32[]{:S(2)}, u32[]{:S(2)}) collective-permute-start(bf16[64,1536]{1,0:T(8,128)(2,1)} %add_convert_fusion.4), channel_id=1, source_target_pairs={{0,8},{4,12},{8,0},{12,4},{1,9},{5,13},{9,1},{13,5},{2,10},{6,14},... | collective-permute-start | bytes 589832 | tf_op jit(solution)/shard_map/ppermute | solution.py:180
  95.6 11.6 %collective-permute-start.24 = (bf16[64,1536]{1,0:T(8,128)(2,1)S(1)}, bf16[64,1536]{1,0:T(8,128)(2,1)S(1)}, u32[]{:S(2)}, u32[]{:S(2)}) collective-permute-start(bf16[64,1536]{1,0:T(8,128)(2,1)S(1)} %get-tuple-element.71.refs_0_), channel_id=1, source_target_pairs={{0,4},{4,0},{8,12},{12,8},{1,5},{5,1},{9,13},{13,9},{2,6},{6,2},{1... | collective-permute-start | bytes 589832 | tf_op jit(solution)/shard_map/ppermute | solution.py:180
  98.2 11.9 %collective-permute-start.26 = (bf16[64,1536]{1,0:T(8,128)(2,1)S(1)}, bf16[64,1536]{1,0:T(8,128)(2,1)S(1)}, u32[]{:S(2)}, u32[]{:S(2)}) collective-permute-start(bf16[64,1536]{1,0:T(8,128)(2,1)S(1)} %collective-permute-done.25.refs_2_), channel_id=1, source_target_pairs={{0,4},{4,0},{8,12},{12,8},{1,5},{5,1},{9,13},{13,9},{2,6},{6,2},{1... | collective-permute-start | bytes 589832 | tf_op jit(solution)/shard_map/ppermute | solution.py:180
  105.7 12.1 %collective-permute-start.31 = (bf16[64,1536]{1,0:T(8,128)(2,1)S(1)}, bf16[64,1536]{1,0:T(8,128)(2,1)S(1)}, u32[]{:S(2)}, u32[]{:S(2)}) collective-permute-start(bf16[64,1536]{1,0:T(8,128)(2,1)S(1)} %shard_map.89.refs_0_), channel_id=1, source_target_pairs={{0,8},{4,12},{8,0},{12,4},{1,9},{5,13},{9,1},{13,5},{2,10},{6,14},... | collective-permute-start | bytes 589832 | tf_op jit(solution)/shard_map/ppermute | solution.py:180
  110.8 16.2 %collective-permute-start.27 = (bf16[256,512]{1,0:T(8,128)(2,1)S(1)}, bf16[256,512]{1,0:T(8,128)(2,1)S(1)}, u32[]{:S(2)}, u32[]{:S(2)}) collective-permute-start(bf16[256,512]{1,0:T(8,128)(2,1)S(1)} %get-tuple-element.73), channel_id=1, source_target_pairs={{0,1},{1,0},{2,3},{3,2},{4,5},{5,4},{6,7},{7,6},{8,9},{9,8},{10,11... | collective-permute-start | bytes 786440 | tf_op jit(solution)/shard_map/ppermute | solution.py:177
  110.8 11.2 %collective-permute-start.30 = (bf16[64,1536]{1,0:T(8,128)(2,1)S(1)}, bf16[64,1536]{1,0:T(8,128)(2,1)S(1)}, u32[]{:S(2)}, u32[]{:S(2)}) collective-permute-start(bf16[64,1536]{1,0:T(8,128)(2,1)S(1)} %shard_map.89.refs_0_), channel_id=1, source_target_pairs={{0,4},{4,0},{8,12},{12,8},{1,5},{5,1},{9,13},{13,9},{2,6},{6,2},{1... | collective-permute-start | bytes 589832 | tf_op jit(solution)/shard_map/ppermute | solution.py:180
  117.9 8.3 %collective-permute-start.32 = (bf16[64,1536]{1,0:T(8,128)(2,1)S(1)}, bf16[64,1536]{1,0:T(8,128)(2,1)S(1)}, u32[]{:S(2)}, u32[]{:S(2)}) collective-permute-start(bf16[64,1536]{1,0:T(8,128)(2,1)S(1)} %collective-permute-done.31.refs_2_), channel_id=1, source_target_pairs={{0,4},{4,0},{8,12},{12,8},{1,5},{5,1},{9,13},{13,9},{2,6},{6,2},{1... | collective-permute-start | bytes 589832 | tf_op jit(solution)/shard_map/ppermute | solution.py:180
  126.8 1.6 %collective-permute-start.33 = (bf16[256,512]{1,0:T(8,128)(2,1)S(1)}, bf16[256,512]{1,0:T(8,128)(2,1)S(1)}, u32[]{:S(2)}, u32[]{:S(2)}) collective-permute-start(bf16[256,512]{1,0:T(8,128)(2,1)S(1)} %get-tuple-element.82), channel_id=1, source_target_pairs={{0,1},{1,0},{2,3},{3,2},{4,5},{5,4},{6,7},{7,6},{8,9},{9,8},{10,11... | collective-permute-start | bytes 786440 | tf_op jit(solution)/shard_map/ppermute | solution.py:177
  127.1 6.4 %collective-permute-start.28 = (bf16[128,512]{1,0:T(8,128)(2,1)S(1)}, bf16[128,512]{1,0:T(8,128)(2,1)S(1)}, u32[]{:S(2)}, u32[]{:S(2)}) collective-permute-start(bf16[128,512]{1,0:T(8,128)(2,1)S(1)} %get-tuple-element.96), channel_id=1, source_target_pairs={{0,2},{1,3},{2,0},{3,1},{4,6},{5,7},{6,4},{7,5},{8,10},{9,11},{10,... | collective-permute-start | bytes 393224 | tf_op jit(solution)/shard_map/ppermute | solution.py:177
  128.6 7.3 %collective-permute-start.34 = (bf16[128,512]{1,0:T(8,128)(2,1)S(1)}, bf16[128,512]{1,0:T(8,128)(2,1)S(1)}, u32[]{:S(2)}, u32[]{:S(2)}) collective-permute-start(bf16[128,512]{1,0:T(8,128)(2,1)S(1)} %get-tuple-element.98), channel_id=1, source_target_pairs={{0,2},{1,3},{2,0},{3,1},{4,6},{5,7},{6,4},{7,5},{8,10},{9,11},{10,... | collective-permute-start | bytes 393224 | tf_op jit(solution)/shard_map/ppermute | solution.py:177
  (22 other events, 48.1 us)

commit v7 on v6

--- a/solution.py
+++ b/solution.py
@@ -11,19 +11,31 @@
 WIDE = jnp.float32
 
 
-def call(kernel, outs, flops, *operands, scratch=()):
+def call(kernel, outs, flops, *operands, scratch=(), behind=()):
+    inner, used = kernel, len(operands)
+
+    def kernel(*refs):
+        inner(*refs[:used], *refs[used + len(behind) :])
+
     shapes = [jax.ShapeDtypeStruct(s, d) for s, d in outs]
     return pl.pallas_call(
         kernel,
         out_shape=shapes,
         in_specs=[
             pl.BlockSpec(memory_space=pltpu.SMEM if a.ndim == 1 else pltpu.VMEM) for a in operands
-        ],
+        ]
+        + [pl.BlockSpec(memory_space=pl.ANY)] * len(behind),
         out_specs=[pl.BlockSpec(memory_space=pltpu.VMEM)] * len(shapes),
         scratch_shapes=[pltpu.VMEM(s, d) for s, d in scratch],
-        compiler_params=pltpu.CompilerParams(vmem_limit_bytes=40 * 2**20),
+        compiler_params=pltpu.CompilerParams(vmem_limit_bytes=20 * 2**20),
         cost_estimate=pl.CostEstimate(flops=flops, bytes_accessed=1024, transcendentals=0),
-    )(*operands)
+    )(*operands, *behind)
+
+
+def after(value, others, sink):
+    value, others = lax.optimization_barrier((value, list(others)))
+    sink.extend(others)
+    return value
 
 
 def dot(a, b, dims):
@@ -180,19 +192,27 @@
         return lax.ppermute(array, "plane", [(z, z ^ bit) for z in range(planes)])
 
     def spread(own):
-        pieces = {0: own}
-        bit = planes // 2
+        return {0: own, planes // 2: to_plane(own, planes // 2)}
+
+    def spread_on(pieces, gate=None, sink=None):
+        bit = planes // 4
         while bit:
             for distance in list(pieces):
-                pieces[distance | bit] = to_plane(pieces[distance], bit)
+                piece = pieces[distance]
+                if distance and gate is not None:
+                    piece = after(piece, gate, sink)
+                pieces[distance | bit] = to_plane(piece, bit)
             bit //= 2
         return [pieces[d] for d in range(planes)]
 
-    def halve(parts, bit):
-        for distance in range(planes - bit, 0, -2 * bit):
-            total = parts[distance][0]
-            if len(parts[distance]) > 1:
-                total = sum(p.astype(WIDE) for p in parts[distance]).astype(LOW)
+    def totals(parts, bit):
+        return {
+            d: sum(p.astype(WIDE) for p in parts[d]).astype(LOW)
+            for d in range(planes - bit, 0, -2 * bit)
+        }
+
+    def halve(parts, bit, sent):
+        for distance, total in sent.items():
             parts[distance ^ bit].append(to_plane(total, bit))
 
     def pick(flag, a, b):
@@ -201,10 +221,11 @@
     def ordered(flag, a, b, axis):
         return jnp.where(flag == 0, jnp.concatenate([a, b], axis), jnp.concatenate([b, a], axis))
 
-    def to_quad(array):
+    def to_quad(array, gate=None, sink=None):
         mine, other = pick(y, array[..., :width], array[..., width:])
         far = send(other, 2)
-        return mine, far, send(mine, 1), send(far, 1)
+        passed = far if gate is None else after(far, gate, sink)
+        return mine, far, send(mine, 1), send(passed, 1)
 
     columns = fast_second.reshape(2, own_rows, 2 * planes, 2, own_rows)
     split = [columns[:, :, :, i].reshape(2, own_rows, half) for i in range(2)]
@@ -218,60 +239,94 @@
     second_mine = ordered(c, same_mine[:, 2 * width :], near_mine, 0)
     second_far = ordered(c, same_far[:, 2 * width :], near_far, 0)
     zero = jnp.concatenate([layers, ordered(y, second_mine, second_far, 1)], axis=1)
-    full_zero = spread(zero)
+    full_zero = spread_on(spread(zero))
 
     scaled = learn_rates[:2, :, :, None] * value_tokens[:2].reshape(2, tokens, 2, width).astype(WIDE)
     scaled = scaled.astype(LOW).reshape(2, tokens, 2 * width)
     pairs = [jnp.stack([key_tokens[b], scaled[b]]) for b in range(2)]
-    pairs[0] = to_quad(pairs[0])
-    second_pair, pairs[0] = lax.optimization_barrier((pairs[1], pairs[0]))
-    pairs[1] = to_quad(second_pair)
-    query_tokens, pairs[1] = lax.optimization_barrier((query_tokens, pairs[1]))
-    queries = to_quad(query_tokens)
-
     flat = (rows, 3 * width)
     unit = 2 * 4 * tokens * width * half
     where = lax.axis_index("plane").astype(jnp.int32).reshape(1)
     held = [((half, width), LOW), ((half, width), LOW), ((width, half), LOW)]
 
+    behind = {name: [] for name in ("steps0", "steps1", "out0", "new0", "new1", "out1", "out2")}
+
     def steps(block):
         kernel = functools.partial(steps_kernel, planes)
         outs = [(flat, WIDE if d % 2 == 0 else LOW) for d in range(planes)]
         made = [(s, WIDE) for s, _ in held]
-        made = call(kernel, outs, 6 * unit, where, *full_zero, *pairs[block], scratch=held + made)
+        made = call(
+            kernel,
+            outs,
+            6 * unit,
+            where,
+            *full_zero,
+            *pairs[block],
+            scratch=held + made,
+            behind=behind["steps%d" % block],
+        )
         return [[part] for part in made]
 
     def readout(block, full):
         kernel = functools.partial(readout_kernel, planes, block)
         outs = [((2 * tokens, width), WIDE), ((2 * tokens, width), LOW)]
-        kept, sent = call(kernel, outs, 3 * unit, where, *full, *queries, scratch=held)
-        total = (kept + send(sent, 1).astype(WIDE)).astype(LOW)
+        kept, sent = call(
+            kernel,
+            outs,
+            3 * unit,
+            where,
+            *full,
+            *queries,
+            scratch=held,
+            behind=behind["out%d" % block],
+        )
+        return (kept + send(sent, 1).astype(WIDE)).astype(LOW)
+
+    def returned(total):
         return ordered(y, total[:tokens], send(total[tokens:], 2), 1)
 
-    parts = [steps(0), steps(1)]
+    pairs[0] = to_quad(
+        after(pairs[0], [full_zero[planes // 2]], behind["steps0"]),
+        [full_zero[1], full_zero[planes - 1]],
+        behind["steps0"],
+    )
+    zeros = steps(0)
+    halve(zeros, 1, totals(zeros, 1))
+    came = [zeros[d][-1] for d in range(2, planes, 2)]
+    pairs[1] = to_quad(
+        after(pairs[1], pairs[0], behind["steps1"]), came or zeros[0], behind["steps1"]
+    )
+    bit = 2
+    while bit < planes:
+        sent = totals(zeros, bit)
+        behind["steps1"].extend(sent.values())
+        halve(zeros, bit, sent)
+        bit *= 2
+    ones = steps(1)
     bit = 1
     while bit < planes:
-        halve(parts[0], bit)
-        later = slice(2 * bit, None, 2 * bit)
-        if parts[0][later]:
-            parts[0][later], parts[1][bit :: 2 * bit] = lax.optimization_barrier(
-                (parts[0][later], parts[1][bit :: 2 * bit])
-            )
-        halve(parts[1], bit)
+        sent = totals(ones, bit)
+        halve(ones, bit, sent)
         bit *= 2
-    got_zero, got_one = parts[0][0], parts[1][0]
-    out_zero = readout(0, full_zero)
+    got_zero, got_one = zeros[0], ones[0]
+    behind["new0"].extend(sent.values())
 
     sums_shape = (rows, 128)
     step_zero, moved, sums = call(
-        first_moved_kernel, [(flat, WIDE), (flat, WIDE), (sums_shape, WIDE)], 0, zero, *got_zero
+        first_moved_kernel,
+        [(flat, WIDE), (flat, WIDE), (sums_shape, WIDE)],
+        0,
+        zero,
+        *got_zero,
+        behind=behind["new0"],
     )
     weights_one, payload = call(
         scaled_kernel, [(flat, WIDE), (flat, LOW)], 0, moved, zero, sums, send(sums, 1)
     )
     full_one = spread(payload)
-
-    got_one, out_zero = lax.optimization_barrier((got_one, out_zero))
+    queries = to_quad(after(query_tokens, pairs[1], behind["out0"]), [payload], behind["out0"])
+    out_zero = returned(readout(0, full_zero))
+
     decay = jnp.broadcast_to(jnp.where(y == 0, momentum_decay[0], momentum_decay[1]), (8, 128))
     moved, sums = call(
         second_moved_kernel,
@@ -281,11 +336,17 @@
         step_zero,
         decay,
         *got_one,
-    )
-    payload = call(last_scaled_kernel, [(flat, LOW)], 0, moved, weights_one, sums, send(sums, 1))[0]
-    full_two = spread(payload)
-    out_one = readout(1, full_one)
-    out_two = readout(2, full_two)
+        behind=behind["new1"],
+    )
+    far_sums = send(sums, 1)
+    payload = call(last_scaled_kernel, [(flat, LOW)], 0, moved, weights_one, sums, far_sums)[0]
+    full_two = spread_on(spread(payload))
+    full_one = spread_on(full_one, [payload], behind["out2"])
+    behind["out1"].extend([out_zero, full_two[planes // 2]])
+    total_one = readout(1, full_one)
+    behind["out2"].append(total_one)
+    out_one = returned(total_one)
+    out_two = returned(readout(2, full_two))
     return jnp.stack([out_zero, out_one, out_two])
 
 

time: 137 us -> 123 us (0.90)
  waiting for transfers between devices: 82.7 us -> 70.3 us
  local copies, waits for them, and re-layouts: 10.9 us -> 6.77 us
  starting transfers between devices: 30.2 us -> 32.2 us
    ppermute x20, waiting for transfers between devices: 22.5 us -> 10.4 us  [send(): return lax.ppermute(array, 'quad', [(q, q ^ offset) for q in range(4)])]
    unnamed x38 -> x22, local copies, waits for them, and re-layouts: 6.2 us -> 2.22 us
  transfers between devices with their start and end apart: 35 -> 35, of which waited for: 19 -> 19; matrix products, arithmetic and copies ran while one was open for 4% -> 5% of each run, Pallas kernels for 4% -> 4%
where the time goes in v7:
time: 123 us; the launch traced here: 122 us
  waiting for transfers between devices  70.3 us (57%)
  starting transfers between devices  32.2 us (26%)
  Pallas kernels  6.94 us (6%)
  local copies, waits for them, and re-layouts  6.77 us (6%)
  other arithmetic  4.5 us (4%)
  between operations  1.76 us (1%)
    ppermute x15, waiting for transfers between devices, to_plane(): return lax.ppermute(array, 'plane', [(z, z ^ bit) for z in range(planes)])  59.9 us
    ppermute x15, starting transfers between devices, to_plane(): return lax.ppermute(array, 'plane', [(z, z ^ bit) for z in range(planes)])  19.6 us
    ppermute x20, starting transfers between devices, send(): return lax.ppermute(array, 'quad', [(q, q ^ offset) for q in range(4)])  12.6 us
    ppermute x20, waiting for transfers between devices, send(): return lax.ppermute(array, 'quad', [(q, q ^ offset) for q in range(4)])  10.4 us
    pallas_call x9, Pallas kernels, call(): pl.pallas_call(kernel, out_shape=shapes, in_specs=[pl.BlockSpec(memory_sp...  6.94 us
  transfers between devices with their start and end apart: 35, of which 19 were waited for; matrix products, arithmetic and copies ran while one was open for 5% of the time, Pallas kernels for 4%

profile of v7, /device:TPU:0, one launch (start us, length us, event | category | flops | bytes accessed | tf_op | source)
XLA Modules:
  0.0 122.4 jit_solution(5770708329066052896)
XLA Ops:
  2.3 3.0 %collective-permute-start = (bf16[32,1280]{1,0:T(8,128)(2,1)S(1)}, bf16[32,1280]{1,0:T(8,128)(2,1)S(1)}, u32[]{:S(2)}, u32[]{:S(2)}) collective-permute-start(bf16[32,1280]{1,0:T(8,128)(2,1)S(1)} %get-tuple-element.111), channel_id=1, source_target_pairs={{0,2},{1,3},{2,0},{3,1},{4,6},{5,7},{6,4},{7,5},{8,10},{9,11},{10,... | collective-permute-start | bytes 245768 | tf_op jit(solution)/shard_map/ppermute | solution.py:189
  8.9 2.7 %collective-permute-start.4 = (bf16[64,1536]{1,0:T(8,128)(2,1)S(1)}, bf16[64,1536]{1,0:T(8,128)(2,1)S(1)}, u32[]{:S(2)}, u32[]{:S(2)}) collective-permute-start(bf16[64,1536]{1,0:T(8,128)(2,1)S(1)} %pad_maximum_fusion.3.refs_1_.refs_0_), channel_id=1, source_target_pairs={{0,8},{4,12},{8,0},{12,4},{1,9},{5,13},{9,1},{13,5},{2,10},{6,14},... | collective-permute-start | bytes 589832 | tf_op jit(solution)/shard_map/ppermute | solution.py:192
  12.1 9.3 %collective-permute-done.4.refs_3_.refs_9_ = bf16[64,1536]{1,0:T(8,128)(2,1)S(1)} collective-permute-done((bf16[64,1536]{1,0:T(8,128)(2,1)S(1)}, bf16[64,1536]{1,0:T(8,128)(2,1)S(1)}, u32[]{:S(2)}, u32[]{:S(2)}) %collective-permute-start.4) | collective-permute-done | bytes 196640 | tf_op jit(solution)/shard_map/ppermute | solution.py:192
  21.5 1.6 %collective-permute-start.6 = (bf16[2,128,512]{2,1,0:T(8,128)(2,1)S(1)}, bf16[2,128,512]{2,1,0:T(8,128)(2,1)S(1)}, u32[]{:S(2)}, u32[]{:S(2)}) collective-permute-start(bf16[2,128,512]{2,1,0:T(8,128)(2,1)S(1)} %get-tuple-element.97), channel_id=1, source_target_pairs={{0,2},{1,3},{2,0},{3,1},{4,6},{5,7},{6,4},{7,5},{8,10},{9,11},{10,... | collective-permute-start | bytes 786440 | tf_op jit(solution)/shard_map/ppermute | solution.py:189
  23.8 1.3 %collective-permute-start.5 = (bf16[64,1536]{1,0:T(8,128)(2,1)S(1)}, bf16[64,1536]{1,0:T(8,128)(2,1)S(1)}, u32[]{:S(2)}, u32[]{:S(2)}) collective-permute-start(bf16[64,1536]{1,0:T(8,128)(2,1)S(1)} %collective-permute-done.4.refs_3_.refs_9_), channel_id=1, source_target_pairs={{0,4},{4,0},{8,12},{12,8},{1,5},{5,1},{9,13},{13,9},{2,6},{6,2},{1... | collective-permute-start | bytes 589832 | tf_op jit(solution)/shard_map/ppermute | solution.py:192
  25.1 5.8 %collective-permute-done.3.refs_2_.refs_10_ = bf16[64,1536]{1,0:T(8,128)(2,1)S(1)} collective-permute-done((bf16[64,1536]{1,0:T(8,128)(2,1)S(1)}, bf16[64,1536]{1,0:T(8,128)(2,1)S(1)}, u32[]{:S(2)}, u32[]{:S(2)}) %collective-permute-start.3) | collective-permute-done | bytes 196640 | tf_op jit(solution)/shard_map/ppermute | solution.py:192
  30.9 2.8 %collective-permute-done.5.refs_4_.refs_11_ = bf16[64,1536]{1,0:T(8,128)(2,1)S(1)} collective-permute-done((bf16[64,1536]{1,0:T(8,128)(2,1)S(1)}, bf16[64,1536]{1,0:T(8,128)(2,1)S(1)}, u32[]{:S(2)}, u32[]{:S(2)}) %collective-permute-start.5) | collective-permute-done | bytes 196640 | tf_op jit(solution)/shard_map/ppermute | solution.py:192
  33.9 1.3 %collective-permute-done.8.refs_8_.refs_12_ = bf16[2,128,512]{2,1,0:T(8,128)(2,1)S(1)} collective-permute-done((bf16[2,128,512]{2,1,0:T(8,128)(2,1)S(1)}, bf16[2,128,512]{2,1,0:T(8,128)(2,1)S(1)}, u32[]{:S(2)}, u32[]{:S(2)}) %collective-permute-start.8) | collective-permute-done | bytes 262176 | tf_op jit(solution)/shard_map/ppermute | solution.py:189
  35.7 1.3 %shard_map.82 = (f32[64,1536]{1,0:T(8,128)S(1)}, bf16[64,1536]{1,0:T(8,128)(2,1)S(1)}, f32[64,1536]{1,0:T(8,128)S(1)}, bf16[64,1536]{1,0:T(8,128)(2,1)S(1)}) custom-call(s32[1]{0:T(128)} %bitcast.refs_0_, bf16[64,1536]{1,0:T(8,128)(2,1)S(1)} %pad_maximum_fusion.3.refs_1_.refs_0_, bf16[64,1536]{1,0:T(8,128)(2,1)S(1)} %collective-permute-done.3.refs_2_.refs_10_, ...), custom_call_target="tpu_custom_call" | custom-call | flops 805306368 | bytes 1024 | tf_op jit(solution)/shard_map/pallas_call | solution.py:21
  39.1 5.8 %collective-permute-done.11.refs_13_ = bf16[64,1536]{1,0:T(8,128)(2,1)S(1)} collective-permute-done((bf16[64,1536]{1,0:T(8,128)(2,1)S(1)}, bf16[64,1536]{1,0:T(8,128)(2,1)S(1)}, u32[]{:S(2)}, u32[]{:S(2)}) %collective-permute-start.11) | collective-permute-done | bytes 196640 | tf_op jit(solution)/shard_map/ppermute | solution.py:192
  44.9 2.7 %collective-permute-start.16 = (bf16[64,1536]{1,0:T(8,128)(2,1)S(1)}, bf16[64,1536]{1,0:T(8,128)(2,1)S(1)}, u32[]{:S(2)}, u32[]{:S(2)}) collective-permute-start(bf16[64,1536]{1,0:T(8,128)(2,1)S(1)} %add_convert_fusion.4.refs_14_), channel_id=1, source_target_pairs={{0,8},{4,12},{8,0},{12,4},{1,9},{5,13},{9,1},{13,5},{2,10},{6,14},... | collective-permute-start | bytes 589832 | tf_op jit(solution)/shard_map/ppermute | solution.py:192
  47.7 2.0 %shard_map.83 = (f32[64,1536]{1,0:T(8,128)S(1)}, bf16[64,1536]{1,0:T(8,128)(2,1)}, f32[64,1536]{1,0:T(8,128)S(1)}, bf16[64,1536]{1,0:T(8,128)(2,1)S(1)}) custom-call(s32[1]{0:T(128)} %bitcast.refs_0_, bf16[64,1536]{1,0:T(8,128)(2,1)S(1)} %pad_maximum_fusion.3.refs_1_.refs_0_, bf16[64,1536]{1,0:T(8,128)(2,1)S(1)} %collective-permute-done.3.refs_2_.refs_10_, ...), custom_call_target="tpu_custom_call" | custom-call | flops 805306368 | bytes 1024 | tf_op jit(solution)/shard_map/pallas_call | solution.py:21
  49.7 1.7 %collective-permute-start.17 = (bf16[64,1536]{1,0:T(8,128)(2,1)S(1)}, bf16[64,1536]{1,0:T(8,128)(2,1)S(1)}, u32[]{:S(2)}, u32[]{:S(2)}) collective-permute-start(bf16[64,1536]{1,0:T(8,128)(2,1)S(1)} %get-tuple-element.65), channel_id=1, source_target_pairs={{0,4},{4,0},{8,12},{12,8},{1,5},{5,1},{9,13},{13,9},{2,6},{6,2},{1... | collective-permute-start | bytes 589832 | tf_op jit(solution)/shard_map/ppermute | solution.py:192
  51.5 1.6 %collective-permute-start.13 = (bf16[3,128,512]{2,1,0:T(8,128)(2,1)S(1)}, bf16[3,128,512]{2,1,0:T(8,128)(2,1)S(1)}, u32[]{:S(2)}, u32[]{:S(2)}) collective-permute-start(bf16[3,128,512]{2,1,0:T(8,128)(2,1)S(1)} %get-tuple-element.89), channel_id=1, source_target_pairs={{0,2},{1,3},{2,0},{3,1},{4,6},{5,7},{6,4},{7,5},{8,10},{9,11},{10,... | collective-permute-start | bytes 1179656 | tf_op jit(solution)/shard_map/ppermute | solution.py:189
  53.0 6.6 %collective-permute-done.17 = bf16[64,1536]{1,0:T(8,128)(2,1)S(1)} collective-permute-done((bf16[64,1536]{1,0:T(8,128)(2,1)S(1)}, bf16[64,1536]{1,0:T(8,128)(2,1)S(1)}, u32[]{:S(2)}, u32[]{:S(2)}) %collective-permute-start.17) | collective-permute-done | bytes 196640 | tf_op jit(solution)/shard_map/ppermute | solution.py:192
  61.4 1.1 collective-permute-done.13.refs_6_
  62.5 1.7 %collective-permute-done.19.refs_8_ = bf16[3,128,512]{2,1,0:T(8,128)(2,1)S(1)} collective-permute-done((bf16[3,128,512]{2,1,0:T(8,128)(2,1)S(1)}, bf16[3,128,512]{2,1,0:T(8,128)(2,1)S(1)}, u32[]{:S(2)}, u32[]{:S(2)}) %collective-permute-start.19) | collective-permute-done | bytes 393248 | tf_op jit(solution)/shard_map/ppermute | solution.py:189
  65.4 2.9 %collective-permute-start.25 = (bf16[64,1536]{1,0:T(8,128)(2,1)S(1)}, bf16[64,1536]{1,0:T(8,128)(2,1)}, u32[]{:S(2)}, u32[]{:S(2)}) collective-permute-start(bf16[64,1536]{1,0:T(8,128)(2,1)S(1)} %add_convert_fusion.3.refs_4_), channel_id=1, source_target_pairs={{0,8},{4,12},{8,0},{12,4},{1,9},{5,13},{9,1},{13,5},{2,10},{6,14},... | collective-permute-start | bytes 589832 | tf_op jit(solution)/shard_map/ppermute | solution.py:192
  69.2 1.5 %collective-permute-start.21 = (bf16[128,512]{1,0:T(8,128)(2,1)}, bf16[128,512]{1,0:T(8,128)(2,1)}, u32[]{:S(2)}, u32[]{:S(2)}) collective-permute-start(bf16[128,512]{1,0:T(8,128)(2,1)} %get-tuple-element.102), channel_id=1, source_target_pairs={{0,2},{1,3},{2,0},{3,1},{4,6},{5,7},{6,4},{7,5},{8,10},{9,11},{10,... | collective-permute-start | bytes 393224 | tf_op jit(solution)/shard_map/ppermute | solution.py:189
  72.6 4.1 %collective-permute-done.24.refs_4_ = bf16[64,1536]{1,0:T(8,128)(2,1)S(1)} collective-permute-done((bf16[64,1536]{1,0:T(8,128)(2,1)}, bf16[64,1536]{1,0:T(8,128)(2,1)S(1)}, u32[]{:S(2)}, u32[]{:S(2)}) %collective-permute-start.24) | collective-permute-done | bytes 196640 | tf_op jit(solution)/shard_map/ppermute | solution.py:192
  76.7 5.9 %collective-permute-done.25.refs_5_ = bf16[64,1536]{1,0:T(8,128)(2,1)} collective-permute-done((bf16[64,1536]{1,0:T(8,128)(2,1)S(1)}, bf16[64,1536]{1,0:T(8,128)(2,1)}, u32[]{:S(2)}, u32[]{:S(2)}) %collective-permute-start.25) | collective-permute-done | bytes 196640 | tf_op jit(solution)/shard_map/ppermute | solution.py:192
  82.6 1.1 shard_map.87
  86.2 2.9 %collective-permute-start.28 = (bf16[64,1536]{1,0:T(8,128)(2,1)S(1)}, bf16[64,1536]{1,0:T(8,128)(2,1)S(1)}, u32[]{:S(2)}, u32[]{:S(2)}) collective-permute-start(bf16[64,1536]{1,0:T(8,128)(2,1)S(1)} %shard_map.88.refs_1_.refs_9_), channel_id=1, source_target_pairs={{0,8},{4,12},{8,0},{12,4},{1,9},{5,13},{9,1},{13,5},{2,10},{6,14},... | collective-permute-start | bytes 589832 | tf_op jit(solution)/shard_map/ppermute | solution.py:192
  90.1 5.7 %collective-permute-done.22.refs_2_ = bf16[64,1536]{1,0:T(8,128)(2,1)S(1)} collective-permute-done((bf16[64,1536]{1,0:T(8,128)(2,1)S(1)}, bf16[64,1536]{1,0:T(8,128)(2,1)S(1)}, u32[]{:S(2)}, u32[]{:S(2)}) %collective-permute-start.22) | collective-permute-done | bytes 196640 | tf_op jit(solution)/shard_map/ppermute | solution.py:192
  95.8 3.8 %collective-permute-done.27.refs_4_ = bf16[64,1536]{1,0:T(8,128)(2,1)S(1)} collective-permute-done((bf16[64,1536]{1,0:T(8,128)(2,1)S(1)}, bf16[64,1536]{1,0:T(8,128)(2,1)S(1)}, u32[]{:S(2)}, u32[]{:S(2)}) %collective-permute-start.27) | collective-permute-done | bytes 196640 | tf_op jit(solution)/shard_map/ppermute | solution.py:192
  100.3 1.4 %collective-permute-start.31 = (bf16[64,1536]{1,0:T(8,128)(2,1)S(1)}, bf16[64,1536]{1,0:T(8,128)(2,1)S(1)}, u32[]{:S(2)}, u32[]{:S(2)}) collective-permute-start(bf16[64,1536]{1,0:T(8,128)(2,1)S(1)} %shard_map.88.refs_1_.refs_9_), channel_id=1, source_target_pairs={{0,4},{4,0},{8,12},{12,8},{1,5},{5,1},{9,13},{13,9},{2,6},{6,2},{1... | collective-permute-start | bytes 589832 | tf_op jit(solution)/shard_map/ppermute | solution.py:192
  102.5 5.6 %collective-permute-done.31.refs_2_ = bf16[64,1536]{1,0:T(8,128)(2,1)S(1)} collective-permute-done((bf16[64,1536]{1,0:T(8,128)(2,1)S(1)}, bf16[64,1536]{1,0:T(8,128)(2,1)S(1)}, u32[]{:S(2)}, u32[]{:S(2)}) %collective-permute-start.31) | collective-permute-done | bytes 196640 | tf_op jit(solution)/shard_map/ppermute | solution.py:192
  108.1 3.8 %collective-permute-done.32.refs_4_ = bf16[64,1536]{1,0:T(8,128)(2,1)S(1)} collective-permute-done((bf16[64,1536]{1,0:T(8,128)(2,1)S(1)}, bf16[64,1536]{1,0:T(8,128)(2,1)S(1)}, u32[]{:S(2)}, u32[]{:S(2)}) %collective-permute-start.32) | collective-permute-done | bytes 196640 | tf_op jit(solution)/shard_map/ppermute | solution.py:192
  112.6 1.6 %collective-permute-start.30 = (bf16[128,512]{1,0:T(8,128)(2,1)S(1)}, bf16[128,512]{1,0:T(8,128)(2,1)S(1)}, u32[]{:S(2)}, u32[]{:S(2)}) collective-permute-start(bf16[128,512]{1,0:T(8,128)(2,1)S(1)} %get-tuple-element.105), channel_id=1, source_target_pairs={{0,2},{1,3},{2,0},{3,1},{4,6},{5,7},{6,4},{7,5},{8,10},{9,11},{10,... | collective-permute-start | bytes 393224 | tf_op jit(solution)/shard_map/ppermute | solution.py:189
  114.3 1.5 %collective-permute-start.34 = (bf16[128,512]{1,0:T(8,128)(2,1)S(1)}, bf16[128,512]{1,0:T(8,128)(2,1)S(1)}, u32[]{:S(2)}, u32[]{:S(2)}) collective-permute-start(bf16[128,512]{1,0:T(8,128)(2,1)S(1)} %get-tuple-element.107), channel_id=1, source_target_pairs={{0,2},{1,3},{2,0},{3,1},{4,6},{5,7},{6,4},{7,5},{8,10},{9,11},{10,... | collective-permute-start | bytes 393224 | tf_op jit(solution)/shard_map/ppermute | solution.py:189
  116.8 2.1 %collective-permute-done.30 = bf16[128,512]{1,0:T(8,128)(2,1)S(1)} collective-permute-done((bf16[128,512]{1,0:T(8,128)(2,1)S(1)}, bf16[128,512]{1,0:T(8,128)(2,1)S(1)}, u32[]{:S(2)}, u32[]{:S(2)}) %collective-permute-start.30) | collective-permute-done | bytes 131104 | tf_op jit(solution)/shard_map/ppermute | solution.py:189
  119.0 2.3 %collective-permute-done.34 = bf16[128,512]{1,0:T(8,128)(2,1)S(1)} collective-permute-done((bf16[128,512]{1,0:T(8,128)(2,1)S(1)}, bf16[128,512]{1,0:T(8,128)(2,1)S(1)}, u32[]{:S(2)}, u32[]{:S(2)}) %collective-permute-start.34) | collective-permute-done | bytes 131104 | tf_op jit(solution)/shard_map/ppermute | solution.py:189
  (117 shorter events, 22.2 us)
Async XLA Ops:
  2.3 6.4 %collective-permute-start = (bf16[32,1280]{1,0:T(8,128)(2,1)S(1)}, bf16[32,1280]{1,0:T(8,128)(2,1)S(1)}, u32[]{:S(2)}, u32[]{:S(2)}) collective-permute-start(bf16[32,1280]{1,0:T(8,128)(2,1)S(1)} %get-tuple-element.111), channel_id=1, source_target_pairs={{0,2},{1,3},{2,0},{3,1},{4,6},{5,7},{6,4},{7,5},{8,10},{9,11},{10,... | collective-permute-start | bytes 245768 | tf_op jit(solution)/shard_map/ppermute | solution.py:189
  5.5 3.3 %collective-permute-start.2 = (bf16[32,256]{1,0:T(8,128)(2,1)S(1)}, bf16[32,256]{1,0:T(8,128)(2,1)S(1)}, u32[]{:S(2)}, u32[]{:S(2)}) collective-permute-start(bf16[32,256]{1,0:T(8,128)(2,1)S(1)} %select_n.184), channel_id=1, source_target_pairs={{0,3},{1,2},{2,1},{3,0},{4,7},{5,6},{6,5},{7,4},{8,11},{9,10},{10,... | collective-permute-start | bytes 49160 | tf_op jit(solution)/shard_map/ppermute | solution.py:189
  5.7 3.0 %collective-permute-start.1 = (bf16[32,256]{1,0:T(8,128)(2,1)S(1)}, bf16[32,256]{1,0:T(8,128)(2,1)S(1)}, u32[]{:S(2)}, u32[]{:S(2)}) collective-permute-start(bf16[32,256]{1,0:T(8,128)(2,1)S(1)} %select_n.181), channel_id=1, source_target_pairs={{0,1},{1,0},{2,3},{3,2},{4,5},{5,4},{6,7},{7,6},{8,9},{9,8},{10,11... | collective-permute-start | bytes 49160 | tf_op jit(solution)/shard_map/ppermute | solution.py:189
  8.9 12.5 %collective-permute-start.4 = (bf16[64,1536]{1,0:T(8,128)(2,1)S(1)}, bf16[64,1536]{1,0:T(8,128)(2,1)S(1)}, u32[]{:S(2)}, u32[]{:S(2)}) collective-permute-start(bf16[64,1536]{1,0:T(8,128)(2,1)S(1)} %pad_maximum_fusion.3.refs_1_.refs_0_), channel_id=1, source_target_pairs={{0,8},{4,12},{8,0},{12,4},{1,9},{5,13},{9,1},{13,5},{2,10},{6,14},... | collective-permute-start | bytes 589832 | tf_op jit(solution)/shard_map/ppermute | solution.py:192
  21.5 12.2 %collective-permute-start.6 = (bf16[2,128,512]{2,1,0:T(8,128)(2,1)S(1)}, bf16[2,128,512]{2,1,0:T(8,128)(2,1)S(1)}, u32[]{:S(2)}, u32[]{:S(2)}) collective-permute-start(bf16[2,128,512]{2,1,0:T(8,128)(2,1)S(1)} %get-tuple-element.97), channel_id=1, source_target_pairs={{0,2},{1,3},{2,0},{3,1},{4,6},{5,7},{6,4},{7,5},{8,10},{9,11},{10,... | collective-permute-start | bytes 786440 | tf_op jit(solution)/shard_map/ppermute | solution.py:189
  23.1 7.8 %collective-permute-start.3 = (bf16[64,1536]{1,0:T(8,128)(2,1)S(1)}, bf16[64,1536]{1,0:T(8,128)(2,1)S(1)}, u32[]{:S(2)}, u32[]{:S(2)}) collective-permute-start(bf16[64,1536]{1,0:T(8,128)(2,1)S(1)} %pad_maximum_fusion.3.refs_1_.refs_0_), channel_id=1, source_target_pairs={{0,4},{4,0},{8,12},{12,8},{1,5},{5,1},{9,13},{13,9},{2,6},{6,2},{1... | collective-permute-start | bytes 589832 | tf_op jit(solution)/shard_map/ppermute | solution.py:192
  23.8 9.9 %collective-permute-start.5 = (bf16[64,1536]{1,0:T(8,128)(2,1)S(1)}, bf16[64,1536]{1,0:T(8,128)(2,1)S(1)}, u32[]{:S(2)}, u32[]{:S(2)}) collective-permute-start(bf16[64,1536]{1,0:T(8,128)(2,1)S(1)} %collective-permute-done.4.refs_3_.refs_9_), channel_id=1, source_target_pairs={{0,4},{4,0},{8,12},{12,8},{1,5},{5,1},{9,13},{13,9},{2,6},{6,2},{1... | collective-permute-start | bytes 589832 | tf_op jit(solution)/shard_map/ppermute | solution.py:192
  25.1 8.8 %collective-permute-start.7 = (bf16[2,128,512]{2,1,0:T(8,128)(2,1)S(1)}, bf16[2,128,512]{2,1,0:T(8,128)(2,1)S(1)}, u32[]{:S(2)}, u32[]{:S(2)}) collective-permute-start(bf16[2,128,512]{2,1,0:T(8,128)(2,1)S(1)} %get-tuple-element.59.refs_5_.refs_9_), channel_id=1, source_target_pairs={{0,1},{1,0},{2,3},{3,2},{4,5},{5,4},{6,7},{7,6},{8,9},{9,8},{10,11... | collective-permute-start | bytes 786440 | tf_op jit(solution)/shard_map/ppermute | solution.py:189
  35.3 9.6 %collective-permute-start.9 = (bf16[2,128,512]{2,1,0:T(8,128)(2,1)S(1)}, bf16[2,128,512]{2,1,0:T(8,128)(2,1)S(1)}, u32[]{:S(2)}, u32[]{:S(2)}) collective-permute-start(bf16[2,128,512]{2,1,0:T(8,128)(2,1)S(1)} %get-tuple-element.93), channel_id=1, source_target_pairs={{0,2},{1,3},{2,0},{3,1},{4,6},{5,7},{6,4},{7,5},{8,10},{9,11},{10,... | collective-permute-start | bytes 786440 | tf_op jit(solution)/shard_map/ppermute | solution.py:189
  37.0 7.8 %collective-permute-start.11 = (bf16[64,1536]{1,0:T(8,128)(2,1)S(1)}, bf16[64,1536]{1,0:T(8,128)(2,1)S(1)}, u32[]{:S(2)}, u32[]{:S(2)}) collective-permute-start(bf16[64,1536]{1,0:T(8,128)(2,1)S(1)} %get-tuple-element.53), channel_id=1, source_target_pairs={{0,4},{4,0},{8,12},{12,8},{1,5},{5,1},{9,13},{13,9},{2,6},{6,2},{1... | collective-permute-start | bytes 589832 | tf_op jit(solution)/shard_map/ppermute | solution.py:192
  38.1 9.5 %collective-permute-start.10 = (bf16[2,128,512]{2,1,0:T(8,128)(2,1)S(1)}, bf16[2,128,512]{2,1,0:T(8,128)(2,1)S(1)}, u32[]{:S(2)}, u32[]{:S(2)}) collective-permute-start(bf16[2,128,512]{2,1,0:T(8,128)(2,1)S(1)} %get-tuple-element.70.refs_5_.refs_9_), channel_id=1, source_target_pairs={{0,1},{1,0},{2,3},{3,2},{4,5},{5,4},{6,7},{7,6},{8,9},{9,8},{10,11... | collective-permute-start | bytes 786440 | tf_op jit(solution)/shard_map/ppermute | solution.py:189
  38.1 21.5 %collective-permute-start.15 = (bf16[64,1536]{1,0:T(8,128)(2,1)S(1)}, bf16[64,1536]{1,0:T(8,128)(2,1)S(1)}, u32[]{:S(2)}, u32[]{:S(2)}) collective-permute-start(bf16[64,1536]{1,0:T(8,128)(2,1)S(1)} %get-tuple-element.57), channel_id=1, source_target_pairs={{0,4},{4,0},{8,12},{12,8},{1,5},{5,1},{9,13},{13,9},{2,6},{6,2},{1... | collective-permute-start | bytes 589832 | tf_op jit(solution)/shard_map/ppermute | solution.py:192
  44.9 2.8 %collective-permute-start.12 = (bf16[2,128,512]{2,1,0:T(8,128)(2,1)S(1)}, bf16[2,128,512]{2,1,0:T(8,128)(2,1)S(1)}, u32[]{:S(2)}, u32[]{:S(2)}) collective-permute-start(bf16[2,128,512]{2,1,0:T(8,128)(2,1)S(1)} %collective-permute-done.9.refs_6_.refs_10_), channel_id=1, source_target_pairs={{0,1},{1,0},{2,3},{3,2},{4,5},{5,4},{6,7},{7,6},{8,9},{9,8},{10,11... | collective-permute-start | bytes 786440 | tf_op jit(solution)/shard_map/ppermute | solution.py:189
  44.9 14.7 %collective-permute-start.16 = (bf16[64,1536]{1,0:T(8,128)(2,1)S(1)}, bf16[64,1536]{1,0:T(8,128)(2,1)S(1)}, u32[]{:S(2)}, u32[]{:S(2)}) collective-permute-start(bf16[64,1536]{1,0:T(8,128)(2,1)S(1)} %add_convert_fusion.4.refs_14_), channel_id=1, source_target_pairs={{0,8},{4,12},{8,0},{12,4},{1,9},{5,13},{9,1},{13,5},{2,10},{6,14},... | collective-permute-start | bytes 589832 | tf_op jit(solution)/shard_map/ppermute | solution.py:192
  49.7 10.0 %collective-permute-start.17 = (bf16[64,1536]{1,0:T(8,128)(2,1)S(1)}, bf16[64,1536]{1,0:T(8,128)(2,1)S(1)}, u32[]{:S(2)}, u32[]{:S(2)}) collective-permute-start(bf16[64,1536]{1,0:T(8,128)(2,1)S(1)} %get-tuple-element.65), channel_id=1, source_target_pairs={{0,4},{4,0},{8,12},{12,8},{1,5},{5,1},{9,13},{13,9},{2,6},{6,2},{1... | collective-permute-start | bytes 589832 | tf_op jit(solution)/shard_map/ppermute | solution.py:192
  51.5 11.0 %collective-permute-start.13 = (bf16[3,128,512]{2,1,0:T(8,128)(2,1)S(1)}, bf16[3,128,512]{2,1,0:T(8,128)(2,1)S(1)}, u32[]{:S(2)}, u32[]{:S(2)}) collective-permute-start(bf16[3,128,512]{2,1,0:T(8,128)(2,1)S(1)} %get-tuple-element.89), channel_id=1, source_target_pairs={{0,2},{1,3},{2,0},{3,1},{4,6},{5,7},{6,4},{7,5},{8,10},{9,11},{10,... | collective-permute-start | bytes 1179656 | tf_op jit(solution)/shard_map/ppermute | solution.py:189
  60.0 2.5 %collective-permute-start.14 = (bf16[3,128,512]{2,1,0:T(8,128)(2,1)S(1)}, bf16[3,128,512]{2,1,0:T(8,128)(2,1)S(1)}, u32[]{:S(2)}, u32[]{:S(2)}) collective-permute-start(bf16[3,128,512]{2,1,0:T(8,128)(2,1)S(1)} %get-tuple-element.90.refs_5_), channel_id=1, source_target_pairs={{0,1},{1,0},{2,3},{3,2},{4,5},{5,4},{6,7},{7,6},{8,9},{9,8},{10,11... | collective-permute-start | bytes 1179656 | tf_op jit(solution)/shard_map/ppermute | solution.py:189
  62.5 1.7 %collective-permute-start.19 = (bf16[3,128,512]{2,1,0:T(8,128)(2,1)S(1)}, bf16[3,128,512]{2,1,0:T(8,128)(2,1)S(1)}, u32[]{:S(2)}, u32[]{:S(2)}) collective-permute-start(bf16[3,128,512]{2,1,0:T(8,128)(2,1)S(1)} %collective-permute-done.13.refs_6_), channel_id=1, source_target_pairs={{0,1},{1,0},{2,3},{3,2},{4,5},{5,4},{6,7},{7,6},{8,9},{9,8},{10,11... | collective-permute-start | bytes 1179656 | tf_op jit(solution)/shard_map/ppermute | solution.py:189
  64.9 3.5 %collective-permute-start.20 = (bf16[256,512]{1,0:T(8,128)(2,1)S(1)}, bf16[256,512]{1,0:T(8,128)(2,1)S(1)}, u32[]{:S(2)}, u32[]{:S(2)}) collective-permute-start(bf16[256,512]{1,0:T(8,128)(2,1)S(1)} %get-tuple-element.76), channel_id=1, source_target_pairs={{0,1},{1,0},{2,3},{3,2},{4,5},{5,4},{6,7},{7,6},{8,9},{9,8},{10,11... | collective-permute-start | bytes 786440 | tf_op jit(solution)/shard_map/ppermute | solution.py:189
  65.1 11.6 %collective-permute-start.24 = (bf16[64,1536]{1,0:T(8,128)(2,1)}, bf16[64,1536]{1,0:T(8,128)(2,1)S(1)}, u32[]{:S(2)}, u32[]{:S(2)}) collective-permute-start(bf16[64,1536]{1,0:T(8,128)(2,1)} %get-tuple-element.80), channel_id=1, source_target_pairs={{0,4},{4,0},{8,12},{12,8},{1,5},{5,1},{9,13},{13,9},{2,6},{6,2},{1... | collective-permute-start | bytes 589832 | tf_op jit(solution)/shard_map/ppermute | solution.py:192
  65.4 17.2 %collective-permute-start.25 = (bf16[64,1536]{1,0:T(8,128)(2,1)S(1)}, bf16[64,1536]{1,0:T(8,128)(2,1)}, u32[]{:S(2)}, u32[]{:S(2)}) collective-permute-start(bf16[64,1536]{1,0:T(8,128)(2,1)S(1)} %add_convert_fusion.3.refs_4_), channel_id=1, source_target_pairs={{0,8},{4,12},{8,0},{12,4},{1,9},{5,13},{9,1},{13,5},{2,10},{6,14},... | collective-permute-start | bytes 589832 | tf_op jit(solution)/shard_map/ppermute | solution.py:192
  68.3 17.8 %collective-permute-start.23 = (bf16[64,1536]{1,0:T(8,128)(2,1)S(1)}, bf16[64,1536]{1,0:T(8,128)(2,1)S(1)}, u32[]{:S(2)}, u32[]{:S(2)}) collective-permute-start(bf16[64,1536]{1,0:T(8,128)(2,1)S(1)} %get-tuple-element.74.refs_13_.refs_1_), channel_id=1, source_target_pairs={{0,8},{4,12},{8,0},{12,4},{1,9},{5,13},{9,1},{13,5},{2,10},{6,14},... | collective-permute-start | bytes 589832 | tf_op jit(solution)/shard_map/ppermute | solution.py:192
  69.2 19.9 %collective-permute-start.21 = (bf16[128,512]{1,0:T(8,128)(2,1)}, bf16[128,512]{1,0:T(8,128)(2,1)}, u32[]{:S(2)}, u32[]{:S(2)}) collective-permute-start(bf16[128,512]{1,0:T(8,128)(2,1)} %get-tuple-element.102), channel_id=1, source_target_pairs={{0,2},{1,3},{2,0},{3,1},{4,6},{5,7},{6,4},{7,5},{8,10},{9,11},{10,... | collective-permute-start | bytes 393224 | tf_op jit(solution)/shard_map/ppermute | solution.py:189
  83.8 12.0 %collective-permute-start.22 = (bf16[64,1536]{1,0:T(8,128)(2,1)S(1)}, bf16[64,1536]{1,0:T(8,128)(2,1)S(1)}, u32[]{:S(2)}, u32[]{:S(2)}) collective-permute-start(bf16[64,1536]{1,0:T(8,128)(2,1)S(1)} %get-tuple-element.74.refs_13_.refs_1_), channel_id=1, source_target_pairs={{0,4},{4,0},{8,12},{12,8},{1,5},{5,1},{9,13},{13,9},{2,6},{6,2},{1... | collective-permute-start | bytes 589832 | tf_op jit(solution)/shard_map/ppermute | solution.py:192
  86.1 13.4 %collective-permute-start.27 = (bf16[64,1536]{1,0:T(8,128)(2,1)S(1)}, bf16[64,1536]{1,0:T(8,128)(2,1)S(1)}, u32[]{:S(2)}, u32[]{:S(2)}) collective-permute-start(bf16[64,1536]{1,0:T(8,128)(2,1)S(1)} %collective-permute-done.23.refs_3_), channel_id=1, source_target_pairs={{0,4},{4,0},{8,12},{12,8},{1,5},{5,1},{9,13},{13,9},{2,6},{6,2},{1... | collective-permute-start | bytes 589832 | tf_op jit(solution)/shard_map/ppermute | solution.py:192
  86.2 13.4 %collective-permute-start.28 = (bf16[64,1536]{1,0:T(8,128)(2,1)S(1)}, bf16[64,1536]{1,0:T(8,128)(2,1)S(1)}, u32[]{:S(2)}, u32[]{:S(2)}) collective-permute-start(bf16[64,1536]{1,0:T(8,128)(2,1)S(1)} %shard_map.88.refs_1_.refs_9_), channel_id=1, source_target_pairs={{0,8},{4,12},{8,0},{12,4},{1,9},{5,13},{9,1},{13,5},{2,10},{6,14},... | collective-permute-start | bytes 589832 | tf_op jit(solution)/shard_map/ppermute | solution.py:192
  100.2 2.2 %collective-permute-start.29 = (bf16[256,512]{1,0:T(8,128)(2,1)S(1)}, bf16[256,512]{1,0:T(8,128)(2,1)S(1)}, u32[]{:S(2)}, u32[]{:S(2)}) collective-permute-start(bf16[256,512]{1,0:T(8,128)(2,1)S(1)} %get-tuple-element.85), channel_id=1, source_target_pairs={{0,1},{1,0},{2,3},{3,2},{4,5},{5,4},{6,7},{7,6},{8,9},{9,8},{10,11... | collective-permute-start | bytes 786440 | tf_op jit(solution)/shard_map/ppermute | solution.py:189
  100.3 7.8 %collective-permute-start.31 = (bf16[64,1536]{1,0:T(8,128)(2,1)S(1)}, bf16[64,1536]{1,0:T(8,128)(2,1)S(1)}, u32[]{:S(2)}, u32[]{:S(2)}) collective-permute-start(bf16[64,1536]{1,0:T(8,128)(2,1)S(1)} %shard_map.88.refs_1_.refs_9_), channel_id=1, source_target_pairs={{0,4},{4,0},{8,12},{12,8},{1,5},{5,1},{9,13},{13,9},{2,6},{6,2},{1... | collective-permute-start | bytes 589832 | tf_op jit(solution)/shard_map/ppermute | solution.py:192
  101.7 10.2 %collective-permute-start.32 = (bf16[64,1536]{1,0:T(8,128)(2,1)S(1)}, bf16[64,1536]{1,0:T(8,128)(2,1)S(1)}, u32[]{:S(2)}, u32[]{:S(2)}) collective-permute-start(bf16[64,1536]{1,0:T(8,128)(2,1)S(1)} %collective-permute-done.28.refs_10_.refs_3_), channel_id=1, source_target_pairs={{0,4},{4,0},{8,12},{12,8},{1,5},{5,1},{9,13},{13,9},{2,6},{6,2},{1... | collective-permute-start | bytes 589832 | tf_op jit(solution)/shard_map/ppermute | solution.py:192
  112.5 1.7 %collective-permute-start.33 = (bf16[256,512]{1,0:T(8,128)(2,1)S(1)}, bf16[256,512]{1,0:T(8,128)(2,1)S(1)}, u32[]{:S(2)}, u32[]{:S(2)}) collective-permute-start(bf16[256,512]{1,0:T(8,128)(2,1)S(1)} %get-tuple-element.88), channel_id=1, source_target_pairs={{0,1},{1,0},{2,3},{3,2},{4,5},{5,4},{6,7},{7,6},{8,9},{9,8},{10,11... | collective-permute-start | bytes 786440 | tf_op jit(solution)/shard_map/ppermute | solution.py:189
  112.6 6.4 %collective-permute-start.30 = (bf16[128,512]{1,0:T(8,128)(2,1)S(1)}, bf16[128,512]{1,0:T(8,128)(2,1)S(1)}, u32[]{:S(2)}, u32[]{:S(2)}) collective-permute-start(bf16[128,512]{1,0:T(8,128)(2,1)S(1)} %get-tuple-element.105), channel_id=1, source_target_pairs={{0,2},{1,3},{2,0},{3,1},{4,6},{5,7},{6,4},{7,5},{8,10},{9,11},{10,... | collective-permute-start | bytes 393224 | tf_op jit(solution)/shard_map/ppermute | solution.py:189
  114.3 7.1 %collective-permute-start.34 = (bf16[128,512]{1,0:T(8,128)(2,1)S(1)}, bf16[128,512]{1,0:T(8,128)(2,1)S(1)}, u32[]{:S(2)}, u32[]{:S(2)}) collective-permute-start(bf16[128,512]{1,0:T(8,128)(2,1)S(1)} %get-tuple-element.107), channel_id=1, source_target_pairs={{0,2},{1,3},{2,0},{3,1},{4,6},{5,7},{6,4},{7,5},{8,10},{9,11},{10,... | collective-permute-start | bytes 393224 | tf_op jit(solution)/shard_map/ppermute | solution.py:189
  (14 other events, 45.3 us)

commit v8 on v7

--- a/solution.py
+++ b/solution.py
@@ -194,14 +194,15 @@
     def spread(own):
         return {0: own, planes // 2: to_plane(own, planes // 2)}
 
-    def spread_on(pieces, gate=None, sink=None):
+    def spread_on(pieces, gate, sink):
         bit = planes // 4
         while bit:
+            direct = to_plane(pieces[0], bit)
             for distance in list(pieces):
-                piece = pieces[distance]
-                if distance and gate is not None:
-                    piece = after(piece, gate, sink)
-                pieces[distance | bit] = to_plane(piece, bit)
+                if distance:
+                    piece = after(pieces[distance], [direct] + gate, sink)
+                    pieces[distance | bit] = to_plane(piece, bit)
+            pieces[bit] = direct
             bit //= 2
         return [pieces[d] for d in range(planes)]
 
@@ -211,9 +212,13 @@
             for d in range(planes - bit, 0, -2 * bit)
         }
 
-    def halve(parts, bit, sent):
+    def halve(parts, bit, sent, sink):
+        came = []
         for distance, total in sent.items():
-            parts[distance ^ bit].append(to_plane(total, bit))
+            if distance == bit and came:
+                total = after(total, came[-1:], sink)
+            came.append(to_plane(total, bit))
+            parts[distance ^ bit].append(came[-1])
 
     def pick(flag, a, b):
         return jnp.where(flag == 0, a, b), jnp.where(flag == 0, b, a)
@@ -239,7 +244,9 @@
     second_mine = ordered(c, same_mine[:, 2 * width :], near_mine, 0)
     second_far = ordered(c, same_far[:, 2 * width :], near_far, 0)
     zero = jnp.concatenate([layers, ordered(y, second_mine, second_far, 1)], axis=1)
-    full_zero = spread_on(spread(zero))
+    names = ("steps0", "steps1", "out0", "new0", "new1", "out1", "out2")
+    behind = {name: [] for name in names}
+    full_zero = spread_on(spread(zero), [], behind["steps0"])
 
     scaled = learn_rates[:2, :, :, None] * value_tokens[:2].reshape(2, tokens, 2, width).astype(WIDE)
     scaled = scaled.astype(LOW).reshape(2, tokens, 2 * width)
@@ -248,8 +255,6 @@
     unit = 2 * 4 * tokens * width * half
     where = lax.axis_index("plane").astype(jnp.int32).reshape(1)
     held = [((half, width), LOW), ((half, width), LOW), ((width, half), LOW)]
-
-    behind = {name: [] for name in ("steps0", "steps1", "out0", "new0", "new1", "out1", "out2")}
 
     def steps(block):
         kernel = functools.partial(steps_kernel, planes)
@@ -286,12 +291,12 @@
         return ordered(y, total[:tokens], send(total[tokens:], 2), 1)
 
     pairs[0] = to_quad(
-        after(pairs[0], [full_zero[planes // 2]], behind["steps0"]),
-        [full_zero[1], full_zero[planes - 1]],
+        after(pairs[0], [zero], behind["new0"]),
+        [full_zero[1], full_zero[planes // 2]],
         behind["steps0"],
     )
     zeros = steps(0)
-    halve(zeros, 1, totals(zeros, 1))
+    halve(zeros, 1, totals(zeros, 1), behind["new0"])
     came = [zeros[d][-1] for d in range(2, planes, 2)]
     pairs[1] = to_quad(
         after(pairs[1], pairs[0], behind["steps1"]), came or zeros[0], behind["steps1"]
@@ -300,13 +305,13 @@
     while bit < planes:
         sent = totals(zeros, bit)
         behind["steps1"].extend(sent.values())
-        halve(zeros, bit, sent)
+        halve(zeros, bit, sent, behind["new0"])
         bit *= 2
     ones = steps(1)
     bit = 1
     while bit < planes:
         sent = totals(ones, bit)
-        halve(ones, bit, sent)
+        halve(ones, bit, sent, behind["new1"])
         bit *= 2
     got_zero, got_one = zeros[0], ones[0]
     behind["new0"].extend(sent.values())
@@ -323,9 +328,8 @@
     weights_one, payload = call(
         scaled_kernel, [(flat, WIDE), (flat, LOW)], 0, moved, zero, sums, send(sums, 1)
     )
-    full_one = spread(payload)
-    queries = to_quad(after(query_tokens, pairs[1], behind["out0"]), [payload], behind["out0"])
-    out_zero = returned(readout(0, full_zero))
+    full_one = spread_on(spread(payload), [], behind["out1"])
+    behind["new1"].extend([full_one[1], full_one[planes // 2]])
 
     decay = jnp.broadcast_to(jnp.where(y == 0, momentum_decay[0], momentum_decay[1]), (8, 128))
     moved, sums = call(
@@ -340,9 +344,13 @@
     )
     far_sums = send(sums, 1)
     payload = call(last_scaled_kernel, [(flat, LOW)], 0, moved, weights_one, sums, far_sums)[0]
-    full_two = spread_on(spread(payload))
-    full_one = spread_on(full_one, [payload], behind["out2"])
-    behind["out1"].extend([out_zero, full_two[planes // 2]])
+    full_two = spread_on(spread(payload), [], behind["out2"])
+    queries = to_quad(
+        after(query_tokens, pairs[1], behind["out0"]), [weights_one], behind["out0"]
+    )
+    behind["out0"].extend([full_one[planes - 1], full_two[1], full_two[planes // 2]])
+    out_zero = returned(readout(0, full_zero))
+    behind["out1"].extend([out_zero, full_two[planes - 1]])
     total_one = readout(1, full_one)
     behind["out2"].append(total_one)
     out_one = returned(total_one)

time: 123 us -> 121 us (0.984)
  local copies, waits for them, and re-layouts: 6.77 us -> 10.1 us
  waiting for transfers between devices: 70.3 us -> 67.4 us
  starting transfers between devices: 32.2 us -> 30.1 us
  other arithmetic: 4.5 us -> 3.26 us
    ppermute x15, waiting for transfers between devices: 59.9 us -> 53 us  [to_plane(): return lax.ppermute(array, 'plane', [(z, z ^ bit) for z in range(planes)])]
    unnamed x22 -> x42, local copies, waits for them, and re-layouts: 2.22 us -> 6.66 us
    ppermute x20, waiting for transfers between devices: 10.4 us -> 14.3 us  [send(): return lax.ppermute(array, 'quad', [(q, q ^ offset) for q in range(4)])]
    ppermute x20, starting transfers between devices: 12.6 us -> 10.1 us  [send(): return lax.ppermute(array, 'quad', [(q, q ^ offset) for q in range(4)])]
    select_n x8, other arithmetic: 2.33 us -> 0.4 us  [ordered(): jnp.where(flag == 0, jnp.concatenate([a, b], axis), jnp.concatenate([b, a...]
  transfers between devices with their start and end apart: 35 -> 35, of which waited for: 19 -> 19; matrix products, arithmetic and copies ran while one was open for 5% -> 4% of each run, Pallas kernels for 4% -> 4%
where the time goes in v8:
time: 121 us; the launch traced here: 120 us
  waiting for transfers between devices  67.4 us (56%)
  starting transfers between devices  30.1 us (25%)
  local copies, waits for them, and re-layouts  10.1 us (8%)
  Pallas kernels  7.95 us (7%)
  other arithmetic  3.26 us (3%)
  between operations  1.74 us (1%)
    ppermute x15, waiting for transfers between devices, to_plane(): return lax.ppermute(array, 'plane', [(z, z ^ bit) for z in range(planes)])  53 us
    ppermute x15, starting transfers between devices, to_plane(): return lax.ppermute(array, 'plane', [(z, z ^ bit) for z in range(planes)])  20 us
    ppermute x20, waiting for transfers between devices, send(): return lax.ppermute(array, 'quad', [(q, q ^ offset) for q in range(4)])  14.3 us
    ppermute x20, starting transfers between devices, send(): return lax.ppermute(array, 'quad', [(q, q ^ offset) for q in range(4)])  10.1 us
    pallas_call x9, Pallas kernels, call(): pl.pallas_call(kernel, out_shape=shapes, in_specs=[pl.BlockSpec(memory_sp...  7.95 us
    unnamed x42, local copies, waits for them, and re-layouts  6.66 us
  transfers between devices with their start and end apart: 35, of which 19 were waited for; matrix products, arithmetic and copies ran while one was open for 4% of the time, Pallas kernels for 4%

profile of v8, /device:TPU:0, one launch (start us, length us, event | category | flops | bytes accessed | tf_op | source)
XLA Modules:
  0.0 120.5 jit_solution(12572338257495215327)
XLA Ops:
  2.3 3.0 %collective-permute-start = (bf16[32,1280]{1,0:T(8,128)(2,1)S(1)}, bf16[32,1280]{1,0:T(8,128)(2,1)S(1)}, u32[]{:S(2)}, u32[]{:S(2)}) collective-permute-start(bf16[32,1280]{1,0:T(8,128)(2,1)S(1)} %get-tuple-element.127), channel_id=1, source_target_pairs={{0,2},{1,3},{2,0},{3,1},{4,6},{5,7},{6,4},{7,5},{8,10},{9,11},{10,... | collective-permute-start | bytes 245768 | tf_op jit(solution)/shard_map/ppermute | solution.py:189
  8.8 1.6 %collective-permute-start.6 = (bf16[2,128,512]{2,1,0:T(8,128)(2,1)S(1)}, bf16[2,128,512]{2,1,0:T(8,128)(2,1)S(1)}, u32[]{:S(2)}, u32[]{:S(2)}) collective-permute-start(bf16[2,128,512]{2,1,0:T(8,128)(2,1)S(1)} %get-tuple-element.113), channel_id=1, source_target_pairs={{0,2},{1,3},{2,0},{3,1},{4,6},{5,7},{6,4},{7,5},{8,10},{9,11},{10,... | collective-permute-start | bytes 786440 | tf_op jit(solution)/shard_map/ppermute | solution.py:189
  10.5 2.6 %collective-permute-start.4 = (bf16[64,1536]{1,0:T(8,128)(2,1)S(1)}, bf16[64,1536]{1,0:T(8,128)(2,1)S(1)}, u32[]{:S(2)}, u32[]{:S(2)}) collective-permute-start(bf16[64,1536]{1,0:T(8,128)(2,1)S(1)} %pad_maximum_fusion.3.refs_1_.refs_0_.refs_4_), channel_id=1, source_target_pairs={{0,8},{4,12},{8,0},{12,4},{1,9},{5,13},{9,1},{13,5},{2,10},{6,14},... | collective-permute-start | bytes 589832 | tf_op jit(solution)/shard_map/ppermute | solution.py:192
  13.1 1.6 %collective-permute-start.3 = (bf16[64,1536]{1,0:T(8,128)(2,1)S(1)}, bf16[64,1536]{1,0:T(8,128)(2,1)S(1)}, u32[]{:S(2)}, u32[]{:S(2)}) collective-permute-start(bf16[64,1536]{1,0:T(8,128)(2,1)S(1)} %pad_maximum_fusion.3.refs_1_.refs_0_.refs_4_), channel_id=1, source_target_pairs={{0,4},{4,0},{8,12},{12,8},{1,5},{5,1},{9,13},{13,9},{2,6},{6,2},{1... | collective-permute-start | bytes 589832 | tf_op jit(solution)/shard_map/ppermute | solution.py:192
  14.7 7.6 %collective-permute-done.4.refs_3_.refs_11_ = bf16[64,1536]{1,0:T(8,128)(2,1)S(1)} collective-permute-done((bf16[64,1536]{1,0:T(8,128)(2,1)S(1)}, bf16[64,1536]{1,0:T(8,128)(2,1)S(1)}, u32[]{:S(2)}, u32[]{:S(2)}) %collective-permute-start.4) | collective-permute-done | bytes 196640 | tf_op jit(solution)/shard_map/ppermute | solution.py:192
  22.7 1.5 %collective-permute-start.5 = (bf16[64,1536]{1,0:T(8,128)(2,1)S(1)}, bf16[64,1536]{1,0:T(8,128)(2,1)S(1)}, u32[]{:S(2)}, u32[]{:S(2)}) collective-permute-start(bf16[64,1536]{1,0:T(8,128)(2,1)S(1)} %collective-permute-done.4.refs_3_.refs_11_), channel_id=1, source_target_pairs={{0,4},{4,0},{8,12},{12,8},{1,5},{5,1},{9,13},{13,9},{2,6},{6,2},{1... | collective-permute-start | bytes 589832 | tf_op jit(solution)/shard_map/ppermute | solution.py:192
  24.8 5.2 %collective-permute-done.5.refs_4_ = bf16[64,1536]{1,0:T(8,128)(2,1)S(1)} collective-permute-done((bf16[64,1536]{1,0:T(8,128)(2,1)S(1)}, bf16[64,1536]{1,0:T(8,128)(2,1)S(1)}, u32[]{:S(2)}, u32[]{:S(2)}) %collective-permute-start.5) | collective-permute-done | bytes 196640 | tf_op jit(solution)/shard_map/ppermute | solution.py:192
  30.1 1.3 %shard_map.82 = (f32[64,1536]{1,0:T(8,128)S(1)}, bf16[64,1536]{1,0:T(8,128)(2,1)S(1)}, f32[64,1536]{1,0:T(8,128)S(1)}, bf16[64,1536]{1,0:T(8,128)(2,1)S(1)}) custom-call(s32[1]{0:T(128)} %bitcast.refs_0_, bf16[64,1536]{1,0:T(8,128)(2,1)S(1)} %pad_maximum_fusion.3.refs_1_.refs_0_.refs_4_, ...), custom_call_target="tpu_custom_call" | custom-call | flops 805306368 | bytes 1024 | tf_op jit(solution)/shard_map/pallas_call | solution.py:21
  31.4 1.5 %collective-permute-start.11 = (bf16[64,1536]{1,0:T(8,128)(2,1)S(1)}, bf16[64,1536]{1,0:T(8,128)(2,1)S(1)}, u32[]{:S(2)}, u32[]{:S(2)}) collective-permute-start(bf16[64,1536]{1,0:T(8,128)(2,1)S(1)} %get-tuple-element.62), channel_id=1, source_target_pairs={{0,4},{4,0},{8,12},{12,8},{1,5},{5,1},{9,13},{13,9},{2,6},{6,2},{1... | collective-permute-start | bytes 589832 | tf_op jit(solution)/shard_map/ppermute | solution.py:192
  32.9 5.1 %collective-permute-done.11.refs_13_.refs_5_ = bf16[64,1536]{1,0:T(8,128)(2,1)S(1)} collective-permute-done((bf16[64,1536]{1,0:T(8,128)(2,1)S(1)}, bf16[64,1536]{1,0:T(8,128)(2,1)S(1)}, u32[]{:S(2)}, u32[]{:S(2)}) %collective-permute-start.11) | collective-permute-done | bytes 196640 | tf_op jit(solution)/shard_map/ppermute | solution.py:192
  38.0 1.4 %collective-permute-start.15 = (bf16[64,1536]{1,0:T(8,128)(2,1)S(1)}, bf16[64,1536]{1,0:T(8,128)(2,1)S(1)}, u32[]{:S(2)}, u32[]{:S(2)}) collective-permute-start(bf16[64,1536]{1,0:T(8,128)(2,1)S(1)} %get-tuple-element.67), channel_id=1, source_target_pairs={{0,4},{4,0},{8,12},{12,8},{1,5},{5,1},{9,13},{13,9},{2,6},{6,2},{1... | collective-permute-start | bytes 589832 | tf_op jit(solution)/shard_map/ppermute | solution.py:192
  39.5 2.4 %collective-permute-start.16 = (bf16[64,1536]{1,0:T(8,128)(2,1)S(1)}, bf16[64,1536]{1,0:T(8,128)(2,1)S(1)}, u32[]{:S(2)}, u32[]{:S(2)}) collective-permute-start(bf16[64,1536]{1,0:T(8,128)(2,1)S(1)} %add_convert_fusion.4.refs_14_), channel_id=1, source_target_pairs={{0,8},{4,12},{8,0},{12,4},{1,9},{5,13},{9,1},{13,5},{2,10},{6,14},... | collective-permute-start | bytes 589832 | tf_op jit(solution)/shard_map/ppermute | solution.py:192
  41.9 1.3 %shard_map.83 = (f32[64,1536]{1,0:T(8,128)S(1)}, bf16[64,1536]{1,0:T(8,128)(2,1)S(1)}, f32[64,1536]{1,0:T(8,128)S(1)}, bf16[64,1536]{1,0:T(8,128)(2,1)S(1)}) custom-call(s32[1]{0:T(128)} %bitcast.refs_0_, bf16[64,1536]{1,0:T(8,128)(2,1)S(1)} %pad_maximum_fusion.3.refs_1_.refs_0_.refs_4_, ...), custom_call_target="tpu_custom_call" | custom-call | flops 805306368 | bytes 1024 | tf_op jit(solution)/shard_map/pallas_call | solution.py:21
  44.5 8.7 %collective-permute-done.17.refs_6_ = bf16[64,1536]{1,0:T(8,128)(2,1)S(1)} collective-permute-done((bf16[64,1536]{1,0:T(8,128)(2,1)S(1)}, bf16[64,1536]{1,0:T(8,128)(2,1)S(1)}, u32[]{:S(2)}, u32[]{:S(2)}) %collective-permute-start.17) | collective-permute-done | bytes 196640 | tf_op jit(solution)/shard_map/ppermute | solution.py:192
  54.6 2.4 %collective-permute-start.24 = (bf16[64,1536]{1,0:T(8,128)(2,1)}, bf16[64,1536]{1,0:T(8,128)(2,1)}, u32[]{:S(2)}, u32[]{:S(2)}) collective-permute-start(bf16[64,1536]{1,0:T(8,128)(2,1)} %add_convert_fusion.3.refs_6_), channel_id=1, source_target_pairs={{0,8},{4,12},{8,0},{12,4},{1,9},{5,13},{9,1},{13,5},{2,10},{6,14},... | collective-permute-start | bytes 589832 | tf_op jit(solution)/shard_map/ppermute | solution.py:192
  58.5 1.6 %collective-permute-start.20 = (bf16[64,1536]{1,0:T(8,128)(2,1)}, bf16[64,1536]{1,0:T(8,128)(2,1)}, u32[]{:S(2)}, u32[]{:S(2)}) collective-permute-start(bf16[64,1536]{1,0:T(8,128)(2,1)} %get-tuple-element.87.refs_1_), channel_id=1, source_target_pairs={{0,8},{4,12},{8,0},{12,4},{1,9},{5,13},{9,1},{13,5},{2,10},{6,14},... | collective-permute-start | bytes 589832 | tf_op jit(solution)/shard_map/ppermute | solution.py:192
  63.7 4.2 %collective-permute-done.24.refs_5_ = bf16[64,1536]{1,0:T(8,128)(2,1)} collective-permute-done((bf16[64,1536]{1,0:T(8,128)(2,1)}, bf16[64,1536]{1,0:T(8,128)(2,1)}, u32[]{:S(2)}, u32[]{:S(2)}) %collective-permute-start.24) | collective-permute-done | bytes 196640 | tf_op jit(solution)/shard_map/ppermute | solution.py:192
  67.9 1.6 %collective-permute-done.21.refs_7_.refs_2_.refs_9_ = bf16[64,1536]{1,0:T(8,128)(2,1)S(1)} collective-permute-done((bf16[64,1536]{1,0:T(8,128)(2,1)}, bf16[64,1536]{1,0:T(8,128)(2,1)S(1)}, u32[]{:S(2)}, u32[]{:S(2)}) %collective-permute-start.21) | collective-permute-done | bytes 196640 | tf_op jit(solution)/shard_map/ppermute | solution.py:192
  69.5 6.4 %collective-permute-done.20.refs_8_.refs_3_ = bf16[64,1536]{1,0:T(8,128)(2,1)} collective-permute-done((bf16[64,1536]{1,0:T(8,128)(2,1)}, bf16[64,1536]{1,0:T(8,128)(2,1)}, u32[]{:S(2)}, u32[]{:S(2)}) %collective-permute-start.20) | collective-permute-done | bytes 196640 | tf_op jit(solution)/shard_map/ppermute | solution.py:192
  82.3 1.9 %collective-permute-start.27 = (bf16[64,1536]{1,0:T(8,128)(2,1)S(1)}, bf16[64,1536]{1,0:T(8,128)(2,1)S(1)}, u32[]{:S(2)}, u32[]{:S(2)}) collective-permute-start(bf16[64,1536]{1,0:T(8,128)(2,1)S(1)} %shard_map.87.refs_1_), channel_id=1, source_target_pairs={{0,8},{4,12},{8,0},{12,4},{1,9},{5,13},{9,1},{13,5},{2,10},{6,14},... | collective-permute-start | bytes 589832 | tf_op jit(solution)/shard_map/ppermute | solution.py:192
  85.4 6.7 %collective-permute-done.22.refs_14_.refs_4_ = bf16[64,1536]{1,0:T(8,128)(2,1)S(1)} collective-permute-done((bf16[64,1536]{1,0:T(8,128)(2,1)}, bf16[64,1536]{1,0:T(8,128)(2,1)S(1)}, u32[]{:S(2)}, u32[]{:S(2)}) %collective-permute-start.22) | collective-permute-done | bytes 196640 | tf_op jit(solution)/shard_map/ppermute | solution.py:192
  92.0 2.6 %collective-permute-done.27.refs_16_.refs_3_ = bf16[64,1536]{1,0:T(8,128)(2,1)S(1)} collective-permute-done((bf16[64,1536]{1,0:T(8,128)(2,1)S(1)}, bf16[64,1536]{1,0:T(8,128)(2,1)S(1)}, u32[]{:S(2)}, u32[]{:S(2)}) %collective-permute-start.27) | collective-permute-done | bytes 196640 | tf_op jit(solution)/shard_map/ppermute | solution.py:192
  94.6 2.3 %collective-permute-done.26.refs_15_.refs_2_.refs_9_ = bf16[64,1536]{1,0:T(8,128)(2,1)S(1)} collective-permute-done((bf16[64,1536]{1,0:T(8,128)(2,1)S(1)}, bf16[64,1536]{1,0:T(8,128)(2,1)S(1)}, u32[]{:S(2)}, u32[]{:S(2)}) %collective-permute-start.26) | collective-permute-done | bytes 196640 | tf_op jit(solution)/shard_map/ppermute | solution.py:192
  97.6 1.5 %collective-permute-done.28 = bf16[256,512]{1,0:T(8,128)(2,1)S(1)} collective-permute-done((bf16[256,512]{1,0:T(8,128)(2,1)S(1)}, bf16[256,512]{1,0:T(8,128)(2,1)S(1)}, u32[]{:S(2)}, u32[]{:S(2)}) %collective-permute-start.28) | collective-permute-done | bytes 262176 | tf_op jit(solution)/shard_map/ppermute | solution.py:189
  100.1 4.7 %collective-permute-done.29 = bf16[128,512]{1,0:T(8,128)(2,1)S(1)} collective-permute-done((bf16[128,512]{1,0:T(8,128)(2,1)S(1)}, bf16[128,512]{1,0:T(8,128)(2,1)S(1)}, u32[]{:S(2)}, u32[]{:S(2)}) %collective-permute-start.29) | collective-permute-done | bytes 131104 | tf_op jit(solution)/shard_map/ppermute | solution.py:189
  105.0 1.5 %collective-permute-done.30.refs_11_.refs_4_ = bf16[64,1536]{1,0:T(8,128)(2,1)S(1)} collective-permute-done((bf16[64,1536]{1,0:T(8,128)(2,1)S(1)}, bf16[64,1536]{1,0:T(8,128)(2,1)S(1)}, u32[]{:S(2)}, u32[]{:S(2)}) %collective-permute-start.30) | collective-permute-done | bytes 196640 | tf_op jit(solution)/shard_map/ppermute | solution.py:192
  106.5 1.7 %shard_map.89 = (f32[256,512]{1,0:T(8,128)S(1)}, bf16[256,512]{1,0:T(8,128)(2,1)S(1)}) custom-call(s32[1]{0:T(128)} %bitcast.refs_0_, bf16[64,1536]{1,0:T(8,128)(2,1)} %get-tuple-element.87.refs_1_, bf16[64,1536]{1,0:T(8,128)(2,1)S(1)} %collective-permute-done.21.refs_7_.refs_2_.refs_9_, bf16[64,1536]{1,0:T(8,128)(2,1)} %collective-permute-done.20.refs_8_.refs_3_, ...), custom_call_target="tpu_custom_call" | custom-call | flops 402653184 | bytes 1024 | tf_op jit(solution)/shard_map/pallas_call | solution.py:21
  108.3 1.5 %collective-permute-done.31 = bf16[256,512]{1,0:T(8,128)(2,1)S(1)} collective-permute-done((bf16[256,512]{1,0:T(8,128)(2,1)S(1)}, bf16[256,512]{1,0:T(8,128)(2,1)S(1)}, u32[]{:S(2)}, u32[]{:S(2)}) %collective-permute-start.31) | collective-permute-done | bytes 262176 | tf_op jit(solution)/shard_map/ppermute | solution.py:189
  110.7 1.6 %collective-permute-start.32 = (bf16[128,512]{1,0:T(8,128)(2,1)S(1)}, bf16[128,512]{1,0:T(8,128)(2,1)S(1)}, u32[]{:S(2)}, u32[]{:S(2)}) collective-permute-start(bf16[128,512]{1,0:T(8,128)(2,1)S(1)} %get-tuple-element.121), channel_id=1, source_target_pairs={{0,2},{1,3},{2,0},{3,1},{4,6},{5,7},{6,4},{7,5},{8,10},{9,11},{10,... | collective-permute-start | bytes 393224 | tf_op jit(solution)/shard_map/ppermute | solution.py:189
  112.5 1.4 %collective-permute-start.34 = (bf16[128,512]{1,0:T(8,128)(2,1)S(1)}, bf16[128,512]{1,0:T(8,128)(2,1)S(1)}, u32[]{:S(2)}, u32[]{:S(2)}) collective-permute-start(bf16[128,512]{1,0:T(8,128)(2,1)S(1)} %get-tuple-element.123), channel_id=1, source_target_pairs={{0,2},{1,3},{2,0},{3,1},{4,6},{5,7},{6,4},{7,5},{8,10},{9,11},{10,... | collective-permute-start | bytes 393224 | tf_op jit(solution)/shard_map/ppermute | solution.py:189
  113.9 3.2 %collective-permute-done.32 = bf16[128,512]{1,0:T(8,128)(2,1)S(1)} collective-permute-done((bf16[128,512]{1,0:T(8,128)(2,1)S(1)}, bf16[128,512]{1,0:T(8,128)(2,1)S(1)}, u32[]{:S(2)}, u32[]{:S(2)}) %collective-permute-start.32) | collective-permute-done | bytes 131104 | tf_op jit(solution)/shard_map/ppermute | solution.py:189
  117.2 2.2 %collective-permute-done.34 = bf16[128,512]{1,0:T(8,128)(2,1)S(1)} collective-permute-done((bf16[128,512]{1,0:T(8,128)(2,1)S(1)}, bf16[128,512]{1,0:T(8,128)(2,1)S(1)}, u32[]{:S(2)}, u32[]{:S(2)}) %collective-permute-start.34) | collective-permute-done | bytes 131104 | tf_op jit(solution)/shard_map/ppermute | solution.py:189
  (137 shorter events, 24.8 us)
Async XLA Ops:
  2.3 6.3 %collective-permute-start = (bf16[32,1280]{1,0:T(8,128)(2,1)S(1)}, bf16[32,1280]{1,0:T(8,128)(2,1)S(1)}, u32[]{:S(2)}, u32[]{:S(2)}) collective-permute-start(bf16[32,1280]{1,0:T(8,128)(2,1)S(1)} %get-tuple-element.127), channel_id=1, source_target_pairs={{0,2},{1,3},{2,0},{3,1},{4,6},{5,7},{6,4},{7,5},{8,10},{9,11},{10,... | collective-permute-start | bytes 245768 | tf_op jit(solution)/shard_map/ppermute | solution.py:189
  5.5 3.2 %collective-permute-start.2 = (bf16[32,256]{1,0:T(8,128)(2,1)S(1)}, bf16[32,256]{1,0:T(8,128)(2,1)S(1)}, u32[]{:S(2)}, u32[]{:S(2)}) collective-permute-start(bf16[32,256]{1,0:T(8,128)(2,1)S(1)} %select_n.184), channel_id=1, source_target_pairs={{0,3},{1,2},{2,1},{3,0},{4,7},{5,6},{6,5},{7,4},{8,11},{9,10},{10,... | collective-permute-start | bytes 49160 | tf_op jit(solution)/shard_map/ppermute | solution.py:189
  5.7 2.9 %collective-permute-start.1 = (bf16[32,256]{1,0:T(8,128)(2,1)S(1)}, bf16[32,256]{1,0:T(8,128)(2,1)S(1)}, u32[]{:S(2)}, u32[]{:S(2)}) collective-permute-start(bf16[32,256]{1,0:T(8,128)(2,1)S(1)} %select_n.181), channel_id=1, source_target_pairs={{0,1},{1,0},{2,3},{3,2},{4,5},{5,4},{6,7},{7,6},{8,9},{9,8},{10,11... | collective-permute-start | bytes 49160 | tf_op jit(solution)/shard_map/ppermute | solution.py:189
  8.8 13.6 %collective-permute-start.6 = (bf16[2,128,512]{2,1,0:T(8,128)(2,1)S(1)}, bf16[2,128,512]{2,1,0:T(8,128)(2,1)S(1)}, u32[]{:S(2)}, u32[]{:S(2)}) collective-permute-start(bf16[2,128,512]{2,1,0:T(8,128)(2,1)S(1)} %get-tuple-element.113), channel_id=1, source_target_pairs={{0,2},{1,3},{2,0},{3,1},{4,6},{5,7},{6,4},{7,5},{8,10},{9,11},{10,... | collective-permute-start | bytes 786440 | tf_op jit(solution)/shard_map/ppermute | solution.py:189
  10.5 11.8 %collective-permute-start.4 = (bf16[64,1536]{1,0:T(8,128)(2,1)S(1)}, bf16[64,1536]{1,0:T(8,128)(2,1)S(1)}, u32[]{:S(2)}, u32[]{:S(2)}) collective-permute-start(bf16[64,1536]{1,0:T(8,128)(2,1)S(1)} %pad_maximum_fusion.3.refs_1_.refs_0_.refs_4_), channel_id=1, source_target_pairs={{0,8},{4,12},{8,0},{12,4},{1,9},{5,13},{9,1},{13,5},{2,10},{6,14},... | collective-permute-start | bytes 589832 | tf_op jit(solution)/shard_map/ppermute | solution.py:192
  13.1 9.4 %collective-permute-start.3 = (bf16[64,1536]{1,0:T(8,128)(2,1)S(1)}, bf16[64,1536]{1,0:T(8,128)(2,1)S(1)}, u32[]{:S(2)}, u32[]{:S(2)}) collective-permute-start(bf16[64,1536]{1,0:T(8,128)(2,1)S(1)} %pad_maximum_fusion.3.refs_1_.refs_0_.refs_4_), channel_id=1, source_target_pairs={{0,4},{4,0},{8,12},{12,8},{1,5},{5,1},{9,13},{13,9},{2,6},{6,2},{1... | collective-permute-start | bytes 589832 | tf_op jit(solution)/shard_map/ppermute | solution.py:192
  14.7 9.5 %collective-permute-start.7 = (bf16[2,128,512]{2,1,0:T(8,128)(2,1)S(1)}, bf16[2,128,512]{2,1,0:T(8,128)(2,1)S(1)}, u32[]{:S(2)}, u32[]{:S(2)}) collective-permute-start(bf16[2,128,512]{2,1,0:T(8,128)(2,1)S(1)} %get-tuple-element.71.refs_5_.refs_9_), channel_id=1, source_target_pairs={{0,1},{1,0},{2,3},{3,2},{4,5},{5,4},{6,7},{7,6},{8,9},{9,8},{10,11... | collective-permute-start | bytes 786440 | tf_op jit(solution)/shard_map/ppermute | solution.py:189
  22.5 1.8 %collective-permute-start.8 = (bf16[2,128,512]{2,1,0:T(8,128)(2,1)S(1)}, bf16[2,128,512]{2,1,0:T(8,128)(2,1)S(1)}, u32[]{:S(2)}, u32[]{:S(2)}) collective-permute-start(bf16[2,128,512]{2,1,0:T(8,128)(2,1)S(1)} %collective-permute-done.6.refs_6_.refs_10_), channel_id=1, source_target_pairs={{0,1},{1,0},{2,3},{3,2},{4,5},{5,4},{6,7},{7,6},{8,9},{9,8},{10,11... | collective-permute-start | bytes 786440 | tf_op jit(solution)/shard_map/ppermute | solution.py:189
  22.7 7.4 %collective-permute-start.5 = (bf16[64,1536]{1,0:T(8,128)(2,1)S(1)}, bf16[64,1536]{1,0:T(8,128)(2,1)S(1)}, u32[]{:S(2)}, u32[]{:S(2)}) collective-permute-start(bf16[64,1536]{1,0:T(8,128)(2,1)S(1)} %collective-permute-done.4.refs_3_.refs_11_), channel_id=1, source_target_pairs={{0,4},{4,0},{8,12},{12,8},{1,5},{5,1},{9,13},{13,9},{2,6},{6,2},{1... | collective-permute-start | bytes 589832 | tf_op jit(solution)/shard_map/ppermute | solution.py:192
  24.3 15.1 %collective-permute-start.9 = (bf16[2,128,512]{2,1,0:T(8,128)(2,1)S(1)}, bf16[2,128,512]{2,1,0:T(8,128)(2,1)S(1)}, u32[]{:S(2)}, u32[]{:S(2)}) collective-permute-start(bf16[2,128,512]{2,1,0:T(8,128)(2,1)S(1)} %get-tuple-element.109), channel_id=1, source_target_pairs={{0,2},{1,3},{2,0},{3,1},{4,6},{5,7},{6,4},{7,5},{8,10},{9,11},{10,... | collective-permute-start | bytes 786440 | tf_op jit(solution)/shard_map/ppermute | solution.py:189
  31.4 6.6 %collective-permute-start.11 = (bf16[64,1536]{1,0:T(8,128)(2,1)S(1)}, bf16[64,1536]{1,0:T(8,128)(2,1)S(1)}, u32[]{:S(2)}, u32[]{:S(2)}) collective-permute-start(bf16[64,1536]{1,0:T(8,128)(2,1)S(1)} %get-tuple-element.62), channel_id=1, source_target_pairs={{0,4},{4,0},{8,12},{12,8},{1,5},{5,1},{9,13},{13,9},{2,6},{6,2},{1... | collective-permute-start | bytes 589832 | tf_op jit(solution)/shard_map/ppermute | solution.py:192
  32.9 9.0 %collective-permute-start.10 = (bf16[2,128,512]{2,1,0:T(8,128)(2,1)S(1)}, bf16[2,128,512]{2,1,0:T(8,128)(2,1)S(1)}, u32[]{:S(2)}, u32[]{:S(2)}) collective-permute-start(bf16[2,128,512]{2,1,0:T(8,128)(2,1)S(1)} %get-tuple-element.82.refs_5_.refs_9_), channel_id=1, source_target_pairs={{0,1},{1,0},{2,3},{3,2},{4,5},{5,4},{6,7},{7,6},{8,9},{9,8},{10,11... | collective-permute-start | bytes 786440 | tf_op jit(solution)/shard_map/ppermute | solution.py:189
  38.0 16.3 %collective-permute-start.15 = (bf16[64,1536]{1,0:T(8,128)(2,1)S(1)}, bf16[64,1536]{1,0:T(8,128)(2,1)S(1)}, u32[]{:S(2)}, u32[]{:S(2)}) collective-permute-start(bf16[64,1536]{1,0:T(8,128)(2,1)S(1)} %get-tuple-element.67), channel_id=1, source_target_pairs={{0,4},{4,0},{8,12},{12,8},{1,5},{5,1},{9,13},{13,9},{2,6},{6,2},{1... | collective-permute-start | bytes 589832 | tf_op jit(solution)/shard_map/ppermute | solution.py:192
  39.4 2.5 %collective-permute-start.12 = (bf16[2,128,512]{2,1,0:T(8,128)(2,1)S(1)}, bf16[2,128,512]{2,1,0:T(8,128)(2,1)S(1)}, u32[]{:S(2)}, u32[]{:S(2)}) collective-permute-start(bf16[2,128,512]{2,1,0:T(8,128)(2,1)S(1)} %collective-permute-done.9.refs_6_.refs_10_), channel_id=1, source_target_pairs={{0,1},{1,0},{2,3},{3,2},{4,5},{5,4},{6,7},{7,6},{8,9},{9,8},{10,11... | collective-permute-start | bytes 786440 | tf_op jit(solution)/shard_map/ppermute | solution.py:189
  39.5 14.8 %collective-permute-start.16 = (bf16[64,1536]{1,0:T(8,128)(2,1)S(1)}, bf16[64,1536]{1,0:T(8,128)(2,1)S(1)}, u32[]{:S(2)}, u32[]{:S(2)}) collective-permute-start(bf16[64,1536]{1,0:T(8,128)(2,1)S(1)} %add_convert_fusion.4.refs_14_), channel_id=1, source_target_pairs={{0,8},{4,12},{8,0},{12,4},{1,9},{5,13},{9,1},{13,5},{2,10},{6,14},... | collective-permute-start | bytes 589832 | tf_op jit(solution)/shard_map/ppermute | solution.py:192
  43.2 10.0 %collective-permute-start.17 = (bf16[64,1536]{1,0:T(8,128)(2,1)S(1)}, bf16[64,1536]{1,0:T(8,128)(2,1)S(1)}, u32[]{:S(2)}, u32[]{:S(2)}) collective-permute-start(bf16[64,1536]{1,0:T(8,128)(2,1)S(1)} %get-tuple-element.77), channel_id=1, source_target_pairs={{0,4},{4,0},{8,12},{12,8},{1,5},{5,1},{9,13},{13,9},{2,6},{6,2},{1... | collective-permute-start | bytes 589832 | tf_op jit(solution)/shard_map/ppermute | solution.py:192
  44.0 16.2 %collective-permute-start.13 = (bf16[3,128,512]{2,1,0:T(8,128)(2,1)S(1)}, bf16[3,128,512]{2,1,0:T(8,128)(2,1)S(1)}, u32[]{:S(2)}, u32[]{:S(2)}) collective-permute-start(bf16[3,128,512]{2,1,0:T(8,128)(2,1)S(1)} %get-tuple-element.105), channel_id=1, source_target_pairs={{0,2},{1,3},{2,0},{3,1},{4,6},{5,7},{6,4},{7,5},{8,10},{9,11},{10,... | collective-permute-start | bytes 1179656 | tf_op jit(solution)/shard_map/ppermute | solution.py:189
  53.2 8.0 %collective-permute-start.23 = (bf16[64,1536]{1,0:T(8,128)(2,1)S(1)}, bf16[64,1536]{1,0:T(8,128)(2,1)S(1)}, u32[]{:S(2)}, u32[]{:S(2)}) collective-permute-start(bf16[64,1536]{1,0:T(8,128)(2,1)S(1)} %get-tuple-element.92), channel_id=1, source_target_pairs={{0,4},{4,0},{8,12},{12,8},{1,5},{5,1},{9,13},{13,9},{2,6},{6,2},{1... | collective-permute-start | bytes 589832 | tf_op jit(solution)/shard_map/ppermute | solution.py:192
  54.5 2.5 %collective-permute-start.18 = (f32[64,128]{1,0:T(8,128)S(1)}, f32[64,128]{1,0:T(8,128)S(1)}, u32[]{:S(2)}, u32[]{:S(2)}) collective-permute-start(f32[64,128]{1,0:T(8,128)S(1)} %get-tuple-element.79.refs_2_), channel_id=1, source_target_pairs={{0,1},{1,0},{2,3},{3,2},{4,5},{5,4},{6,7},{7,6},{8,9},{9,8},{10,11... | collective-permute-start | bytes 98312 | tf_op jit(solution)/shard_map/ppermute | solution.py:189
  54.6 13.3 %collective-permute-start.24 = (bf16[64,1536]{1,0:T(8,128)(2,1)}, bf16[64,1536]{1,0:T(8,128)(2,1)}, u32[]{:S(2)}, u32[]{:S(2)}) collective-permute-start(bf16[64,1536]{1,0:T(8,128)(2,1)} %add_convert_fusion.3.refs_6_), channel_id=1, source_target_pairs={{0,8},{4,12},{8,0},{12,4},{1,9},{5,13},{9,1},{13,5},{2,10},{6,14},... | collective-permute-start | bytes 589832 | tf_op jit(solution)/shard_map/ppermute | solution.py:192
  57.9 11.6 %collective-permute-start.21 = (bf16[64,1536]{1,0:T(8,128)(2,1)}, bf16[64,1536]{1,0:T(8,128)(2,1)S(1)}, u32[]{:S(2)}, u32[]{:S(2)}) collective-permute-start(bf16[64,1536]{1,0:T(8,128)(2,1)} %get-tuple-element.87.refs_1_), channel_id=1, source_target_pairs={{0,4},{4,0},{8,12},{12,8},{1,5},{5,1},{9,13},{13,9},{2,6},{6,2},{1... | collective-permute-start | bytes 589832 | tf_op jit(solution)/shard_map/ppermute | solution.py:192
  58.5 17.3 %collective-permute-start.20 = (bf16[64,1536]{1,0:T(8,128)(2,1)}, bf16[64,1536]{1,0:T(8,128)(2,1)}, u32[]{:S(2)}, u32[]{:S(2)}) collective-permute-start(bf16[64,1536]{1,0:T(8,128)(2,1)} %get-tuple-element.87.refs_1_), channel_id=1, source_target_pairs={{0,8},{4,12},{8,0},{12,4},{1,9},{5,13},{9,1},{13,5},{2,10},{6,14},... | collective-permute-start | bytes 589832 | tf_op jit(solution)/shard_map/ppermute | solution.py:192
  60.2 25.2 %collective-permute-start.14 = (bf16[3,128,512]{2,1,0:T(8,128)(2,1)S(1)}, bf16[3,128,512]{2,1,0:T(8,128)(2,1)S(1)}, u32[]{:S(2)}, u32[]{:S(2)}) collective-permute-start(bf16[3,128,512]{2,1,0:T(8,128)(2,1)S(1)} %get-tuple-element.106.refs_5_), channel_id=1, source_target_pairs={{0,1},{1,0},{2,3},{3,2},{4,5},{5,4},{6,7},{7,6},{8,9},{9,8},{10,11... | collective-permute-start | bytes 1179656 | tf_op jit(solution)/shard_map/ppermute | solution.py:189
  61.9 35.0 %collective-permute-start.19 = (bf16[3,128,512]{2,1,0:T(8,128)(2,1)S(1)}, bf16[3,128,512]{2,1,0:T(8,128)(2,1)S(1)}, u32[]{:S(2)}, u32[]{:S(2)}) collective-permute-start(bf16[3,128,512]{2,1,0:T(8,128)(2,1)S(1)} %collective-permute-done.13.refs_6_), channel_id=1, source_target_pairs={{0,1},{1,0},{2,3},{3,2},{4,5},{5,4},{6,7},{7,6},{8,9},{9,8},{10,11... | collective-permute-start | bytes 1179656 | tf_op jit(solution)/shard_map/ppermute | solution.py:189
  80.9 11.1 %collective-permute-start.22 = (bf16[64,1536]{1,0:T(8,128)(2,1)}, bf16[64,1536]{1,0:T(8,128)(2,1)S(1)}, u32[]{:S(2)}, u32[]{:S(2)}) collective-permute-start(bf16[64,1536]{1,0:T(8,128)(2,1)} %collective-permute-done.20.refs_8_.refs_3_), channel_id=1, source_target_pairs={{0,4},{4,0},{8,12},{12,8},{1,5},{5,1},{9,13},{13,9},{2,6},{6,2},{1... | collective-permute-start | bytes 589832 | tf_op jit(solution)/shard_map/ppermute | solution.py:192
  82.3 12.3 %collective-permute-start.27 = (bf16[64,1536]{1,0:T(8,128)(2,1)S(1)}, bf16[64,1536]{1,0:T(8,128)(2,1)S(1)}, u32[]{:S(2)}, u32[]{:S(2)}) collective-permute-start(bf16[64,1536]{1,0:T(8,128)(2,1)S(1)} %shard_map.87.refs_1_), channel_id=1, source_target_pairs={{0,8},{4,12},{8,0},{12,4},{1,9},{5,13},{9,1},{13,5},{2,10},{6,14},... | collective-permute-start | bytes 589832 | tf_op jit(solution)/shard_map/ppermute | solution.py:192
  84.2 12.7 %collective-permute-start.26 = (bf16[64,1536]{1,0:T(8,128)(2,1)S(1)}, bf16[64,1536]{1,0:T(8,128)(2,1)S(1)}, u32[]{:S(2)}, u32[]{:S(2)}) collective-permute-start(bf16[64,1536]{1,0:T(8,128)(2,1)S(1)} %shard_map.87.refs_1_), channel_id=1, source_target_pairs={{0,4},{4,0},{8,12},{12,8},{1,5},{5,1},{9,13},{13,9},{2,6},{6,2},{1... | collective-permute-start | bytes 589832 | tf_op jit(solution)/shard_map/ppermute | solution.py:192
  99.3 5.6 %collective-permute-start.29 = (bf16[128,512]{1,0:T(8,128)(2,1)S(1)}, bf16[128,512]{1,0:T(8,128)(2,1)S(1)}, u32[]{:S(2)}, u32[]{:S(2)}) collective-permute-start(bf16[128,512]{1,0:T(8,128)(2,1)S(1)} %get-tuple-element.118), channel_id=1, source_target_pairs={{0,2},{1,3},{2,0},{3,1},{4,6},{5,7},{6,4},{7,5},{8,10},{9,11},{10,... | collective-permute-start | bytes 393224 | tf_op jit(solution)/shard_map/ppermute | solution.py:189
  99.8 6.7 %collective-permute-start.30 = (bf16[64,1536]{1,0:T(8,128)(2,1)S(1)}, bf16[64,1536]{1,0:T(8,128)(2,1)S(1)}, u32[]{:S(2)}, u32[]{:S(2)}) collective-permute-start(bf16[64,1536]{1,0:T(8,128)(2,1)S(1)} %collective-permute-done.27.refs_16_.refs_3_), channel_id=1, source_target_pairs={{0,4},{4,0},{8,12},{12,8},{1,5},{5,1},{9,13},{13,9},{2,6},{6,2},{1... | collective-permute-start | bytes 589832 | tf_op jit(solution)/shard_map/ppermute | solution.py:192
  110.5 1.8 %collective-permute-start.33 = (bf16[256,512]{1,0:T(8,128)(2,1)S(1)}, bf16[256,512]{1,0:T(8,128)(2,1)S(1)}, u32[]{:S(2)}, u32[]{:S(2)}) collective-permute-start(bf16[256,512]{1,0:T(8,128)(2,1)S(1)} %get-tuple-element.104), channel_id=1, source_target_pairs={{0,1},{1,0},{2,3},{3,2},{4,5},{5,4},{6,7},{7,6},{8,9},{9,8},{10,11... | collective-permute-start | bytes 786440 | tf_op jit(solution)/shard_map/ppermute | solution.py:189
  110.7 6.4 %collective-permute-start.32 = (bf16[128,512]{1,0:T(8,128)(2,1)S(1)}, bf16[128,512]{1,0:T(8,128)(2,1)S(1)}, u32[]{:S(2)}, u32[]{:S(2)}) collective-permute-start(bf16[128,512]{1,0:T(8,128)(2,1)S(1)} %get-tuple-element.121), channel_id=1, source_target_pairs={{0,2},{1,3},{2,0},{3,1},{4,6},{5,7},{6,4},{7,5},{8,10},{9,11},{10,... | collective-permute-start | bytes 393224 | tf_op jit(solution)/shard_map/ppermute | solution.py:189
  112.5 6.9 %collective-permute-start.34 = (bf16[128,512]{1,0:T(8,128)(2,1)S(1)}, bf16[128,512]{1,0:T(8,128)(2,1)S(1)}, u32[]{:S(2)}, u32[]{:S(2)}) collective-permute-start(bf16[128,512]{1,0:T(8,128)(2,1)S(1)} %get-tuple-element.123), channel_id=1, source_target_pairs={{0,2},{1,3},{2,0},{3,1},{4,6},{5,7},{6,4},{7,5},{8,10},{9,11},{10,... | collective-permute-start | bytes 393224 | tf_op jit(solution)/shard_map/ppermute | solution.py:189
  (24 other events, 128.8 us)

commit v9 on v8

--- a/solution.py
+++ b/solution.py
@@ -194,13 +194,15 @@
     def spread(own):
         return {0: own, planes // 2: to_plane(own, planes // 2)}
 
-    def spread_on(pieces, gate, sink):
+    def spread_on(pieces, sink=None):
         bit = planes // 4
         while bit:
             direct = to_plane(pieces[0], bit)
             for distance in list(pieces):
                 if distance:
-                    piece = after(pieces[distance], [direct] + gate, sink)
+                    piece = pieces[distance]
+                    if sink is not None:
+                        piece = after(piece, [direct], sink)
                     pieces[distance | bit] = to_plane(piece, bit)
             pieces[bit] = direct
             bit //= 2
@@ -212,13 +214,14 @@
             for d in range(planes - bit, 0, -2 * bit)
         }
 
-    def halve(parts, bit, sent, sink):
-        came = []
+    def halve(parts, bit, sent):
+        relayed = None
         for distance, total in sent.items():
-            if distance == bit and came:
-                total = after(total, came[-1:], sink)
-            came.append(to_plane(total, bit))
-            parts[distance ^ bit].append(came[-1])
+            if distance == bit and relayed is not None:
+                total, came = lax.optimization_barrier((total, parts[relayed][-1]))
+                parts[relayed][-1] = came
+            parts[distance ^ bit].append(to_plane(total, bit))
+            relayed = distance ^ bit
 
     def pick(flag, a, b):
         return jnp.where(flag == 0, a, b), jnp.where(flag == 0, b, a)
@@ -246,7 +249,7 @@
     zero = jnp.concatenate([layers, ordered(y, second_mine, second_far, 1)], axis=1)
     names = ("steps0", "steps1", "out0", "new0", "new1", "out1", "out2")
     behind = {name: [] for name in names}
-    full_zero = spread_on(spread(zero), [], behind["steps0"])
+    full_zero = spread_on(spread(zero), behind["steps0"])
 
     scaled = learn_rates[:2, :, :, None] * value_tokens[:2].reshape(2, tokens, 2, width).astype(WIDE)
     scaled = scaled.astype(LOW).reshape(2, tokens, 2 * width)
@@ -296,7 +299,7 @@
         behind["steps0"],
     )
     zeros = steps(0)
-    halve(zeros, 1, totals(zeros, 1), behind["new0"])
+    halve(zeros, 1, totals(zeros, 1))
     came = [zeros[d][-1] for d in range(2, planes, 2)]
     pairs[1] = to_quad(
         after(pairs[1], pairs[0], behind["steps1"]), came or zeros[0], behind["steps1"]
@@ -305,13 +308,13 @@
     while bit < planes:
         sent = totals(zeros, bit)
         behind["steps1"].extend(sent.values())
-        halve(zeros, bit, sent, behind["new0"])
+        halve(zeros, bit, sent)
         bit *= 2
     ones = steps(1)
     bit = 1
     while bit < planes:
         sent = totals(ones, bit)
-        halve(ones, bit, sent, behind["new1"])
+        halve(ones, bit, sent)
         bit *= 2
     got_zero, got_one = zeros[0], ones[0]
     behind["new0"].extend(sent.values())
@@ -328,9 +331,15 @@
     weights_one, payload = call(
         scaled_kernel, [(flat, WIDE), (flat, LOW)], 0, moved, zero, sums, send(sums, 1)
     )
-    full_one = spread_on(spread(payload), [], behind["out1"])
-    behind["new1"].extend([full_one[1], full_one[planes // 2]])
-
+    first_one = spread(payload)
+    direct_one = to_plane(payload, 1)
+    queries = to_quad(
+        after(query_tokens, pairs[1], behind["out0"]), [weights_one], behind["out0"]
+    )
+
+    half_way = planes // 2
+    waited = (got_one, first_one[half_way], direct_one)
+    got_one, first_one[half_way], direct_one = lax.optimization_barrier(waited)
     decay = jnp.broadcast_to(jnp.where(y == 0, momentum_decay[0], momentum_decay[1]), (8, 128))
     moved, sums = call(
         second_moved_kernel,
@@ -344,15 +353,21 @@
     )
     far_sums = send(sums, 1)
     payload = call(last_scaled_kernel, [(flat, LOW)], 0, moved, weights_one, sums, far_sums)[0]
-    full_two = spread_on(spread(payload), [], behind["out2"])
-    queries = to_quad(
-        after(query_tokens, pairs[1], behind["out0"]), [weights_one], behind["out0"]
-    )
-    behind["out0"].extend([full_one[planes - 1], full_two[1], full_two[planes // 2]])
+    first_two = spread(payload)
+    direct_two = to_plane(payload, 1)
+    full_one = spread_on(first_one)
+    full_one[1] = direct_one
+    waited = (first_two[half_way], direct_two, queries[0], full_one[planes - 1])
+    first_two[half_way], direct_two, first_query, full_one[planes - 1] = (
+        lax.optimization_barrier(waited)
+    )
+    queries = (first_query,) + queries[1:]
+    full_two = spread_on(first_two)
+    full_two[1] = direct_two
     out_zero = returned(readout(0, full_zero))
-    behind["out1"].extend([out_zero, full_two[planes - 1]])
     total_one = readout(1, full_one)
-    behind["out2"].append(total_one)
+    waited = (full_two[planes - 1], out_zero, total_one)
+    full_two[planes - 1], out_zero, total_one = lax.optimization_barrier(waited)
     out_one = returned(total_one)
     out_two = returned(readout(2, full_two))
     return jnp.stack([out_zero, out_one, out_two])

time: 121 us -> 118 us (0.975)
  starting transfers between devices: 30.1 us -> 26.2 us
  waiting for transfers between devices: 67.4 us -> 68.9 us
    ppermute x15, starting transfers between devices: 20 us -> 17.4 us  [to_plane(): return lax.ppermute(array, 'plane', [(z, z ^ bit) for z in range(planes)])]
    unnamed x42 -> x34, local copies, waits for them, and re-layouts: 6.66 us -> 5.12 us
    ppermute x15, waiting for transfers between devices: 53 us -> 54.5 us  [to_plane(): return lax.ppermute(array, 'plane', [(z, z ^ bit) for z in range(planes)])]
    ppermute x20, starting transfers between devices: 10.1 us -> 8.77 us  [send(): return lax.ppermute(array, 'quad', [(q, q ^ offset) for q in range(4)])]
  transfers between devices with their start and end apart: 35 -> 35, of which waited for: 19 -> 18; matrix products, arithmetic and copies ran while one was open for 4% -> 3% of each run, Pallas kernels for 4% -> 6%
where the time goes in v9:
time: 118 us
  waiting for transfers between devices  68.9 us (58%)
  starting transfers between devices  26.2 us (22%)
  local copies, waits for them, and re-layouts  9.97 us (8%)
  Pallas kernels  8.73 us (7%)
  other arithmetic  2.49 us (2%)
  between operations  1.65 us (1%)
    ppermute x15, waiting for transfers between devices, to_plane(): return lax.ppermute(array, 'plane', [(z, z ^ bit) for z in range(planes)])  54.5 us
    ppermute x15, starting transfers between devices, to_plane(): return lax.ppermute(array, 'plane', [(z, z ^ bit) for z in range(planes)])  17.4 us
    ppermute x20, waiting for transfers between devices, send(): return lax.ppermute(array, 'quad', [(q, q ^ offset) for q in range(4)])  14.4 us
    ppermute x20, starting transfers between devices, send(): return lax.ppermute(array, 'quad', [(q, q ^ offset) for q in range(4)])  8.77 us
    pallas_call x9, Pallas kernels, call(): pl.pallas_call(kernel, out_shape=shapes, in_specs=[pl.BlockSpec(memory_sp...  8.73 us
    unnamed x34, local copies, waits for them, and re-layouts  5.12 us
  transfers between devices with their start and end apart: 35, of which 18 were waited for; matrix products, arithmetic and copies ran while one was open for 3% of the time, Pallas kernels for 6%

profile of v9, /device:TPU:0, one launch (start us, length us, event | category | flops | bytes accessed | tf_op | source)
XLA Modules:
  0.0 117.9 jit_solution(12320786651489347282)
XLA Ops:
  0.0 1.0 reshape.143
  2.3 3.0 %collective-permute-start = (bf16[32,1280]{1,0:T(8,128)(2,1)S(1)}, bf16[32,1280]{1,0:T(8,128)(2,1)S(1)}, u32[]{:S(2)}, u32[]{:S(2)}) collective-permute-start(bf16[32,1280]{1,0:T(8,128)(2,1)S(1)} %get-tuple-element.142), channel_id=1, source_target_pairs={{0,2},{1,3},{2,0},{3,1},{4,6},{5,7},{6,4},{7,5},{8,10},{9,11},{10,... | collective-permute-start | bytes 245768 | tf_op jit(solution)/shard_map/ppermute | solution.py:189
  9.7 2.1 %collective-permute-start.6 = (bf16[2,128,512]{2,1,0:T(8,128)(2,1)S(1)}, bf16[2,128,512]{2,1,0:T(8,128)(2,1)S(1)}, u32[]{:S(2)}, u32[]{:S(2)}) collective-permute-start(bf16[2,128,512]{2,1,0:T(8,128)(2,1)S(1)} %get-tuple-element.129), channel_id=1, source_target_pairs={{0,2},{1,3},{2,0},{3,1},{4,6},{5,7},{6,4},{7,5},{8,10},{9,11},{10,... | collective-permute-start | bytes 786440 | tf_op jit(solution)/shard_map/ppermute | solution.py:189
  11.7 1.6 %collective-permute-start.3 = (bf16[64,1536]{1,0:T(8,128)(2,1)S(1)}, bf16[64,1536]{1,0:T(8,128)(2,1)S(1)}, u32[]{:S(2)}, u32[]{:S(2)}) collective-permute-start(bf16[64,1536]{1,0:T(8,128)(2,1)S(1)} %pad_maximum_fusion.3.refs_1_.refs_0_.refs_4_), channel_id=1, source_target_pairs={{0,4},{4,0},{8,12},{12,8},{1,5},{5,1},{9,13},{13,9},{2,6},{6,2},{1... | collective-permute-start | bytes 589832 | tf_op jit(solution)/shard_map/ppermute | solution.py:192
  13.3 2.6 %collective-permute-start.4 = (bf16[64,1536]{1,0:T(8,128)(2,1)S(1)}, bf16[64,1536]{1,0:T(8,128)(2,1)S(1)}, u32[]{:S(2)}, u32[]{:S(2)}) collective-permute-start(bf16[64,1536]{1,0:T(8,128)(2,1)S(1)} %pad_maximum_fusion.3.refs_1_.refs_0_.refs_4_), channel_id=1, source_target_pairs={{0,8},{4,12},{8,0},{12,4},{1,9},{5,13},{9,1},{13,5},{2,10},{6,14},... | collective-permute-start | bytes 589832 | tf_op jit(solution)/shard_map/ppermute | solution.py:192
  15.9 6.5 %collective-permute-done.3.refs_2_.refs_9_.refs_10_ = bf16[64,1536]{1,0:T(8,128)(2,1)S(1)} collective-permute-done((bf16[64,1536]{1,0:T(8,128)(2,1)S(1)}, bf16[64,1536]{1,0:T(8,128)(2,1)S(1)}, u32[]{:S(2)}, u32[]{:S(2)}) %collective-permute-start.3) | collective-permute-done | bytes 196640 | tf_op jit(solution)/shard_map/ppermute | solution.py:192
  22.4 2.4 %collective-permute-done.4.refs_3_.refs_11_ = bf16[64,1536]{1,0:T(8,128)(2,1)S(1)} collective-permute-done((bf16[64,1536]{1,0:T(8,128)(2,1)S(1)}, bf16[64,1536]{1,0:T(8,128)(2,1)S(1)}, u32[]{:S(2)}, u32[]{:S(2)}) %collective-permute-start.4) | collective-permute-done | bytes 196640 | tf_op jit(solution)/shard_map/ppermute | solution.py:192
  26.9 5.5 %collective-permute-done.5.refs_4_ = bf16[64,1536]{1,0:T(8,128)(2,1)S(1)} collective-permute-done((bf16[64,1536]{1,0:T(8,128)(2,1)S(1)}, bf16[64,1536]{1,0:T(8,128)(2,1)S(1)}, u32[]{:S(2)}, u32[]{:S(2)}) %collective-permute-start.5) | collective-permute-done | bytes 196640 | tf_op jit(solution)/shard_map/ppermute | solution.py:192
  32.4 1.3 %shard_map.82 = (f32[64,1536]{1,0:T(8,128)S(1)}, bf16[64,1536]{1,0:T(8,128)(2,1)S(1)}, f32[64,1536]{1,0:T(8,128)S(1)}, bf16[64,1536]{1,0:T(8,128)(2,1)S(1)}) custom-call(s32[1]{0:T(128)} %bitcast.2.refs_0_, bf16[64,1536]{1,0:T(8,128)(2,1)S(1)} %pad_maximum_fusion.3.refs_1_.refs_0_.refs_4_, ...), custom_call_target="tpu_custom_call" | custom-call | flops 805306368 | bytes 1024 | tf_op jit(solution)/shard_map/pallas_call | solution.py:21
  34.2 6.1 %collective-permute-done.9.refs_13_ = bf16[64,1536]{1,0:T(8,128)(2,1)S(1)} collective-permute-done((bf16[64,1536]{1,0:T(8,128)(2,1)S(1)}, bf16[64,1536]{1,0:T(8,128)(2,1)S(1)}, u32[]{:S(2)}, u32[]{:S(2)}) %collective-permute-start.9) | collective-permute-done | bytes 196640 | tf_op jit(solution)/shard_map/ppermute | solution.py:192
  40.3 1.6 %collective-permute-start.11 = (bf16[64,1536]{1,0:T(8,128)(2,1)S(1)}, bf16[64,1536]{1,0:T(8,128)(2,1)S(1)}, u32[]{:S(2)}, u32[]{:S(2)}) collective-permute-start(bf16[64,1536]{1,0:T(8,128)(2,1)S(1)} %add_convert_fusion.4.refs_14_), channel_id=1, source_target_pairs={{0,8},{4,12},{8,0},{12,4},{1,9},{5,13},{9,1},{13,5},{2,10},{6,14},... | collective-permute-start | bytes 589832 | tf_op jit(solution)/shard_map/ppermute | solution.py:192
  41.9 1.5 %collective-permute-start.10 = (bf16[64,1536]{1,0:T(8,128)(2,1)S(1)}, bf16[64,1536]{1,0:T(8,128)(2,1)S(1)}, u32[]{:S(2)}, u32[]{:S(2)}) collective-permute-start(bf16[64,1536]{1,0:T(8,128)(2,1)S(1)} %get-tuple-element.72), channel_id=1, source_target_pairs={{0,4},{4,0},{8,12},{12,8},{1,5},{5,1},{9,13},{13,9},{2,6},{6,2},{1... | collective-permute-start | bytes 589832 | tf_op jit(solution)/shard_map/ppermute | solution.py:192
  43.4 2.0 %shard_map.83 = (f32[64,1536]{1,0:T(8,128)S(1)}, bf16[64,1536]{1,0:T(8,128)(2,1)}, f32[64,1536]{1,0:T(8,128)S(1)}, bf16[64,1536]{1,0:T(8,128)(2,1)S(1)}) custom-call(s32[1]{0:T(128)} %bitcast.2.refs_0_, bf16[64,1536]{1,0:T(8,128)(2,1)S(1)} %pad_maximum_fusion.3.refs_1_.refs_0_.refs_4_, bf16[64,1536]{1,0:T(8,128)(2,1)S(1)} %collective-permute-done.3.refs_2_.refs_9_.refs_10_, ...), custom_call_target="tpu_custom_call" | custom-call | flops 805306368 | bytes 1024 | tf_op jit(solution)/shard_map/pallas_call | solution.py:21
  46.7 10.6 %collective-permute-done.15 = bf16[64,1536]{1,0:T(8,128)(2,1)S(1)} collective-permute-done((bf16[64,1536]{1,0:T(8,128)(2,1)S(1)}, bf16[64,1536]{1,0:T(8,128)(2,1)S(1)}, u32[]{:S(2)}, u32[]{:S(2)}) %collective-permute-start.15) | collective-permute-done | bytes 196640 | tf_op jit(solution)/shard_map/ppermute | solution.py:192
  57.9 1.8 %collective-permute-start.17 = (bf16[64,1536]{1,0:T(8,128)(2,1)}, bf16[64,1536]{1,0:T(8,128)(2,1)}, u32[]{:S(2)}, u32[]{:S(2)}) collective-permute-start(bf16[64,1536]{1,0:T(8,128)(2,1)} %get-tuple-element.92), channel_id=1, source_target_pairs={{0,4},{4,0},{8,12},{12,8},{1,5},{5,1},{9,13},{13,9},{2,6},{6,2},{1... | collective-permute-start | bytes 589832 | tf_op jit(solution)/shard_map/ppermute | solution.py:192
  60.6 2.1 %collective-permute-start.19 = (bf16[64,1536]{1,0:T(8,128)(2,1)}, bf16[64,1536]{1,0:T(8,128)(2,1)}, u32[]{:S(2)}, u32[]{:S(2)}) collective-permute-start(bf16[64,1536]{1,0:T(8,128)(2,1)} %get-tuple-element.93.refs_1_), channel_id=1, source_target_pairs={{0,8},{4,12},{8,0},{12,4},{1,9},{5,13},{9,1},{13,5},{2,10},{6,14},... | collective-permute-start | bytes 589832 | tf_op jit(solution)/shard_map/ppermute | solution.py:192
  63.6 6.6 %collective-permute-done.18.refs_5_ = bf16[64,1536]{1,0:T(8,128)(2,1)S(1)} collective-permute-done((bf16[64,1536]{1,0:T(8,128)(2,1)S(1)}, bf16[64,1536]{1,0:T(8,128)(2,1)S(1)}, u32[]{:S(2)}, u32[]{:S(2)}) %collective-permute-start.18) | collective-permute-done | bytes 196640 | tf_op jit(solution)/shard_map/ppermute | solution.py:192
  72.7 4.8 %collective-permute-done.19.refs_3_ = bf16[64,1536]{1,0:T(8,128)(2,1)} collective-permute-done((bf16[64,1536]{1,0:T(8,128)(2,1)}, bf16[64,1536]{1,0:T(8,128)(2,1)}, u32[]{:S(2)}, u32[]{:S(2)}) %collective-permute-start.19) | collective-permute-done | bytes 196640 | tf_op jit(solution)/shard_map/ppermute | solution.py:192
  78.1 1.0 copy-done.5
  79.1 1.0 copy-done.7
  81.0 1.1 shard_map.86
  82.3 1.1 collective-permute-done.21.refs_3_
  83.6 2.0 %collective-permute-start.22 = (bf16[64,1536]{1,0:T(8,128)(2,1)S(1)}, bf16[64,1536]{1,0:T(8,128)(2,1)S(1)}, u32[]{:S(2)}, u32[]{:S(2)}) collective-permute-start(bf16[64,1536]{1,0:T(8,128)(2,1)S(1)} %shard_map.87.refs_1_), channel_id=1, source_target_pairs={{0,8},{4,12},{8,0},{12,4},{1,9},{5,13},{9,1},{13,5},{2,10},{6,14},... | collective-permute-start | bytes 589832 | tf_op jit(solution)/shard_map/ppermute | solution.py:192
  85.6 1.1 collective-permute-start.23
  86.7 6.7 %collective-permute-done.24.refs_4_ = bf16[64,1536]{1,0:T(8,128)(2,1)S(1)} collective-permute-done((bf16[64,1536]{1,0:T(8,128)(2,1)}, bf16[64,1536]{1,0:T(8,128)(2,1)S(1)}, u32[]{:S(2)}, u32[]{:S(2)}) %collective-permute-start.24) | collective-permute-done | bytes 196640 | tf_op jit(solution)/shard_map/ppermute | solution.py:192
  93.4 2.5 %collective-permute-done.22.refs_3_ = bf16[64,1536]{1,0:T(8,128)(2,1)S(1)} collective-permute-done((bf16[64,1536]{1,0:T(8,128)(2,1)S(1)}, bf16[64,1536]{1,0:T(8,128)(2,1)S(1)}, u32[]{:S(2)}, u32[]{:S(2)}) %collective-permute-start.22) | collective-permute-done | bytes 196640 | tf_op jit(solution)/shard_map/ppermute | solution.py:192
  95.9 2.3 %collective-permute-done.23.refs_2_ = bf16[64,1536]{1,0:T(8,128)(2,1)S(1)} collective-permute-done((bf16[64,1536]{1,0:T(8,128)(2,1)S(1)}, bf16[64,1536]{1,0:T(8,128)(2,1)S(1)}, u32[]{:S(2)}, u32[]{:S(2)}) %collective-permute-start.23) | collective-permute-done | bytes 196640 | tf_op jit(solution)/shard_map/ppermute | solution.py:192
  99.3 1.8 %shard_map.89 = (f32[256,512]{1,0:T(8,128)S(1)}, bf16[256,512]{1,0:T(8,128)(2,1)S(1)}) custom-call(s32[1]{0:T(128)} %bitcast.2.refs_0_, bf16[64,1536]{1,0:T(8,128)(2,1)} %get-tuple-element.93.refs_1_, bf16[64,1536]{1,0:T(8,128)(2,1)} %collective-permute-done.20.refs_2_, bf16[64,1536]{1,0:T(8,128)(2,1)} %collective-permute-done.19.refs_3_, ...), custom_call_target="tpu_custom_call" | custom-call | flops 402653184 | bytes 1024 | tf_op jit(solution)/shard_map/pallas_call | solution.py:21
  102.8 4.5 %collective-permute-done.30 = bf16[128,512]{1,0:T(8,128)(2,1)S(1)} collective-permute-done((bf16[128,512]{1,0:T(8,128)(2,1)S(1)}, bf16[128,512]{1,0:T(8,128)(2,1)S(1)}, u32[]{:S(2)}, u32[]{:S(2)}) %collective-permute-start.30) | collective-permute-done | bytes 131104 | tf_op jit(solution)/shard_map/ppermute | solution.py:189
  110.4 4.1 %collective-permute-done.32 = bf16[128,512]{1,0:T(8,128)(2,1)S(1)} collective-permute-done((bf16[128,512]{1,0:T(8,128)(2,1)S(1)}, bf16[128,512]{1,0:T(8,128)(2,1)S(1)}, u32[]{:S(2)}, u32[]{:S(2)}) %collective-permute-start.32) | collective-permute-done | bytes 131104 | tf_op jit(solution)/shard_map/ppermute | solution.py:189
  114.5 2.3 %collective-permute-done.34 = bf16[128,512]{1,0:T(8,128)(2,1)S(1)} collective-permute-done((bf16[128,512]{1,0:T(8,128)(2,1)S(1)}, bf16[128,512]{1,0:T(8,128)(2,1)S(1)}, u32[]{:S(2)}, u32[]{:S(2)}) %collective-permute-start.34) | collective-permute-done | bytes 131104 | tf_op jit(solution)/shard_map/ppermute | solution.py:189
  117.0 1.0 pad_maximum_fusion
  (128 shorter events, 20.8 us)
Async XLA Ops:
  2.3 7.1 %collective-permute-start = (bf16[32,1280]{1,0:T(8,128)(2,1)S(1)}, bf16[32,1280]{1,0:T(8,128)(2,1)S(1)}, u32[]{:S(2)}, u32[]{:S(2)}) collective-permute-start(bf16[32,1280]{1,0:T(8,128)(2,1)S(1)} %get-tuple-element.142), channel_id=1, source_target_pairs={{0,2},{1,3},{2,0},{3,1},{4,6},{5,7},{6,4},{7,5},{8,10},{9,11},{10,... | collective-permute-start | bytes 245768 | tf_op jit(solution)/shard_map/ppermute | solution.py:189
  5.5 4.0 %collective-permute-start.1 = (bf16[32,256]{1,0:T(8,128)(2,1)S(1)}, bf16[32,256]{1,0:T(8,128)(2,1)S(1)}, u32[]{:S(2)}, u32[]{:S(2)}) collective-permute-start(bf16[32,256]{1,0:T(8,128)(2,1)S(1)} %select_n.178), channel_id=1, source_target_pairs={{0,1},{1,0},{2,3},{3,2},{4,5},{5,4},{6,7},{7,6},{8,9},{9,8},{10,11... | collective-permute-start | bytes 49160 | tf_op jit(solution)/shard_map/ppermute | solution.py:189
  5.7 3.9 %collective-permute-start.2 = (bf16[32,256]{1,0:T(8,128)(2,1)S(1)}, bf16[32,256]{1,0:T(8,128)(2,1)S(1)}, u32[]{:S(2)}, u32[]{:S(2)}) collective-permute-start(bf16[32,256]{1,0:T(8,128)(2,1)S(1)} %select_n.181), channel_id=1, source_target_pairs={{0,3},{1,2},{2,1},{3,0},{4,7},{5,6},{6,5},{7,4},{8,11},{9,10},{10,... | collective-permute-start | bytes 49160 | tf_op jit(solution)/shard_map/ppermute | solution.py:189
  9.7 15.1 %collective-permute-start.6 = (bf16[2,128,512]{2,1,0:T(8,128)(2,1)S(1)}, bf16[2,128,512]{2,1,0:T(8,128)(2,1)S(1)}, u32[]{:S(2)}, u32[]{:S(2)}) collective-permute-start(bf16[2,128,512]{2,1,0:T(8,128)(2,1)S(1)} %get-tuple-element.129), channel_id=1, source_target_pairs={{0,2},{1,3},{2,0},{3,1},{4,6},{5,7},{6,4},{7,5},{8,10},{9,11},{10,... | collective-permute-start | bytes 786440 | tf_op jit(solution)/shard_map/ppermute | solution.py:189
  11.7 10.6 %collective-permute-start.3 = (bf16[64,1536]{1,0:T(8,128)(2,1)S(1)}, bf16[64,1536]{1,0:T(8,128)(2,1)S(1)}, u32[]{:S(2)}, u32[]{:S(2)}) collective-permute-start(bf16[64,1536]{1,0:T(8,128)(2,1)S(1)} %pad_maximum_fusion.3.refs_1_.refs_0_.refs_4_), channel_id=1, source_target_pairs={{0,4},{4,0},{8,12},{12,8},{1,5},{5,1},{9,13},{13,9},{2,6},{6,2},{1... | collective-permute-start | bytes 589832 | tf_op jit(solution)/shard_map/ppermute | solution.py:192
  13.3 11.4 %collective-permute-start.4 = (bf16[64,1536]{1,0:T(8,128)(2,1)S(1)}, bf16[64,1536]{1,0:T(8,128)(2,1)S(1)}, u32[]{:S(2)}, u32[]{:S(2)}) collective-permute-start(bf16[64,1536]{1,0:T(8,128)(2,1)S(1)} %pad_maximum_fusion.3.refs_1_.refs_0_.refs_4_), channel_id=1, source_target_pairs={{0,8},{4,12},{8,0},{12,4},{1,9},{5,13},{9,1},{13,5},{2,10},{6,14},... | collective-permute-start | bytes 589832 | tf_op jit(solution)/shard_map/ppermute | solution.py:192
  15.9 9.6 %collective-permute-start.7 = (bf16[2,128,512]{2,1,0:T(8,128)(2,1)S(1)}, bf16[2,128,512]{2,1,0:T(8,128)(2,1)S(1)}, u32[]{:S(2)}, u32[]{:S(2)}) collective-permute-start(bf16[2,128,512]{2,1,0:T(8,128)(2,1)S(1)} %get-tuple-element.78.refs_5_.refs_9_), channel_id=1, source_target_pairs={{0,1},{1,0},{2,3},{3,2},{4,5},{5,4},{6,7},{7,6},{8,9},{9,8},{10,11... | collective-permute-start | bytes 786440 | tf_op jit(solution)/shard_map/ppermute | solution.py:189
  25.0 7.4 %collective-permute-start.5 = (bf16[64,1536]{1,0:T(8,128)(2,1)S(1)}, bf16[64,1536]{1,0:T(8,128)(2,1)S(1)}, u32[]{:S(2)}, u32[]{:S(2)}) collective-permute-start(bf16[64,1536]{1,0:T(8,128)(2,1)S(1)} %collective-permute-done.4.refs_3_.refs_11_), channel_id=1, source_target_pairs={{0,4},{4,0},{8,12},{12,8},{1,5},{5,1},{9,13},{13,9},{2,6},{6,2},{1... | collective-permute-start | bytes 589832 | tf_op jit(solution)/shard_map/ppermute | solution.py:192
  26.3 13.9 %collective-permute-start.12 = (bf16[2,128,512]{2,1,0:T(8,128)(2,1)S(1)}, bf16[2,128,512]{2,1,0:T(8,128)(2,1)S(1)}, u32[]{:S(2)}, u32[]{:S(2)}) collective-permute-start(bf16[2,128,512]{2,1,0:T(8,128)(2,1)S(1)} %get-tuple-element.125), channel_id=1, source_target_pairs={{0,2},{1,3},{2,0},{3,1},{4,6},{5,7},{6,4},{7,5},{8,10},{9,11},{10,... | collective-permute-start | bytes 786440 | tf_op jit(solution)/shard_map/ppermute | solution.py:189
  33.7 6.6 %collective-permute-start.9 = (bf16[64,1536]{1,0:T(8,128)(2,1)S(1)}, bf16[64,1536]{1,0:T(8,128)(2,1)S(1)}, u32[]{:S(2)}, u32[]{:S(2)}) collective-permute-start(bf16[64,1536]{1,0:T(8,128)(2,1)S(1)} %get-tuple-element.71), channel_id=1, source_target_pairs={{0,4},{4,0},{8,12},{12,8},{1,5},{5,1},{9,13},{13,9},{2,6},{6,2},{1... | collective-permute-start | bytes 589832 | tf_op jit(solution)/shard_map/ppermute | solution.py:192
  34.2 9.2 %collective-permute-start.13 = (bf16[2,128,512]{2,1,0:T(8,128)(2,1)S(1)}, bf16[2,128,512]{2,1,0:T(8,128)(2,1)S(1)}, u32[]{:S(2)}, u32[]{:S(2)}) collective-permute-start(bf16[2,128,512]{2,1,0:T(8,128)(2,1)S(1)} %get-tuple-element.104.refs_5_.refs_9_), channel_id=1, source_target_pairs={{0,1},{1,0},{2,3},{3,2},{4,5},{5,4},{6,7},{7,6},{8,9},{9,8},{10,11... | collective-permute-start | bytes 786440 | tf_op jit(solution)/shard_map/ppermute | solution.py:189
  40.3 3.2 %collective-permute-start.14 = (bf16[2,128,512]{2,1,0:T(8,128)(2,1)S(1)}, bf16[2,128,512]{2,1,0:T(8,128)(2,1)S(1)}, u32[]{:S(2)}, u32[]{:S(2)}) collective-permute-start(bf16[2,128,512]{2,1,0:T(8,128)(2,1)S(1)} %collective-permute-done.12.refs_6_.refs_10_), channel_id=1, source_target_pairs={{0,1},{1,0},{2,3},{3,2},{4,5},{5,4},{6,7},{7,6},{8,9},{9,8},{10,11... | collective-permute-start | bytes 786440 | tf_op jit(solution)/shard_map/ppermute | solution.py:189
  40.3 17.3 %collective-permute-start.11 = (bf16[64,1536]{1,0:T(8,128)(2,1)S(1)}, bf16[64,1536]{1,0:T(8,128)(2,1)S(1)}, u32[]{:S(2)}, u32[]{:S(2)}) collective-permute-start(bf16[64,1536]{1,0:T(8,128)(2,1)S(1)} %add_convert_fusion.4.refs_14_), channel_id=1, source_target_pairs={{0,8},{4,12},{8,0},{12,4},{1,9},{5,13},{9,1},{13,5},{2,10},{6,14},... | collective-permute-start | bytes 589832 | tf_op jit(solution)/shard_map/ppermute | solution.py:192
  41.9 15.7 %collective-permute-start.10 = (bf16[64,1536]{1,0:T(8,128)(2,1)S(1)}, bf16[64,1536]{1,0:T(8,128)(2,1)S(1)}, u32[]{:S(2)}, u32[]{:S(2)}) collective-permute-start(bf16[64,1536]{1,0:T(8,128)(2,1)S(1)} %get-tuple-element.72), channel_id=1, source_target_pairs={{0,4},{4,0},{8,12},{12,8},{1,5},{5,1},{9,13},{13,9},{2,6},{6,2},{1... | collective-permute-start | bytes 589832 | tf_op jit(solution)/shard_map/ppermute | solution.py:192
  45.4 11.9 %collective-permute-start.15 = (bf16[64,1536]{1,0:T(8,128)(2,1)S(1)}, bf16[64,1536]{1,0:T(8,128)(2,1)S(1)}, u32[]{:S(2)}, u32[]{:S(2)}) collective-permute-start(bf16[64,1536]{1,0:T(8,128)(2,1)S(1)} %get-tuple-element.85), channel_id=1, source_target_pairs={{0,4},{4,0},{8,12},{12,8},{1,5},{5,1},{9,13},{13,9},{2,6},{6,2},{1... | collective-permute-start | bytes 589832 | tf_op jit(solution)/shard_map/ppermute | solution.py:192
  46.2 17.4 %collective-permute-start.26 = (bf16[3,128,512]{2,1,0:T(8,128)(2,1)S(1)}, bf16[3,128,512]{2,1,0:T(8,128)(2,1)S(1)}, u32[]{:S(2)}, u32[]{:S(2)}) collective-permute-start(bf16[3,128,512]{2,1,0:T(8,128)(2,1)S(1)} %get-tuple-element.121), channel_id=1, source_target_pairs={{0,2},{1,3},{2,0},{3,1},{4,6},{5,7},{6,4},{7,5},{8,10},{9,11},{10,... | collective-permute-start | bytes 1179656 | tf_op jit(solution)/shard_map/ppermute | solution.py:189
  57.3 12.9 %collective-permute-start.18 = (bf16[64,1536]{1,0:T(8,128)(2,1)S(1)}, bf16[64,1536]{1,0:T(8,128)(2,1)S(1)}, u32[]{:S(2)}, u32[]{:S(2)}) collective-permute-start(bf16[64,1536]{1,0:T(8,128)(2,1)S(1)} %add_convert_fusion.3.refs_5_), channel_id=1, source_target_pairs={{0,8},{4,12},{8,0},{12,4},{1,9},{5,13},{9,1},{13,5},{2,10},{6,14},... | collective-permute-start | bytes 589832 | tf_op jit(solution)/shard_map/ppermute | solution.py:192
  57.8 1.9 %collective-permute-start.16 = (f32[64,128]{1,0:T(8,128)S(1)}, f32[64,128]{1,0:T(8,128)S(1)}, u32[]{:S(2)}, u32[]{:S(2)}) collective-permute-start(f32[64,128]{1,0:T(8,128)S(1)} %get-tuple-element.88.refs_2_), channel_id=1, source_target_pairs={{0,1},{1,0},{2,3},{3,2},{4,5},{5,4},{6,7},{7,6},{8,9},{9,8},{10,11... | collective-permute-start | bytes 98312 | tf_op jit(solution)/shard_map/ppermute | solution.py:189
  57.9 14.7 %collective-permute-start.17 = (bf16[64,1536]{1,0:T(8,128)(2,1)}, bf16[64,1536]{1,0:T(8,128)(2,1)}, u32[]{:S(2)}, u32[]{:S(2)}) collective-permute-start(bf16[64,1536]{1,0:T(8,128)(2,1)} %get-tuple-element.92), channel_id=1, source_target_pairs={{0,4},{4,0},{8,12},{12,8},{1,5},{5,1},{9,13},{13,9},{2,6},{6,2},{1... | collective-permute-start | bytes 589832 | tf_op jit(solution)/shard_map/ppermute | solution.py:192
  60.6 16.9 %collective-permute-start.19 = (bf16[64,1536]{1,0:T(8,128)(2,1)}, bf16[64,1536]{1,0:T(8,128)(2,1)}, u32[]{:S(2)}, u32[]{:S(2)}) collective-permute-start(bf16[64,1536]{1,0:T(8,128)(2,1)} %get-tuple-element.93.refs_1_), channel_id=1, source_target_pairs={{0,8},{4,12},{8,0},{12,4},{1,9},{5,13},{9,1},{13,5},{2,10},{6,14},... | collective-permute-start | bytes 589832 | tf_op jit(solution)/shard_map/ppermute | solution.py:192
  62.7 15.3 %collective-permute-start.20 = (bf16[64,1536]{1,0:T(8,128)(2,1)}, bf16[64,1536]{1,0:T(8,128)(2,1)}, u32[]{:S(2)}, u32[]{:S(2)}) collective-permute-start(bf16[64,1536]{1,0:T(8,128)(2,1)} %get-tuple-element.93.refs_1_), channel_id=1, source_target_pairs={{0,4},{4,0},{8,12},{12,8},{1,5},{5,1},{9,13},{13,9},{2,6},{6,2},{1... | collective-permute-start | bytes 589832 | tf_op jit(solution)/shard_map/ppermute | solution.py:192
  63.6 34.6 %collective-permute-start.27 = (bf16[3,128,512]{2,1,0:T(8,128)(2,1)S(1)}, bf16[3,128,512]{2,1,0:T(8,128)(2,1)S(1)}, u32[]{:S(2)}, u32[]{:S(2)}) collective-permute-start(bf16[3,128,512]{2,1,0:T(8,128)(2,1)S(1)} %get-tuple-element.102.refs_5_), channel_id=1, source_target_pairs={{0,1},{1,0},{2,3},{3,2},{4,5},{5,4},{6,7},{7,6},{8,9},{9,8},{10,11... | collective-permute-start | bytes 1179656 | tf_op jit(solution)/shard_map/ppermute | solution.py:189
  70.9 27.3 %collective-permute-start.28 = (bf16[3,128,512]{2,1,0:T(8,128)(2,1)S(1)}, bf16[3,128,512]{2,1,0:T(8,128)(2,1)S(1)}, u32[]{:S(2)}, u32[]{:S(2)}) collective-permute-start(bf16[3,128,512]{2,1,0:T(8,128)(2,1)S(1)} %collective-permute-done.26.refs_6_), channel_id=1, source_target_pairs={{0,1},{1,0},{2,3},{3,2},{4,5},{5,4},{6,7},{7,6},{8,9},{9,8},{10,11... | collective-permute-start | bytes 1179656 | tf_op jit(solution)/shard_map/ppermute | solution.py:189
  82.2 11.2 %collective-permute-start.24 = (bf16[64,1536]{1,0:T(8,128)(2,1)}, bf16[64,1536]{1,0:T(8,128)(2,1)S(1)}, u32[]{:S(2)}, u32[]{:S(2)}) collective-permute-start(bf16[64,1536]{1,0:T(8,128)(2,1)} %collective-permute-done.19.refs_3_), channel_id=1, source_target_pairs={{0,4},{4,0},{8,12},{12,8},{1,5},{5,1},{9,13},{13,9},{2,6},{6,2},{1... | collective-permute-start | bytes 589832 | tf_op jit(solution)/shard_map/ppermute | solution.py:192
  83.6 12.3 %collective-permute-start.22 = (bf16[64,1536]{1,0:T(8,128)(2,1)S(1)}, bf16[64,1536]{1,0:T(8,128)(2,1)S(1)}, u32[]{:S(2)}, u32[]{:S(2)}) collective-permute-start(bf16[64,1536]{1,0:T(8,128)(2,1)S(1)} %shard_map.87.refs_1_), channel_id=1, source_target_pairs={{0,8},{4,12},{8,0},{12,4},{1,9},{5,13},{9,1},{13,5},{2,10},{6,14},... | collective-permute-start | bytes 589832 | tf_op jit(solution)/shard_map/ppermute | solution.py:192
  85.6 12.6 %collective-permute-start.23 = (bf16[64,1536]{1,0:T(8,128)(2,1)S(1)}, bf16[64,1536]{1,0:T(8,128)(2,1)S(1)}, u32[]{:S(2)}, u32[]{:S(2)}) collective-permute-start(bf16[64,1536]{1,0:T(8,128)(2,1)S(1)} %shard_map.87.refs_1_), channel_id=1, source_target_pairs={{0,4},{4,0},{8,12},{12,8},{1,5},{5,1},{9,13},{13,9},{2,6},{6,2},{1... | collective-permute-start | bytes 589832 | tf_op jit(solution)/shard_map/ppermute | solution.py:192
  98.8 2.5 %collective-permute-start.29 = (bf16[256,512]{1,0:T(8,128)(2,1)S(1)}, bf16[256,512]{1,0:T(8,128)(2,1)S(1)}, u32[]{:S(2)}, u32[]{:S(2)}) collective-permute-start(bf16[256,512]{1,0:T(8,128)(2,1)S(1)} %get-tuple-element.110), channel_id=1, source_target_pairs={{0,1},{1,0},{2,3},{3,2},{4,5},{5,4},{6,7},{7,6},{8,9},{9,8},{10,11... | collective-permute-start | bytes 786440 | tf_op jit(solution)/shard_map/ppermute | solution.py:189
  98.9 8.4 %collective-permute-start.25 = (bf16[64,1536]{1,0:T(8,128)(2,1)S(1)}, bf16[64,1536]{1,0:T(8,128)(2,1)S(1)}, u32[]{:S(2)}, u32[]{:S(2)}) collective-permute-start(bf16[64,1536]{1,0:T(8,128)(2,1)S(1)} %collective-permute-done.22.refs_3_), channel_id=1, source_target_pairs={{0,4},{4,0},{8,12},{12,8},{1,5},{5,1},{9,13},{13,9},{2,6},{6,2},{1... | collective-permute-start | bytes 589832 | tf_op jit(solution)/shard_map/ppermute | solution.py:192
  101.1 1.6 %collective-permute-start.31 = (bf16[256,512]{1,0:T(8,128)(2,1)S(1)}, bf16[256,512]{1,0:T(8,128)(2,1)S(1)}, u32[]{:S(2)}, u32[]{:S(2)}) collective-permute-start(bf16[256,512]{1,0:T(8,128)(2,1)S(1)} %get-tuple-element.114), channel_id=1, source_target_pairs={{0,1},{1,0},{2,3},{3,2},{4,5},{5,4},{6,7},{7,6},{8,9},{9,8},{10,11... | collective-permute-start | bytes 786440 | tf_op jit(solution)/shard_map/ppermute | solution.py:189
  101.4 5.8 %collective-permute-start.30 = (bf16[128,512]{1,0:T(8,128)(2,1)S(1)}, bf16[128,512]{1,0:T(8,128)(2,1)S(1)}, u32[]{:S(2)}, u32[]{:S(2)}) collective-permute-start(bf16[128,512]{1,0:T(8,128)(2,1)S(1)} %get-tuple-element.138), channel_id=1, source_target_pairs={{0,2},{1,3},{2,0},{3,1},{4,6},{5,7},{6,4},{7,5},{8,10},{9,11},{10,... | collective-permute-start | bytes 393224 | tf_op jit(solution)/shard_map/ppermute | solution.py:189
  108.1 6.4 %collective-permute-start.32 = (bf16[128,512]{1,0:T(8,128)(2,1)S(1)}, bf16[128,512]{1,0:T(8,128)(2,1)S(1)}, u32[]{:S(2)}, u32[]{:S(2)}) collective-permute-start(bf16[128,512]{1,0:T(8,128)(2,1)S(1)} %get-tuple-element.134), channel_id=1, source_target_pairs={{0,2},{1,3},{2,0},{3,1},{4,6},{5,7},{6,4},{7,5},{8,10},{9,11},{10,... | collective-permute-start | bytes 393224 | tf_op jit(solution)/shard_map/ppermute | solution.py:189
  109.7 7.2 %collective-permute-start.34 = (bf16[128,512]{1,0:T(8,128)(2,1)S(1)}, bf16[128,512]{1,0:T(8,128)(2,1)S(1)}, u32[]{:S(2)}, u32[]{:S(2)}) collective-permute-start(bf16[128,512]{1,0:T(8,128)(2,1)S(1)} %get-tuple-element.136), channel_id=1, source_target_pairs={{0,2},{1,3},{2,0},{3,1},{4,6},{5,7},{6,4},{7,5},{8,10},{9,11},{10,... | collective-permute-start | bytes 393224 | tf_op jit(solution)/shard_map/ppermute | solution.py:189
  (20 other events, 101.3 us)

commit v10 on v9

--- a/solution.py
+++ b/solution.py
@@ -111,59 +111,65 @@
     return columns
 
 
-def moved_kernel(got, old, momentum, decay, new_momentum, moved, sums):
-    rows, columns = old.shape
-    width = columns // 3
+def sums_of(array, width):
+    parts = [array[:, m * width : (m + 1) * width] for m in range(2)]
+    parts = [jnp.sum(p * p, axis=1, keepdims=True) for p in parts] + square_sums(array, width)
+    return jnp.concatenate(parts + [jnp.zeros((array.shape[0], 124), WIDE)], axis=1)
+
+
+def first_moved_kernel(old, *refs):
+    got, (momentum, moved, sums) = refs[:-3], refs[-3:]
+    rows, width = old.shape[0], old.shape[1] // 3
     total = got[0][...].astype(WIDE)
     for part in got[1:]:
         total = total + part[...].astype(WIDE)
     before = old[...].astype(WIDE)
-    if momentum is not None:
-        total = decay[0:1, 0:1] * momentum[...] + total
-    after = before + total
-    if new_momentum is not None:
-        new_momentum[...] = total
-    moved[...] = after
-    parts = square_sums(after, width) + square_sums(before, width)
-    sums[...] = jnp.concatenate(parts + [jnp.zeros((rows, 124), WIDE)], axis=1)
-
-
-def first_moved_kernel(old, *refs):
-    moved_kernel(refs[:-3], old, None, None, *refs[-3:])
-
-
-def second_moved_kernel(old, momentum, decay, *refs):
-    moved_kernel(refs[:-2], old, momentum, decay, None, *refs[-2:])
-
-
-def scaled_kernel(moved, old, own_sums, far_sums, new, payload):
-    rows, columns = payload.shape
-    width = columns // 3
-    half = width // 2
-    after = moved[...]
-    before = old[...].astype(WIDE)
-    sums = own_sums[...] + far_sums[...]
-
-    def factor(old_sum, moved_sum):
-        return jnp.sqrt(old_sum + 1e-06) / jnp.sqrt(moved_sum + 1e-06)
-
-    pieces = []
-    for m in range(2):
-        a = after[:, m * width : (m + 1) * width]
-        b = before[:, m * width : (m + 1) * width]
-        old_sum = jnp.sum(b * b, axis=1, keepdims=True)
-        pieces.append(a * factor(old_sum, jnp.sum(a * a, axis=1, keepdims=True)))
-    for y in range(2):
-        a = after[:, 2 * width + y * half : 2 * width + (y + 1) * half]
-        pieces.append(a * factor(sums[:, y + 2 : y + 3], sums[:, y : y + 1]))
-    result = jnp.concatenate(pieces, axis=1)
-    if new is not None:
-        new[...] = result
+    after_step = before + total
+    momentum[...] = total
+    moved[...] = after_step
+    sums[:rows, :] = sums_of(after_step, width)
+    sums[rows:, :] = sums_of(before, width)
+
+
+def second_moved_kernel(base, *refs):
+    got, (moved, sums) = refs[:-2], refs[-2:]
+    total = base[...]
+    for part in got:
+        total = total + part[...].astype(WIDE)
+    moved[...] = total
+    sums[...] = sums_of(total, total.shape[1] // 3)
+
+
+def factors(sums, far_sums, old_sums, far_old_sums):
+    def whole(mine, far, m):
+        return mine[:, m : m + 1] + (far[:, m : m + 1] if m > 1 else 0.0)
+
+    return [
+        jnp.sqrt(whole(old_sums, far_old_sums, m) + 1e-06)
+        / jnp.sqrt(whole(sums, far_sums, m) + 1e-06)
+        for m in range(4)
+    ]
+
+
+def rescaled(moved, scales):
+    width = moved.shape[1] // 3
+    half = width // 2
+    edges = [0, width, 2 * width, 2 * width + half, 3 * width]
+    pieces = [moved[:, edges[m] : edges[m + 1]] * scales[m] for m in range(4)]
+    return jnp.concatenate(pieces, axis=1)
+
+
+def scaled_kernel(moved, momentum, decay, part, sums, far, base, payload, new_sums):
+    rows = moved.shape[0]
+    new, old = slice(0, rows), slice(rows, None)
+    result = rescaled(moved, factors(sums[new], far[new], sums[old], far[old]))
     payload[...] = result.astype(LOW)
-
-
-def last_scaled_kernel(moved, old, own_sums, far_sums, payload):
-    scaled_kernel(moved, old, own_sums, far_sums, None, payload)
+    new_sums[...] = sums_of(result, result.shape[1] // 3)
+    base[...] = result + (decay[0:1, 0:1] * momentum[...] + part[...])
+
+
+def last_scaled_kernel(moved, sums, far, old, far_old, payload):
+    payload[...] = rescaled(moved, factors(sums, far, old, far_old)).astype(LOW)
 
 
 def shards(
@@ -320,39 +326,45 @@
     behind["new0"].extend(sent.values())
 
     sums_shape = (rows, 128)
+    flat_sums = [(sums_shape, WIDE)]
     step_zero, moved, sums = call(
         first_moved_kernel,
-        [(flat, WIDE), (flat, WIDE), (sums_shape, WIDE)],
+        [(flat, WIDE), (flat, WIDE), ((2 * rows, 128), WIDE)],
         0,
         zero,
         *got_zero,
         behind=behind["new0"],
     )
-    weights_one, payload = call(
-        scaled_kernel, [(flat, WIDE), (flat, LOW)], 0, moved, zero, sums, send(sums, 1)
-    )
+    decay = jnp.broadcast_to(jnp.where(y == 0, momentum_decay[0], momentum_decay[1]), (8, 128))
+    base, payload, old_sums = call(
+        scaled_kernel,
+        [(flat, WIDE), (flat, LOW)] + flat_sums,
+        0,
+        moved,
+        step_zero,
+        decay,
+        got_one[0],
+        sums,
+        send(sums, 1),
+    )
+    half_way = planes // 2
     first_one = spread(payload)
     direct_one = to_plane(payload, 1)
     queries = to_quad(
-        after(query_tokens, pairs[1], behind["out0"]), [weights_one], behind["out0"]
-    )
-
-    half_way = planes // 2
-    waited = (got_one, first_one[half_way], direct_one)
-    got_one, first_one[half_way], direct_one = lax.optimization_barrier(waited)
-    decay = jnp.broadcast_to(jnp.where(y == 0, momentum_decay[0], momentum_decay[1]), (8, 128))
+        after(query_tokens, pairs[1], behind["out0"]), [old_sums], behind["out0"]
+    )
+    far_old = send(old_sums, 1)
     moved, sums = call(
         second_moved_kernel,
-        [(flat, WIDE), (sums_shape, WIDE)],
+        [(flat, WIDE)] + flat_sums,
         0,
-        weights_one,
-        step_zero,
-        decay,
-        *got_one,
+        base,
+        *got_one[1:],
         behind=behind["new1"],
     )
-    far_sums = send(sums, 1)
-    payload = call(last_scaled_kernel, [(flat, LOW)], 0, moved, weights_one, sums, far_sums)[0]
+    waited = (send(sums, 1), first_one[half_way], direct_one)
+    far, first_one[half_way], direct_one = lax.optimization_barrier(waited)
+    payload = call(last_scaled_kernel, [(flat, LOW)], 0, moved, sums, far, old_sums, far_old)[0]
     first_two = spread(payload)
     direct_two = to_plane(payload, 1)
     full_one = spread_on(first_one)

time: 118 us -> 110 us (0.932)
  waiting for transfers between devices: 68.9 us -> 61.9 us
  Pallas kernels: 8.73 us -> 6.82 us
  starting transfers between devices: 26.2 us -> 27.8 us
  local copies, waits for them, and re-layouts: 9.97 us -> 8.77 us
    ppermute x15, waiting for transfers between devices: 54.5 us -> 48.1 us  [to_plane(): return lax.ppermute(array, 'plane', [(z, z ^ bit) for z in range(planes)])]
    pallas_call x9, Pallas kernels: 8.73 us -> 6.82 us  [call(): pl.pallas_call(kernel, out_shape=shapes, in_specs=[pl.BlockSpec(memory_sp...]
    ppermute x15, starting transfers between devices: 17.4 us -> 19.3 us  [to_plane(): return lax.ppermute(array, 'plane', [(z, z ^ bit) for z in range(planes)])]
    ppermute x20 -> x21, waiting for transfers between devices: 14.4 us -> 13.8 us  [send(): return lax.ppermute(array, 'quad', [(q, q ^ offset) for q in range(4)])]
    unnamed x34 -> x26, local copies, waits for them, and re-layouts: 5.12 us -> 5.45 us
    ppermute x20 -> x21, starting transfers between devices: 8.77 us -> 8.46 us  [send(): return lax.ppermute(array, 'quad', [(q, q ^ offset) for q in range(4)])]
  transfers between devices with their start and end apart: 35 -> 36, of which waited for: 18 -> 18; matrix products, arithmetic and copies ran while one was open for 3% -> 4% of each run, Pallas kernels for 6% -> 5%
where the time goes in v10:
time: 110 us
  waiting for transfers between devices  61.9 us (56%)
  starting transfers between devices  27.8 us (25%)
  local copies, waits for them, and re-layouts  8.77 us (8%)
  Pallas kernels  6.82 us (6%)
  other arithmetic  3.22 us (3%)
  between operations  1.71 us (2%)
    ppermute x15, waiting for transfers between devices, to_plane(): return lax.ppermute(array, 'plane', [(z, z ^ bit) for z in range(planes)])  48.1 us
    ppermute x15, starting transfers between devices, to_plane(): return lax.ppermute(array, 'plane', [(z, z ^ bit) for z in range(planes)])  19.3 us
    ppermute x21, waiting for transfers between devices, send(): return lax.ppermute(array, 'quad', [(q, q ^ offset) for q in range(4)])  13.8 us
    ppermute x21, starting transfers between devices, send(): return lax.ppermute(array, 'quad', [(q, q ^ offset) for q in range(4)])  8.46 us
    pallas_call x9, Pallas kernels, call(): pl.pallas_call(kernel, out_shape=shapes, in_specs=[pl.BlockSpec(memory_sp...  6.82 us
    unnamed x26, local copies, waits for them, and re-layouts  5.45 us
  transfers between devices with their start and end apart: 36, of which 18 were waited for; matrix products, arithmetic and copies ran while one was open for 4% of the time, Pallas kernels for 5%

profile of v10, /device:TPU:0, one launch (start us, length us, event | category | flops | bytes accessed | tf_op | source)
XLA Modules:
  0.0 110.2 jit_solution(769447431081339167)
XLA Ops:
  2.3 3.0 %collective-permute-start = (bf16[32,1280]{1,0:T(8,128)(2,1)S(1)}, bf16[32,1280]{1,0:T(8,128)(2,1)S(1)}, u32[]{:S(2)}, u32[]{:S(2)}) collective-permute-start(bf16[32,1280]{1,0:T(8,128)(2,1)S(1)} %get-tuple-element.140), channel_id=1, source_target_pairs={{0,2},{1,3},{2,0},{3,1},{4,6},{5,7},{6,4},{7,5},{8,10},{9,11},{10,... | collective-permute-start | bytes 245768 | tf_op jit(solution)/shard_map/ppermute | solution.py:195
  6.6 0.9 reshape.145
  8.8 1.6 %collective-permute-start.6 = (bf16[2,128,512]{2,1,0:T(8,128)(2,1)S(1)}, bf16[2,128,512]{2,1,0:T(8,128)(2,1)S(1)}, u32[]{:S(2)}, u32[]{:S(2)}) collective-permute-start(bf16[2,128,512]{2,1,0:T(8,128)(2,1)S(1)} %get-tuple-element.127), channel_id=1, source_target_pairs={{0,2},{1,3},{2,0},{3,1},{4,6},{5,7},{6,4},{7,5},{8,10},{9,11},{10,... | collective-permute-start | bytes 786440 | tf_op jit(solution)/shard_map/ppermute | solution.py:195
  10.5 2.6 %collective-permute-start.4 = (bf16[64,1536]{1,0:T(8,128)(2,1)S(1)}, bf16[64,1536]{1,0:T(8,128)(2,1)S(1)}, u32[]{:S(2)}, u32[]{:S(2)}) collective-permute-start(bf16[64,1536]{1,0:T(8,128)(2,1)S(1)} %pad_maximum_fusion.3.refs_1_.refs_0_.refs_4_), channel_id=1, source_target_pairs={{0,8},{4,12},{8,0},{12,4},{1,9},{5,13},{9,1},{13,5},{2,10},{6,14},... | collective-permute-start | bytes 589832 | tf_op jit(solution)/shard_map/ppermute | solution.py:198
  13.1 1.6 %collective-permute-start.3 = (bf16[64,1536]{1,0:T(8,128)(2,1)S(1)}, bf16[64,1536]{1,0:T(8,128)(2,1)S(1)}, u32[]{:S(2)}, u32[]{:S(2)}) collective-permute-start(bf16[64,1536]{1,0:T(8,128)(2,1)S(1)} %pad_maximum_fusion.3.refs_1_.refs_0_.refs_4_), channel_id=1, source_target_pairs={{0,4},{4,0},{8,12},{12,8},{1,5},{5,1},{9,13},{13,9},{2,6},{6,2},{1... | collective-permute-start | bytes 589832 | tf_op jit(solution)/shard_map/ppermute | solution.py:198
  14.7 7.6 %collective-permute-done.4.refs_3_.refs_11_ = bf16[64,1536]{1,0:T(8,128)(2,1)S(1)} collective-permute-done((bf16[64,1536]{1,0:T(8,128)(2,1)S(1)}, bf16[64,1536]{1,0:T(8,128)(2,1)S(1)}, u32[]{:S(2)}, u32[]{:S(2)}) %collective-permute-start.4) | collective-permute-done | bytes 196640 | tf_op jit(solution)/shard_map/ppermute | solution.py:198
  22.7 1.5 %collective-permute-start.5 = (bf16[64,1536]{1,0:T(8,128)(2,1)S(1)}, bf16[64,1536]{1,0:T(8,128)(2,1)S(1)}, u32[]{:S(2)}, u32[]{:S(2)}) collective-permute-start(bf16[64,1536]{1,0:T(8,128)(2,1)S(1)} %collective-permute-done.4.refs_3_.refs_11_), channel_id=1, source_target_pairs={{0,4},{4,0},{8,12},{12,8},{1,5},{5,1},{9,13},{13,9},{2,6},{6,2},{1... | collective-permute-start | bytes 589832 | tf_op jit(solution)/shard_map/ppermute | solution.py:198
  24.8 5.2 %collective-permute-done.5.refs_4_ = bf16[64,1536]{1,0:T(8,128)(2,1)S(1)} collective-permute-done((bf16[64,1536]{1,0:T(8,128)(2,1)S(1)}, bf16[64,1536]{1,0:T(8,128)(2,1)S(1)}, u32[]{:S(2)}, u32[]{:S(2)}) %collective-permute-start.5) | collective-permute-done | bytes 196640 | tf_op jit(solution)/shard_map/ppermute | solution.py:198
  30.1 1.3 %shard_map.82 = (f32[64,1536]{1,0:T(8,128)S(1)}, bf16[64,1536]{1,0:T(8,128)(2,1)S(1)}, f32[64,1536]{1,0:T(8,128)S(1)}, bf16[64,1536]{1,0:T(8,128)(2,1)S(1)}) custom-call(s32[1]{0:T(128)} %bitcast.2.refs_0_, bf16[64,1536]{1,0:T(8,128)(2,1)S(1)} %pad_maximum_fusion.3.refs_1_.refs_0_.refs_4_, ...), custom_call_target="tpu_custom_call" | custom-call | flops 805306368 | bytes 1024 | tf_op jit(solution)/shard_map/pallas_call | solution.py:21
  31.4 1.5 %collective-permute-start.9 = (bf16[64,1536]{1,0:T(8,128)(2,1)S(1)}, bf16[64,1536]{1,0:T(8,128)(2,1)S(1)}, u32[]{:S(2)}, u32[]{:S(2)}) collective-permute-start(bf16[64,1536]{1,0:T(8,128)(2,1)S(1)} %get-tuple-element.70), channel_id=1, source_target_pairs={{0,4},{4,0},{8,12},{12,8},{1,5},{5,1},{9,13},{13,9},{2,6},{6,2},{1... | collective-permute-start | bytes 589832 | tf_op jit(solution)/shard_map/ppermute | solution.py:198
  32.9 5.1 %collective-permute-done.9.refs_13_ = bf16[64,1536]{1,0:T(8,128)(2,1)S(1)} collective-permute-done((bf16[64,1536]{1,0:T(8,128)(2,1)S(1)}, bf16[64,1536]{1,0:T(8,128)(2,1)S(1)}, u32[]{:S(2)}, u32[]{:S(2)}) %collective-permute-start.9) | collective-permute-done | bytes 196640 | tf_op jit(solution)/shard_map/ppermute | solution.py:198
  38.0 1.4 %collective-permute-start.10 = (bf16[64,1536]{1,0:T(8,128)(2,1)S(1)}, bf16[64,1536]{1,0:T(8,128)(2,1)S(1)}, u32[]{:S(2)}, u32[]{:S(2)}) collective-permute-start(bf16[64,1536]{1,0:T(8,128)(2,1)S(1)} %get-tuple-element.71), channel_id=1, source_target_pairs={{0,4},{4,0},{8,12},{12,8},{1,5},{5,1},{9,13},{13,9},{2,6},{6,2},{1... | collective-permute-start | bytes 589832 | tf_op jit(solution)/shard_map/ppermute | solution.py:198
  39.5 2.4 %collective-permute-start.11 = (bf16[64,1536]{1,0:T(8,128)(2,1)S(1)}, bf16[64,1536]{1,0:T(8,128)(2,1)S(1)}, u32[]{:S(2)}, u32[]{:S(2)}) collective-permute-start(bf16[64,1536]{1,0:T(8,128)(2,1)S(1)} %add_convert_fusion.4.refs_14_), channel_id=1, source_target_pairs={{0,8},{4,12},{8,0},{12,4},{1,9},{5,13},{9,1},{13,5},{2,10},{6,14},... | collective-permute-start | bytes 589832 | tf_op jit(solution)/shard_map/ppermute | solution.py:198
  41.8 2.0 %shard_map.83 = (f32[64,1536]{1,0:T(8,128)S(1)}, bf16[64,1536]{1,0:T(8,128)(2,1)}, f32[64,1536]{1,0:T(8,128)S(1)}, bf16[64,1536]{1,0:T(8,128)(2,1)S(1)}) custom-call(s32[1]{0:T(128)} %bitcast.2.refs_0_, bf16[64,1536]{1,0:T(8,128)(2,1)S(1)} %pad_maximum_fusion.3.refs_1_.refs_0_.refs_4_, bf16[64,1536]{1,0:T(8,128)(2,1)S(1)} %collective-permute-done.3.refs_2_.refs_9_.refs_10_, ...), custom_call_target="tpu_custom_call" | custom-call | flops 805306368 | bytes 1024 | tf_op jit(solution)/shard_map/pallas_call | solution.py:21
  45.6 7.9 %collective-permute-done.15 = bf16[64,1536]{1,0:T(8,128)(2,1)S(1)} collective-permute-done((bf16[64,1536]{1,0:T(8,128)(2,1)S(1)}, bf16[64,1536]{1,0:T(8,128)(2,1)S(1)}, u32[]{:S(2)}, u32[]{:S(2)}) %collective-permute-start.15) | collective-permute-done | bytes 196640 | tf_op jit(solution)/shard_map/ppermute | solution.py:198
  53.5 1.0 collective-permute-start.18
  56.3 1.3 %collective-permute-start.17 = (bf16[64,1536]{1,0:T(8,128)(2,1)}, bf16[64,1536]{1,0:T(8,128)(2,1)}, u32[]{:S(2)}, u32[]{:S(2)}) collective-permute-start(bf16[64,1536]{1,0:T(8,128)(2,1)} %get-tuple-element.91), channel_id=1, source_target_pairs={{0,4},{4,0},{8,12},{12,8},{1,5},{5,1},{9,13},{13,9},{2,6},{6,2},{1... | collective-permute-start | bytes 589832 | tf_op jit(solution)/shard_map/ppermute | solution.py:198
  59.4 1.0 copy-done.1
  60.4 1.0 copy-done.3
  62.4 2.0 %collective-permute-start.20 = (bf16[64,1536]{1,0:T(8,128)(2,1)S(1)}, bf16[64,1536]{1,0:T(8,128)(2,1)S(1)}, u32[]{:S(2)}, u32[]{:S(2)}) collective-permute-start(bf16[64,1536]{1,0:T(8,128)(2,1)S(1)} %get-tuple-element.94.refs_1_), channel_id=1, source_target_pairs={{0,8},{4,12},{8,0},{12,4},{1,9},{5,13},{9,1},{13,5},{2,10},{6,14},... | collective-permute-start | bytes 589832 | tf_op jit(solution)/shard_map/ppermute | solution.py:198
  64.9 7.2 %collective-permute-done.17.refs_1_ = bf16[64,1536]{1,0:T(8,128)(2,1)} collective-permute-done((bf16[64,1536]{1,0:T(8,128)(2,1)}, bf16[64,1536]{1,0:T(8,128)(2,1)}, u32[]{:S(2)}, u32[]{:S(2)}) %collective-permute-start.17) | collective-permute-done | bytes 196640 | tf_op jit(solution)/shard_map/ppermute | solution.py:198
  72.0 1.1 shard_map.86
  73.2 1.2 %collective-permute-done.19.refs_2_ = f32[64,128]{1,0:T(8,128)S(1)} collective-permute-done((f32[64,128]{1,0:T(8,128)S(1)}, f32[64,128]{1,0:T(8,128)S(1)}, u32[]{:S(2)}, u32[]{:S(2)}) %collective-permute-start.19) | collective-permute-done | bytes 32800 | tf_op jit(solution)/shard_map/ppermute | solution.py:195
  74.5 1.8 %collective-permute-done.21.refs_2_ = bf16[64,1536]{1,0:T(8,128)(2,1)S(1)} collective-permute-done((bf16[64,1536]{1,0:T(8,128)(2,1)S(1)}, bf16[64,1536]{1,0:T(8,128)(2,1)S(1)}, u32[]{:S(2)}, u32[]{:S(2)}) %collective-permute-start.21) | collective-permute-done | bytes 196640 | tf_op jit(solution)/shard_map/ppermute | solution.py:198
  76.6 2.2 %collective-permute-start.23 = (bf16[64,1536]{1,0:T(8,128)(2,1)S(1)}, bf16[64,1536]{1,0:T(8,128)(2,1)S(1)}, u32[]{:S(2)}, u32[]{:S(2)}) collective-permute-start(bf16[64,1536]{1,0:T(8,128)(2,1)S(1)} %shard_map.87.refs_1_), channel_id=1, source_target_pairs={{0,8},{4,12},{8,0},{12,4},{1,9},{5,13},{9,1},{13,5},{2,10},{6,14},... | collective-permute-start | bytes 589832 | tf_op jit(solution)/shard_map/ppermute | solution.py:198
  78.9 9.4 %collective-permute-done.24.refs_2_ = bf16[64,1536]{1,0:T(8,128)(2,1)S(1)} collective-permute-done((bf16[64,1536]{1,0:T(8,128)(2,1)S(1)}, bf16[64,1536]{1,0:T(8,128)(2,1)S(1)}, u32[]{:S(2)}, u32[]{:S(2)}) %collective-permute-start.24) | collective-permute-done | bytes 196640 | tf_op jit(solution)/shard_map/ppermute | solution.py:198
  88.4 3.1 %collective-permute-done.25.refs_4_ = bf16[64,1536]{1,0:T(8,128)(2,1)S(1)} collective-permute-done((bf16[64,1536]{1,0:T(8,128)(2,1)S(1)}, bf16[64,1536]{1,0:T(8,128)(2,1)S(1)}, u32[]{:S(2)}, u32[]{:S(2)}) %collective-permute-start.25) | collective-permute-done | bytes 196640 | tf_op jit(solution)/shard_map/ppermute | solution.py:198
  95.0 4.5 %collective-permute-done.31 = bf16[128,512]{1,0:T(8,128)(2,1)S(1)} collective-permute-done((bf16[128,512]{1,0:T(8,128)(2,1)S(1)}, bf16[128,512]{1,0:T(8,128)(2,1)S(1)}, u32[]{:S(2)}, u32[]{:S(2)}) %collective-permute-start.31) | collective-permute-done | bytes 131104 | tf_op jit(solution)/shard_map/ppermute | solution.py:195
  100.9 0.9 collective-permute-done.34
  102.6 4.1 %collective-permute-done.33 = bf16[128,512]{1,0:T(8,128)(2,1)S(1)} collective-permute-done((bf16[128,512]{1,0:T(8,128)(2,1)S(1)}, bf16[128,512]{1,0:T(8,128)(2,1)S(1)}, u32[]{:S(2)}, u32[]{:S(2)}) %collective-permute-start.33) | collective-permute-done | bytes 131104 | tf_op jit(solution)/shard_map/ppermute | solution.py:195
  106.8 2.3 %collective-permute-done.35 = bf16[128,512]{1,0:T(8,128)(2,1)S(1)} collective-permute-done((bf16[128,512]{1,0:T(8,128)(2,1)S(1)}, bf16[128,512]{1,0:T(8,128)(2,1)S(1)}, u32[]{:S(2)}, u32[]{:S(2)}) %collective-permute-start.35) | collective-permute-done | bytes 131104 | tf_op jit(solution)/shard_map/ppermute | solution.py:195
  109.2 1.0 pad_maximum_fusion
  (122 shorter events, 17.8 us)
Async XLA Ops:
  2.3 6.3 %collective-permute-start = (bf16[32,1280]{1,0:T(8,128)(2,1)S(1)}, bf16[32,1280]{1,0:T(8,128)(2,1)S(1)}, u32[]{:S(2)}, u32[]{:S(2)}) collective-permute-start(bf16[32,1280]{1,0:T(8,128)(2,1)S(1)} %get-tuple-element.140), channel_id=1, source_target_pairs={{0,2},{1,3},{2,0},{3,1},{4,6},{5,7},{6,4},{7,5},{8,10},{9,11},{10,... | collective-permute-start | bytes 245768 | tf_op jit(solution)/shard_map/ppermute | solution.py:195
  5.5 3.2 %collective-permute-start.2 = (bf16[32,256]{1,0:T(8,128)(2,1)S(1)}, bf16[32,256]{1,0:T(8,128)(2,1)S(1)}, u32[]{:S(2)}, u32[]{:S(2)}) collective-permute-start(bf16[32,256]{1,0:T(8,128)(2,1)S(1)} %select_n.181), channel_id=1, source_target_pairs={{0,3},{1,2},{2,1},{3,0},{4,7},{5,6},{6,5},{7,4},{8,11},{9,10},{10,... | collective-permute-start | bytes 49160 | tf_op jit(solution)/shard_map/ppermute | solution.py:195
  5.7 2.9 %collective-permute-start.1 = (bf16[32,256]{1,0:T(8,128)(2,1)S(1)}, bf16[32,256]{1,0:T(8,128)(2,1)S(1)}, u32[]{:S(2)}, u32[]{:S(2)}) collective-permute-start(bf16[32,256]{1,0:T(8,128)(2,1)S(1)} %select_n.178), channel_id=1, source_target_pairs={{0,1},{1,0},{2,3},{3,2},{4,5},{5,4},{6,7},{7,6},{8,9},{9,8},{10,11... | collective-permute-start | bytes 49160 | tf_op jit(solution)/shard_map/ppermute | solution.py:195
  8.8 13.6 %collective-permute-start.6 = (bf16[2,128,512]{2,1,0:T(8,128)(2,1)S(1)}, bf16[2,128,512]{2,1,0:T(8,128)(2,1)S(1)}, u32[]{:S(2)}, u32[]{:S(2)}) collective-permute-start(bf16[2,128,512]{2,1,0:T(8,128)(2,1)S(1)} %get-tuple-element.127), channel_id=1, source_target_pairs={{0,2},{1,3},{2,0},{3,1},{4,6},{5,7},{6,4},{7,5},{8,10},{9,11},{10,... | collective-permute-start | bytes 786440 | tf_op jit(solution)/shard_map/ppermute | solution.py:195
  10.5 11.8 %collective-permute-start.4 = (bf16[64,1536]{1,0:T(8,128)(2,1)S(1)}, bf16[64,1536]{1,0:T(8,128)(2,1)S(1)}, u32[]{:S(2)}, u32[]{:S(2)}) collective-permute-start(bf16[64,1536]{1,0:T(8,128)(2,1)S(1)} %pad_maximum_fusion.3.refs_1_.refs_0_.refs_4_), channel_id=1, source_target_pairs={{0,8},{4,12},{8,0},{12,4},{1,9},{5,13},{9,1},{13,5},{2,10},{6,14},... | collective-permute-start | bytes 589832 | tf_op jit(solution)/shard_map/ppermute | solution.py:198
  13.1 9.4 %collective-permute-start.3 = (bf16[64,1536]{1,0:T(8,128)(2,1)S(1)}, bf16[64,1536]{1,0:T(8,128)(2,1)S(1)}, u32[]{:S(2)}, u32[]{:S(2)}) collective-permute-start(bf16[64,1536]{1,0:T(8,128)(2,1)S(1)} %pad_maximum_fusion.3.refs_1_.refs_0_.refs_4_), channel_id=1, source_target_pairs={{0,4},{4,0},{8,12},{12,8},{1,5},{5,1},{9,13},{13,9},{2,6},{6,2},{1... | collective-permute-start | bytes 589832 | tf_op jit(solution)/shard_map/ppermute | solution.py:198
  14.7 9.5 %collective-permute-start.7 = (bf16[2,128,512]{2,1,0:T(8,128)(2,1)S(1)}, bf16[2,128,512]{2,1,0:T(8,128)(2,1)S(1)}, u32[]{:S(2)}, u32[]{:S(2)}) collective-permute-start(bf16[2,128,512]{2,1,0:T(8,128)(2,1)S(1)} %get-tuple-element.77.refs_5_.refs_9_), channel_id=1, source_target_pairs={{0,1},{1,0},{2,3},{3,2},{4,5},{5,4},{6,7},{7,6},{8,9},{9,8},{10,11... | collective-permute-start | bytes 786440 | tf_op jit(solution)/shard_map/ppermute | solution.py:195
  22.5 1.7 %collective-permute-start.8 = (bf16[2,128,512]{2,1,0:T(8,128)(2,1)S(1)}, bf16[2,128,512]{2,1,0:T(8,128)(2,1)S(1)}, u32[]{:S(2)}, u32[]{:S(2)}) collective-permute-start(bf16[2,128,512]{2,1,0:T(8,128)(2,1)S(1)} %collective-permute-done.6.refs_6_.refs_10_), channel_id=1, source_target_pairs={{0,1},{1,0},{2,3},{3,2},{4,5},{5,4},{6,7},{7,6},{8,9},{9,8},{10,11... | collective-permute-start | bytes 786440 | tf_op jit(solution)/shard_map/ppermute | solution.py:195
  22.7 7.4 %collective-permute-start.5 = (bf16[64,1536]{1,0:T(8,128)(2,1)S(1)}, bf16[64,1536]{1,0:T(8,128)(2,1)S(1)}, u32[]{:S(2)}, u32[]{:S(2)}) collective-permute-start(bf16[64,1536]{1,0:T(8,128)(2,1)S(1)} %collective-permute-done.4.refs_3_.refs_11_), channel_id=1, source_target_pairs={{0,4},{4,0},{8,12},{12,8},{1,5},{5,1},{9,13},{13,9},{2,6},{6,2},{1... | collective-permute-start | bytes 589832 | tf_op jit(solution)/shard_map/ppermute | solution.py:198
  24.3 15.1 %collective-permute-start.12 = (bf16[2,128,512]{2,1,0:T(8,128)(2,1)S(1)}, bf16[2,128,512]{2,1,0:T(8,128)(2,1)S(1)}, u32[]{:S(2)}, u32[]{:S(2)}) collective-permute-start(bf16[2,128,512]{2,1,0:T(8,128)(2,1)S(1)} %get-tuple-element.123), channel_id=1, source_target_pairs={{0,2},{1,3},{2,0},{3,1},{4,6},{5,7},{6,4},{7,5},{8,10},{9,11},{10,... | collective-permute-start | bytes 786440 | tf_op jit(solution)/shard_map/ppermute | solution.py:195
  31.4 6.6 %collective-permute-start.9 = (bf16[64,1536]{1,0:T(8,128)(2,1)S(1)}, bf16[64,1536]{1,0:T(8,128)(2,1)S(1)}, u32[]{:S(2)}, u32[]{:S(2)}) collective-permute-start(bf16[64,1536]{1,0:T(8,128)(2,1)S(1)} %get-tuple-element.70), channel_id=1, source_target_pairs={{0,4},{4,0},{8,12},{12,8},{1,5},{5,1},{9,13},{13,9},{2,6},{6,2},{1... | collective-permute-start | bytes 589832 | tf_op jit(solution)/shard_map/ppermute | solution.py:198
  32.9 9.0 %collective-permute-start.13 = (bf16[2,128,512]{2,1,0:T(8,128)(2,1)S(1)}, bf16[2,128,512]{2,1,0:T(8,128)(2,1)S(1)}, u32[]{:S(2)}, u32[]{:S(2)}) collective-permute-start(bf16[2,128,512]{2,1,0:T(8,128)(2,1)S(1)} %get-tuple-element.102.refs_5_.refs_9_), channel_id=1, source_target_pairs={{0,1},{1,0},{2,3},{3,2},{4,5},{5,4},{6,7},{7,6},{8,9},{9,8},{10,11... | collective-permute-start | bytes 786440 | tf_op jit(solution)/shard_map/ppermute | solution.py:195
  38.0 16.6 %collective-permute-start.10 = (bf16[64,1536]{1,0:T(8,128)(2,1)S(1)}, bf16[64,1536]{1,0:T(8,128)(2,1)S(1)}, u32[]{:S(2)}, u32[]{:S(2)}) collective-permute-start(bf16[64,1536]{1,0:T(8,128)(2,1)S(1)} %get-tuple-element.71), channel_id=1, source_target_pairs={{0,4},{4,0},{8,12},{12,8},{1,5},{5,1},{9,13},{13,9},{2,6},{6,2},{1... | collective-permute-start | bytes 589832 | tf_op jit(solution)/shard_map/ppermute | solution.py:198
  39.4 2.4 %collective-permute-start.14 = (bf16[2,128,512]{2,1,0:T(8,128)(2,1)S(1)}, bf16[2,128,512]{2,1,0:T(8,128)(2,1)S(1)}, u32[]{:S(2)}, u32[]{:S(2)}) collective-permute-start(bf16[2,128,512]{2,1,0:T(8,128)(2,1)S(1)} %collective-permute-done.12.refs_6_.refs_10_), channel_id=1, source_target_pairs={{0,1},{1,0},{2,3},{3,2},{4,5},{5,4},{6,7},{7,6},{8,9},{9,8},{10,11... | collective-permute-start | bytes 786440 | tf_op jit(solution)/shard_map/ppermute | solution.py:195
  39.5 15.1 %collective-permute-start.11 = (bf16[64,1536]{1,0:T(8,128)(2,1)S(1)}, bf16[64,1536]{1,0:T(8,128)(2,1)S(1)}, u32[]{:S(2)}, u32[]{:S(2)}) collective-permute-start(bf16[64,1536]{1,0:T(8,128)(2,1)S(1)} %add_convert_fusion.4.refs_14_), channel_id=1, source_target_pairs={{0,8},{4,12},{8,0},{12,4},{1,9},{5,13},{9,1},{13,5},{2,10},{6,14},... | collective-permute-start | bytes 589832 | tf_op jit(solution)/shard_map/ppermute | solution.py:198
  43.8 9.7 %collective-permute-start.15 = (bf16[64,1536]{1,0:T(8,128)(2,1)S(1)}, bf16[64,1536]{1,0:T(8,128)(2,1)S(1)}, u32[]{:S(2)}, u32[]{:S(2)}) collective-permute-start(bf16[64,1536]{1,0:T(8,128)(2,1)S(1)} %get-tuple-element.84), channel_id=1, source_target_pairs={{0,4},{4,0},{8,12},{12,8},{1,5},{5,1},{9,13},{13,9},{2,6},{6,2},{1... | collective-permute-start | bytes 589832 | tf_op jit(solution)/shard_map/ppermute | solution.py:198
  45.1 19.2 %collective-permute-start.27 = (bf16[3,128,512]{2,1,0:T(8,128)(2,1)}, bf16[3,128,512]{2,1,0:T(8,128)(2,1)S(1)}, u32[]{:S(2)}, u32[]{:S(2)}) collective-permute-start(bf16[3,128,512]{2,1,0:T(8,128)(2,1)} %get-tuple-element.119), channel_id=1, source_target_pairs={{0,2},{1,3},{2,0},{3,1},{4,6},{5,7},{6,4},{7,5},{8,10},{9,11},{10,... | collective-permute-start | bytes 1179656 | tf_op jit(solution)/shard_map/ppermute | solution.py:195
  53.5 11.4 %collective-permute-start.18 = (bf16[64,1536]{1,0:T(8,128)(2,1)S(1)}, bf16[64,1536]{1,0:T(8,128)(2,1)S(1)}, u32[]{:S(2)}, u32[]{:S(2)}) collective-permute-start(bf16[64,1536]{1,0:T(8,128)(2,1)S(1)} %add_convert_fusion.3.refs_5_), channel_id=1, source_target_pairs={{0,8},{4,12},{8,0},{12,4},{1,9},{5,13},{9,1},{13,5},{2,10},{6,14},... | collective-permute-start | bytes 589832 | tf_op jit(solution)/shard_map/ppermute | solution.py:198
  56.3 3.1 %collective-permute-start.16 = (f32[128,128]{1,0:T(8,128)S(1)}, f32[128,128]{1,0:T(8,128)S(1)}, u32[]{:S(2)}, u32[]{:S(2)}) collective-permute-start(f32[128,128]{1,0:T(8,128)S(1)} %get-tuple-element.89.refs_4_), channel_id=1, source_target_pairs={{0,1},{1,0},{2,3},{3,2},{4,5},{5,4},{6,7},{7,6},{8,9},{9,8},{10,11... | collective-permute-start | bytes 196616 | tf_op jit(solution)/shard_map/ppermute | solution.py:195
  56.3 15.8 %collective-permute-start.17 = (bf16[64,1536]{1,0:T(8,128)(2,1)}, bf16[64,1536]{1,0:T(8,128)(2,1)}, u32[]{:S(2)}, u32[]{:S(2)}) collective-permute-start(bf16[64,1536]{1,0:T(8,128)(2,1)} %get-tuple-element.91), channel_id=1, source_target_pairs={{0,4},{4,0},{8,12},{12,8},{1,5},{5,1},{9,13},{13,9},{2,6},{6,2},{1... | collective-permute-start | bytes 589832 | tf_op jit(solution)/shard_map/ppermute | solution.py:198
  61.6 14.7 %collective-permute-start.21 = (bf16[64,1536]{1,0:T(8,128)(2,1)S(1)}, bf16[64,1536]{1,0:T(8,128)(2,1)S(1)}, u32[]{:S(2)}, u32[]{:S(2)}) collective-permute-start(bf16[64,1536]{1,0:T(8,128)(2,1)S(1)} %get-tuple-element.94.refs_1_), channel_id=1, source_target_pairs={{0,4},{4,0},{8,12},{12,8},{1,5},{5,1},{9,13},{13,9},{2,6},{6,2},{1... | collective-permute-start | bytes 589832 | tf_op jit(solution)/shard_map/ppermute | solution.py:198
  62.4 14.0 %collective-permute-start.20 = (bf16[64,1536]{1,0:T(8,128)(2,1)S(1)}, bf16[64,1536]{1,0:T(8,128)(2,1)S(1)}, u32[]{:S(2)}, u32[]{:S(2)}) collective-permute-start(bf16[64,1536]{1,0:T(8,128)(2,1)S(1)} %get-tuple-element.94.refs_1_), channel_id=1, source_target_pairs={{0,8},{4,12},{8,0},{12,4},{1,9},{5,13},{9,1},{13,5},{2,10},{6,14},... | collective-permute-start | bytes 589832 | tf_op jit(solution)/shard_map/ppermute | solution.py:198
  64.3 27.2 %collective-permute-start.28 = (bf16[3,128,512]{2,1,0:T(8,128)(2,1)S(1)}, bf16[3,128,512]{2,1,0:T(8,128)(2,1)S(1)}, u32[]{:S(2)}, u32[]{:S(2)}) collective-permute-start(bf16[3,128,512]{2,1,0:T(8,128)(2,1)S(1)} %get-tuple-element.100.refs_5_), channel_id=1, source_target_pairs={{0,1},{1,0},{2,3},{3,2},{4,5},{5,4},{6,7},{7,6},{8,9},{9,8},{10,11... | collective-permute-start | bytes 1179656 | tf_op jit(solution)/shard_map/ppermute | solution.py:195
  64.9 26.6 %collective-permute-start.29 = (bf16[3,128,512]{2,1,0:T(8,128)(2,1)S(1)}, bf16[3,128,512]{2,1,0:T(8,128)(2,1)S(1)}, u32[]{:S(2)}, u32[]{:S(2)}) collective-permute-start(bf16[3,128,512]{2,1,0:T(8,128)(2,1)S(1)} %collective-permute-done.27.refs_6_), channel_id=1, source_target_pairs={{0,1},{1,0},{2,3},{3,2},{4,5},{5,4},{6,7},{7,6},{8,9},{9,8},{10,11... | collective-permute-start | bytes 1179656 | tf_op jit(solution)/shard_map/ppermute | solution.py:195
  74.4 2.0 %collective-permute-start.22 = (f32[64,128]{1,0:T(8,128)S(1)}, f32[64,128]{1,0:T(8,128)S(1)}, u32[]{:S(2)}, u32[]{:S(2)}) collective-permute-start(f32[64,128]{1,0:T(8,128)S(1)} %get-tuple-element.106.refs_3_.refs_13_), channel_id=1, source_target_pairs={{0,1},{1,0},{2,3},{3,2},{4,5},{5,4},{6,7},{7,6},{8,9},{9,8},{10,11... | collective-permute-start | bytes 98312 | tf_op jit(solution)/shard_map/ppermute | solution.py:195
  76.5 11.8 %collective-permute-start.24 = (bf16[64,1536]{1,0:T(8,128)(2,1)S(1)}, bf16[64,1536]{1,0:T(8,128)(2,1)S(1)}, u32[]{:S(2)}, u32[]{:S(2)}) collective-permute-start(bf16[64,1536]{1,0:T(8,128)(2,1)S(1)} %shard_map.87.refs_1_), channel_id=1, source_target_pairs={{0,4},{4,0},{8,12},{12,8},{1,5},{5,1},{9,13},{13,9},{2,6},{6,2},{1... | collective-permute-start | bytes 589832 | tf_op jit(solution)/shard_map/ppermute | solution.py:198
  76.6 11.9 %collective-permute-start.23 = (bf16[64,1536]{1,0:T(8,128)(2,1)S(1)}, bf16[64,1536]{1,0:T(8,128)(2,1)S(1)}, u32[]{:S(2)}, u32[]{:S(2)}) collective-permute-start(bf16[64,1536]{1,0:T(8,128)(2,1)S(1)} %shard_map.87.refs_1_), channel_id=1, source_target_pairs={{0,8},{4,12},{8,0},{12,4},{1,9},{5,13},{9,1},{13,5},{2,10},{6,14},... | collective-permute-start | bytes 589832 | tf_op jit(solution)/shard_map/ppermute | solution.py:198
  78.8 12.7 %collective-permute-start.25 = (bf16[64,1536]{1,0:T(8,128)(2,1)S(1)}, bf16[64,1536]{1,0:T(8,128)(2,1)S(1)}, u32[]{:S(2)}, u32[]{:S(2)}) collective-permute-start(bf16[64,1536]{1,0:T(8,128)(2,1)S(1)} %collective-permute-done.20.refs_3_), channel_id=1, source_target_pairs={{0,4},{4,0},{8,12},{12,8},{1,5},{5,1},{9,13},{13,9},{2,6},{6,2},{1... | collective-permute-start | bytes 589832 | tf_op jit(solution)/shard_map/ppermute | solution.py:198
  92.2 7.3 %collective-permute-start.26 = (bf16[64,1536]{1,0:T(8,128)(2,1)S(1)}, bf16[64,1536]{1,0:T(8,128)(2,1)S(1)}, u32[]{:S(2)}, u32[]{:S(2)}) collective-permute-start(bf16[64,1536]{1,0:T(8,128)(2,1)S(1)} %collective-permute-done.23.refs_3_), channel_id=1, source_target_pairs={{0,4},{4,0},{8,12},{12,8},{1,5},{5,1},{9,13},{13,9},{2,6},{6,2},{1... | collective-permute-start | bytes 589832 | tf_op jit(solution)/shard_map/ppermute | solution.py:198
  93.9 5.6 %collective-permute-start.31 = (bf16[128,512]{1,0:T(8,128)(2,1)S(1)}, bf16[128,512]{1,0:T(8,128)(2,1)S(1)}, u32[]{:S(2)}, u32[]{:S(2)}) collective-permute-start(bf16[128,512]{1,0:T(8,128)(2,1)S(1)} %get-tuple-element.136), channel_id=1, source_target_pairs={{0,2},{1,3},{2,0},{3,1},{4,6},{5,7},{6,4},{7,5},{8,10},{9,11},{10,... | collective-permute-start | bytes 393224 | tf_op jit(solution)/shard_map/ppermute | solution.py:195
  100.3 6.4 %collective-permute-start.33 = (bf16[128,512]{1,0:T(8,128)(2,1)S(1)}, bf16[128,512]{1,0:T(8,128)(2,1)S(1)}, u32[]{:S(2)}, u32[]{:S(2)}) collective-permute-start(bf16[128,512]{1,0:T(8,128)(2,1)S(1)} %get-tuple-element.132), channel_id=1, source_target_pairs={{0,2},{1,3},{2,0},{3,1},{4,6},{5,7},{6,4},{7,5},{8,10},{9,11},{10,... | collective-permute-start | bytes 393224 | tf_op jit(solution)/shard_map/ppermute | solution.py:195
  101.9 7.2 %collective-permute-start.35 = (bf16[128,512]{1,0:T(8,128)(2,1)S(1)}, bf16[128,512]{1,0:T(8,128)(2,1)S(1)}, u32[]{:S(2)}, u32[]{:S(2)}) collective-permute-start(bf16[128,512]{1,0:T(8,128)(2,1)S(1)} %get-tuple-element.134), channel_id=1, source_target_pairs={{0,2},{1,3},{2,0},{3,1},{4,6},{5,7},{6,4},{7,5},{8,10},{9,11},{10,... | collective-permute-start | bytes 393224 | tf_op jit(solution)/shard_map/ppermute | solution.py:195
  (17 other events, 35.0 us)

commit v11 on v10

--- a/solution.py
+++ b/solution.py
@@ -220,10 +220,10 @@
             for d in range(planes - bit, 0, -2 * bit)
         }
 
-    def halve(parts, bit, sent):
+    def halve(parts, bit, sent, relayed_first):
         relayed = None
         for distance, total in sent.items():
-            if distance == bit and relayed is not None:
+            if relayed_first and distance == bit and relayed is not None:
                 total, came = lax.optimization_barrier((total, parts[relayed][-1]))
                 parts[relayed][-1] = came
             parts[distance ^ bit].append(to_plane(total, bit))
@@ -305,7 +305,7 @@
         behind["steps0"],
     )
     zeros = steps(0)
-    halve(zeros, 1, totals(zeros, 1))
+    halve(zeros, 1, totals(zeros, 1), True)
     came = [zeros[d][-1] for d in range(2, planes, 2)]
     pairs[1] = to_quad(
         after(pairs[1], pairs[0], behind["steps1"]), came or zeros[0], behind["steps1"]
@@ -314,13 +314,13 @@
     while bit < planes:
         sent = totals(zeros, bit)
         behind["steps1"].extend(sent.values())
-        halve(zeros, bit, sent)
+        halve(zeros, bit, sent, True)
         bit *= 2
     ones = steps(1)
     bit = 1
     while bit < planes:
         sent = totals(ones, bit)
-        halve(ones, bit, sent)
+        halve(ones, bit, sent, False)
         bit *= 2
     got_zero, got_one = zeros[0], ones[0]
     behind["new0"].extend(sent.values())

time: 110 us -> 108 us (0.982)
  waiting for transfers between devices: 61.9 us -> 58.8 us
    ppermute x15, waiting for transfers between devices: 48.1 us -> 45.2 us  [to_plane(): return lax.ppermute(array, 'plane', [(z, z ^ bit) for z in range(planes)])]
  transfers between devices with their start and end apart: 36 -> 36, of which waited for: 18 -> 17; matrix products, arithmetic and copies ran while one was open for 4% -> 4% of each run, Pallas kernels for 5% -> 5%
where the time goes in v11:
time: 108 us
  waiting for transfers between devices  58.8 us (54%)
  starting transfers between devices  28 us (26%)
  local copies, waits for them, and re-layouts  9.41 us (9%)
  Pallas kernels  6.83 us (6%)
  other arithmetic  3.22 us (3%)
  between operations  1.71 us (2%)
    ppermute x15, waiting for transfers between devices, to_plane(): return lax.ppermute(array, 'plane', [(z, z ^ bit) for z in range(planes)])  45.2 us
    ppermute x15, starting transfers between devices, to_plane(): return lax.ppermute(array, 'plane', [(z, z ^ bit) for z in range(planes)])  18.8 us
    ppermute x21, waiting for transfers between devices, send(): return lax.ppermute(array, 'quad', [(q, q ^ offset) for q in range(4)])  13.6 us
    ppermute x21, starting transfers between devices, send(): return lax.ppermute(array, 'quad', [(q, q ^ offset) for q in range(4)])  9.14 us
    pallas_call x9, Pallas kernels, call(): pl.pallas_call(kernel, out_shape=shapes, in_specs=[pl.BlockSpec(memory_sp...  6.83 us
    unnamed x26, local copies, waits for them, and re-layouts  6.09 us
  transfers between devices with their start and end apart: 36, of which 17 were waited for; matrix products, arithmetic and copies ran while one was open for 4% of the time, Pallas kernels for 5%

profile of v11, /device:TPU:0, one launch (start us, length us, event | category | flops | bytes accessed | tf_op | source)
XLA Modules:
  0.0 107.9 jit_solution(17262226515030144771)
XLA Ops:
  0.0 0.9 constant_dynamic-update-slice_fusion.2
  2.3 3.0 %collective-permute-start = (bf16[32,1280]{1,0:T(8,128)(2,1)S(1)}, bf16[32,1280]{1,0:T(8,128)(2,1)S(1)}, u32[]{:S(2)}, u32[]{:S(2)}) collective-permute-start(bf16[32,1280]{1,0:T(8,128)(2,1)S(1)} %get-tuple-element.136), channel_id=1, source_target_pairs={{0,2},{1,3},{2,0},{3,1},{4,6},{5,7},{6,4},{7,5},{8,10},{9,11},{10,... | collective-permute-start | bytes 245768 | tf_op jit(solution)/shard_map/ppermute | solution.py:195
  6.6 0.9 reshape.145
  8.8 1.6 %collective-permute-start.6 = (bf16[2,128,512]{2,1,0:T(8,128)(2,1)S(1)}, bf16[2,128,512]{2,1,0:T(8,128)(2,1)S(1)}, u32[]{:S(2)}, u32[]{:S(2)}) collective-permute-start(bf16[2,128,512]{2,1,0:T(8,128)(2,1)S(1)} %get-tuple-element.123), channel_id=1, source_target_pairs={{0,2},{1,3},{2,0},{3,1},{4,6},{5,7},{6,4},{7,5},{8,10},{9,11},{10,... | collective-permute-start | bytes 786440 | tf_op jit(solution)/shard_map/ppermute | solution.py:195
  10.5 2.6 %collective-permute-start.4 = (bf16[64,1536]{1,0:T(8,128)(2,1)S(1)}, bf16[64,1536]{1,0:T(8,128)(2,1)S(1)}, u32[]{:S(2)}, u32[]{:S(2)}) collective-permute-start(bf16[64,1536]{1,0:T(8,128)(2,1)S(1)} %pad_maximum_fusion.3.refs_1_.refs_0_.refs_4_), channel_id=1, source_target_pairs={{0,8},{4,12},{8,0},{12,4},{1,9},{5,13},{9,1},{13,5},{2,10},{6,14},... | collective-permute-start | bytes 589832 | tf_op jit(solution)/shard_map/ppermute | solution.py:198
  13.1 1.6 %collective-permute-start.3 = (bf16[64,1536]{1,0:T(8,128)(2,1)S(1)}, bf16[64,1536]{1,0:T(8,128)(2,1)S(1)}, u32[]{:S(2)}, u32[]{:S(2)}) collective-permute-start(bf16[64,1536]{1,0:T(8,128)(2,1)S(1)} %pad_maximum_fusion.3.refs_1_.refs_0_.refs_4_), channel_id=1, source_target_pairs={{0,4},{4,0},{8,12},{12,8},{1,5},{5,1},{9,13},{13,9},{2,6},{6,2},{1... | collective-permute-start | bytes 589832 | tf_op jit(solution)/shard_map/ppermute | solution.py:198
  14.7 7.6 %collective-permute-done.4.refs_3_.refs_11_ = bf16[64,1536]{1,0:T(8,128)(2,1)S(1)} collective-permute-done((bf16[64,1536]{1,0:T(8,128)(2,1)S(1)}, bf16[64,1536]{1,0:T(8,128)(2,1)S(1)}, u32[]{:S(2)}, u32[]{:S(2)}) %collective-permute-start.4) | collective-permute-done | bytes 196640 | tf_op jit(solution)/shard_map/ppermute | solution.py:198
  22.7 1.5 %collective-permute-start.5 = (bf16[64,1536]{1,0:T(8,128)(2,1)S(1)}, bf16[64,1536]{1,0:T(8,128)(2,1)S(1)}, u32[]{:S(2)}, u32[]{:S(2)}) collective-permute-start(bf16[64,1536]{1,0:T(8,128)(2,1)S(1)} %collective-permute-done.4.refs_3_.refs_11_), channel_id=1, source_target_pairs={{0,4},{4,0},{8,12},{12,8},{1,5},{5,1},{9,13},{13,9},{2,6},{6,2},{1... | collective-permute-start | bytes 589832 | tf_op jit(solution)/shard_map/ppermute | solution.py:198
  24.8 5.2 %collective-permute-done.5.refs_4_ = bf16[64,1536]{1,0:T(8,128)(2,1)S(1)} collective-permute-done((bf16[64,1536]{1,0:T(8,128)(2,1)S(1)}, bf16[64,1536]{1,0:T(8,128)(2,1)S(1)}, u32[]{:S(2)}, u32[]{:S(2)}) %collective-permute-start.5) | collective-permute-done | bytes 196640 | tf_op jit(solution)/shard_map/ppermute | solution.py:198
  30.1 1.3 %shard_map.82 = (f32[64,1536]{1,0:T(8,128)S(1)}, bf16[64,1536]{1,0:T(8,128)(2,1)S(1)}, f32[64,1536]{1,0:T(8,128)S(1)}, bf16[64,1536]{1,0:T(8,128)(2,1)S(1)}) custom-call(s32[1]{0:T(128)} %bitcast.2.refs_0_, bf16[64,1536]{1,0:T(8,128)(2,1)S(1)} %pad_maximum_fusion.3.refs_1_.refs_0_.refs_4_, ...), custom_call_target="tpu_custom_call" | custom-call | flops 805306368 | bytes 1024 | tf_op jit(solution)/shard_map/pallas_call | solution.py:21
  31.4 1.5 %collective-permute-start.9 = (bf16[64,1536]{1,0:T(8,128)(2,1)S(1)}, bf16[64,1536]{1,0:T(8,128)(2,1)S(1)}, u32[]{:S(2)}, u32[]{:S(2)}) collective-permute-start(bf16[64,1536]{1,0:T(8,128)(2,1)S(1)} %get-tuple-element.68), channel_id=1, source_target_pairs={{0,4},{4,0},{8,12},{12,8},{1,5},{5,1},{9,13},{13,9},{2,6},{6,2},{1... | collective-permute-start | bytes 589832 | tf_op jit(solution)/shard_map/ppermute | solution.py:198
  32.9 5.1 %collective-permute-done.9.refs_13_ = bf16[64,1536]{1,0:T(8,128)(2,1)S(1)} collective-permute-done((bf16[64,1536]{1,0:T(8,128)(2,1)S(1)}, bf16[64,1536]{1,0:T(8,128)(2,1)S(1)}, u32[]{:S(2)}, u32[]{:S(2)}) %collective-permute-start.9) | collective-permute-done | bytes 196640 | tf_op jit(solution)/shard_map/ppermute | solution.py:198
  38.0 1.4 %collective-permute-start.10 = (bf16[64,1536]{1,0:T(8,128)(2,1)S(1)}, bf16[64,1536]{1,0:T(8,128)(2,1)S(1)}, u32[]{:S(2)}, u32[]{:S(2)}) collective-permute-start(bf16[64,1536]{1,0:T(8,128)(2,1)S(1)} %get-tuple-element.69), channel_id=1, source_target_pairs={{0,4},{4,0},{8,12},{12,8},{1,5},{5,1},{9,13},{13,9},{2,6},{6,2},{1... | collective-permute-start | bytes 589832 | tf_op jit(solution)/shard_map/ppermute | solution.py:198
  39.5 2.4 %collective-permute-start.11 = (bf16[64,1536]{1,0:T(8,128)(2,1)S(1)}, bf16[64,1536]{1,0:T(8,128)(2,1)S(1)}, u32[]{:S(2)}, u32[]{:S(2)}) collective-permute-start(bf16[64,1536]{1,0:T(8,128)(2,1)S(1)} %add_convert_fusion.4.refs_14_), channel_id=1, source_target_pairs={{0,8},{4,12},{8,0},{12,4},{1,9},{5,13},{9,1},{13,5},{2,10},{6,14},... | collective-permute-start | bytes 589832 | tf_op jit(solution)/shard_map/ppermute | solution.py:198
  41.8 2.0 %shard_map.83 = (f32[64,1536]{1,0:T(8,128)S(1)}, bf16[64,1536]{1,0:T(8,128)(2,1)}, f32[64,1536]{1,0:T(8,128)S(1)}, bf16[64,1536]{1,0:T(8,128)(2,1)S(1)}) custom-call(s32[1]{0:T(128)} %bitcast.2.refs_0_, bf16[64,1536]{1,0:T(8,128)(2,1)S(1)} %pad_maximum_fusion.3.refs_1_.refs_0_.refs_4_, bf16[64,1536]{1,0:T(8,128)(2,1)S(1)} %collective-permute-done.3.refs_2_.refs_9_.refs_10_, ...), custom_call_target="tpu_custom_call" | custom-call | flops 805306368 | bytes 1024 | tf_op jit(solution)/shard_map/pallas_call | solution.py:21
  44.3 1.5 %collective-permute-start.17 = (bf16[64,1536]{1,0:T(8,128)(2,1)}, bf16[64,1536]{1,0:T(8,128)(2,1)S(1)}, u32[]{:S(2)}, u32[]{:S(2)}) collective-permute-start(bf16[64,1536]{1,0:T(8,128)(2,1)} %get-tuple-element.87), channel_id=1, source_target_pairs={{0,4},{4,0},{8,12},{12,8},{1,5},{5,1},{9,13},{13,9},{2,6},{6,2},{1... | collective-permute-start | bytes 589832 | tf_op jit(solution)/shard_map/ppermute | solution.py:198
  47.2 6.6 %collective-permute-done.15 = bf16[64,1536]{1,0:T(8,128)(2,1)S(1)} collective-permute-done((bf16[64,1536]{1,0:T(8,128)(2,1)S(1)}, bf16[64,1536]{1,0:T(8,128)(2,1)S(1)}, u32[]{:S(2)}, u32[]{:S(2)}) %collective-permute-start.15) | collective-permute-done | bytes 196640 | tf_op jit(solution)/shard_map/ppermute | solution.py:198
  53.9 2.6 %collective-permute-start.18 = (bf16[64,1536]{1,0:T(8,128)(2,1)S(1)}, bf16[64,1536]{1,0:T(8,128)(2,1)}, u32[]{:S(2)}, u32[]{:S(2)}) collective-permute-start(bf16[64,1536]{1,0:T(8,128)(2,1)S(1)} %add_convert_fusion.3.refs_5_), channel_id=1, source_target_pairs={{0,8},{4,12},{8,0},{12,4},{1,9},{5,13},{9,1},{13,5},{2,10},{6,14},... | collective-permute-start | bytes 589832 | tf_op jit(solution)/shard_map/ppermute | solution.py:198
  60.6 1.0 copy-done.1
  61.6 1.0 copy-done.3
  63.9 1.3 %collective-permute-done.18.refs_2_ = bf16[64,1536]{1,0:T(8,128)(2,1)} collective-permute-done((bf16[64,1536]{1,0:T(8,128)(2,1)S(1)}, bf16[64,1536]{1,0:T(8,128)(2,1)}, u32[]{:S(2)}, u32[]{:S(2)}) %collective-permute-start.18) | collective-permute-done | bytes 196640 | tf_op jit(solution)/shard_map/ppermute | solution.py:198
  65.2 1.1 shard_map.86
  66.3 1.2 %collective-permute-done.19.refs_2_ = f32[64,128]{1,0:T(8,128)S(1)} collective-permute-done((f32[64,128]{1,0:T(8,128)S(1)}, f32[64,128]{1,0:T(8,128)S(1)}, u32[]{:S(2)}, u32[]{:S(2)}) %collective-permute-start.19) | collective-permute-done | bytes 32800 | tf_op jit(solution)/shard_map/ppermute | solution.py:195
  67.7 5.0 %collective-permute-done.21.refs_2_ = bf16[64,1536]{1,0:T(8,128)(2,1)S(1)} collective-permute-done((bf16[64,1536]{1,0:T(8,128)(2,1)S(1)}, bf16[64,1536]{1,0:T(8,128)(2,1)S(1)}, u32[]{:S(2)}, u32[]{:S(2)}) %collective-permute-start.21) | collective-permute-done | bytes 196640 | tf_op jit(solution)/shard_map/ppermute | solution.py:198
  72.7 2.1 %collective-permute-done.20.refs_3_ = bf16[64,1536]{1,0:T(8,128)(2,1)S(1)} collective-permute-done((bf16[64,1536]{1,0:T(8,128)(2,1)S(1)}, bf16[64,1536]{1,0:T(8,128)(2,1)S(1)}, u32[]{:S(2)}, u32[]{:S(2)}) %collective-permute-start.20) | collective-permute-done | bytes 196640 | tf_op jit(solution)/shard_map/ppermute | solution.py:198
  75.1 2.0 %collective-permute-start.23 = (bf16[64,1536]{1,0:T(8,128)(2,1)S(1)}, bf16[64,1536]{1,0:T(8,128)(2,1)S(1)}, u32[]{:S(2)}, u32[]{:S(2)}) collective-permute-start(bf16[64,1536]{1,0:T(8,128)(2,1)S(1)} %shard_map.87.refs_1_), channel_id=1, source_target_pairs={{0,8},{4,12},{8,0},{12,4},{1,9},{5,13},{9,1},{13,5},{2,10},{6,14},... | collective-permute-start | bytes 589832 | tf_op jit(solution)/shard_map/ppermute | solution.py:198
  77.3 8.9 %collective-permute-done.24.refs_2_ = bf16[64,1536]{1,0:T(8,128)(2,1)S(1)} collective-permute-done((bf16[64,1536]{1,0:T(8,128)(2,1)S(1)}, bf16[64,1536]{1,0:T(8,128)(2,1)S(1)}, u32[]{:S(2)}, u32[]{:S(2)}) %collective-permute-start.24) | collective-permute-done | bytes 196640 | tf_op jit(solution)/shard_map/ppermute | solution.py:198
  86.2 3.1 %collective-permute-done.25.refs_4_ = bf16[64,1536]{1,0:T(8,128)(2,1)S(1)} collective-permute-done((bf16[64,1536]{1,0:T(8,128)(2,1)S(1)}, bf16[64,1536]{1,0:T(8,128)(2,1)S(1)}, u32[]{:S(2)}, u32[]{:S(2)}) %collective-permute-start.25) | collective-permute-done | bytes 196640 | tf_op jit(solution)/shard_map/ppermute | solution.py:198
  92.7 4.6 %collective-permute-done.31 = bf16[128,512]{1,0:T(8,128)(2,1)S(1)} collective-permute-done((bf16[128,512]{1,0:T(8,128)(2,1)S(1)}, bf16[128,512]{1,0:T(8,128)(2,1)S(1)}, u32[]{:S(2)}, u32[]{:S(2)}) %collective-permute-start.31) | collective-permute-done | bytes 131104 | tf_op jit(solution)/shard_map/ppermute | solution.py:195
  100.4 4.1 %collective-permute-done.33 = bf16[128,512]{1,0:T(8,128)(2,1)S(1)} collective-permute-done((bf16[128,512]{1,0:T(8,128)(2,1)S(1)}, bf16[128,512]{1,0:T(8,128)(2,1)S(1)}, u32[]{:S(2)}, u32[]{:S(2)}) %collective-permute-start.33) | collective-permute-done | bytes 131104 | tf_op jit(solution)/shard_map/ppermute | solution.py:195
  104.6 2.3 %collective-permute-done.35 = bf16[128,512]{1,0:T(8,128)(2,1)S(1)} collective-permute-done((bf16[128,512]{1,0:T(8,128)(2,1)S(1)}, bf16[128,512]{1,0:T(8,128)(2,1)S(1)}, u32[]{:S(2)}, u32[]{:S(2)}) %collective-permute-start.35) | collective-permute-done | bytes 131104 | tf_op jit(solution)/shard_map/ppermute | solution.py:195
  107.0 1.0 pad_maximum_fusion
  (122 shorter events, 18.3 us)
Async XLA Ops:
  2.3 6.3 %collective-permute-start = (bf16[32,1280]{1,0:T(8,128)(2,1)S(1)}, bf16[32,1280]{1,0:T(8,128)(2,1)S(1)}, u32[]{:S(2)}, u32[]{:S(2)}) collective-permute-start(bf16[32,1280]{1,0:T(8,128)(2,1)S(1)} %get-tuple-element.136), channel_id=1, source_target_pairs={{0,2},{1,3},{2,0},{3,1},{4,6},{5,7},{6,4},{7,5},{8,10},{9,11},{10,... | collective-permute-start | bytes 245768 | tf_op jit(solution)/shard_map/ppermute | solution.py:195
  5.5 3.2 %collective-permute-start.2 = (bf16[32,256]{1,0:T(8,128)(2,1)S(1)}, bf16[32,256]{1,0:T(8,128)(2,1)S(1)}, u32[]{:S(2)}, u32[]{:S(2)}) collective-permute-start(bf16[32,256]{1,0:T(8,128)(2,1)S(1)} %select_n.181), channel_id=1, source_target_pairs={{0,3},{1,2},{2,1},{3,0},{4,7},{5,6},{6,5},{7,4},{8,11},{9,10},{10,... | collective-permute-start | bytes 49160 | tf_op jit(solution)/shard_map/ppermute | solution.py:195
  5.7 2.9 %collective-permute-start.1 = (bf16[32,256]{1,0:T(8,128)(2,1)S(1)}, bf16[32,256]{1,0:T(8,128)(2,1)S(1)}, u32[]{:S(2)}, u32[]{:S(2)}) collective-permute-start(bf16[32,256]{1,0:T(8,128)(2,1)S(1)} %select_n.178), channel_id=1, source_target_pairs={{0,1},{1,0},{2,3},{3,2},{4,5},{5,4},{6,7},{7,6},{8,9},{9,8},{10,11... | collective-permute-start | bytes 49160 | tf_op jit(solution)/shard_map/ppermute | solution.py:195
  8.8 13.6 %collective-permute-start.6 = (bf16[2,128,512]{2,1,0:T(8,128)(2,1)S(1)}, bf16[2,128,512]{2,1,0:T(8,128)(2,1)S(1)}, u32[]{:S(2)}, u32[]{:S(2)}) collective-permute-start(bf16[2,128,512]{2,1,0:T(8,128)(2,1)S(1)} %get-tuple-element.123), channel_id=1, source_target_pairs={{0,2},{1,3},{2,0},{3,1},{4,6},{5,7},{6,4},{7,5},{8,10},{9,11},{10,... | collective-permute-start | bytes 786440 | tf_op jit(solution)/shard_map/ppermute | solution.py:195
  10.5 11.8 %collective-permute-start.4 = (bf16[64,1536]{1,0:T(8,128)(2,1)S(1)}, bf16[64,1536]{1,0:T(8,128)(2,1)S(1)}, u32[]{:S(2)}, u32[]{:S(2)}) collective-permute-start(bf16[64,1536]{1,0:T(8,128)(2,1)S(1)} %pad_maximum_fusion.3.refs_1_.refs_0_.refs_4_), channel_id=1, source_target_pairs={{0,8},{4,12},{8,0},{12,4},{1,9},{5,13},{9,1},{13,5},{2,10},{6,14},... | collective-permute-start | bytes 589832 | tf_op jit(solution)/shard_map/ppermute | solution.py:198
  13.1 9.4 %collective-permute-start.3 = (bf16[64,1536]{1,0:T(8,128)(2,1)S(1)}, bf16[64,1536]{1,0:T(8,128)(2,1)S(1)}, u32[]{:S(2)}, u32[]{:S(2)}) collective-permute-start(bf16[64,1536]{1,0:T(8,128)(2,1)S(1)} %pad_maximum_fusion.3.refs_1_.refs_0_.refs_4_), channel_id=1, source_target_pairs={{0,4},{4,0},{8,12},{12,8},{1,5},{5,1},{9,13},{13,9},{2,6},{6,2},{1... | collective-permute-start | bytes 589832 | tf_op jit(solution)/shard_map/ppermute | solution.py:198
  14.7 9.5 %collective-permute-start.7 = (bf16[2,128,512]{2,1,0:T(8,128)(2,1)S(1)}, bf16[2,128,512]{2,1,0:T(8,128)(2,1)S(1)}, u32[]{:S(2)}, u32[]{:S(2)}) collective-permute-start(bf16[2,128,512]{2,1,0:T(8,128)(2,1)S(1)} %get-tuple-element.75.refs_5_.refs_9_), channel_id=1, source_target_pairs={{0,1},{1,0},{2,3},{3,2},{4,5},{5,4},{6,7},{7,6},{8,9},{9,8},{10,11... | collective-permute-start | bytes 786440 | tf_op jit(solution)/shard_map/ppermute | solution.py:195
  22.5 1.7 %collective-permute-start.8 = (bf16[2,128,512]{2,1,0:T(8,128)(2,1)S(1)}, bf16[2,128,512]{2,1,0:T(8,128)(2,1)S(1)}, u32[]{:S(2)}, u32[]{:S(2)}) collective-permute-start(bf16[2,128,512]{2,1,0:T(8,128)(2,1)S(1)} %collective-permute-done.6.refs_6_.refs_10_), channel_id=1, source_target_pairs={{0,1},{1,0},{2,3},{3,2},{4,5},{5,4},{6,7},{7,6},{8,9},{9,8},{10,11... | collective-permute-start | bytes 786440 | tf_op jit(solution)/shard_map/ppermute | solution.py:195
  22.7 7.4 %collective-permute-start.5 = (bf16[64,1536]{1,0:T(8,128)(2,1)S(1)}, bf16[64,1536]{1,0:T(8,128)(2,1)S(1)}, u32[]{:S(2)}, u32[]{:S(2)}) collective-permute-start(bf16[64,1536]{1,0:T(8,128)(2,1)S(1)} %collective-permute-done.4.refs_3_.refs_11_), channel_id=1, source_target_pairs={{0,4},{4,0},{8,12},{12,8},{1,5},{5,1},{9,13},{13,9},{2,6},{6,2},{1... | collective-permute-start | bytes 589832 | tf_op jit(solution)/shard_map/ppermute | solution.py:198
  24.3 15.1 %collective-permute-start.12 = (bf16[2,128,512]{2,1,0:T(8,128)(2,1)S(1)}, bf16[2,128,512]{2,1,0:T(8,128)(2,1)S(1)}, u32[]{:S(2)}, u32[]{:S(2)}) collective-permute-start(bf16[2,128,512]{2,1,0:T(8,128)(2,1)S(1)} %get-tuple-element.119), channel_id=1, source_target_pairs={{0,2},{1,3},{2,0},{3,1},{4,6},{5,7},{6,4},{7,5},{8,10},{9,11},{10,... | collective-permute-start | bytes 786440 | tf_op jit(solution)/shard_map/ppermute | solution.py:195
  31.4 6.6 %collective-permute-start.9 = (bf16[64,1536]{1,0:T(8,128)(2,1)S(1)}, bf16[64,1536]{1,0:T(8,128)(2,1)S(1)}, u32[]{:S(2)}, u32[]{:S(2)}) collective-permute-start(bf16[64,1536]{1,0:T(8,128)(2,1)S(1)} %get-tuple-element.68), channel_id=1, source_target_pairs={{0,4},{4,0},{8,12},{12,8},{1,5},{5,1},{9,13},{13,9},{2,6},{6,2},{1... | collective-permute-start | bytes 589832 | tf_op jit(solution)/shard_map/ppermute | solution.py:198
  32.9 9.0 %collective-permute-start.13 = (bf16[2,128,512]{2,1,0:T(8,128)(2,1)S(1)}, bf16[2,128,512]{2,1,0:T(8,128)(2,1)S(1)}, u32[]{:S(2)}, u32[]{:S(2)}) collective-permute-start(bf16[2,128,512]{2,1,0:T(8,128)(2,1)S(1)} %get-tuple-element.98.refs_5_.refs_9_), channel_id=1, source_target_pairs={{0,1},{1,0},{2,3},{3,2},{4,5},{5,4},{6,7},{7,6},{8,9},{9,8},{10,11... | collective-permute-start | bytes 786440 | tf_op jit(solution)/shard_map/ppermute | solution.py:195
  38.0 18.5 %collective-permute-start.10 = (bf16[64,1536]{1,0:T(8,128)(2,1)S(1)}, bf16[64,1536]{1,0:T(8,128)(2,1)S(1)}, u32[]{:S(2)}, u32[]{:S(2)}) collective-permute-start(bf16[64,1536]{1,0:T(8,128)(2,1)S(1)} %get-tuple-element.69), channel_id=1, source_target_pairs={{0,4},{4,0},{8,12},{12,8},{1,5},{5,1},{9,13},{13,9},{2,6},{6,2},{1... | collective-permute-start | bytes 589832 | tf_op jit(solution)/shard_map/ppermute | solution.py:198
  39.4 2.4 %collective-permute-start.14 = (bf16[2,128,512]{2,1,0:T(8,128)(2,1)S(1)}, bf16[2,128,512]{2,1,0:T(8,128)(2,1)S(1)}, u32[]{:S(2)}, u32[]{:S(2)}) collective-permute-start(bf16[2,128,512]{2,1,0:T(8,128)(2,1)S(1)} %collective-permute-done.12.refs_6_.refs_10_), channel_id=1, source_target_pairs={{0,1},{1,0},{2,3},{3,2},{4,5},{5,4},{6,7},{7,6},{8,9},{9,8},{10,11... | collective-permute-start | bytes 786440 | tf_op jit(solution)/shard_map/ppermute | solution.py:195
  39.5 17.0 %collective-permute-start.11 = (bf16[64,1536]{1,0:T(8,128)(2,1)S(1)}, bf16[64,1536]{1,0:T(8,128)(2,1)S(1)}, u32[]{:S(2)}, u32[]{:S(2)}) collective-permute-start(bf16[64,1536]{1,0:T(8,128)(2,1)S(1)} %add_convert_fusion.4.refs_14_), channel_id=1, source_target_pairs={{0,8},{4,12},{8,0},{12,4},{1,9},{5,13},{9,1},{13,5},{2,10},{6,14},... | collective-permute-start | bytes 589832 | tf_op jit(solution)/shard_map/ppermute | solution.py:198
  43.8 10.0 %collective-permute-start.15 = (bf16[64,1536]{1,0:T(8,128)(2,1)S(1)}, bf16[64,1536]{1,0:T(8,128)(2,1)S(1)}, u32[]{:S(2)}, u32[]{:S(2)}) collective-permute-start(bf16[64,1536]{1,0:T(8,128)(2,1)S(1)} %get-tuple-element.81), channel_id=1, source_target_pairs={{0,4},{4,0},{8,12},{12,8},{1,5},{5,1},{9,13},{13,9},{2,6},{6,2},{1... | collective-permute-start | bytes 589832 | tf_op jit(solution)/shard_map/ppermute | solution.py:198
  44.3 19.1 %collective-permute-start.17 = (bf16[64,1536]{1,0:T(8,128)(2,1)}, bf16[64,1536]{1,0:T(8,128)(2,1)S(1)}, u32[]{:S(2)}, u32[]{:S(2)}) collective-permute-start(bf16[64,1536]{1,0:T(8,128)(2,1)} %get-tuple-element.87), channel_id=1, source_target_pairs={{0,4},{4,0},{8,12},{12,8},{1,5},{5,1},{9,13},{13,9},{2,6},{6,2},{1... | collective-permute-start | bytes 589832 | tf_op jit(solution)/shard_map/ppermute | solution.py:198
  46.7 16.7 %collective-permute-start.27 = (bf16[3,128,512]{2,1,0:T(8,128)(2,1)}, bf16[3,128,512]{2,1,0:T(8,128)(2,1)S(1)}, u32[]{:S(2)}, u32[]{:S(2)}) collective-permute-start(bf16[3,128,512]{2,1,0:T(8,128)(2,1)} %get-tuple-element.115), channel_id=1, source_target_pairs={{0,2},{1,3},{2,0},{3,1},{4,6},{5,7},{6,4},{7,5},{8,10},{9,11},{10,... | collective-permute-start | bytes 1179656 | tf_op jit(solution)/shard_map/ppermute | solution.py:195
  53.9 11.3 %collective-permute-start.18 = (bf16[64,1536]{1,0:T(8,128)(2,1)S(1)}, bf16[64,1536]{1,0:T(8,128)(2,1)}, u32[]{:S(2)}, u32[]{:S(2)}) collective-permute-start(bf16[64,1536]{1,0:T(8,128)(2,1)S(1)} %add_convert_fusion.3.refs_5_), channel_id=1, source_target_pairs={{0,8},{4,12},{8,0},{12,4},{1,9},{5,13},{9,1},{13,5},{2,10},{6,14},... | collective-permute-start | bytes 589832 | tf_op jit(solution)/shard_map/ppermute | solution.py:198
  58.2 2.4 %collective-permute-start.16 = (f32[128,128]{1,0:T(8,128)S(1)}, f32[128,128]{1,0:T(8,128)S(1)}, u32[]{:S(2)}, u32[]{:S(2)}) collective-permute-start(f32[128,128]{1,0:T(8,128)S(1)} %get-tuple-element.85.refs_4_), channel_id=1, source_target_pairs={{0,1},{1,0},{2,3},{3,2},{4,5},{5,4},{6,7},{7,6},{8,9},{9,8},{10,11... | collective-permute-start | bytes 196616 | tf_op jit(solution)/shard_map/ppermute | solution.py:195
  62.9 9.8 %collective-permute-start.21 = (bf16[64,1536]{1,0:T(8,128)(2,1)S(1)}, bf16[64,1536]{1,0:T(8,128)(2,1)S(1)}, u32[]{:S(2)}, u32[]{:S(2)}) collective-permute-start(bf16[64,1536]{1,0:T(8,128)(2,1)S(1)} %get-tuple-element.90.refs_1_), channel_id=1, source_target_pairs={{0,4},{4,0},{8,12},{12,8},{1,5},{5,1},{9,13},{13,9},{2,6},{6,2},{1... | collective-permute-start | bytes 589832 | tf_op jit(solution)/shard_map/ppermute | solution.py:198
  63.0 11.8 %collective-permute-start.20 = (bf16[64,1536]{1,0:T(8,128)(2,1)S(1)}, bf16[64,1536]{1,0:T(8,128)(2,1)S(1)}, u32[]{:S(2)}, u32[]{:S(2)}) collective-permute-start(bf16[64,1536]{1,0:T(8,128)(2,1)S(1)} %get-tuple-element.90.refs_1_), channel_id=1, source_target_pairs={{0,8},{4,12},{8,0},{12,4},{1,9},{5,13},{9,1},{13,5},{2,10},{6,14},... | collective-permute-start | bytes 589832 | tf_op jit(solution)/shard_map/ppermute | solution.py:198
  63.4 25.9 %collective-permute-start.28 = (bf16[3,128,512]{2,1,0:T(8,128)(2,1)S(1)}, bf16[3,128,512]{2,1,0:T(8,128)(2,1)S(1)}, u32[]{:S(2)}, u32[]{:S(2)}) collective-permute-start(bf16[3,128,512]{2,1,0:T(8,128)(2,1)S(1)} %get-tuple-element.96.refs_5_), channel_id=1, source_target_pairs={{0,1},{1,0},{2,3},{3,2},{4,5},{5,4},{6,7},{7,6},{8,9},{9,8},{10,11... | collective-permute-start | bytes 1179656 | tf_op jit(solution)/shard_map/ppermute | solution.py:195
  63.4 25.9 %collective-permute-start.29 = (bf16[3,128,512]{2,1,0:T(8,128)(2,1)S(1)}, bf16[3,128,512]{2,1,0:T(8,128)(2,1)S(1)}, u32[]{:S(2)}, u32[]{:S(2)}) collective-permute-start(bf16[3,128,512]{2,1,0:T(8,128)(2,1)S(1)} %collective-permute-done.27.refs_6_), channel_id=1, source_target_pairs={{0,1},{1,0},{2,3},{3,2},{4,5},{5,4},{6,7},{7,6},{8,9},{9,8},{10,11... | collective-permute-start | bytes 1179656 | tf_op jit(solution)/shard_map/ppermute | solution.py:195
  67.5 7.3 %collective-permute-start.22 = (f32[64,128]{1,0:T(8,128)S(1)}, f32[64,128]{1,0:T(8,128)S(1)}, u32[]{:S(2)}, u32[]{:S(2)}) collective-permute-start(f32[64,128]{1,0:T(8,128)S(1)} %get-tuple-element.102.refs_3_.refs_13_), channel_id=1, source_target_pairs={{0,1},{1,0},{2,3},{3,2},{4,5},{5,4},{6,7},{7,6},{8,9},{9,8},{10,11... | collective-permute-start | bytes 98312 | tf_op jit(solution)/shard_map/ppermute | solution.py:195
  75.0 11.2 %collective-permute-start.24 = (bf16[64,1536]{1,0:T(8,128)(2,1)S(1)}, bf16[64,1536]{1,0:T(8,128)(2,1)S(1)}, u32[]{:S(2)}, u32[]{:S(2)}) collective-permute-start(bf16[64,1536]{1,0:T(8,128)(2,1)S(1)} %shard_map.87.refs_1_), channel_id=1, source_target_pairs={{0,4},{4,0},{8,12},{12,8},{1,5},{5,1},{9,13},{13,9},{2,6},{6,2},{1... | collective-permute-start | bytes 589832 | tf_op jit(solution)/shard_map/ppermute | solution.py:198
  75.1 11.2 %collective-permute-start.23 = (bf16[64,1536]{1,0:T(8,128)(2,1)S(1)}, bf16[64,1536]{1,0:T(8,128)(2,1)S(1)}, u32[]{:S(2)}, u32[]{:S(2)}) collective-permute-start(bf16[64,1536]{1,0:T(8,128)(2,1)S(1)} %shard_map.87.refs_1_), channel_id=1, source_target_pairs={{0,8},{4,12},{8,0},{12,4},{1,9},{5,13},{9,1},{13,5},{2,10},{6,14},... | collective-permute-start | bytes 589832 | tf_op jit(solution)/shard_map/ppermute | solution.py:198
  77.1 12.2 %collective-permute-start.25 = (bf16[64,1536]{1,0:T(8,128)(2,1)S(1)}, bf16[64,1536]{1,0:T(8,128)(2,1)S(1)}, u32[]{:S(2)}, u32[]{:S(2)}) collective-permute-start(bf16[64,1536]{1,0:T(8,128)(2,1)S(1)} %collective-permute-done.20.refs_3_), channel_id=1, source_target_pairs={{0,4},{4,0},{8,12},{12,8},{1,5},{5,1},{9,13},{13,9},{2,6},{6,2},{1... | collective-permute-start | bytes 589832 | tf_op jit(solution)/shard_map/ppermute | solution.py:198
  90.0 7.3 %collective-permute-start.26 = (bf16[64,1536]{1,0:T(8,128)(2,1)S(1)}, bf16[64,1536]{1,0:T(8,128)(2,1)S(1)}, u32[]{:S(2)}, u32[]{:S(2)}) collective-permute-start(bf16[64,1536]{1,0:T(8,128)(2,1)S(1)} %collective-permute-done.23.refs_3_), channel_id=1, source_target_pairs={{0,4},{4,0},{8,12},{12,8},{1,5},{5,1},{9,13},{13,9},{2,6},{6,2},{1... | collective-permute-start | bytes 589832 | tf_op jit(solution)/shard_map/ppermute | solution.py:198
  91.6 5.6 %collective-permute-start.31 = (bf16[128,512]{1,0:T(8,128)(2,1)S(1)}, bf16[128,512]{1,0:T(8,128)(2,1)S(1)}, u32[]{:S(2)}, u32[]{:S(2)}) collective-permute-start(bf16[128,512]{1,0:T(8,128)(2,1)S(1)} %get-tuple-element.132), channel_id=1, source_target_pairs={{0,2},{1,3},{2,0},{3,1},{4,6},{5,7},{6,4},{7,5},{8,10},{9,11},{10,... | collective-permute-start | bytes 393224 | tf_op jit(solution)/shard_map/ppermute | solution.py:195
  98.1 6.4 %collective-permute-start.33 = (bf16[128,512]{1,0:T(8,128)(2,1)S(1)}, bf16[128,512]{1,0:T(8,128)(2,1)S(1)}, u32[]{:S(2)}, u32[]{:S(2)}) collective-permute-start(bf16[128,512]{1,0:T(8,128)(2,1)S(1)} %get-tuple-element.128), channel_id=1, source_target_pairs={{0,2},{1,3},{2,0},{3,1},{4,6},{5,7},{6,4},{7,5},{8,10},{9,11},{10,... | collective-permute-start | bytes 393224 | tf_op jit(solution)/shard_map/ppermute | solution.py:195
  99.7 7.2 %collective-permute-start.35 = (bf16[128,512]{1,0:T(8,128)(2,1)S(1)}, bf16[128,512]{1,0:T(8,128)(2,1)S(1)}, u32[]{:S(2)}, u32[]{:S(2)}) collective-permute-start(bf16[128,512]{1,0:T(8,128)(2,1)S(1)} %get-tuple-element.130), channel_id=1, source_target_pairs={{0,2},{1,3},{2,0},{3,1},{4,6},{5,7},{6,4},{7,5},{8,10},{9,11},{10,... | collective-permute-start | bytes 393224 | tf_op jit(solution)/shard_map/ppermute | solution.py:195
  (17 other events, 35.9 us)

commit v12 on v11

--- a/solution.py
+++ b/solution.py
@@ -376,11 +376,13 @@
     queries = (first_query,) + queries[1:]
     full_two = spread_on(first_two)
     full_two[1] = direct_two
-    out_zero = returned(readout(0, full_zero))
+    total_zero = readout(0, full_zero)
     total_one = readout(1, full_one)
-    waited = (full_two[planes - 1], out_zero, total_one)
-    full_two[planes - 1], out_zero, total_one = lax.optimization_barrier(waited)
-    out_one = returned(total_one)
+    both = jnp.stack([total_zero, total_one])
+    far_both = send(both[:, tokens:], 2)
+    full_two[planes - 1], far_both = lax.optimization_barrier((full_two[planes - 1], far_both))
+    out_zero = ordered(y, both[0, :tokens], far_both[0], 1)
+    out_one = ordered(y, both[1, :tokens], far_both[1], 1)
     out_two = returned(readout(2, full_two))
     return jnp.stack([out_zero, out_one, out_two])
 

time: 108 us -> 111 us (1.028)
  starting transfers between devices: 28 us -> 30.8 us
  waiting for transfers between devices: 58.8 us -> 57.4 us
    ppermute x21 -> x20, waiting for transfers between devices: 13.6 us -> 7.48 us  [send(): return lax.ppermute(array, 'quad', [(q, q ^ offset) for q in range(4)])]
    ppermute x15, waiting for transfers between devices: 45.2 us -> 50 us  [to_plane(): return lax.ppermute(array, 'plane', [(z, z ^ bit) for z in range(planes)])]
    ppermute x21 -> x20, starting transfers between devices: 9.14 us -> 12.1 us  [send(): return lax.ppermute(array, 'quad', [(q, q ^ offset) for q in range(4)])]
    unnamed x26 -> x30, local copies, waits for them, and re-layouts: 6.09 us -> 5.69 us
  transfers between devices with their start and end apart: 36 -> 35, of which waited for: 17 -> 16; matrix products, arithmetic and copies ran while one was open for 4% -> 6% of each run, Pallas kernels for 5% -> 5%
where the time goes in v12:
time: 111 us
  waiting for transfers between devices  57.4 us (52%)
  starting transfers between devices  30.8 us (28%)
  local copies, waits for them, and re-layouts  9.7 us (9%)
  Pallas kernels  6.85 us (6%)
  other arithmetic  4.18 us (4%)
  between operations  1.74 us (2%)
    ppermute x15, waiting for transfers between devices, to_plane(): return lax.ppermute(array, 'plane', [(z, z ^ bit) for z in range(planes)])  50 us
    ppermute x15, starting transfers between devices, to_plane(): return lax.ppermute(array, 'plane', [(z, z ^ bit) for z in range(planes)])  18.7 us
    ppermute x20, starting transfers between devices, send(): return lax.ppermute(array, 'quad', [(q, q ^ offset) for q in range(4)])  12.1 us
    ppermute x20, waiting for transfers between devices, send(): return lax.ppermute(array, 'quad', [(q, q ^ offset) for q in range(4)])  7.48 us
    pallas_call x9, Pallas kernels, call(): pl.pallas_call(kernel, out_shape=shapes, in_specs=[pl.BlockSpec(memory_sp...  6.85 us
    unnamed x30, local copies, waits for them, and re-layouts  5.69 us
  transfers between devices with their start and end apart: 35, of which 16 were waited for; matrix products, arithmetic and copies ran while one was open for 6% of the time, Pallas kernels for 5%

profile of v12, /device:TPU:0, one launch (start us, length us, event | category | flops | bytes accessed | tf_op | source)
XLA Modules:
  0.0 110.8 jit_solution(4181291336556589428)
XLA Ops:
  2.3 3.0 %collective-permute-start = (bf16[32,1280]{1,0:T(8,128)(2,1)S(1)}, bf16[32,1280]{1,0:T(8,128)(2,1)S(1)}, u32[]{:S(2)}, u32[]{:S(2)}) collective-permute-start(bf16[32,1280]{1,0:T(8,128)(2,1)S(1)} %get-tuple-element.132), channel_id=1, source_target_pairs={{0,2},{1,3},{2,0},{3,1},{4,6},{5,7},{6,4},{7,5},{8,10},{9,11},{10,... | collective-permute-start | bytes 245768 | tf_op jit(solution)/shard_map/ppermute | solution.py:195
  9.1 2.1 %collective-permute-start.6 = (bf16[2,128,512]{2,1,0:T(8,128)(2,1)S(1)}, bf16[2,128,512]{2,1,0:T(8,128)(2,1)S(1)}, u32[]{:S(2)}, u32[]{:S(2)}) collective-permute-start(bf16[2,128,512]{2,1,0:T(8,128)(2,1)S(1)} %get-tuple-element.121), channel_id=1, source_target_pairs={{0,2},{1,3},{2,0},{3,1},{4,6},{5,7},{6,4},{7,5},{8,10},{9,11},{10,... | collective-permute-start | bytes 786440 | tf_op jit(solution)/shard_map/ppermute | solution.py:195
  11.2 2.6 %collective-permute-start.4 = (bf16[64,1536]{1,0:T(8,128)(2,1)S(1)}, bf16[64,1536]{1,0:T(8,128)(2,1)S(1)}, u32[]{:S(2)}, u32[]{:S(2)}) collective-permute-start(bf16[64,1536]{1,0:T(8,128)(2,1)S(1)} %pad_maximum_fusion.4.refs_1_.refs_0_.refs_4_), channel_id=1, source_target_pairs={{0,8},{4,12},{8,0},{12,4},{1,9},{5,13},{9,1},{13,5},{2,10},{6,14},... | collective-permute-start | bytes 589832 | tf_op jit(solution)/shard_map/ppermute | solution.py:198
  13.8 1.6 %collective-permute-start.3 = (bf16[64,1536]{1,0:T(8,128)(2,1)S(1)}, bf16[64,1536]{1,0:T(8,128)(2,1)S(1)}, u32[]{:S(2)}, u32[]{:S(2)}) collective-permute-start(bf16[64,1536]{1,0:T(8,128)(2,1)S(1)} %pad_maximum_fusion.4.refs_1_.refs_0_.refs_4_), channel_id=1, source_target_pairs={{0,4},{4,0},{8,12},{12,8},{1,5},{5,1},{9,13},{13,9},{2,6},{6,2},{1... | collective-permute-start | bytes 589832 | tf_op jit(solution)/shard_map/ppermute | solution.py:198
  15.3 7.6 %collective-permute-done.4.refs_3_.refs_11_ = bf16[64,1536]{1,0:T(8,128)(2,1)S(1)} collective-permute-done((bf16[64,1536]{1,0:T(8,128)(2,1)S(1)}, bf16[64,1536]{1,0:T(8,128)(2,1)S(1)}, u32[]{:S(2)}, u32[]{:S(2)}) %collective-permute-start.4) | collective-permute-done | bytes 196640 | tf_op jit(solution)/shard_map/ppermute | solution.py:198
  23.3 1.0 pad_maximum_fusion.2
  24.3 1.5 %collective-permute-start.5 = (bf16[64,1536]{1,0:T(8,128)(2,1)S(1)}, bf16[64,1536]{1,0:T(8,128)(2,1)S(1)}, u32[]{:S(2)}, u32[]{:S(2)}) collective-permute-start(bf16[64,1536]{1,0:T(8,128)(2,1)S(1)} %collective-permute-done.4.refs_3_.refs_11_), channel_id=1, source_target_pairs={{0,4},{4,0},{8,12},{12,8},{1,5},{5,1},{9,13},{13,9},{2,6},{6,2},{1... | collective-permute-start | bytes 589832 | tf_op jit(solution)/shard_map/ppermute | solution.py:198
  26.5 5.2 %collective-permute-done.5.refs_4_ = bf16[64,1536]{1,0:T(8,128)(2,1)S(1)} collective-permute-done((bf16[64,1536]{1,0:T(8,128)(2,1)S(1)}, bf16[64,1536]{1,0:T(8,128)(2,1)S(1)}, u32[]{:S(2)}, u32[]{:S(2)}) %collective-permute-start.5) | collective-permute-done | bytes 196640 | tf_op jit(solution)/shard_map/ppermute | solution.py:198
  31.7 1.3 %shard_map.82 = (f32[64,1536]{1,0:T(8,128)S(1)}, bf16[64,1536]{1,0:T(8,128)(2,1)S(1)}, f32[64,1536]{1,0:T(8,128)S(1)}, bf16[64,1536]{1,0:T(8,128)(2,1)S(1)}) custom-call(s32[1]{0:T(128)} %bitcast.refs_0_, bf16[64,1536]{1,0:T(8,128)(2,1)S(1)} %pad_maximum_fusion.4.refs_1_.refs_0_.refs_4_, ...), custom_call_target="tpu_custom_call" | custom-call | flops 805306368 | bytes 1024 | tf_op jit(solution)/shard_map/pallas_call | solution.py:21
  33.0 1.5 %collective-permute-start.9 = (bf16[64,1536]{1,0:T(8,128)(2,1)S(1)}, bf16[64,1536]{1,0:T(8,128)(2,1)S(1)}, u32[]{:S(2)}, u32[]{:S(2)}) collective-permute-start(bf16[64,1536]{1,0:T(8,128)(2,1)S(1)} %get-tuple-element.67), channel_id=1, source_target_pairs={{0,4},{4,0},{8,12},{12,8},{1,5},{5,1},{9,13},{13,9},{2,6},{6,2},{1... | collective-permute-start | bytes 589832 | tf_op jit(solution)/shard_map/ppermute | solution.py:198
  34.5 5.1 %collective-permute-done.9.refs_13_ = bf16[64,1536]{1,0:T(8,128)(2,1)S(1)} collective-permute-done((bf16[64,1536]{1,0:T(8,128)(2,1)S(1)}, bf16[64,1536]{1,0:T(8,128)(2,1)S(1)}, u32[]{:S(2)}, u32[]{:S(2)}) %collective-permute-start.9) | collective-permute-done | bytes 196640 | tf_op jit(solution)/shard_map/ppermute | solution.py:198
  39.6 1.4 %collective-permute-start.10 = (bf16[64,1536]{1,0:T(8,128)(2,1)S(1)}, bf16[64,1536]{1,0:T(8,128)(2,1)S(1)}, u32[]{:S(2)}, u32[]{:S(2)}) collective-permute-start(bf16[64,1536]{1,0:T(8,128)(2,1)S(1)} %get-tuple-element.68), channel_id=1, source_target_pairs={{0,4},{4,0},{8,12},{12,8},{1,5},{5,1},{9,13},{13,9},{2,6},{6,2},{1... | collective-permute-start | bytes 589832 | tf_op jit(solution)/shard_map/ppermute | solution.py:198
  41.1 2.4 %collective-permute-start.11 = (bf16[64,1536]{1,0:T(8,128)(2,1)S(1)}, bf16[64,1536]{1,0:T(8,128)(2,1)S(1)}, u32[]{:S(2)}, u32[]{:S(2)}) collective-permute-start(bf16[64,1536]{1,0:T(8,128)(2,1)S(1)} %add_convert_fusion.4.refs_14_), channel_id=1, source_target_pairs={{0,8},{4,12},{8,0},{12,4},{1,9},{5,13},{9,1},{13,5},{2,10},{6,14},... | collective-permute-start | bytes 589832 | tf_op jit(solution)/shard_map/ppermute | solution.py:198
  43.5 2.0 %shard_map.83 = (f32[64,1536]{1,0:T(8,128)S(1)}, bf16[64,1536]{1,0:T(8,128)(2,1)}, f32[64,1536]{1,0:T(8,128)S(1)}, bf16[64,1536]{1,0:T(8,128)(2,1)S(1)}) custom-call(s32[1]{0:T(128)} %bitcast.refs_0_, bf16[64,1536]{1,0:T(8,128)(2,1)S(1)} %pad_maximum_fusion.4.refs_1_.refs_0_.refs_4_, bf16[64,1536]{1,0:T(8,128)(2,1)S(1)} %collective-permute-done.3.refs_2_.refs_9_.refs_10_, ...), custom_call_target="tpu_custom_call" | custom-call | flops 805306368 | bytes 1024 | tf_op jit(solution)/shard_map/pallas_call | solution.py:21
  45.9 1.5 %collective-permute-start.17 = (bf16[64,1536]{1,0:T(8,128)(2,1)}, bf16[64,1536]{1,0:T(8,128)(2,1)S(1)}, u32[]{:S(2)}, u32[]{:S(2)}) collective-permute-start(bf16[64,1536]{1,0:T(8,128)(2,1)} %get-tuple-element.86), channel_id=1, source_target_pairs={{0,4},{4,0},{8,12},{12,8},{1,5},{5,1},{9,13},{13,9},{2,6},{6,2},{1... | collective-permute-start | bytes 589832 | tf_op jit(solution)/shard_map/ppermute | solution.py:198
  48.8 6.6 %collective-permute-done.15 = bf16[64,1536]{1,0:T(8,128)(2,1)S(1)} collective-permute-done((bf16[64,1536]{1,0:T(8,128)(2,1)S(1)}, bf16[64,1536]{1,0:T(8,128)(2,1)S(1)}, u32[]{:S(2)}, u32[]{:S(2)}) %collective-permute-start.15) | collective-permute-done | bytes 196640 | tf_op jit(solution)/shard_map/ppermute | solution.py:198
  55.5 2.6 %collective-permute-start.18 = (bf16[64,1536]{1,0:T(8,128)(2,1)S(1)}, bf16[64,1536]{1,0:T(8,128)(2,1)}, u32[]{:S(2)}, u32[]{:S(2)}) collective-permute-start(bf16[64,1536]{1,0:T(8,128)(2,1)S(1)} %add_convert_fusion.3.refs_5_), channel_id=1, source_target_pairs={{0,8},{4,12},{8,0},{12,4},{1,9},{5,13},{9,1},{13,5},{2,10},{6,14},... | collective-permute-start | bytes 589832 | tf_op jit(solution)/shard_map/ppermute | solution.py:198
  62.3 1.0 copy-done.1
  63.3 1.0 copy-done.3
  65.6 1.2 %collective-permute-done.18.refs_2_ = bf16[64,1536]{1,0:T(8,128)(2,1)} collective-permute-done((bf16[64,1536]{1,0:T(8,128)(2,1)S(1)}, bf16[64,1536]{1,0:T(8,128)(2,1)}, u32[]{:S(2)}, u32[]{:S(2)}) %collective-permute-start.18) | collective-permute-done | bytes 196640 | tf_op jit(solution)/shard_map/ppermute | solution.py:198
  66.8 1.1 shard_map.86
  68.0 1.2 %collective-permute-done.19.refs_2_ = f32[64,128]{1,0:T(8,128)S(1)} collective-permute-done((f32[64,128]{1,0:T(8,128)S(1)}, f32[64,128]{1,0:T(8,128)S(1)}, u32[]{:S(2)}, u32[]{:S(2)}) %collective-permute-start.19) | collective-permute-done | bytes 32800 | tf_op jit(solution)/shard_map/ppermute | solution.py:195
  69.3 5.0 %collective-permute-done.21.refs_2_ = bf16[64,1536]{1,0:T(8,128)(2,1)S(1)} collective-permute-done((bf16[64,1536]{1,0:T(8,128)(2,1)S(1)}, bf16[64,1536]{1,0:T(8,128)(2,1)S(1)}, u32[]{:S(2)}, u32[]{:S(2)}) %collective-permute-start.21) | collective-permute-done | bytes 196640 | tf_op jit(solution)/shard_map/ppermute | solution.py:198
  74.4 2.2 %collective-permute-done.20.refs_3_ = bf16[64,1536]{1,0:T(8,128)(2,1)S(1)} collective-permute-done((bf16[64,1536]{1,0:T(8,128)(2,1)S(1)}, bf16[64,1536]{1,0:T(8,128)(2,1)S(1)}, u32[]{:S(2)}, u32[]{:S(2)}) %collective-permute-start.20) | collective-permute-done | bytes 196640 | tf_op jit(solution)/shard_map/ppermute | solution.py:198
  76.7 2.0 %collective-permute-start.23 = (bf16[64,1536]{1,0:T(8,128)(2,1)S(1)}, bf16[64,1536]{1,0:T(8,128)(2,1)S(1)}, u32[]{:S(2)}, u32[]{:S(2)}) collective-permute-start(bf16[64,1536]{1,0:T(8,128)(2,1)S(1)} %shard_map.87.refs_1_), channel_id=1, source_target_pairs={{0,8},{4,12},{8,0},{12,4},{1,9},{5,13},{9,1},{13,5},{2,10},{6,14},... | collective-permute-start | bytes 589832 | tf_op jit(solution)/shard_map/ppermute | solution.py:198
  79.0 7.9 %collective-permute-done.24.refs_2_ = bf16[64,1536]{1,0:T(8,128)(2,1)S(1)} collective-permute-done((bf16[64,1536]{1,0:T(8,128)(2,1)S(1)}, bf16[64,1536]{1,0:T(8,128)(2,1)S(1)}, u32[]{:S(2)}, u32[]{:S(2)}) %collective-permute-start.24) | collective-permute-done | bytes 196640 | tf_op jit(solution)/shard_map/ppermute | solution.py:198
  86.9 2.3 %collective-permute-done.25.refs_4_ = bf16[64,1536]{1,0:T(8,128)(2,1)S(1)} collective-permute-done((bf16[64,1536]{1,0:T(8,128)(2,1)S(1)}, bf16[64,1536]{1,0:T(8,128)(2,1)S(1)}, u32[]{:S(2)}, u32[]{:S(2)}) %collective-permute-start.25) | collective-permute-done | bytes 196640 | tf_op jit(solution)/shard_map/ppermute | solution.py:198
  92.4 2.5 %collective-permute-start.32 = (bf16[2,128,512]{2,1,0:T(8,128)(2,1)S(1)}, bf16[2,128,512]{2,1,0:T(8,128)(2,1)S(1)}, u32[]{:S(2)}, u32[]{:S(2)}) collective-permute-start(bf16[2,128,512]{2,1,0:T(8,128)(2,1)S(1)} %pad_maximum_fusion.3), channel_id=1, source_target_pairs={{0,2},{1,3},{2,0},{3,1},{4,6},{5,7},{6,4},{7,5},{8,10},{9,11},{10,... | collective-permute-start | bytes 786440 | tf_op jit(solution)/shard_map/ppermute | solution.py:195
  95.1 6.6 %collective-permute-done.30.refs_4_ = bf16[64,1536]{1,0:T(8,128)(2,1)S(1)} collective-permute-done((bf16[64,1536]{1,0:T(8,128)(2,1)S(1)}, bf16[64,1536]{1,0:T(8,128)(2,1)S(1)}, u32[]{:S(2)}, u32[]{:S(2)}) %collective-permute-start.30) | collective-permute-done | bytes 196640 | tf_op jit(solution)/shard_map/ppermute | solution.py:198
  102.5 1.5 %collective-permute-done.33 = bf16[256,512]{1,0:T(8,128)(2,1)S(1)} collective-permute-done((bf16[256,512]{1,0:T(8,128)(2,1)S(1)}, bf16[256,512]{1,0:T(8,128)(2,1)S(1)}, u32[]{:S(2)}, u32[]{:S(2)}) %collective-permute-start.33) | collective-permute-done | bytes 262176 | tf_op jit(solution)/shard_map/ppermute | solution.py:195
  104.1 1.7 %collective-permute-start.34 = (bf16[128,512]{1,0:T(8,128)(2,1)S(1)}, bf16[128,512]{1,0:T(8,128)(2,1)S(1)}, u32[]{:S(2)}, u32[]{:S(2)}) collective-permute-start(bf16[128,512]{1,0:T(8,128)(2,1)S(1)} %get-tuple-element.128), channel_id=1, source_target_pairs={{0,2},{1,3},{2,0},{3,1},{4,6},{5,7},{6,4},{7,5},{8,10},{9,11},{10,... | collective-permute-start | bytes 393224 | tf_op jit(solution)/shard_map/ppermute | solution.py:195
  106.0 3.7 %collective-permute-done.34 = bf16[128,512]{1,0:T(8,128)(2,1)S(1)} collective-permute-done((bf16[128,512]{1,0:T(8,128)(2,1)S(1)}, bf16[128,512]{1,0:T(8,128)(2,1)S(1)}, u32[]{:S(2)}, u32[]{:S(2)}) %collective-permute-start.34) | collective-permute-done | bytes 131104 | tf_op jit(solution)/shard_map/ppermute | solution.py:195
  (127 shorter events, 19.1 us)
Async XLA Ops:
  2.3 6.6 %collective-permute-start = (bf16[32,1280]{1,0:T(8,128)(2,1)S(1)}, bf16[32,1280]{1,0:T(8,128)(2,1)S(1)}, u32[]{:S(2)}, u32[]{:S(2)}) collective-permute-start(bf16[32,1280]{1,0:T(8,128)(2,1)S(1)} %get-tuple-element.132), channel_id=1, source_target_pairs={{0,2},{1,3},{2,0},{3,1},{4,6},{5,7},{6,4},{7,5},{8,10},{9,11},{10,... | collective-permute-start | bytes 245768 | tf_op jit(solution)/shard_map/ppermute | solution.py:195
  5.5 3.5 %collective-permute-start.2 = (bf16[32,256]{1,0:T(8,128)(2,1)S(1)}, bf16[32,256]{1,0:T(8,128)(2,1)S(1)}, u32[]{:S(2)}, u32[]{:S(2)}) collective-permute-start(bf16[32,256]{1,0:T(8,128)(2,1)S(1)} %select_n.187), channel_id=1, source_target_pairs={{0,3},{1,2},{2,1},{3,0},{4,7},{5,6},{6,5},{7,4},{8,11},{9,10},{10,... | collective-permute-start | bytes 49160 | tf_op jit(solution)/shard_map/ppermute | solution.py:195
  5.7 3.2 %collective-permute-start.1 = (bf16[32,256]{1,0:T(8,128)(2,1)S(1)}, bf16[32,256]{1,0:T(8,128)(2,1)S(1)}, u32[]{:S(2)}, u32[]{:S(2)}) collective-permute-start(bf16[32,256]{1,0:T(8,128)(2,1)S(1)} %select_n.184), channel_id=1, source_target_pairs={{0,1},{1,0},{2,3},{3,2},{4,5},{5,4},{6,7},{7,6},{8,9},{9,8},{10,11... | collective-permute-start | bytes 49160 | tf_op jit(solution)/shard_map/ppermute | solution.py:195
  9.1 14.0 %collective-permute-start.6 = (bf16[2,128,512]{2,1,0:T(8,128)(2,1)S(1)}, bf16[2,128,512]{2,1,0:T(8,128)(2,1)S(1)}, u32[]{:S(2)}, u32[]{:S(2)}) collective-permute-start(bf16[2,128,512]{2,1,0:T(8,128)(2,1)S(1)} %get-tuple-element.121), channel_id=1, source_target_pairs={{0,2},{1,3},{2,0},{3,1},{4,6},{5,7},{6,4},{7,5},{8,10},{9,11},{10,... | collective-permute-start | bytes 786440 | tf_op jit(solution)/shard_map/ppermute | solution.py:195
  11.2 11.8 %collective-permute-start.4 = (bf16[64,1536]{1,0:T(8,128)(2,1)S(1)}, bf16[64,1536]{1,0:T(8,128)(2,1)S(1)}, u32[]{:S(2)}, u32[]{:S(2)}) collective-permute-start(bf16[64,1536]{1,0:T(8,128)(2,1)S(1)} %pad_maximum_fusion.4.refs_1_.refs_0_.refs_4_), channel_id=1, source_target_pairs={{0,8},{4,12},{8,0},{12,4},{1,9},{5,13},{9,1},{13,5},{2,10},{6,14},... | collective-permute-start | bytes 589832 | tf_op jit(solution)/shard_map/ppermute | solution.py:198
  13.8 9.4 %collective-permute-start.3 = (bf16[64,1536]{1,0:T(8,128)(2,1)S(1)}, bf16[64,1536]{1,0:T(8,128)(2,1)S(1)}, u32[]{:S(2)}, u32[]{:S(2)}) collective-permute-start(bf16[64,1536]{1,0:T(8,128)(2,1)S(1)} %pad_maximum_fusion.4.refs_1_.refs_0_.refs_4_), channel_id=1, source_target_pairs={{0,4},{4,0},{8,12},{12,8},{1,5},{5,1},{9,13},{13,9},{2,6},{6,2},{1... | collective-permute-start | bytes 589832 | tf_op jit(solution)/shard_map/ppermute | solution.py:198
  15.3 10.5 %collective-permute-start.7 = (bf16[2,128,512]{2,1,0:T(8,128)(2,1)S(1)}, bf16[2,128,512]{2,1,0:T(8,128)(2,1)S(1)}, u32[]{:S(2)}, u32[]{:S(2)}) collective-permute-start(bf16[2,128,512]{2,1,0:T(8,128)(2,1)S(1)} %get-tuple-element.74.refs_5_.refs_9_), channel_id=1, source_target_pairs={{0,1},{1,0},{2,3},{3,2},{4,5},{5,4},{6,7},{7,6},{8,9},{9,8},{10,11... | collective-permute-start | bytes 786440 | tf_op jit(solution)/shard_map/ppermute | solution.py:195
  23.1 2.7 %collective-permute-start.8 = (bf16[2,128,512]{2,1,0:T(8,128)(2,1)S(1)}, bf16[2,128,512]{2,1,0:T(8,128)(2,1)S(1)}, u32[]{:S(2)}, u32[]{:S(2)}) collective-permute-start(bf16[2,128,512]{2,1,0:T(8,128)(2,1)S(1)} %collective-permute-done.6.refs_6_.refs_10_), channel_id=1, source_target_pairs={{0,1},{1,0},{2,3},{3,2},{4,5},{5,4},{6,7},{7,6},{8,9},{9,8},{10,11... | collective-permute-start | bytes 786440 | tf_op jit(solution)/shard_map/ppermute | solution.py:195
  24.3 7.4 %collective-permute-start.5 = (bf16[64,1536]{1,0:T(8,128)(2,1)S(1)}, bf16[64,1536]{1,0:T(8,128)(2,1)S(1)}, u32[]{:S(2)}, u32[]{:S(2)}) collective-permute-start(bf16[64,1536]{1,0:T(8,128)(2,1)S(1)} %collective-permute-done.4.refs_3_.refs_11_), channel_id=1, source_target_pairs={{0,4},{4,0},{8,12},{12,8},{1,5},{5,1},{9,13},{13,9},{2,6},{6,2},{1... | collective-permute-start | bytes 589832 | tf_op jit(solution)/shard_map/ppermute | solution.py:198
  25.9 15.1 %collective-permute-start.12 = (bf16[2,128,512]{2,1,0:T(8,128)(2,1)S(1)}, bf16[2,128,512]{2,1,0:T(8,128)(2,1)S(1)}, u32[]{:S(2)}, u32[]{:S(2)}) collective-permute-start(bf16[2,128,512]{2,1,0:T(8,128)(2,1)S(1)} %get-tuple-element.117), channel_id=1, source_target_pairs={{0,2},{1,3},{2,0},{3,1},{4,6},{5,7},{6,4},{7,5},{8,10},{9,11},{10,... | collective-permute-start | bytes 786440 | tf_op jit(solution)/shard_map/ppermute | solution.py:195
  33.0 6.6 %collective-permute-start.9 = (bf16[64,1536]{1,0:T(8,128)(2,1)S(1)}, bf16[64,1536]{1,0:T(8,128)(2,1)S(1)}, u32[]{:S(2)}, u32[]{:S(2)}) collective-permute-start(bf16[64,1536]{1,0:T(8,128)(2,1)S(1)} %get-tuple-element.67), channel_id=1, source_target_pairs={{0,4},{4,0},{8,12},{12,8},{1,5},{5,1},{9,13},{13,9},{2,6},{6,2},{1... | collective-permute-start | bytes 589832 | tf_op jit(solution)/shard_map/ppermute | solution.py:198
  34.5 9.0 %collective-permute-start.13 = (bf16[2,128,512]{2,1,0:T(8,128)(2,1)S(1)}, bf16[2,128,512]{2,1,0:T(8,128)(2,1)S(1)}, u32[]{:S(2)}, u32[]{:S(2)}) collective-permute-start(bf16[2,128,512]{2,1,0:T(8,128)(2,1)S(1)} %get-tuple-element.96.refs_5_.refs_9_), channel_id=1, source_target_pairs={{0,1},{1,0},{2,3},{3,2},{4,5},{5,4},{6,7},{7,6},{8,9},{9,8},{10,11... | collective-permute-start | bytes 786440 | tf_op jit(solution)/shard_map/ppermute | solution.py:195
  39.6 18.5 %collective-permute-start.10 = (bf16[64,1536]{1,0:T(8,128)(2,1)S(1)}, bf16[64,1536]{1,0:T(8,128)(2,1)S(1)}, u32[]{:S(2)}, u32[]{:S(2)}) collective-permute-start(bf16[64,1536]{1,0:T(8,128)(2,1)S(1)} %get-tuple-element.68), channel_id=1, source_target_pairs={{0,4},{4,0},{8,12},{12,8},{1,5},{5,1},{9,13},{13,9},{2,6},{6,2},{1... | collective-permute-start | bytes 589832 | tf_op jit(solution)/shard_map/ppermute | solution.py:198
  41.0 2.4 %collective-permute-start.14 = (bf16[2,128,512]{2,1,0:T(8,128)(2,1)S(1)}, bf16[2,128,512]{2,1,0:T(8,128)(2,1)S(1)}, u32[]{:S(2)}, u32[]{:S(2)}) collective-permute-start(bf16[2,128,512]{2,1,0:T(8,128)(2,1)S(1)} %collective-permute-done.12.refs_6_.refs_10_), channel_id=1, source_target_pairs={{0,1},{1,0},{2,3},{3,2},{4,5},{5,4},{6,7},{7,6},{8,9},{9,8},{10,11... | collective-permute-start | bytes 786440 | tf_op jit(solution)/shard_map/ppermute | solution.py:195
  41.1 17.0 %collective-permute-start.11 = (bf16[64,1536]{1,0:T(8,128)(2,1)S(1)}, bf16[64,1536]{1,0:T(8,128)(2,1)S(1)}, u32[]{:S(2)}, u32[]{:S(2)}) collective-permute-start(bf16[64,1536]{1,0:T(8,128)(2,1)S(1)} %add_convert_fusion.4.refs_14_), channel_id=1, source_target_pairs={{0,8},{4,12},{8,0},{12,4},{1,9},{5,13},{9,1},{13,5},{2,10},{6,14},... | collective-permute-start | bytes 589832 | tf_op jit(solution)/shard_map/ppermute | solution.py:198
  45.5 10.0 %collective-permute-start.15 = (bf16[64,1536]{1,0:T(8,128)(2,1)S(1)}, bf16[64,1536]{1,0:T(8,128)(2,1)S(1)}, u32[]{:S(2)}, u32[]{:S(2)}) collective-permute-start(bf16[64,1536]{1,0:T(8,128)(2,1)S(1)} %get-tuple-element.80), channel_id=1, source_target_pairs={{0,4},{4,0},{8,12},{12,8},{1,5},{5,1},{9,13},{13,9},{2,6},{6,2},{1... | collective-permute-start | bytes 589832 | tf_op jit(solution)/shard_map/ppermute | solution.py:198
  45.9 19.1 %collective-permute-start.17 = (bf16[64,1536]{1,0:T(8,128)(2,1)}, bf16[64,1536]{1,0:T(8,128)(2,1)S(1)}, u32[]{:S(2)}, u32[]{:S(2)}) collective-permute-start(bf16[64,1536]{1,0:T(8,128)(2,1)} %get-tuple-element.86), channel_id=1, source_target_pairs={{0,4},{4,0},{8,12},{12,8},{1,5},{5,1},{9,13},{13,9},{2,6},{6,2},{1... | collective-permute-start | bytes 589832 | tf_op jit(solution)/shard_map/ppermute | solution.py:198
  48.3 16.7 %collective-permute-start.26 = (bf16[3,128,512]{2,1,0:T(8,128)(2,1)}, bf16[3,128,512]{2,1,0:T(8,128)(2,1)S(1)}, u32[]{:S(2)}, u32[]{:S(2)}) collective-permute-start(bf16[3,128,512]{2,1,0:T(8,128)(2,1)} %get-tuple-element.113), channel_id=1, source_target_pairs={{0,2},{1,3},{2,0},{3,1},{4,6},{5,7},{6,4},{7,5},{8,10},{9,11},{10,... | collective-permute-start | bytes 1179656 | tf_op jit(solution)/shard_map/ppermute | solution.py:195
  55.5 11.3 %collective-permute-start.18 = (bf16[64,1536]{1,0:T(8,128)(2,1)S(1)}, bf16[64,1536]{1,0:T(8,128)(2,1)}, u32[]{:S(2)}, u32[]{:S(2)}) collective-permute-start(bf16[64,1536]{1,0:T(8,128)(2,1)S(1)} %add_convert_fusion.3.refs_5_), channel_id=1, source_target_pairs={{0,8},{4,12},{8,0},{12,4},{1,9},{5,13},{9,1},{13,5},{2,10},{6,14},... | collective-permute-start | bytes 589832 | tf_op jit(solution)/shard_map/ppermute | solution.py:198
  59.8 2.4 %collective-permute-start.16 = (f32[128,128]{1,0:T(8,128)S(1)}, f32[128,128]{1,0:T(8,128)S(1)}, u32[]{:S(2)}, u32[]{:S(2)}) collective-permute-start(f32[128,128]{1,0:T(8,128)S(1)} %get-tuple-element.84.refs_4_), channel_id=1, source_target_pairs={{0,1},{1,0},{2,3},{3,2},{4,5},{5,4},{6,7},{7,6},{8,9},{9,8},{10,11... | collective-permute-start | bytes 196616 | tf_op jit(solution)/shard_map/ppermute | solution.py:195
  64.5 9.8 %collective-permute-start.21 = (bf16[64,1536]{1,0:T(8,128)(2,1)S(1)}, bf16[64,1536]{1,0:T(8,128)(2,1)S(1)}, u32[]{:S(2)}, u32[]{:S(2)}) collective-permute-start(bf16[64,1536]{1,0:T(8,128)(2,1)S(1)} %get-tuple-element.89.refs_1_), channel_id=1, source_target_pairs={{0,4},{4,0},{8,12},{12,8},{1,5},{5,1},{9,13},{13,9},{2,6},{6,2},{1... | collective-permute-start | bytes 589832 | tf_op jit(solution)/shard_map/ppermute | solution.py:198
  64.7 11.8 %collective-permute-start.20 = (bf16[64,1536]{1,0:T(8,128)(2,1)S(1)}, bf16[64,1536]{1,0:T(8,128)(2,1)S(1)}, u32[]{:S(2)}, u32[]{:S(2)}) collective-permute-start(bf16[64,1536]{1,0:T(8,128)(2,1)S(1)} %get-tuple-element.89.refs_1_), channel_id=1, source_target_pairs={{0,8},{4,12},{8,0},{12,4},{1,9},{5,13},{9,1},{13,5},{2,10},{6,14},... | collective-permute-start | bytes 589832 | tf_op jit(solution)/shard_map/ppermute | solution.py:198
  65.0 24.1 %collective-permute-start.27 = (bf16[3,128,512]{2,1,0:T(8,128)(2,1)S(1)}, bf16[3,128,512]{2,1,0:T(8,128)(2,1)S(1)}, u32[]{:S(2)}, u32[]{:S(2)}) collective-permute-start(bf16[3,128,512]{2,1,0:T(8,128)(2,1)S(1)} %get-tuple-element.94.refs_5_), channel_id=1, source_target_pairs={{0,1},{1,0},{2,3},{3,2},{4,5},{5,4},{6,7},{7,6},{8,9},{9,8},{10,11... | collective-permute-start | bytes 1179656 | tf_op jit(solution)/shard_map/ppermute | solution.py:195
  65.1 24.1 %collective-permute-start.28 = (bf16[3,128,512]{2,1,0:T(8,128)(2,1)S(1)}, bf16[3,128,512]{2,1,0:T(8,128)(2,1)S(1)}, u32[]{:S(2)}, u32[]{:S(2)}) collective-permute-start(bf16[3,128,512]{2,1,0:T(8,128)(2,1)S(1)} %collective-permute-done.26.refs_6_), channel_id=1, source_target_pairs={{0,1},{1,0},{2,3},{3,2},{4,5},{5,4},{6,7},{7,6},{8,9},{9,8},{10,11... | collective-permute-start | bytes 1179656 | tf_op jit(solution)/shard_map/ppermute | solution.py:195
  69.2 7.4 %collective-permute-start.22 = (f32[64,128]{1,0:T(8,128)S(1)}, f32[64,128]{1,0:T(8,128)S(1)}, u32[]{:S(2)}, u32[]{:S(2)}) collective-permute-start(f32[64,128]{1,0:T(8,128)S(1)} %get-tuple-element.100.refs_3_.refs_13_), channel_id=1, source_target_pairs={{0,1},{1,0},{2,3},{3,2},{4,5},{5,4},{6,7},{7,6},{8,9},{9,8},{10,11... | collective-permute-start | bytes 98312 | tf_op jit(solution)/shard_map/ppermute | solution.py:195
  76.7 10.2 %collective-permute-start.24 = (bf16[64,1536]{1,0:T(8,128)(2,1)S(1)}, bf16[64,1536]{1,0:T(8,128)(2,1)S(1)}, u32[]{:S(2)}, u32[]{:S(2)}) collective-permute-start(bf16[64,1536]{1,0:T(8,128)(2,1)S(1)} %shard_map.87.refs_1_), channel_id=1, source_target_pairs={{0,4},{4,0},{8,12},{12,8},{1,5},{5,1},{9,13},{13,9},{2,6},{6,2},{1... | collective-permute-start | bytes 589832 | tf_op jit(solution)/shard_map/ppermute | solution.py:198
  76.7 10.1 %collective-permute-start.23 = (bf16[64,1536]{1,0:T(8,128)(2,1)S(1)}, bf16[64,1536]{1,0:T(8,128)(2,1)S(1)}, u32[]{:S(2)}, u32[]{:S(2)}) collective-permute-start(bf16[64,1536]{1,0:T(8,128)(2,1)S(1)} %shard_map.87.refs_1_), channel_id=1, source_target_pairs={{0,8},{4,12},{8,0},{12,4},{1,9},{5,13},{9,1},{13,5},{2,10},{6,14},... | collective-permute-start | bytes 589832 | tf_op jit(solution)/shard_map/ppermute | solution.py:198
  78.7 10.4 %collective-permute-start.25 = (bf16[64,1536]{1,0:T(8,128)(2,1)S(1)}, bf16[64,1536]{1,0:T(8,128)(2,1)S(1)}, u32[]{:S(2)}, u32[]{:S(2)}) collective-permute-start(bf16[64,1536]{1,0:T(8,128)(2,1)S(1)} %collective-permute-done.20.refs_3_), channel_id=1, source_target_pairs={{0,4},{4,0},{8,12},{12,8},{1,5},{5,1},{9,13},{13,9},{2,6},{6,2},{1... | collective-permute-start | bytes 589832 | tf_op jit(solution)/shard_map/ppermute | solution.py:198
  90.5 1.7 %collective-permute-start.29 = (bf16[256,512]{1,0:T(8,128)(2,1)S(1)}, bf16[256,512]{1,0:T(8,128)(2,1)S(1)}, u32[]{:S(2)}, u32[]{:S(2)}) collective-permute-start(bf16[256,512]{1,0:T(8,128)(2,1)S(1)} %get-tuple-element.102), channel_id=1, source_target_pairs={{0,1},{1,0},{2,3},{3,2},{4,5},{5,4},{6,7},{7,6},{8,9},{9,8},{10,11... | collective-permute-start | bytes 786440 | tf_op jit(solution)/shard_map/ppermute | solution.py:195
  92.4 9.4 %collective-permute-start.32 = (bf16[2,128,512]{2,1,0:T(8,128)(2,1)S(1)}, bf16[2,128,512]{2,1,0:T(8,128)(2,1)S(1)}, u32[]{:S(2)}, u32[]{:S(2)}) collective-permute-start(bf16[2,128,512]{2,1,0:T(8,128)(2,1)S(1)} %pad_maximum_fusion.3), channel_id=1, source_target_pairs={{0,2},{1,3},{2,0},{3,1},{4,6},{5,7},{6,4},{7,5},{8,10},{9,11},{10,... | collective-permute-start | bytes 786440 | tf_op jit(solution)/shard_map/ppermute | solution.py:195
  94.8 6.9 %collective-permute-start.30 = (bf16[64,1536]{1,0:T(8,128)(2,1)S(1)}, bf16[64,1536]{1,0:T(8,128)(2,1)S(1)}, u32[]{:S(2)}, u32[]{:S(2)}) collective-permute-start(bf16[64,1536]{1,0:T(8,128)(2,1)S(1)} %collective-permute-done.23.refs_3_), channel_id=1, source_target_pairs={{0,4},{4,0},{8,12},{12,8},{1,5},{5,1},{9,13},{13,9},{2,6},{6,2},{1... | collective-permute-start | bytes 589832 | tf_op jit(solution)/shard_map/ppermute | solution.py:198
  104.1 5.6 %collective-permute-start.34 = (bf16[128,512]{1,0:T(8,128)(2,1)S(1)}, bf16[128,512]{1,0:T(8,128)(2,1)S(1)}, u32[]{:S(2)}, u32[]{:S(2)}) collective-permute-start(bf16[128,512]{1,0:T(8,128)(2,1)S(1)} %get-tuple-element.128), channel_id=1, source_target_pairs={{0,2},{1,3},{2,0},{3,1},{4,6},{5,7},{6,4},{7,5},{8,10},{9,11},{10,... | collective-permute-start | bytes 393224 | tf_op jit(solution)/shard_map/ppermute | solution.py:195
  (20 other events, 59.3 us)
